TPU v7x, 32 devices: a whole 2x2x4 slice. The times are simulated.
32 devices in a mesh: member: 2 (over y), lat: 4 (over z), lev: 2 (over x), fld: 2 (over core).
Axes of the slice: x: 2, y: 2, z: 4, core: 2. Of those that a mesh axis runs over, the one named last changes fastest.
Arguments:
- tracer: bfloat16 [8, 800, 1600], P('member', 'lat', ('lev', 'fld')), parts along dimension 0, may hold values from -6 to 6
- wind_east: bfloat16 [8, 800, 1600], P('member', 'lat', ('lev', 'fld')), parts along dimension 0, may hold values from -3 to 3
- wind_north: bfloat16 [8, 800, 1600], P('member', 'lat', ('lev', 'fld')), parts along dimension 0, may hold values from -3 to 3
- keep_m: int32 [800], P('lat'), may hold values from 9 to 400, as said below
- slot_wave: int32 [400], replicated, may hold values from 0 to 399, each once
Outputs:
- spectral: float32 [8, 400, 2, 400], P(('member', 'lev', 'fld'), 'lat'), parts along dimension 0
There are 2 independent parts, one for each index of `member`. A program takes and returns all parts, laid end to end along the dimension named above; an argument that names none is the same for every part. Nothing has to cross between parts.
Inputs may be any that keep to these rules, and one draw needn't show every extreme that they name: keep_m equals 400 at rows 399 and 400, and 9 at rows 0 and 799. Slot s of the output holds wavenumber slot_wave[s]; values of 400 or more mark empty slots.
All inputs are finite; a program needn't handle non-finite values.
Results may differ from a plain program's by a relative error of at most 0.0003.
Values may be sent and summed in bfloat16 or wider, within the bound.
No kernel may reach another device: no remote copies, remote signals or barrier semaphores. Data moves between devices by JAX's collectives and lax.ppermute only.
A program may use at most 64 MiB of HBM per device.

v0:
```python
import math

import jax
import jax.numpy as jnp
from jax import lax
from jax.sharding import PartitionSpec as P

M = 400
NLAT = 800
NLON = 1600


precise = lax.Precision.HIGHEST
block_rows = 16


def with_halo(block, sides, width):
    for axis, dim in sides:
        count = lax.axis_size(axis)
        forward = [(i, i + 1) for i in range(count - 1)]
        forward.append((count - 1, 0))
        backward = [(target, source) for source, target in forward]
        low = lax.ppermute(
            lax.slice_in_dim(block, block.shape[dim] - width, None, axis=dim), axis, forward
        )
        high = lax.ppermute(lax.slice_in_dim(block, 0, width, axis=dim), axis, backward)
        block = jnp.concatenate([low, block, high], axis=dim)
    return block


def fourier_table(wave_ids, lon_count):
    grid_index = jnp.arange(lon_count, dtype=jnp.int32)
    phase_index = wave_ids[:, None] * grid_index[None, :] % lon_count
    angles = 2.0 * math.pi / lon_count * phase_index.astype(jnp.float32)
    factor = 1.0 / math.sqrt(lon_count)
    return jnp.stack([jnp.cos(angles), -jnp.sin(angles)], axis=1) * factor


def advect(padded, east_wind, north_wind, first_row, lat_total):
    rows_here = padded.shape[1] - 2
    row_ids = first_row - 1 + jnp.arange(rows_here + 2, dtype=jnp.int32)
    inside = ((row_ids >= 0) & (row_ids < lat_total)).astype(jnp.float32)
    field_rows = padded.astype(jnp.float32) * inside[None, :, None]
    centre = field_rows[:, 1:-1, 1:-1]
    east_diff = field_rows[:, 1:-1, 2:] - field_rows[:, 1:-1, :-2]
    north_diff = field_rows[:, 2:, 1:-1] - field_rows[:, :-2, 1:-1]
    return (
        centre
        - 0.5 * east_wind.astype(jnp.float32) * east_diff
        - 0.5 * north_wind.astype(jnp.float32) * north_diff
    )


def legendre_setup(wave_ids, trunc_count, lat_total, lat_used):
    degree = jnp.minimum(wave_ids, trunc_count - 1).astype(jnp.float32)
    counter = jnp.arange(1, trunc_count, dtype=jnp.float32)
    log_terms = jnp.log1p(0.5 / counter)
    log_norm = jnp.sum(
        jnp.where(counter[None, :] <= degree[:, None], log_terms[None, :], 0.0), axis=1
    )
    colatitude = math.pi / lat_total * (jnp.arange(lat_used, dtype=jnp.float32) + 0.5)
    sine_rows = jnp.sin(colatitude)
    cosines = jnp.cos(colatitude)
    start_log = (
        0.5 * (log_norm[:, None] - math.log(2.0)) + degree[:, None] * jnp.log(sine_rows)[None, :]
    )
    return (degree, cosines, start_log)


def legendre_rows(recurrence, degree, cosines, first_order):
    before, current, log_scale = recurrence
    rows_list = [current]
    for offset in range(1, block_rows + 1):
        order_value = (first_order + offset).astype(jnp.float32)
        total_degree = degree[:, None] + order_value
        growth = jnp.sqrt(
            (4.0 * total_degree * total_degree - 1.0)
            / (total_degree * total_degree - degree[:, None] * degree[:, None])
        )
        lower_degree = total_degree - 1.0
        damping = jnp.sqrt(
            (lower_degree * lower_degree - degree[:, None] * degree[:, None])
            / jnp.maximum(4.0 * lower_degree * lower_degree - 1.0, 1.0)
        )
        advanced = growth * (cosines[None, :] * current - damping * before)
        before, current = (current, advanced)
        if offset < block_rows:
            rows_list.append(current)
    biggest = jnp.maximum(jnp.abs(before), jnp.abs(current))
    table_rows = jnp.stack(rows_list, axis=1) * jnp.exp(log_scale)[:, None, :]
    return (table_rows, (before / biggest, current / biggest, log_scale + jnp.log(biggest)))


def legendre_sweep(legendre_basis, contract, level_count, trunc_count):
    degree, cosines, start_log = legendre_basis
    slot_count = degree.shape[0]
    lat_used = cosines.shape[0]
    before = jnp.zeros((slot_count, lat_used), jnp.float32)
    current = jnp.ones((slot_count, lat_used), jnp.float32)
    result_init = jnp.zeros((level_count, slot_count, 2, trunc_count), jnp.float32)

    def advance(block_index, loop_carry):
        recurrence, result_now = loop_carry
        first_order = block_index * block_rows
        table_rows, recurrence = legendre_rows(recurrence, degree, cosines, first_order)
        orders = (first_order + jnp.arange(block_rows, dtype=jnp.int32)).astype(jnp.float32)
        inside_triangle = (orders[None, :] < trunc_count - degree[:, None]).astype(jnp.float32)
        partial_value = contract(table_rows * inside_triangle[:, :, None])
        result_now = lax.dynamic_update_slice_in_dim(result_now, partial_value, first_order, 3)
        return (recurrence, result_now)

    finished = lax.fori_loop(
        0, trunc_count // block_rows, advance, ((before, current, start_log), result_init)
    )
    return finished[1]


def shards(tracer, wind_east, wind_north, keep_m, slot_wave):
    lat_rows = tracer.shape[1]
    first_row = lax.axis_index("lat") * lat_rows
    fourier_matrix = fourier_table(slot_wave, NLON)
    padded = with_halo(tracer, (("lat", 1), (("lev", "fld"), 2)), 1)
    advected = advect(padded, wind_east, wind_north, first_row, NLAT)
    fourier = jnp.einsum(
        "sck,ijk->scij",
        fourier_matrix,
        lax.all_to_all(advected, ("lev", "fld"), split_axis=0, concat_axis=2, tiled=True),
        precision=precise,
    )
    kept_mask = (slot_wave[:, None] < keep_m[None, :]).astype(jnp.float32)
    fourier = fourier * kept_mask[:, None, None, :]
    spectral_in = lax.all_to_all(fourier, "lat", split_axis=0, concat_axis=3, tiled=True)
    slot_count = spectral_in.shape[0]
    my_waves = lax.dynamic_slice_in_dim(slot_wave, lax.axis_index("lat") * slot_count, slot_count)
    sines_all = jnp.sin(math.pi / NLAT * (jnp.arange(NLAT, dtype=jnp.float32) + 0.5))
    weighted = spectral_in * (sines_all * math.sqrt(2.0 / NLAT))[None, None, None, :]
    legendre_basis = legendre_setup(my_waves, M, NLAT, NLAT)

    def contract(table_rows):
        return jnp.einsum("stj,scij->isct", table_rows, weighted, precision=precise)

    return legendre_sweep(legendre_basis, contract, weighted.shape[2], M)


def solution(mesh):
    return jax.shard_map(
        shards,
        mesh=mesh,
        in_specs=(
            P("member", "lat", ("lev", "fld")),
            P("member", "lat", ("lev", "fld")),
            P("member", "lat", ("lev", "fld")),
            P("lat"),
            P(),
        ),
        out_specs=P(("member", "lev", "fld"), "lat", None, None),
        check_vma=False,
    )
```

profile of v0, /device:TPU:0, one launch (start us, length us, event | category | flops | bytes accessed | tf_op | source)
XLA Modules:
  0.0 815.6 jit_solution(2466917130893633722)
XLA Ops:
  26.6 12.4 %fusion.132 = (f32[400,1,1600]{2,0,1:T(8,128)S(1)}, f32[400,1,1600]{2,0,1:T(8,128)}) fusion(s32[400]{0:T(512)S(1)} %copy-done.1), kind=kLoop, calls=%fused_computation.236 | loop fusion | flops 6400000 | bytes 5121600 | tf_op jit(solution)/shard_map/cos | solution.py:36
  68.1 20.3 %all-to-all-done.1 = f32[400,2,1,200]{3,1,2,0:T(2,128)S(1)} async-done(((f32[400,2,1,200]{3,1,2,0:T(2,128)}), f32[400,2,1,200]{3,1,2,0:T(2,128)S(1)}, u32[]{:S(2)}, u32[]{:S(2)}) %all-to-all-start.1) | async-done | bytes 640032 | tf_op jit(solution)/shard_map/all_to_all | solution.py:132
  89.9 724.9 %while.24 = (s32[]{:T(128)}, f32[100,800]{1,0:T(8,128)S(1)}, f32[100,800]{1,0:T(8,128)S(1)}, f32[100,800]{1,0:T(8,128)S(1)}, f32[1,100,2,400]{3,2,1,0:T(2,128)S(...) while((s32[]{:T(128)}, f32[100,800]{1,0:T(8,128)S(1)}, ...), condition=%wide.region_2.3_spmd.clone.clone, body=%wide.region_1.2_spmd.clone.clone.sunk | while | flops 44908968 | bytes 40665256 | solution.py:112
  120.8 18.4 %dynamic_update_slice.14 = f32[1,100,2,400]{3,2,1,0:T(2,128)S(1)} dynamic-update-slice(f32[1,100,2,400]{3,2,1,0:T(2,128)S(1)} %get-tuple-element.711, f32[1,100,2,16]{3,2,1,0:T(2,128)S(1)} %fusion.153, s32[]{:T(128)} %constant.302.clone.1..sunk, s32[]{:T(128)} %constant.302.clone.1..sunk, s32[]{:T(128)} %constant.302.clone.1..sunk, s32[]{:T(128)S(6)} %select_n.52) | dynamic-update-slice | bytes 25604 | tf_op jit(solution)/shard_map/while/body/eval_jaxpr/dynamic_update_slice | solution.py:109
  151.9 18.4 %dynamic_update_slice.14 = f32[1,100,2,400]{3,2,1,0:T(2,128)S(1)} dynamic-update-slice(f32[1,100,2,400]{3,2,1,0:T(2,128)S(1)} %get-tuple-element.711, f32[1,100,2,16]{3,2,1,0:T(2,128)S(1)} %fusion.153, s32[]{:T(128)} %constant.302.clone.1..sunk, s32[]{:T(128)} %constant.302.clone.1..sunk, s32[]{:T(128)} %constant.302.clone.1..sunk, s32[]{:T(128)S(6)} %select_n.52) | dynamic-update-slice | bytes 25604 | tf_op jit(solution)/shard_map/while/body/eval_jaxpr/dynamic_update_slice | solution.py:109
  183.0 18.4 %dynamic_update_slice.14 = f32[1,100,2,400]{3,2,1,0:T(2,128)S(1)} dynamic-update-slice(f32[1,100,2,400]{3,2,1,0:T(2,128)S(1)} %get-tuple-element.711, f32[1,100,2,16]{3,2,1,0:T(2,128)S(1)} %fusion.153, s32[]{:T(128)} %constant.302.clone.1..sunk, s32[]{:T(128)} %constant.302.clone.1..sunk, s32[]{:T(128)} %constant.302.clone.1..sunk, s32[]{:T(128)S(6)} %select_n.52) | dynamic-update-slice | bytes 25604 | tf_op jit(solution)/shard_map/while/body/eval_jaxpr/dynamic_update_slice | solution.py:109
  214.1 18.4 %dynamic_update_slice.14 = f32[1,100,2,400]{3,2,1,0:T(2,128)S(1)} dynamic-update-slice(f32[1,100,2,400]{3,2,1,0:T(2,128)S(1)} %get-tuple-element.711, f32[1,100,2,16]{3,2,1,0:T(2,128)S(1)} %fusion.153, s32[]{:T(128)} %constant.302.clone.1..sunk, s32[]{:T(128)} %constant.302.clone.1..sunk, s32[]{:T(128)} %constant.302.clone.1..sunk, s32[]{:T(128)S(6)} %select_n.52) | dynamic-update-slice | bytes 25604 | tf_op jit(solution)/shard_map/while/body/eval_jaxpr/dynamic_update_slice | solution.py:109
  245.2 18.4 %dynamic_update_slice.14 = f32[1,100,2,400]{3,2,1,0:T(2,128)S(1)} dynamic-update-slice(f32[1,100,2,400]{3,2,1,0:T(2,128)S(1)} %get-tuple-element.711, f32[1,100,2,16]{3,2,1,0:T(2,128)S(1)} %fusion.153, s32[]{:T(128)} %constant.302.clone.1..sunk, s32[]{:T(128)} %constant.302.clone.1..sunk, s32[]{:T(128)} %constant.302.clone.1..sunk, s32[]{:T(128)S(6)} %select_n.52) | dynamic-update-slice | bytes 25604 | tf_op jit(solution)/shard_map/while/body/eval_jaxpr/dynamic_update_slice | solution.py:109
  276.3 18.4 %dynamic_update_slice.14 = f32[1,100,2,400]{3,2,1,0:T(2,128)S(1)} dynamic-update-slice(f32[1,100,2,400]{3,2,1,0:T(2,128)S(1)} %get-tuple-element.711, f32[1,100,2,16]{3,2,1,0:T(2,128)S(1)} %fusion.153, s32[]{:T(128)} %constant.302.clone.1..sunk, s32[]{:T(128)} %constant.302.clone.1..sunk, s32[]{:T(128)} %constant.302.clone.1..sunk, s32[]{:T(128)S(6)} %select_n.52) | dynamic-update-slice | bytes 25604 | tf_op jit(solution)/shard_map/while/body/eval_jaxpr/dynamic_update_slice | solution.py:109
  307.4 18.4 %dynamic_update_slice.14 = f32[1,100,2,400]{3,2,1,0:T(2,128)S(1)} dynamic-update-slice(f32[1,100,2,400]{3,2,1,0:T(2,128)S(1)} %get-tuple-element.711, f32[1,100,2,16]{3,2,1,0:T(2,128)S(1)} %fusion.153, s32[]{:T(128)} %constant.302.clone.1..sunk, s32[]{:T(128)} %constant.302.clone.1..sunk, s32[]{:T(128)} %constant.302.clone.1..sunk, s32[]{:T(128)S(6)} %select_n.52) | dynamic-update-slice | bytes 25604 | tf_op jit(solution)/shard_map/while/body/eval_jaxpr/dynamic_update_slice | solution.py:109
  356.5 18.4 %dynamic_update_slice.14 = f32[1,100,2,400]{3,2,1,0:T(2,128)S(1)} dynamic-update-slice(f32[1,100,2,400]{3,2,1,0:T(2,128)S(1)} %get-tuple-element.711, f32[1,100,2,16]{3,2,1,0:T(2,128)S(1)} %fusion.153, s32[]{:T(128)} %constant.302.clone.1..sunk, s32[]{:T(128)} %constant.302.clone.1..sunk, s32[]{:T(128)} %constant.302.clone.1..sunk, s32[]{:T(128)S(6)} %select_n.52) | dynamic-update-slice | bytes 25604 | tf_op jit(solution)/shard_map/while/body/eval_jaxpr/dynamic_update_slice | solution.py:109
  387.6 18.4 %dynamic_update_slice.14 = f32[1,100,2,400]{3,2,1,0:T(2,128)S(1)} dynamic-update-slice(f32[1,100,2,400]{3,2,1,0:T(2,128)S(1)} %get-tuple-element.711, f32[1,100,2,16]{3,2,1,0:T(2,128)S(1)} %fusion.153, s32[]{:T(128)} %constant.302.clone.1..sunk, s32[]{:T(128)} %constant.302.clone.1..sunk, s32[]{:T(128)} %constant.302.clone.1..sunk, s32[]{:T(128)S(6)} %select_n.52) | dynamic-update-slice | bytes 25604 | tf_op jit(solution)/shard_map/while/body/eval_jaxpr/dynamic_update_slice | solution.py:109
  418.7 18.4 %dynamic_update_slice.14 = f32[1,100,2,400]{3,2,1,0:T(2,128)S(1)} dynamic-update-slice(f32[1,100,2,400]{3,2,1,0:T(2,128)S(1)} %get-tuple-element.711, f32[1,100,2,16]{3,2,1,0:T(2,128)S(1)} %fusion.153, s32[]{:T(128)} %constant.302.clone.1..sunk, s32[]{:T(128)} %constant.302.clone.1..sunk, s32[]{:T(128)} %constant.302.clone.1..sunk, s32[]{:T(128)S(6)} %select_n.52) | dynamic-update-slice | bytes 25604 | tf_op jit(solution)/shard_map/while/body/eval_jaxpr/dynamic_update_slice | solution.py:109
  449.8 18.4 %dynamic_update_slice.14 = f32[1,100,2,400]{3,2,1,0:T(2,128)S(1)} dynamic-update-slice(f32[1,100,2,400]{3,2,1,0:T(2,128)S(1)} %get-tuple-element.711, f32[1,100,2,16]{3,2,1,0:T(2,128)S(1)} %fusion.153, s32[]{:T(128)} %constant.302.clone.1..sunk, s32[]{:T(128)} %constant.302.clone.1..sunk, s32[]{:T(128)} %constant.302.clone.1..sunk, s32[]{:T(128)S(6)} %select_n.52) | dynamic-update-slice | bytes 25604 | tf_op jit(solution)/shard_map/while/body/eval_jaxpr/dynamic_update_slice | solution.py:109
  480.9 18.4 %dynamic_update_slice.14 = f32[1,100,2,400]{3,2,1,0:T(2,128)S(1)} dynamic-update-slice(f32[1,100,2,400]{3,2,1,0:T(2,128)S(1)} %get-tuple-element.711, f32[1,100,2,16]{3,2,1,0:T(2,128)S(1)} %fusion.153, s32[]{:T(128)} %constant.302.clone.1..sunk, s32[]{:T(128)} %constant.302.clone.1..sunk, s32[]{:T(128)} %constant.302.clone.1..sunk, s32[]{:T(128)S(6)} %select_n.52) | dynamic-update-slice | bytes 25604 | tf_op jit(solution)/shard_map/while/body/eval_jaxpr/dynamic_update_slice | solution.py:109
  512.0 18.4 %dynamic_update_slice.14 = f32[1,100,2,400]{3,2,1,0:T(2,128)S(1)} dynamic-update-slice(f32[1,100,2,400]{3,2,1,0:T(2,128)S(1)} %get-tuple-element.711, f32[1,100,2,16]{3,2,1,0:T(2,128)S(1)} %fusion.153, s32[]{:T(128)} %constant.302.clone.1..sunk, s32[]{:T(128)} %constant.302.clone.1..sunk, s32[]{:T(128)} %constant.302.clone.1..sunk, s32[]{:T(128)S(6)} %select_n.52) | dynamic-update-slice | bytes 25604 | tf_op jit(solution)/shard_map/while/body/eval_jaxpr/dynamic_update_slice | solution.py:109
  543.1 18.4 %dynamic_update_slice.14 = f32[1,100,2,400]{3,2,1,0:T(2,128)S(1)} dynamic-update-slice(f32[1,100,2,400]{3,2,1,0:T(2,128)S(1)} %get-tuple-element.711, f32[1,100,2,16]{3,2,1,0:T(2,128)S(1)} %fusion.153, s32[]{:T(128)} %constant.302.clone.1..sunk, s32[]{:T(128)} %constant.302.clone.1..sunk, s32[]{:T(128)} %constant.302.clone.1..sunk, s32[]{:T(128)S(6)} %select_n.52) | dynamic-update-slice | bytes 25604 | tf_op jit(solution)/shard_map/while/body/eval_jaxpr/dynamic_update_slice | solution.py:109
  592.2 18.4 %dynamic_update_slice.14 = f32[1,100,2,400]{3,2,1,0:T(2,128)S(1)} dynamic-update-slice(f32[1,100,2,400]{3,2,1,0:T(2,128)S(1)} %get-tuple-element.711, f32[1,100,2,16]{3,2,1,0:T(2,128)S(1)} %fusion.153, s32[]{:T(128)} %constant.302.clone.1..sunk, s32[]{:T(128)} %constant.302.clone.1..sunk, s32[]{:T(128)} %constant.302.clone.1..sunk, s32[]{:T(128)S(6)} %select_n.52) | dynamic-update-slice | bytes 25604 | tf_op jit(solution)/shard_map/while/body/eval_jaxpr/dynamic_update_slice | solution.py:109
  623.3 18.4 %dynamic_update_slice.14 = f32[1,100,2,400]{3,2,1,0:T(2,128)S(1)} dynamic-update-slice(f32[1,100,2,400]{3,2,1,0:T(2,128)S(1)} %get-tuple-element.711, f32[1,100,2,16]{3,2,1,0:T(2,128)S(1)} %fusion.153, s32[]{:T(128)} %constant.302.clone.1..sunk, s32[]{:T(128)} %constant.302.clone.1..sunk, s32[]{:T(128)} %constant.302.clone.1..sunk, s32[]{:T(128)S(6)} %select_n.52) | dynamic-update-slice | bytes 25604 | tf_op jit(solution)/shard_map/while/body/eval_jaxpr/dynamic_update_slice | solution.py:109
  654.4 18.4 %dynamic_update_slice.14 = f32[1,100,2,400]{3,2,1,0:T(2,128)S(1)} dynamic-update-slice(f32[1,100,2,400]{3,2,1,0:T(2,128)S(1)} %get-tuple-element.711, f32[1,100,2,16]{3,2,1,0:T(2,128)S(1)} %fusion.153, s32[]{:T(128)} %constant.302.clone.1..sunk, s32[]{:T(128)} %constant.302.clone.1..sunk, s32[]{:T(128)} %constant.302.clone.1..sunk, s32[]{:T(128)S(6)} %select_n.52) | dynamic-update-slice | bytes 25604 | tf_op jit(solution)/shard_map/while/body/eval_jaxpr/dynamic_update_slice | solution.py:109
  685.5 18.4 %dynamic_update_slice.14 = f32[1,100,2,400]{3,2,1,0:T(2,128)S(1)} dynamic-update-slice(f32[1,100,2,400]{3,2,1,0:T(2,128)S(1)} %get-tuple-element.711, f32[1,100,2,16]{3,2,1,0:T(2,128)S(1)} %fusion.153, s32[]{:T(128)} %constant.302.clone.1..sunk, s32[]{:T(128)} %constant.302.clone.1..sunk, s32[]{:T(128)} %constant.302.clone.1..sunk, s32[]{:T(128)S(6)} %select_n.52) | dynamic-update-slice | bytes 25604 | tf_op jit(solution)/shard_map/while/body/eval_jaxpr/dynamic_update_slice | solution.py:109
  716.6 18.4 %dynamic_update_slice.14 = f32[1,100,2,400]{3,2,1,0:T(2,128)S(1)} dynamic-update-slice(f32[1,100,2,400]{3,2,1,0:T(2,128)S(1)} %get-tuple-element.711, f32[1,100,2,16]{3,2,1,0:T(2,128)S(1)} %fusion.153, s32[]{:T(128)} %constant.302.clone.1..sunk, s32[]{:T(128)} %constant.302.clone.1..sunk, s32[]{:T(128)} %constant.302.clone.1..sunk, s32[]{:T(128)S(6)} %select_n.52) | dynamic-update-slice | bytes 25604 | tf_op jit(solution)/shard_map/while/body/eval_jaxpr/dynamic_update_slice | solution.py:109
  747.7 18.4 %dynamic_update_slice.14 = f32[1,100,2,400]{3,2,1,0:T(2,128)S(1)} dynamic-update-slice(f32[1,100,2,400]{3,2,1,0:T(2,128)S(1)} %get-tuple-element.711, f32[1,100,2,16]{3,2,1,0:T(2,128)S(1)} %fusion.153, s32[]{:T(128)} %constant.302.clone.1..sunk, s32[]{:T(128)} %constant.302.clone.1..sunk, s32[]{:T(128)} %constant.302.clone.1..sunk, s32[]{:T(128)S(6)} %select_n.52) | dynamic-update-slice | bytes 25604 | tf_op jit(solution)/shard_map/while/body/eval_jaxpr/dynamic_update_slice | solution.py:109
  778.8 18.4 %dynamic_update_slice.14 = f32[1,100,2,400]{3,2,1,0:T(2,128)S(1)} dynamic-update-slice(f32[1,100,2,400]{3,2,1,0:T(2,128)S(1)} %get-tuple-element.711, f32[1,100,2,16]{3,2,1,0:T(2,128)S(1)} %fusion.153, s32[]{:T(128)} %constant.302.clone.1..sunk, s32[]{:T(128)} %constant.302.clone.1..sunk, s32[]{:T(128)} %constant.302.clone.1..sunk, s32[]{:T(128)S(6)} %select_n.52) | dynamic-update-slice | bytes 25604 | tf_op jit(solution)/shard_map/while/body/eval_jaxpr/dynamic_update_slice | solution.py:109
  (619 shorter events, 391.1 us)
Async XLA Ops:
  0.8 6.8 collective-permute-start
  3.9 3.7 collective-permute-start.1
  8.9 5.6 collective-permute-start.2
  8.9 6.7 collective-permute-start.3
  17.5 8.9 %copy-start.1 = (s32[400]{0:T(512)S(1)}, s32[400]{0:T(512)}, u32[]{:S(2)}) copy-start(s32[400]{0:T(512)} %param.11) | copy-start | bytes 4804
  17.5 8.9 %copy-start.2 = (s32[200]{0:T(256)S(1)}, s32[200]{0:T(256)}, u32[]{:S(2)}) copy-start(s32[200]{0:T(256)} %param.10) | copy-start | bytes 2404
  21.9 25.5 %all-to-all-start = ((f32[4,200,400]{2,1,0:T(8,128)}), f32[4,200,400]{2,1,0:T(8,128)}, u32[]{:S(2)}, u32[]{:S(2)}) async-start(f32[4,200,400]{2,1,0:T(8,128)} %fusion.135), calls=%async_computation | async-start | bytes 3276800 | tf_op jit(solution)/shard_map/all_to_all | solution.py:127
  62.5 25.9 %all-to-all-start.1 = ((f32[400,2,1,200]{3,1,2,0:T(2,128)}), f32[400,2,1,200]{3,1,2,0:T(2,128)S(1)}, u32[]{:S(2)}, u32[]{:S(2)}) async-start(f32[400,2,1,200]{3,1,2,0:T(2,128)} %copy.23), calls=%async_computation.1 | async-start | bytes 1638400 | tf_op jit(solution)/shard_map/all_to_all | solution.py:132
  814.8 0.8 copy-start
where the time goes:
time: 816 us
  local copies, waits for them, and re-layouts  419 us (51%)
  matrix products  211 us (26%)
  other arithmetic  129 us (16%)
  waiting for transfers between devices  35.3 us (4%)
  starting transfers between devices  16.6 us (2%)
    dynamic_update_slice x25, local copies, waits for them, and re-layouts, advance(): lax.dynamic_update_slice_in_dim(result_now, partial_value, first_order, 3)  408 us
    dot_general x25, matrix products, contract(): return jnp.einsum('stj,scij->isct', table_rows, weighted, precision=precise)  205 us
    while x375, other arithmetic  72.1 us
    all_to_all x1, waiting for transfers between devices, shards(): lax.all_to_all(fourier, 'lat', split_axis=0, concat_axis=3, tiled=True)  20.3 us
  transfers between devices with their start and end apart: 6, of which 5 were waited for; matrix products, arithmetic and copies ran while one was open for 2% of the time, Pallas kernels for 0%

commit v1 on v0

v1 whole, which is shorter than its diff:
```python
import math

import jax
import jax.numpy as jnp
import numpy as np
from jax import lax
from jax.experimental import pallas as pl
from jax.experimental.pallas import tpu as pltpu
from jax.sharding import PartitionSpec as P

M = 400
NLAT = 800
NLON = 1600
LANES = 128
BLOCK = 40
CHUNK = 40


def split_bf16(values):
    high = values.astype(jnp.bfloat16)
    low = (values - high.astype(jnp.float32)).astype(jnp.bfloat16)
    return high, low


def table_bf16(table):
    high = table.astype(jnp.bfloat16)
    low = (table - high.astype(np.float64)).astype(jnp.bfloat16)
    return high, low


def fourier_table(pieces):
    phase = np.arange(NLON)[:, None] * np.arange(M)[None, :] % NLON
    angles = 2.0 * math.pi / NLON * phase
    table = np.concatenate([np.cos(angles), -np.sin(angles)], axis=1) / math.sqrt(NLON)
    return table.reshape(pieces, NLON // pieces, 2 * M)


def resample_table():
    half = M // 2
    coarse = math.pi / M * (np.arange(M) + 0.5)
    fine = math.pi / NLAT * (np.arange(NLAT) + 0.5)
    waves = np.arange(M)
    weight = np.where(waves == 0, 1.0, 2.0) / M
    even = (np.cos(np.outer(coarse, waves)) * weight) @ np.cos(np.outer(waves, fine))
    odd = (np.sin(np.outer(coarse, waves)) * weight) @ np.sin(np.outer(waves, fine))
    rows = []
    for full in (even, odd):
        for sign in (1.0, -1.0):
            rows.append(full[:half] + sign * full[::-1][:half])
    return np.concatenate(rows, axis=0)


def latitude_table():
    half = M // 2
    angles = math.pi / M * (np.arange(half) + 0.5)
    log_sine = np.log2(np.sin(angles))
    coarse = np.round(log_sine * 1024.0) / 1024.0
    rows = np.stack([2.0 * np.cos(angles), coarse, log_sine - coarse])
    return np.broadcast_to(rows[:, :, None], (3, half, LANES)).astype(np.float32)


def advect(tracer, east_wind, north_wind):
    rows = tracer.shape[1]
    lat_count = lax.axis_size("lat")
    ring = ("lev", "fld")
    lon_count = lax.axis_size(ring)
    down = [(i, i + 1) for i in range(lat_count - 1)]
    up = [(i + 1, i) for i in range(lat_count - 1)]
    right = [(i, (i + 1) % lon_count) for i in range(lon_count)]
    left = [((i + 1) % lon_count, i) for i in range(lon_count)]
    north = lax.ppermute(tracer[:, rows - 1 :, :], "lat", down)
    south = lax.ppermute(tracer[:, :1, :], "lat", up)
    west = lax.ppermute(tracer[:, :, -1:], ring, right)
    east = lax.ppermute(tracer[:, :, :1], ring, left)
    wide = jnp.concatenate([west, tracer, east], axis=2).astype(jnp.float32)
    tall = jnp.concatenate([north, tracer, south], axis=1).astype(jnp.float32)
    east_diff = wide[:, :, 2:] - wide[:, :, :-2]
    north_diff = tall[:, 2:, :] - tall[:, :-2, :]
    return (
        tracer.astype(jnp.float32)
        - 0.5 * east_wind.astype(jnp.float32) * east_diff
        - 0.5 * north_wind.astype(jnp.float32) * north_diff
    )


def fourier_kernel(grid_ref, high_ref, low_ref, place_ref, wave_ref, keep_ref, sine_ref, out_ref):
    pieces = grid_ref.shape[0]
    total = None
    for piece in range(pieces):
        high, low = split_bf16(grid_ref[piece])
        part = jnp.dot(high, high_ref[piece], preferred_element_type=jnp.float32)
        part += jnp.dot(low, high_ref[piece], preferred_element_type=jnp.float32)
        part += jnp.dot(high, low_ref[piece], preferred_element_type=jnp.float32)
        total = part if total is None else total + part
    high, low = split_bf16(total)
    placed = jnp.dot(high, place_ref[...], preferred_element_type=jnp.float32)
    placed += jnp.dot(low, place_ref[...], preferred_element_type=jnp.float32)
    kept = jnp.where(wave_ref[...] < keep_ref[...], placed * sine_ref[...], 0.0)
    targets, _, width = out_ref.shape
    for target in range(targets):
        out_ref[target] = kept[:, target * width : (target + 1) * width]


def fourier(grid, places, wave_row, keep_col, sine_col, targets):
    pieces, rows, lons = grid.shape
    width = wave_row.shape[1] // targets
    high, low = table_bf16(fourier_table(pieces))
    return pl.pallas_call(
        fourier_kernel,
        out_shape=jax.ShapeDtypeStruct((targets, rows, width), jnp.float32),
        in_specs=[pl.BlockSpec(memory_space=pltpu.VMEM)] * 7,
        out_specs=pl.BlockSpec(memory_space=pltpu.VMEM),
        compiler_params=pltpu.CompilerParams(vmem_limit_bytes=48 * 2**20),
        cost_estimate=pl.CostEstimate(
            flops=6 * rows * NLON * 2 * M, bytes_accessed=12 * 2**20, transcendentals=0
        ),
    )(grid, high, low, places, wave_row, keep_col, sine_col)


def legendre_kernel(
    fields_ref, high_ref, low_ref, lat_ref, wave_ref, norm_ref, beta_ref, scale_ref, growth_ref,
    out_ref, weight, before, current, level, sums, result,
):
    half = lat_ref.shape[1]
    lanes = wave_ref.shape[1]
    slots = out_ref.shape[0]
    groups = lanes // LANES
    wave = wave_ref[...]
    odd = wave - 2.0 * jnp.floor(wave * 0.5) > 0.5

    for comp in range(2):
        high, low = split_bf16(fields_ref[:, comp * lanes : (comp + 1) * lanes])
        for parity in range(2):
            both = []
            for wave_parity in range(2):
                rows = pl.ds((2 * wave_parity + parity) * half, half)
                value = jnp.dot(high_ref[rows], high, preferred_element_type=jnp.float32)
                value += jnp.dot(high_ref[rows], low, preferred_element_type=jnp.float32)
                value += jnp.dot(low_ref[rows], high, preferred_element_type=jnp.float32)
                both.append(value)
            weight[2 * parity + comp] = jnp.where(odd, both[1], both[0])

    for group in range(groups):
        cols = slice(group * LANES, (group + 1) * LANES)
        coarse = lat_ref[1] * wave[:, cols]
        whole = jnp.floor(coarse)
        level[:, cols] = whole
        current[:, cols] = jnp.exp2(
            (coarse - whole) + lat_ref[2] * wave[:, cols] + norm_ref[:, cols]
        )
        before[:, cols] = jnp.zeros((half, LANES), jnp.float32)

    def step(block, carry):
        first = pl.multiple_of(block * BLOCK, 8)
        for group in range(groups):
            cols = slice(group * LANES, (group + 1) * LANES)
            grow = growth_ref[pl.ds(block, 1), cols]
            for chunk in range(half // CHUNK):
                rows = slice(chunk * CHUNK, (chunk + 1) * CHUNK)
                height = level[rows, cols]
                factor = jnp.exp2(height)
                weights = [weight[k, rows, cols] * factor for k in range(4)]
                cosine = lat_ref[0, rows]
                old = before[rows, cols]
                new = current[rows, cols]
                for order in range(BLOCK):
                    for comp in range(2):
                        product = new * weights[2 * (order % 2) + comp]
                        partial = product.reshape(CHUNK // 8, 8, LANES).sum(axis=0)
                        place = pl.ds((order * 2 + comp) * 8, 8)
                        if chunk == 0:
                            sums[place] = partial
                        else:
                            sums[place] += partial
                    beta = beta_ref[pl.ds(first + order, 1), cols]
                    old, new = new, cosine * new - beta * old
                biggest = jnp.maximum(jnp.abs(old), jnp.abs(new)) * grow
                shift = jnp.floor(jnp.log(biggest) * (1.0 / math.log(2.0)))
                factor = grow * jnp.exp2(-shift)
                before[rows, cols] = old * factor
                current[rows, cols] = new * factor
                level[rows, cols] = height + shift
            for comp in range(2):
                total = sums[pl.ds(comp * 8, BLOCK, stride=16)]
                for lane in range(1, 8):
                    total += sums[pl.ds(comp * 8 + lane, BLOCK, stride=16)]
                result[comp, pl.ds(first, BLOCK), cols] = (
                    total * scale_ref[pl.ds(first, BLOCK), cols]
                )
        return carry

    lax.fori_loop(0, M // BLOCK, step, 0)
    for comp in range(2):
        out_ref[:, comp, :] = result[comp].T[:slots]


def legendre(fields, slot_wave):
    slots = slot_wave.shape[0]
    lanes = fields.shape[1] // 2
    half = M // 2
    wave_row = jnp.pad(slot_wave, (0, lanes - slots), constant_values=2 * M)
    inside_wave = jnp.minimum(wave_row, M - 1).astype(jnp.float32)[None, :]
    counter = np.arange(1, M)
    log_terms = np.log1p(0.5 / counter) / math.log(2.0)
    log_norm = jnp.sum(
        jnp.where(
            counter.astype(np.float32)[:, None] <= inside_wave, log_terms.astype(np.float32)[:, None], 0.0
        ),
        axis=0,
        keepdims=True,
    )
    norm = 0.5 * (log_norm - 1.0)
    order = jnp.arange(M + 1, dtype=jnp.float32)[:, None]
    degree = inside_wave + order
    square = 4.0 * degree * degree - 1.0
    beta = 4.0 * order * (degree + inside_wave) / jnp.maximum(square, 1.0)
    ratio = jnp.sqrt(square[1:] / (4.0 * order[1:] * (degree[1:] + inside_wave)))
    ratio = ratio.reshape(M // BLOCK, BLOCK, lanes)
    scales = [jnp.ones_like(ratio[:, 0])]
    for index in range(BLOCK):
        scales.append(scales[-1] * ratio[:, index])
    growth = scales[-1]
    scale = jnp.stack(scales[:-1], axis=1).reshape(M, lanes)
    scale = jnp.where(order[:-1] < (M - wave_row).astype(jnp.float32)[None, :], scale, 0.0)
    high, low = table_bf16(resample_table())
    vector = pltpu.VMEM((half, lanes), jnp.float32)
    return pl.pallas_call(
        legendre_kernel,
        out_shape=jax.ShapeDtypeStruct((slots, 2, M), jnp.float32),
        in_specs=[pl.BlockSpec(memory_space=pltpu.VMEM)] * 9,
        out_specs=pl.BlockSpec(memory_space=pltpu.VMEM),
        scratch_shapes=[
            pltpu.VMEM((4, half, lanes), jnp.float32),
            vector,
            vector,
            vector,
            pltpu.VMEM((BLOCK * 16, LANES), jnp.float32),
            pltpu.VMEM((2, M, lanes), jnp.float32),
        ],
        compiler_params=pltpu.CompilerParams(vmem_limit_bytes=48 * 2**20),
        cost_estimate=pl.CostEstimate(
            flops=7 * half * lanes * M, bytes_accessed=6 * 2**20, transcendentals=0
        ),
    )(fields, high, low, latitude_table(), inside_wave, norm, beta[:-1], scale, growth)


def shards(tracer, wind_east, wind_north, keep_m, slot_wave):
    rows = tracer.shape[1]
    lat_count = lax.axis_size("lat")
    slots = slot_wave.shape[0] // lat_count
    lanes = -(-slots // LANES) * LANES
    lat_index = lax.axis_index("lat")

    advected = advect(tracer, wind_east, wind_north)
    grid = lax.all_to_all(advected, ("lev", "fld"), split_axis=0, concat_axis=0, tiled=True)

    waves = jnp.pad(
        slot_wave.reshape(lat_count, 1, slots), ((0, 0), (0, 0), (0, lanes - slots)),
        constant_values=2 * NLON,
    )
    waves = jnp.broadcast_to(waves, (lat_count, 2, lanes))
    offsets = jnp.array([0, M], jnp.int32)[None, :, None]
    columns = jnp.where(waves < M, waves + offsets, -1).reshape(1, -1)
    places = (jnp.arange(2 * M, dtype=jnp.int32)[:, None] == columns).astype(jnp.bfloat16)
    row_ids = (lat_index * rows + jnp.arange(rows, dtype=jnp.int32)).astype(jnp.float32)
    sines = jnp.sin(math.pi / NLAT * (row_ids + 0.5)) * math.sqrt(2.0 / NLAT)
    waved = fourier(
        grid, places, waves.reshape(1, -1), keep_m[:, None], sines[:, None], lat_count
    )
    fields = lax.all_to_all(waved, "lat", split_axis=0, concat_axis=0, tiled=True)
    fields = fields.reshape(lat_count * rows, 2 * lanes)
    my_waves = lax.dynamic_slice_in_dim(slot_wave, lat_index * slots, slots)
    return legendre(fields, my_waves)[None]


def solution(mesh):
    return jax.shard_map(
        shards,
        mesh=mesh,
        in_specs=(
            P("member", "lat", ("lev", "fld")),
            P("member", "lat", ("lev", "fld")),
            P("member", "lat", ("lev", "fld")),
            P("lat"),
            P(),
        ),
        out_specs=P(("member", "lev", "fld"), "lat", None, None),
        check_vma=False,
    )
```

time: 816 us -> 111 us (0.14)
  local copies, waits for them, and re-layouts: 419 us -> 16 us
  matrix products: 211 us -> 0 us
  other arithmetic: 129 us -> 23.9 us
  Pallas kernels: 0 us -> 20.9 us
    dynamic_update_slice x25 -> x0, local copies, waits for them, and re-layouts: 408 us -> none  [advance(): lax.dynamic_update_slice_in_dim(result_now, partial_value, first_order, 3)]
    dot_general x26 -> x0, matrix products: 211 us -> none  [the longest x25 205 us: contract(): return jnp.einsum('stj,scij->isct', table_rows, weighted, precision=precise)]
    while x375 -> x0, other arithmetic: 72.1 us -> none
    pallas_call x0 -> x2, Pallas kernels: none -> 20.9 us  [the longest x1 14.5 us: legendre(): pl.pallas_call(legendre_kernel, out_shape=jax.ShapeDtypeStruct((slots, 2,...]
    unnamed x2 -> x30, other arithmetic: 0.01 us -> 18 us
    mul x30 -> x5, other arithmetic: 18 us -> 1.08 us  [the longest x1 1.01 us: shards(): sines = jnp.sin(math.pi / NLAT * (row_ids + 0.5)) * math.sqrt(2.0 / NLAT)]
    cos x26 -> x0, other arithmetic: 13.6 us -> none  [the longest x1 12.4 us: fourier_table(): return jnp.stack([jnp.cos(angles), -jnp.sin(angles)], axis=1) * factor]
    add x26 -> x1, other arithmetic: 11.1 us -> 0.08 us  [legendre(): degree = inside_wave + order]
  transfers between devices with their start and end apart: 6 -> 6, of which waited for: 5 -> 2; matrix products, arithmetic and copies ran while one was open for 2% -> 29% of each run, Pallas kernels for 0% -> 0%
where the time goes in v1:
time: 111 us
  waiting for transfers between devices  34 us (31%)
  other arithmetic  23.9 us (22%)
  Pallas kernels  20.9 us (19%)
  local copies, waits for them, and re-layouts  16 us (14%)
  starting transfers between devices  15.6 us (14%)
    unnamed x30, other arithmetic  18 us
    all_to_all x1, waiting for transfers between devices, shards(): lax.all_to_all(waved, 'lat', split_axis=0, concat_axis=0, tiled=True)  17.4 us
    all_to_all x1, waiting for transfers between devices, shards(): lax.all_to_all(advected, ('lev', 'fld'), split_axis=0, concat_axis=0, til...  16.5 us
    pallas_call x1, Pallas kernels, legendre(): pl.pallas_call(legendre_kernel, out_shape=jax.ShapeDtypeStruct((slots, 2,...  14.5 us
    unnamed x33, local copies, waits for them, and re-layouts  10.5 us
    pallas_call x1, Pallas kernels, fourier(): pl.pallas_call(fourier_kernel, out_shape=jax.ShapeDtypeStruct((targets, r...  6.38 us
    ppermute x1, starting transfers between devices, advect(): north = lax.ppermute(tracer[:, rows - 1:, :], 'lat', down)  5.56 us
    all_to_all x1, starting transfers between devices, shards(): lax.all_to_all(waved, 'lat', split_axis=0, concat_axis=0, tiled=True)  4.15 us
  transfers between devices with their start and end apart: 6, of which 2 were waited for; matrix products, arithmetic and copies ran while one was open for 29% of the time, Pallas kernels for 0%

profile of v1, /device:TPU:0, one launch (start us, length us, event | category | flops | bytes accessed | tf_op | source)
XLA Modules:
  0.0 110.5 jit_solution(5757491509490016625)
XLA Ops:
  0.0 0.8 fusion.36
  0.8 1.3 %collective-permute-start.3 = (bf16[4,1,400]{2,1,0:T(2,128)(2,1)S(1)}, bf16[4,1,400]{2,1,0:T(2,128)(2,1)S(1)}, u32[]{:S(2)}, u32[]{:S(2)}) collective-permute-start(bf16[4,1,400]{2,1,0:T(2,128)(2,1)S(1)} %get-tuple-element.36), channel_id=1, source_target_pairs={{4,0},{8,4},{12,8},{5,1},{9,5},{13,9},{6,2},{10,6},{14,10},{7,3},{... | collective-permute-start | bytes 9608 | tf_op jit(solution)/shard_map/ppermute | solution.py:72
  2.1 5.6 %collective-permute-start.2 = (bf16[4,1,400]{2,1,0:T(2,128)(2,1)S(1)}, bf16[4,1,400]{2,1,0:T(2,128)(2,1)S(1)}, u32[]{:S(2)}, u32[]{:S(2)}) collective-permute-start(bf16[4,1,400]{2,1,0:T(2,128)(2,1)S(1)} %get-tuple-element.35), channel_id=1, source_target_pairs={{0,4},{4,8},{8,12},{1,5},{5,9},{9,13},{2,6},{6,10},{10,14},{3,7},{... | collective-permute-start | bytes 9608 | tf_op jit(solution)/shard_map/ppermute | solution.py:71
  7.7 1.2 %fusion.35 = (bf16[4,200,1]{2,1,0:T(8,128)(2,1)S(1)}, bf16[4,200,1]{2,1,0:T(8,128)(2,1)S(1)}) fusion(bf16[4,200,400]{2,1,0:T(8,128)(2,1)} %param.13), kind=kLoop, calls=%fused_computation.159 | loop fusion | bytes 6400 | tf_op jit(solution)/shard_map/slice | solution.py:73
  8.8 0.9 collective-permute-start.1
  9.7 0.8 reshape.87
  11.1 0.8 dynamic_slice.3
  12.4 0.6 constant_dynamic-update-slice_fusion.38
  33.1 0.8 copy-done.7
  34.2 2.2 %fusion.2 = f32[4,200,400]{2,1,0:T(8,128)} fusion(f32[4,202,400]{2,1,0:T(8,128)S(1)} %maximum_convert_fusion, f32[4,200,402]{2,1,0:T(8,128)S(1)} %maximum_convert_fusion.1, bf16[4,200,400]{2,1,0:T(8,128)(2,1)S(1)} %copy-done.7, bf16[4,200,400]{2,1,0:T(8,128)(2,1)S(1)} %copy-done.8, bf16[4,200,400]{2,1,0:T(8,128)(2,1)S(1)} %copy-done.6), kind=kLoop, calls=%fused_computation.4 | loop fusion | flops 3520000 | bytes 8320000 | tf_op jit(solution)/shard_map/sub | solution.py:80
  36.4 3.7 %all-to-all-start = ((f32[4,200,400]{2,1,0:T(8,128)}), f32[4,200,400]{2,1,0:T(8,128)S(1)}, u32[]{:S(2)}, u32[]{:S(2)}) async-start(f32[4,200,400]{2,1,0:T(8,128)} %fusion.2), calls=%async_computation | async-start | bytes 3276800 | tf_op jit(solution)/shard_map/all_to_all | solution.py:255
  40.1 1.0 sine_multiply_fusion.sine_ref
  41.1 0.8 copy.99.keep_ref
  43.6 0.6 fusion.place_ref
  44.3 16.5 %all-to-all-done.grid_ref = f32[4,200,400]{2,1,0:T(8,128)S(1)} async-done(((f32[4,200,400]{2,1,0:T(8,128)}), f32[4,200,400]{2,1,0:T(8,128)S(1)}, u32[]{:S(2)}, u32[]{:S(2)}) %all-to-all-start) | async-done | bytes 1280032 | tf_op jit(solution)/shard_map/all_to_all | solution.py:255
  60.8 0.9 copy-done.3
  61.7 0.9 copy-done.4
  62.6 6.4 %shard_map.127 = f32[4,200,256]{2,1,0:T(8,128)S(1)} custom-call(f32[4,200,400]{2,1,0:T(8,128)S(1)} %all-to-all-done.grid_ref, bf16[4,400,800]{2,1,0:T(8,128)(2,1)} %constant.62.clone.high_ref, bf16[4,400,800]{2,1,0:T(8,128)(2,1)} %constant.63.clone.low_ref, bf16[800,1024]{1,0:T(8,128)(2,1)S(1)} %fusion.place_ref, s32[1,1024]{1,0:T(1,128)S(1)} %bitcast.158, ...), custom_call_target="tpu_custom_call" | custom-call | flops 1536000000 | bytes 12582912 | tf_op jit(solution)/shard_map/pallas_call | solution.py:108
  69.0 0.9 copy-done
  69.9 4.1 %all-to-all-start.1 = ((f32[4,200,256]{2,1,0:T(8,128)}), f32[4,200,256]{2,1,0:T(8,128)S(1)}, u32[]{:S(2)}, u32[]{:S(2)}) async-start(f32[4,200,256]{2,1,0:T(8,128)} %copy-done), calls=%async_computation.1 | async-start | bytes 1638400 | tf_op jit(solution)/shard_map/all_to_all | solution.py:270
  75.9 1.0 copy.139
  77.3 17.4 %all-to-all-done.1 = f32[4,200,256]{2,1,0:T(8,128)S(1)} async-done(((f32[4,200,256]{2,1,0:T(8,128)}), f32[4,200,256]{2,1,0:T(8,128)S(1)}, u32[]{:S(2)}, u32[]{:S(2)}) %all-to-all-start.1) | async-done | bytes 819232 | tf_op jit(solution)/shard_map/all_to_all | solution.py:270
  94.7 1.4 %copy-done.2 = bf16[800,800]{1,0:T(8,128)(2,1)S(1)} copy-done((bf16[800,800]{1,0:T(8,128)(2,1)S(1)}, bf16[800,800]{1,0:T(8,128)(2,1)}, u32[]{:S(2)}) %copy-start.2) | copy-done | bytes 1280024
  96.0 14.5 %shard_map.128 = f32[100,2,400]{2,1,0:T(2,128)} custom-call(f32[800,256]{1,0:T(8,128)S(1)} %bitcast.157, bf16[800,800]{1,0:T(8,128)(2,1)S(1)} %copy-done.1, bf16[800,800]{1,0:T(8,128)(2,1)S(1)} %copy-done.2, f32[3,200,128]{2,1,0:T(8,128)S(1)} %copy-done.5, f32[1,128]{1,0:T(1,128)S(1)} %get-tuple-element.80.wave_ref, ...), custom_call_target="tpu_custom_call" | custom-call | flops 71680000 | bytes 6291456 | tf_op jit(solution)/shard_map/pallas_call | solution.py:227
  (83 shorter events, 25.4 us)
Async XLA Ops:
  0.8 32.0 %collective-permute-start.3 = (bf16[4,1,400]{2,1,0:T(2,128)(2,1)S(1)}, bf16[4,1,400]{2,1,0:T(2,128)(2,1)S(1)}, u32[]{:S(2)}, u32[]{:S(2)}) collective-permute-start(bf16[4,1,400]{2,1,0:T(2,128)(2,1)S(1)} %get-tuple-element.36), channel_id=1, source_target_pairs={{4,0},{8,4},{12,8},{5,1},{9,5},{13,9},{6,2},{10,6},{14,10},{7,3},{... | collective-permute-start | bytes 9608 | tf_op jit(solution)/shard_map/ppermute | solution.py:72
  2.1 30.7 %collective-permute-start.2 = (bf16[4,1,400]{2,1,0:T(2,128)(2,1)S(1)}, bf16[4,1,400]{2,1,0:T(2,128)(2,1)S(1)}, u32[]{:S(2)}, u32[]{:S(2)}) collective-permute-start(bf16[4,1,400]{2,1,0:T(2,128)(2,1)S(1)} %get-tuple-element.35), channel_id=1, source_target_pairs={{0,4},{4,8},{8,12},{1,5},{5,9},{9,13},{2,6},{6,10},{10,14},{3,7},{... | collective-permute-start | bytes 9608 | tf_op jit(solution)/shard_map/ppermute | solution.py:71
  8.8 23.5 %collective-permute-start.1 = (bf16[4,200,1]{2,1,0:T(8,128)(2,1)S(1)}, bf16[4,200,1]{2,1,0:T(8,128)(2,1)S(1)}, u32[]{:S(2)}, u32[]{:S(2)}) collective-permute-start(bf16[4,200,1]{2,1,0:T(8,128)(2,1)S(1)} %get-tuple-element.34), channel_id=1, source_target_pairs={{1,0},{2,1},{3,2},{0,3},{5,4},{6,5},{7,6},{4,7},{9,8},{10,9},{11,1... | collective-permute-start | bytes 4808 | tf_op jit(solution)/shard_map/ppermute | solution.py:74
  9.7 22.6 %collective-permute-start = (bf16[4,200,1]{2,1,0:T(8,128)(2,1)S(1)}, bf16[4,200,1]{2,1,0:T(8,128)(2,1)S(1)}, u32[]{:S(2)}, u32[]{:S(2)}) collective-permute-start(bf16[4,200,1]{2,1,0:T(8,128)(2,1)S(1)} %get-tuple-element.33), channel_id=1, source_target_pairs={{0,1},{1,2},{2,3},{3,0},{4,5},{5,6},{6,7},{7,4},{8,9},{9,10},{10,1... | collective-permute-start | bytes 4808 | tf_op jit(solution)/shard_map/ppermute | solution.py:73
  10.5 21.8 %copy-start.6 = (bf16[4,200,400]{2,1,0:T(8,128)(2,1)S(1)}, bf16[4,200,400]{2,1,0:T(8,128)(2,1)}, u32[]{:S(2)}) copy-start(bf16[4,200,400]{2,1,0:T(8,128)(2,1)} %param.13) | copy-start | bytes 1920004
  32.8 1.1 %copy-start.7 = (bf16[4,200,400]{2,1,0:T(8,128)(2,1)S(1)}, bf16[4,200,400]{2,1,0:T(8,128)(2,1)}, u32[]{:S(2)}) copy-start(bf16[4,200,400]{2,1,0:T(8,128)(2,1)} %param.15) | copy-start | bytes 1920004
  32.8 1.4 %copy-start.8 = (bf16[4,200,400]{2,1,0:T(8,128)(2,1)S(1)}, bf16[4,200,400]{2,1,0:T(8,128)(2,1)}, u32[]{:S(2)}) copy-start(bf16[4,200,400]{2,1,0:T(8,128)(2,1)} %param.14) | copy-start | bytes 1920004
  36.4 4.7 %copy-start.11 = (s32[200]{0:T(256)S(1)}, s32[200]{0:T(256)}, u32[]{:S(2)}) copy-start(s32[200]{0:T(256)} %param.16) | copy-start | bytes 2404
  36.4 24.5 %all-to-all-start = ((f32[4,200,400]{2,1,0:T(8,128)}), f32[4,200,400]{2,1,0:T(8,128)S(1)}, u32[]{:S(2)}, u32[]{:S(2)}) async-start(f32[4,200,400]{2,1,0:T(8,128)} %fusion.2), calls=%async_computation | async-start | bytes 3276800 | tf_op jit(solution)/shard_map/all_to_all | solution.py:255
  60.8 0.9 copy-start.3
  61.7 0.9 copy-start.4
  69.0 0.9 copy-start
  69.9 7.0 %copy-start.9 = (f32[399]{0:T(512)S(1)}, f32[399]{0:T(512)}, u32[]{:S(2)}) copy-start(f32[399]{0:T(512)} %constant.74) | copy-start | bytes 4792
  69.9 7.0 %copy-start.10 = (f32[399]{0:T(512)S(1)}, f32[399]{0:T(512)}, u32[]{:S(2)}) copy-start(f32[399]{0:T(512)} %constant.73) | copy-start | bytes 4792
  69.9 24.8 %copy-start.1 = (bf16[800,800]{1,0:T(8,128)(2,1)S(1)}, bf16[800,800]{1,0:T(8,128)(2,1)}, u32[]{:S(2)}) copy-start(bf16[800,800]{1,0:T(8,128)(2,1)} %constant.66.clone.high_ref) | copy-start | bytes 3840004
  69.9 24.8 %copy-start.5 = (f32[3,200,128]{2,1,0:T(8,128)S(1)}, f32[3,200,128]{2,1,0:T(8,128)}, u32[]{:S(2)}) copy-start(f32[3,200,128]{2,1,0:T(8,128)} %constant.68.clone.lat_ref) | copy-start | bytes 921604
  69.9 24.8 %all-to-all-start.1 = ((f32[4,200,256]{2,1,0:T(8,128)}), f32[4,200,256]{2,1,0:T(8,128)S(1)}, u32[]{:S(2)}, u32[]{:S(2)}) async-start(f32[4,200,256]{2,1,0:T(8,128)} %copy-done), calls=%async_computation.1 | async-start | bytes 1638400 | tf_op jit(solution)/shard_map/all_to_all | solution.py:270
  94.7 1.4 %copy-start.2 = (bf16[800,800]{1,0:T(8,128)(2,1)S(1)}, bf16[800,800]{1,0:T(8,128)(2,1)}, u32[]{:S(2)}) copy-start(bf16[800,800]{1,0:T(8,128)(2,1)} %constant.67.clone.low_ref) | copy-start | bytes 3840004

commit v2 on v1

v2 whole, which is shorter than its diff:
```python
import math

import jax
import jax.numpy as jnp
import numpy as np
from jax import lax
from jax.experimental import pallas as pl
from jax.experimental.pallas import tpu as pltpu
from jax.sharding import PartitionSpec as P

M = 400
NLAT = 800
NLON = 1600
LANES = 128
BLOCK = 40
CHUNK = 40
TOP = 32767.0
VMEM_BYTES = 24 * 2**20


def split_bf16(values):
    high = values.astype(jnp.bfloat16)
    low = (values - high.astype(jnp.float32)).astype(jnp.bfloat16)
    return high, low


def table_bf16(table):
    high = table.astype(jnp.bfloat16)
    low = (table - high.astype(np.float64)).astype(jnp.bfloat16)
    return high, low


def fourier_tables(pieces):
    quarter = NLON // 4
    spots = np.arange(quarter)[:, None]
    factor = 1.0 / math.sqrt(NLON)

    def parts(waves):
        angles = 2.0 * math.pi / NLON * (spots * waves[None, :] % NLON)
        return factor * np.cos(angles), factor * np.sin(angles)

    tables = []
    for first in (0, 2):
        cosine, sine = parts(np.arange(first, M, 4))
        tables.append([cosine, -sine])
    waves = np.arange(1, M, 2)
    sign = np.where(waves % 4 == 1, 1.0, -1.0)[None, :]
    cosine, sine = parts(waves)
    tables.append([cosine, -sine])
    tables.append([-sign * sine, -sign * cosine])
    share = pieces // 4
    result = []
    for columns in tables:
        table = np.concatenate(columns, axis=1)
        table = np.pad(table, ((0, 0), (0, -table.shape[1] % (2 * LANES))))
        result.append(table.reshape(share, quarter // share, table.shape[1]))
    return result


def wave_rows():
    quarter_width = -(-M // 2 // (2 * LANES)) * 2 * LANES
    waves = np.arange(M)
    quarter_count, half_count = M // 4, M // 2
    rows = []
    for part in range(2):
        even = np.where(waves % 4 == 0, 0, quarter_width) + part * quarter_count + waves // 4
        odd = 2 * quarter_width + part * half_count + waves // 2
        rows.append(np.where(waves % 2 == 0, even, odd))
    return np.stack(rows).astype(np.int32)


def resample_table():
    half = M // 2
    coarse = math.pi / M * (np.arange(M) + 0.5)
    fine = math.pi / NLAT * (np.arange(NLAT) + 0.5)
    waves = np.arange(M)
    weight = np.where(waves == 0, 1.0, 2.0) / M
    even = (np.cos(np.outer(coarse, waves)) * weight) @ np.cos(np.outer(waves, fine))
    odd = (np.sin(np.outer(coarse, waves)) * weight) @ np.sin(np.outer(waves, fine))
    rows = []
    for full in (even, odd):
        for sign in (1.0, -1.0):
            rows.append(full[:half] + sign * full[::-1][:half])
    return np.concatenate(rows, axis=0)


def latitude_table():
    half = M // 2
    angles = math.pi / M * (np.arange(half) + 0.5)
    log_sine = np.log2(np.sin(angles))
    coarse = np.round(log_sine * 1024.0) / 1024.0
    rows = np.stack([2.0 * np.cos(angles), coarse, log_sine - coarse])
    return np.broadcast_to(rows[:, :, None], (3, half, LANES)).astype(np.float32)


def scale_code(biggest):
    wanted = jnp.maximum(biggest, 1e-30) * (1.0 / TOP)
    exponent = jnp.floor(jnp.log(wanted) * (1.0 / math.log(2.0)))
    return exponent * 128.0 + jnp.ceil((wanted * jnp.exp2(-exponent) - 1.0) * 128.0)


def scale_of(code):
    exponent = jnp.floor(code * (1.0 / 128.0))
    rest = code - 128.0 * exponent
    return jnp.exp2(exponent) * (1.0 + rest * (1.0 / 128.0))


def coded(values, scale):
    steps = jnp.floor(values * (1.0 / scale) + 0.5)
    return jnp.clip(steps, -TOP, TOP)


def as_int16(values):
    return values.astype(jnp.int32).astype(jnp.int16)


def from_int16(codes):
    return codes.astype(jnp.int32).astype(jnp.float32)


def advect_kernel(tracer_ref, east_ref, north_ref, above_ref, below_ref, west_ref, east_edge_ref, out_ref):
    levels, rows, lons = tracer_ref.shape
    for level in range(levels):
        field = tracer_ref[level].astype(jnp.float32)
        west = jnp.concatenate([west_ref[level].astype(jnp.float32), field[:, :-1]], axis=1)
        east = jnp.concatenate([field[:, 1:], east_edge_ref[level].astype(jnp.float32)], axis=1)
        north = jnp.concatenate([above_ref[level].astype(jnp.float32), field[:-1]], axis=0)
        south = jnp.concatenate([field[1:], below_ref[level].astype(jnp.float32)], axis=0)
        moved = (
            field
            - 0.5 * east_ref[level].astype(jnp.float32) * (east - west)
            - 0.5 * north_ref[level].astype(jnp.float32) * (south - north)
        )
        code = scale_code(jnp.max(jnp.abs(moved), axis=1, keepdims=True))
        steps = coded(moved, scale_of(code))
        out_ref[level] = as_int16(jnp.concatenate([steps, code], axis=1))


def advect(tracer, east_wind, north_wind):
    levels, rows, lons = tracer.shape
    lat_count = lax.axis_size("lat")
    ring = ("lev", "fld")
    lon_count = lax.axis_size(ring)
    down = [(i, i + 1) for i in range(lat_count - 1)]
    up = [(i + 1, i) for i in range(lat_count - 1)]
    right = [(i, (i + 1) % lon_count) for i in range(lon_count)]
    left = [((i + 1) % lon_count, i) for i in range(lon_count)]
    above = lax.ppermute(tracer[:, rows - 1 :, :], "lat", down)
    below = lax.ppermute(tracer[:, :1, :], "lat", up)
    west = lax.ppermute(tracer[:, :, -1:], ring, right)
    east = lax.ppermute(tracer[:, :, :1], ring, left)
    return pl.pallas_call(
        advect_kernel,
        out_shape=jax.ShapeDtypeStruct((levels, rows, lons + 1), jnp.int16),
        in_specs=[pl.BlockSpec(memory_space=pltpu.VMEM)] * 7,
        out_specs=pl.BlockSpec(memory_space=pltpu.VMEM),
        compiler_params=pltpu.CompilerParams(vmem_limit_bytes=VMEM_BYTES),
        cost_estimate=pl.CostEstimate(
            flops=20 * levels * rows * lons, bytes_accessed=8 * levels * rows * lons, transcendentals=0
        ),
    )(tracer, east_wind, north_wind, above, below, west, east)


def fourier_kernel(
    grid_ref, t0h, t0l, t2h, t2l, tah, tal, tbh, tbl, place_ref, wave_ref, keep_ref, sine_ref, out_ref
):
    pieces, rows, width = grid_ref.shape
    lons = width - 1
    share = pieces // 4

    def product(value, high_ref, low_ref, spot):
        high, low = split_bf16(value)
        part = jnp.dot(high, high_ref[spot], preferred_element_type=jnp.float32)
        part += jnp.dot(low, high_ref[spot], preferred_element_type=jnp.float32)
        return part + jnp.dot(high, low_ref[spot], preferred_element_type=jnp.float32)

    sums = [None, None, None]
    for spot in range(share):
        quarters = []
        for quarter in range(4):
            values = from_int16(grid_ref[quarter * share + spot])
            quarters.append(values[:, :lons] * scale_of(values[:, lons:]))
        sum02, dif02 = quarters[0] + quarters[2], quarters[0] - quarters[2]
        sum13, dif13 = quarters[1] + quarters[3], quarters[1] - quarters[3]
        parts = [
            product(sum02 + sum13, t0h, t0l, spot),
            product(sum02 - sum13, t2h, t2l, spot),
            product(dif02, tah, tal, spot) + product(dif13, tbh, tbl, spot),
        ]
        sums = [part if total is None else total + part for total, part in zip(sums, parts)]
    placed = None
    first = 0
    for total in sums:
        last = first + total.shape[1]
        high, low = split_bf16(total)
        part = jnp.dot(high, place_ref[first:last], preferred_element_type=jnp.float32)
        part += jnp.dot(low, place_ref[first:last], preferred_element_type=jnp.float32)
        placed = part if placed is None else placed + part
        first = last
    kept = jnp.where(wave_ref[...] < keep_ref[...], placed * sine_ref[...], 0.0)
    code = scale_code(jnp.max(jnp.abs(kept), axis=0, keepdims=True))
    steps = coded(kept, scale_of(code))
    targets, padded_rows, span = out_ref.shape
    codes = jnp.broadcast_to(code, (padded_rows - rows, code.shape[1]))
    result = as_int16(jnp.concatenate([steps, codes], axis=0))
    for target in range(targets):
        out_ref[target] = result[:, target * span : (target + 1) * span]


def fourier(grid, places, wave_row, keep_col, sine_col, targets):
    pieces, rows, _ = grid.shape
    span = wave_row.shape[1] // targets
    padded_rows = -(-(rows + 1) // 16) * 16
    tables = [part for table in fourier_tables(pieces) for part in table_bf16(table)]
    return pl.pallas_call(
        fourier_kernel,
        out_shape=jax.ShapeDtypeStruct((targets, padded_rows, span), jnp.int16),
        in_specs=[pl.BlockSpec(memory_space=pltpu.VMEM)] * 13,
        out_specs=pl.BlockSpec(memory_space=pltpu.VMEM),
        compiler_params=pltpu.CompilerParams(vmem_limit_bytes=VMEM_BYTES),
        cost_estimate=pl.CostEstimate(
            flops=3 * rows * NLON * M, bytes_accessed=6 * 2**20, transcendentals=0
        ),
    )(grid, *tables, places, wave_row, keep_col, sine_col)


def legendre_kernel(
    fields_ref, high_ref, low_ref, lat_ref, wave_ref, limit_ref, norm_ref,
    out_ref, weight, before, current, level, sums, result, beta_ref, scale_ref, growth_ref,
):
    half = lat_ref.shape[1]
    lanes = wave_ref.shape[1]
    slots = out_ref.shape[0]
    groups = lanes // LANES
    wave = wave_ref[...]
    odd = wave - 2.0 * jnp.floor(wave * 0.5) > 0.5

    def squares(order):
        degree = wave + order
        return 4.0 * degree * degree - 1.0, 4.0 * order * (degree + wave)

    square, spread = squares(
        lax.broadcasted_iota(jnp.int32, (M, lanes), 0).astype(jnp.float32)
    )
    beta_ref[...] = spread / jnp.maximum(square, 1.0)
    blocks = M // BLOCK
    first_order = lax.broadcasted_iota(jnp.int32, (blocks, lanes), 0).astype(jnp.float32) * BLOCK
    scale = jnp.ones((blocks, lanes), jnp.float32)
    for index in range(BLOCK):
        inside = first_order + index < limit_ref[...]
        scale_ref[pl.ds(index, blocks, stride=BLOCK)] = jnp.where(inside, scale, 0.0)
        square, spread = squares(first_order + (index + 1))
        scale = scale * jnp.sqrt(square / spread)
    growth_ref[...] = scale

    pieces, padded_rows, _ = fields_ref.shape
    totals = [None] * 4
    code_row = padded_rows - 1
    for piece in range(pieces):
        values = from_int16(fields_ref[piece])
        values = values * scale_of(values[code_row:])
        high, low = split_bf16(values)
        for table in range(4):
            rows = pl.ds(table * half, half)
            value = jnp.dot(high_ref[piece, rows], high, preferred_element_type=jnp.float32)
            value += jnp.dot(high_ref[piece, rows], low, preferred_element_type=jnp.float32)
            value += jnp.dot(low_ref[piece, rows], high, preferred_element_type=jnp.float32)
            totals[table] = value if piece == 0 else totals[table] + value
    for parity in range(2):
        for comp in range(2):
            cols = slice(comp * lanes, (comp + 1) * lanes)
            weight[2 * parity + comp] = jnp.where(
                odd, totals[2 + parity][:, cols], totals[parity][:, cols]
            )

    for group in range(groups):
        cols = slice(group * LANES, (group + 1) * LANES)
        coarse = lat_ref[1] * wave[:, cols]
        whole = jnp.floor(coarse)
        level[:, cols] = whole
        current[:, cols] = jnp.exp2(
            (coarse - whole) + lat_ref[2] * wave[:, cols] + norm_ref[:, cols]
        )
        before[:, cols] = jnp.zeros((half, LANES), jnp.float32)

    def step(block, carry):
        first = pl.multiple_of(block * BLOCK, 8)
        for group in range(groups):
            cols = slice(group * LANES, (group + 1) * LANES)
            grow = growth_ref[pl.ds(block, 1), cols]
            for chunk in range(half // CHUNK):
                rows = slice(chunk * CHUNK, (chunk + 1) * CHUNK)
                height = level[rows, cols]
                factor = jnp.exp2(height)
                weights = [weight[k, rows, cols] * factor for k in range(4)]
                cosine = lat_ref[0, rows]
                old = before[rows, cols]
                new = current[rows, cols]
                for order in range(BLOCK):
                    for comp in range(2):
                        product = new * weights[2 * (order % 2) + comp]
                        partial = product.reshape(CHUNK // 8, 8, LANES).sum(axis=0)
                        place = pl.ds((order * 2 + comp) * 8, 8)
                        if chunk == 0:
                            sums[place] = partial
                        else:
                            sums[place] += partial
                    beta = beta_ref[pl.ds(first + order, 1), cols]
                    old, new = new, cosine * new - beta * old
                biggest = jnp.maximum(jnp.abs(old), jnp.abs(new)) * grow
                shift = jnp.floor(jnp.log(biggest) * (1.0 / math.log(2.0)))
                factor = grow * jnp.exp2(-shift)
                before[rows, cols] = old * factor
                current[rows, cols] = new * factor
                level[rows, cols] = height + shift
            for comp in range(2):
                total = sums[pl.ds(comp * 8, BLOCK, stride=16)]
                for lane in range(1, 8):
                    total += sums[pl.ds(comp * 8 + lane, BLOCK, stride=16)]
                result[comp, pl.ds(first, BLOCK), cols] = (
                    total * scale_ref[pl.ds(first, BLOCK), cols]
                )
        return carry

    lax.fori_loop(0, M // BLOCK, step, 0)
    for comp in range(2):
        out_ref[:, comp, :] = result[comp].T[:slots]


def legendre(fields, slot_wave, rows):
    slots = slot_wave.shape[0]
    pieces, padded_rows, span = fields.shape
    lanes = span // 2
    half = M // 2
    wave_row = jnp.pad(slot_wave, (0, lanes - slots), constant_values=2 * M)[None, :]
    inside_wave = jnp.minimum(wave_row, M - 1).astype(jnp.float32)
    limit = (M - wave_row).astype(jnp.float32)
    counter = np.arange(1, M)[:, None]
    log_terms = (np.log1p(0.5 / counter) / math.log(2.0)).astype(np.float32)
    log_norm = jnp.sum(
        jnp.where(counter.astype(np.float32) <= inside_wave, log_terms, 0.0), axis=0, keepdims=True
    )
    norm = 0.5 * (log_norm - 1.0)
    table = resample_table().reshape(2 * M, pieces, rows).transpose(1, 0, 2)
    high, low = table_bf16(np.pad(table, ((0, 0), (0, 0), (0, padded_rows - rows))))
    vector = pltpu.VMEM((half, lanes), jnp.float32)
    orders = pltpu.VMEM((M, lanes), jnp.float32)
    return pl.pallas_call(
        legendre_kernel,
        out_shape=jax.ShapeDtypeStruct((slots, 2, M), jnp.float32),
        in_specs=[pl.BlockSpec(memory_space=pltpu.VMEM)] * 7,
        out_specs=pl.BlockSpec(memory_space=pltpu.VMEM),
        scratch_shapes=[
            pltpu.VMEM((4, half, lanes), jnp.float32),
            vector,
            vector,
            vector,
            pltpu.VMEM((BLOCK * 16, LANES), jnp.float32),
            pltpu.VMEM((2, M, lanes), jnp.float32),
            orders,
            orders,
            pltpu.VMEM((M // BLOCK, lanes), jnp.float32),
        ],
        compiler_params=pltpu.CompilerParams(vmem_limit_bytes=VMEM_BYTES),
        cost_estimate=pl.CostEstimate(
            flops=7 * half * lanes * M, bytes_accessed=6 * 2**20, transcendentals=0
        ),
    )(fields, high, low, latitude_table(), inside_wave, limit, norm)


def shards(tracer, wind_east, wind_north, keep_m, slot_wave):
    rows = tracer.shape[1]
    lat_count = lax.axis_size("lat")
    slots = slot_wave.shape[0] // lat_count
    lanes = -(-slots // LANES) * LANES
    lat_index = lax.axis_index("lat")

    advected = advect(tracer, wind_east, wind_north)
    grid = lax.all_to_all(advected, ("lev", "fld"), split_axis=0, concat_axis=0, tiled=True)

    pad = ((0, 0), (0, 0), (0, lanes - slots))
    waves = jnp.pad(slot_wave.reshape(lat_count, 1, slots), pad, constant_values=2 * M)
    waves = jnp.broadcast_to(waves, (lat_count, 2, lanes))
    table_rows = wave_rows()
    spots = np.full(4 * (-(-M // 2 // (2 * LANES)) * 2 * LANES), 4 * M, np.int32)
    for part in range(2):
        spots[table_rows[part]] = np.arange(M) * 2 + part
    columns = (waves * 2 + jnp.array([0, 1], jnp.int32)[None, :, None]).reshape(1, -1)
    places = ((spots[:, None] == columns) & (columns < 2 * M)).astype(jnp.bfloat16)
    row_ids = (lat_index * rows + jnp.arange(rows, dtype=jnp.int32)).astype(jnp.float32)
    sines = jnp.sin(math.pi / NLAT * (row_ids + 0.5)) * math.sqrt(2.0 / NLAT)
    waved = fourier(
        grid, places, waves.reshape(1, -1), keep_m[:, None], sines[:, None], lat_count
    )
    fields = lax.all_to_all(waved, "lat", split_axis=0, concat_axis=0, tiled=True)
    my_waves = lax.dynamic_slice_in_dim(slot_wave, lat_index * slots, slots)
    return legendre(fields, my_waves, rows)[None]


def solution(mesh):
    return jax.shard_map(
        shards,
        mesh=mesh,
        in_specs=(
            P("member", "lat", ("lev", "fld")),
            P("member", "lat", ("lev", "fld")),
            P("member", "lat", ("lev", "fld")),
            P("lat"),
            P(),
        ),
        out_specs=P(("member", "lev", "fld"), "lat", None, None),
        check_vma=False,
    )
```

time: 111 us -> 83.2 us (0.75)
  other arithmetic: 23.9 us -> 1.26 us
  waiting for transfers between devices: 34 us -> 25.4 us
  local copies, waits for them, and re-layouts: 16 us -> 18.3 us
  starting transfers between devices: 15.6 us -> 17.6 us
  Pallas kernels: 20.9 us -> 19.6 us
    unnamed x30 -> x0, other arithmetic: 18 us -> none
    all_to_all x1, waiting for transfers between devices: 17.4 us -> 11.4 us  [shards(): lax.all_to_all(waved, 'lat', split_axis=0, concat_axis=0, tiled=True)]
    all_to_all x1, waiting for transfers between devices: 16.5 us -> 11.4 us  [shards(): lax.all_to_all(advected, ('lev', 'fld'), split_axis=0, concat_axis=0, til...]
    unnamed x33 -> x34, local copies, waits for them, and re-layouts: 10.5 us -> 14 us
    sub x1 -> x0, other arithmetic: 2.18 us -> none  [advect(): tracer.astype(jnp.float32) - 0.5 * east_wind.astype(jnp.float32) * east_diff]
    all_to_all x1, starting transfers between devices: 4.15 us -> 5.94 us  [shards(): lax.all_to_all(waved, 'lat', split_axis=0, concat_axis=0, tiled=True)]
    ppermute x1, waiting for transfers between devices: 0.01 us -> 1.79 us  [advect(): west = lax.ppermute(tracer[:, :, -1:], ring, right)]
    pallas_call x1, Pallas kernels: 14.5 us -> 13.4 us  [legendre(): pl.pallas_call(legendre_kernel, out_shape=jax.ShapeDtypeStruct((slots, 2,...]
  transfers between devices with their start and end apart: 6 -> 6, of which waited for: 2 -> 4; matrix products, arithmetic and copies ran while one was open for 29% -> 6% of each run, Pallas kernels for 0% -> 0%
where the time goes in v2:
time: 83.2 us; the launch traced here: 82.3 us
  waiting for transfers between devices  25.4 us (31%)
  Pallas kernels  19.6 us (24%)
  local copies, waits for them, and re-layouts  18.3 us (22%)
  starting transfers between devices  17.6 us (21%)
  other arithmetic  1.26 us (2%)
    unnamed x34, local copies, waits for them, and re-layouts  14 us
    pallas_call x1, Pallas kernels, legendre(): pl.pallas_call(legendre_kernel, out_shape=jax.ShapeDtypeStruct((slots, 2,...  13.4 us
    all_to_all x1, waiting for transfers between devices, shards(): lax.all_to_all(advected, ('lev', 'fld'), split_axis=0, concat_axis=0, til...  11.4 us
    all_to_all x1, waiting for transfers between devices, shards(): lax.all_to_all(waved, 'lat', split_axis=0, concat_axis=0, tiled=True)  11.4 us
    all_to_all x1, starting transfers between devices, shards(): lax.all_to_all(waved, 'lat', split_axis=0, concat_axis=0, tiled=True)  5.94 us
    ppermute x1, starting transfers between devices, advect(): above = lax.ppermute(tracer[:, rows - 1:, :], 'lat', down)  4.93 us
    all_to_all x1, starting transfers between devices, shards(): lax.all_to_all(advected, ('lev', 'fld'), split_axis=0, concat_axis=0, til...  3.63 us
    pallas_call x1, Pallas kernels, fourier(): pl.pallas_call(fourier_kernel, out_shape=jax.ShapeDtypeStruct((targets, p...  3.32 us
  transfers between devices with their start and end apart: 6, of which 4 were waited for; matrix products, arithmetic and copies ran while one was open for 6% of the time, Pallas kernels for 0%

profile of v2, /device:TPU:0, one launch (start us, length us, event | category | flops | bytes accessed | tf_op | source)
XLA Modules:
  0.0 82.3 jit_solution(9121960536234478482)
XLA Ops:
  0.8 4.9 %collective-permute-start = (bf16[4,1,400]{2,1,0:T(2,128)(2,1)S(1)}, bf16[4,1,400]{2,1,0:T(2,128)(2,1)S(1)}, u32[]{:S(2)}, u32[]{:S(2)}) collective-permute-start(bf16[4,1,400]{2,1,0:T(2,128)(2,1)S(1)} %get-tuple-element.8), channel_id=1, source_target_pairs={{0,4},{4,8},{8,12},{1,5},{5,9},{9,13},{2,6},{6,10},{10,14},{3,7},{... | collective-permute-start | bytes 9608 | tf_op jit(solution)/shard_map/ppermute | solution.py:148
  5.7 1.3 %collective-permute-start.1 = (bf16[4,1,400]{2,1,0:T(2,128)(2,1)S(1)}, bf16[4,1,400]{2,1,0:T(2,128)(2,1)S(1)}, u32[]{:S(2)}, u32[]{:S(2)}) collective-permute-start(bf16[4,1,400]{2,1,0:T(2,128)(2,1)S(1)} %get-tuple-element.7), channel_id=1, source_target_pairs={{4,0},{8,4},{12,8},{5,1},{9,5},{13,9},{6,2},{10,6},{14,10},{7,3},{... | collective-permute-start | bytes 9608 | tf_op jit(solution)/shard_map/ppermute | solution.py:149
  7.0 1.2 %fusion.1 = (bf16[4,200,1]{2,1,0:T(8,128)(2,1)S(1)}, bf16[4,200,1]{2,1,0:T(8,128)(2,1)S(1)}) fusion(bf16[4,200,400]{2,1,0:T(8,128)(2,1)} %tracer_ref.1), kind=kLoop, calls=%fused_computation.11 | loop fusion | bytes 6400 | tf_op jit(solution)/shard_map/slice | solution.py:151
  8.3 1.7 %collective-permute-start.3 = (bf16[4,200,1]{2,1,0:T(8,128)(2,1)S(1)}, bf16[4,200,1]{2,1,0:T(8,128)(2,1)S(1)}, u32[]{:S(2)}, u32[]{:S(2)}) collective-permute-start(bf16[4,200,1]{2,1,0:T(8,128)(2,1)S(1)} %get-tuple-element.5), channel_id=1, source_target_pairs={{1,0},{2,1},{3,2},{0,3},{5,4},{6,5},{7,6},{4,7},{9,8},{10,9},{11,1... | collective-permute-start | bytes 4808 | tf_op jit(solution)/shard_map/ppermute | solution.py:151
  12.0 1.8 %collective-permute-done.2.west_ref = bf16[4,200,1]{2,1,0:T(8,128)(2,1)S(1)} collective-permute-done((bf16[4,200,1]{2,1,0:T(8,128)(2,1)S(1)}, bf16[4,200,1]{2,1,0:T(8,128)(2,1)S(1)}, u32[]{:S(2)}, u32[]{:S(2)}) %collective-permute-start.2) | collective-permute-done | bytes 1632 | tf_op jit(solution)/shard_map/ppermute | solution.py:150
  14.6 1.1 %copy-done = bf16[4,200,400]{2,1,0:T(8,128)(2,1)S(1)} copy-done((bf16[4,200,400]{2,1,0:T(8,128)(2,1)S(1)}, bf16[4,200,400]{2,1,0:T(8,128)(2,1)}, u32[]{:S(2)}) %copy-start) | copy-done | bytes 640024
  15.8 1.1 %copy-done.3 = bf16[4,200,400]{2,1,0:T(8,128)(2,1)S(1)} copy-done((bf16[4,200,400]{2,1,0:T(8,128)(2,1)S(1)}, bf16[4,200,400]{2,1,0:T(8,128)(2,1)}, u32[]{:S(2)}) %copy-start.3) | copy-done | bytes 640024
  16.9 1.1 %copy-done.4 = bf16[4,200,400]{2,1,0:T(8,128)(2,1)S(1)} copy-done((bf16[4,200,400]{2,1,0:T(8,128)(2,1)S(1)}, bf16[4,200,400]{2,1,0:T(8,128)(2,1)}, u32[]{:S(2)}) %copy-start.4) | copy-done | bytes 640024
  18.1 2.9 %shard_map.190 = s16[4,200,401]{2,1,0:T(8,128)(2,1)} custom-call(bf16[4,200,400]{2,1,0:T(8,128)(2,1)S(1)} %copy-done, bf16[4,200,400]{2,1,0:T(8,128)(2,1)S(1)} %copy-done.3, bf16[4,200,400]{2,1,0:T(8,128)(2,1)S(1)} %copy-done.4, bf16[4,1,400]{2,1,0:T(2,128)(2,1)S(1)} %collective-permute-done.above_ref, ...), custom_call_target="tpu_custom_call" | custom-call | flops 6400000 | bytes 2560000 | tf_op jit(solution)/shard_map/pallas_call | solution.py:152
  21.0 3.6 %all-to-all-start = ((s16[4,200,401]{2,1,0:T(8,128)(2,1)}), s16[4,200,401]{2,1,0:T(8,128)(2,1)S(1)}, u32[]{:S(2)}, u32[]{:S(2)}) async-start(s16[4,200,401]{2,1,0:T(8,128)(2,1)} %shard_map.190), calls=%async_computation | async-start | bytes 1638400 | tf_op jit(solution)/shard_map/all_to_all | solution.py:379
  25.3 11.4 %all-to-all-done.grid_ref = s16[4,200,401]{2,1,0:T(8,128)(2,1)S(1)} async-done(((s16[4,200,401]{2,1,0:T(8,128)(2,1)}), s16[4,200,401]{2,1,0:T(8,128)(2,1)S(1)}, u32[]{:S(2)}, u32[]{:S(2)}) %all-to-all-start) | async-done | bytes 641632 | tf_op jit(solution)/shard_map/all_to_all | solution.py:379
  36.7 1.0 %copy-done.6 = bf16[1,400,512]{2,1,0:T(8,128)(2,1)S(1)} copy-done((bf16[1,400,512]{2,1,0:T(8,128)(2,1)S(1)}, bf16[1,400,512]{2,1,0:T(8,128)(2,1)}, u32[]{:S(2)}) %copy-start.6) | copy-done | bytes 409624
  37.7 1.0 %copy-done.7 = bf16[1,400,512]{2,1,0:T(8,128)(2,1)S(1)} copy-done((bf16[1,400,512]{2,1,0:T(8,128)(2,1)S(1)}, bf16[1,400,512]{2,1,0:T(8,128)(2,1)}, u32[]{:S(2)}) %copy-start.7) | copy-done | bytes 409624
  38.7 1.0 %copy-done.8 = bf16[1,400,512]{2,1,0:T(8,128)(2,1)S(1)} copy-done((bf16[1,400,512]{2,1,0:T(8,128)(2,1)S(1)}, bf16[1,400,512]{2,1,0:T(8,128)(2,1)}, u32[]{:S(2)}) %copy-start.8) | copy-done | bytes 409624
  39.7 0.9 %copy-done.10 = bf16[1,400,256]{2,1,0:T(8,128)(2,1)S(1)} copy-done((bf16[1,400,256]{2,1,0:T(8,128)(2,1)S(1)}, bf16[1,400,256]{2,1,0:T(8,128)(2,1)}, u32[]{:S(2)}) %copy-start.10) | copy-done | bytes 204824
  41.6 0.9 %copy-done.12 = bf16[1,400,256]{2,1,0:T(8,128)(2,1)S(1)} copy-done((bf16[1,400,256]{2,1,0:T(8,128)(2,1)S(1)}, bf16[1,400,256]{2,1,0:T(8,128)(2,1)}, u32[]{:S(2)}) %copy-start.12) | copy-done | bytes 204824
  42.5 0.9 %copy-done.13 = bf16[1,400,256]{2,1,0:T(8,128)(2,1)S(1)} copy-done((bf16[1,400,256]{2,1,0:T(8,128)(2,1)S(1)}, bf16[1,400,256]{2,1,0:T(8,128)(2,1)}, u32[]{:S(2)}) %copy-start.13) | copy-done | bytes 204824
  43.5 3.3 %shard_map.191 = s16[4,208,256]{2,1,0:T(8,128)(2,1)} custom-call(s16[4,200,401]{2,1,0:T(8,128)(2,1)S(1)} %all-to-all-done.grid_ref, bf16[1,400,256]{2,1,0:T(8,128)(2,1)S(1)} %copy-done.10, bf16[1,400,256]{2,1,0:T(8,128)(2,1)S(1)} %copy-done.11, bf16[1,400,256]{2,1,0:T(8,128)(2,1)S(1)} %copy-done.12, bf16[1,400,256]{2,1,0:T(8,128)(2,1)S(1)} %copy-done.13, ...), custom_call_target="tpu_custom_call" | custom-call | flops 384000000 | bytes 6291456 | tf_op jit(solution)/shard_map/pallas_call | solution.py:215
  46.8 5.9 %all-to-all-start.1 = ((s16[4,208,256]{2,1,0:T(8,128)(2,1)}), s16[4,208,256]{2,1,0:T(8,128)(2,1)S(1)}, u32[]{:S(2)}, u32[]{:S(2)}) async-start(s16[4,208,256]{2,1,0:T(8,128)(2,1)} %shard_map.191), calls=%async_computation.1 | async-start | bytes 851968 | tf_op jit(solution)/shard_map/all_to_all | solution.py:395
  53.7 11.4 %all-to-all-done.1.fields_ref = s16[4,208,256]{2,1,0:T(8,128)(2,1)S(1)} async-done(((s16[4,208,256]{2,1,0:T(8,128)(2,1)}), s16[4,208,256]{2,1,0:T(8,128)(2,1)S(1)}, u32[]{:S(2)}, u32[]{:S(2)}) %all-to-all-start.1) | async-done | bytes 426016 | tf_op jit(solution)/shard_map/all_to_all | solution.py:395
  65.1 1.4 %copy-done.1 = bf16[4,800,208]{2,1,0:T(8,128)(2,1)S(1)} copy-done((bf16[4,800,208]{2,1,0:T(8,128)(2,1)S(1)}, bf16[4,800,208]{2,1,0:T(8,128)(2,1)}, u32[]{:S(2)}) %copy-start.1) | copy-done | bytes 1331224
  66.5 1.4 %copy-done.2 = bf16[4,800,208]{2,1,0:T(8,128)(2,1)S(1)} copy-done((bf16[4,800,208]{2,1,0:T(8,128)(2,1)S(1)}, bf16[4,800,208]{2,1,0:T(8,128)(2,1)}, u32[]{:S(2)}) %copy-start.2) | copy-done | bytes 1331224
  67.9 1.0 %copy-done.9 = f32[3,200,128]{2,1,0:T(8,128)S(1)} copy-done((f32[3,200,128]{2,1,0:T(8,128)S(1)}, f32[3,200,128]{2,1,0:T(8,128)}, u32[]{:S(2)}) %copy-start.9) | copy-done | bytes 307224
  68.9 13.4 %shard_map.192 = f32[100,2,400]{2,1,0:T(2,128)} custom-call(s16[4,208,256]{2,1,0:T(8,128)(2,1)S(1)} %all-to-all-done.1.fields_ref, bf16[4,800,208]{2,1,0:T(8,128)(2,1)S(1)} %copy-done.1, bf16[4,800,208]{2,1,0:T(8,128)(2,1)S(1)} %copy-done.2, f32[3,200,128]{2,1,0:T(8,128)S(1)} %copy-done.9, f32[1,128]{1,0:T(1,128)S(1)} %get-tuple-element.10.wave_ref, ...), custom_call_target="tpu_custom_call" | custom-call | flops 71680000 | bytes 6291456 | tf_op jit(solution)/shard_map/pallas_call | solution.py:348
  (40 shorter events, 6.3 us)
Async XLA Ops:
  0.8 13.8 %collective-permute-start = (bf16[4,1,400]{2,1,0:T(2,128)(2,1)S(1)}, bf16[4,1,400]{2,1,0:T(2,128)(2,1)S(1)}, u32[]{:S(2)}, u32[]{:S(2)}) collective-permute-start(bf16[4,1,400]{2,1,0:T(2,128)(2,1)S(1)} %get-tuple-element.8), channel_id=1, source_target_pairs={{0,4},{4,8},{8,12},{1,5},{5,9},{9,13},{2,6},{6,10},{10,14},{3,7},{... | collective-permute-start | bytes 9608 | tf_op jit(solution)/shard_map/ppermute | solution.py:148
  5.7 8.9 %collective-permute-start.1 = (bf16[4,1,400]{2,1,0:T(2,128)(2,1)S(1)}, bf16[4,1,400]{2,1,0:T(2,128)(2,1)S(1)}, u32[]{:S(2)}, u32[]{:S(2)}) collective-permute-start(bf16[4,1,400]{2,1,0:T(2,128)(2,1)S(1)} %get-tuple-element.7), channel_id=1, source_target_pairs={{4,0},{8,4},{12,8},{5,1},{9,5},{13,9},{6,2},{10,6},{14,10},{7,3},{... | collective-permute-start | bytes 9608 | tf_op jit(solution)/shard_map/ppermute | solution.py:149
  8.2 5.6 %collective-permute-start.2 = (bf16[4,200,1]{2,1,0:T(8,128)(2,1)S(1)}, bf16[4,200,1]{2,1,0:T(8,128)(2,1)S(1)}, u32[]{:S(2)}, u32[]{:S(2)}) collective-permute-start(bf16[4,200,1]{2,1,0:T(8,128)(2,1)S(1)} %get-tuple-element.6), channel_id=1, source_target_pairs={{0,1},{1,2},{2,3},{3,0},{4,5},{5,6},{6,7},{7,4},{8,9},{9,10},{10,1... | collective-permute-start | bytes 4808 | tf_op jit(solution)/shard_map/ppermute | solution.py:150
  8.3 6.4 %collective-permute-start.3 = (bf16[4,200,1]{2,1,0:T(8,128)(2,1)S(1)}, bf16[4,200,1]{2,1,0:T(8,128)(2,1)S(1)}, u32[]{:S(2)}, u32[]{:S(2)}) collective-permute-start(bf16[4,200,1]{2,1,0:T(8,128)(2,1)S(1)} %get-tuple-element.5), channel_id=1, source_target_pairs={{1,0},{2,1},{3,2},{0,3},{5,4},{6,5},{7,6},{4,7},{9,8},{10,9},{11,1... | collective-permute-start | bytes 4808 | tf_op jit(solution)/shard_map/ppermute | solution.py:151
  11.2 13.5 %copy-start.14 = (s32[1024]{0:T(1024)S(1)}, s32[1024]{0:T(1024)}, u32[]{:S(2)}) copy-start(s32[1024]{0:T(1024)} %constant.81) | copy-start | bytes 12292
  14.6 1.1 %copy-start = (bf16[4,200,400]{2,1,0:T(8,128)(2,1)S(1)}, bf16[4,200,400]{2,1,0:T(8,128)(2,1)}, u32[]{:S(2)}) copy-start(bf16[4,200,400]{2,1,0:T(8,128)(2,1)} %tracer_ref.1) | copy-start | bytes 1920004
  15.8 1.1 %copy-start.3 = (bf16[4,200,400]{2,1,0:T(8,128)(2,1)S(1)}, bf16[4,200,400]{2,1,0:T(8,128)(2,1)}, u32[]{:S(2)}) copy-start(bf16[4,200,400]{2,1,0:T(8,128)(2,1)} %east_ref.1) | copy-start | bytes 1920004
  16.9 1.1 %copy-start.4 = (bf16[4,200,400]{2,1,0:T(8,128)(2,1)S(1)}, bf16[4,200,400]{2,1,0:T(8,128)(2,1)}, u32[]{:S(2)}) copy-start(bf16[4,200,400]{2,1,0:T(8,128)(2,1)} %north_ref.1) | copy-start | bytes 1920004
  21.0 15.7 %copy-start.5 = (bf16[1,400,512]{2,1,0:T(8,128)(2,1)S(1)}, bf16[1,400,512]{2,1,0:T(8,128)(2,1)}, u32[]{:S(2)}) copy-start(bf16[1,400,512]{2,1,0:T(8,128)(2,1)} %constant.68.clone.tah) | copy-start | bytes 1228804
  21.0 15.7 %all-to-all-start = ((s16[4,200,401]{2,1,0:T(8,128)(2,1)}), s16[4,200,401]{2,1,0:T(8,128)(2,1)S(1)}, u32[]{:S(2)}, u32[]{:S(2)}) async-start(s16[4,200,401]{2,1,0:T(8,128)(2,1)} %shard_map.190), calls=%async_computation | async-start | bytes 1638400 | tf_op jit(solution)/shard_map/all_to_all | solution.py:379
  36.7 1.0 %copy-start.6 = (bf16[1,400,512]{2,1,0:T(8,128)(2,1)S(1)}, bf16[1,400,512]{2,1,0:T(8,128)(2,1)}, u32[]{:S(2)}) copy-start(bf16[1,400,512]{2,1,0:T(8,128)(2,1)} %constant.69.clone.tal) | copy-start | bytes 1228804
  37.7 1.0 %copy-start.7 = (bf16[1,400,512]{2,1,0:T(8,128)(2,1)S(1)}, bf16[1,400,512]{2,1,0:T(8,128)(2,1)}, u32[]{:S(2)}) copy-start(bf16[1,400,512]{2,1,0:T(8,128)(2,1)} %constant.70.clone.tbh) | copy-start | bytes 1228804
  38.7 1.0 %copy-start.8 = (bf16[1,400,512]{2,1,0:T(8,128)(2,1)S(1)}, bf16[1,400,512]{2,1,0:T(8,128)(2,1)}, u32[]{:S(2)}) copy-start(bf16[1,400,512]{2,1,0:T(8,128)(2,1)} %constant.71.clone.tbl) | copy-start | bytes 1228804
  39.7 0.9 %copy-start.10 = (bf16[1,400,256]{2,1,0:T(8,128)(2,1)S(1)}, bf16[1,400,256]{2,1,0:T(8,128)(2,1)}, u32[]{:S(2)}) copy-start(bf16[1,400,256]{2,1,0:T(8,128)(2,1)} %constant.64.clone.t0h) | copy-start | bytes 614404
  40.7 0.9 %copy-start.11 = (bf16[1,400,256]{2,1,0:T(8,128)(2,1)S(1)}, bf16[1,400,256]{2,1,0:T(8,128)(2,1)}, u32[]{:S(2)}) copy-start(bf16[1,400,256]{2,1,0:T(8,128)(2,1)} %constant.65.clone.t0l) | copy-start | bytes 614404
  41.6 0.9 %copy-start.12 = (bf16[1,400,256]{2,1,0:T(8,128)(2,1)S(1)}, bf16[1,400,256]{2,1,0:T(8,128)(2,1)}, u32[]{:S(2)}) copy-start(bf16[1,400,256]{2,1,0:T(8,128)(2,1)} %constant.66.clone.t2h) | copy-start | bytes 614404
  42.5 0.9 %copy-start.13 = (bf16[1,400,256]{2,1,0:T(8,128)(2,1)S(1)}, bf16[1,400,256]{2,1,0:T(8,128)(2,1)}, u32[]{:S(2)}) copy-start(bf16[1,400,256]{2,1,0:T(8,128)(2,1)} %constant.67.clone.t2l) | copy-start | bytes 614404
  43.5 10.0 %copy-start.15 = (f32[399]{0:T(512)S(1)}, f32[399]{0:T(512)}, u32[]{:S(2)}) copy-start(f32[399]{0:T(512)} %constant.83) | copy-start | bytes 4792
  43.5 10.0 %copy-start.16 = (f32[399]{0:T(512)S(1)}, f32[399]{0:T(512)}, u32[]{:S(2)}) copy-start(f32[399]{0:T(512)} %constant.82) | copy-start | bytes 4792
  46.8 18.3 %all-to-all-start.1 = ((s16[4,208,256]{2,1,0:T(8,128)(2,1)}), s16[4,208,256]{2,1,0:T(8,128)(2,1)S(1)}, u32[]{:S(2)}, u32[]{:S(2)}) async-start(s16[4,208,256]{2,1,0:T(8,128)(2,1)} %shard_map.191), calls=%async_computation.1 | async-start | bytes 851968 | tf_op jit(solution)/shard_map/all_to_all | solution.py:395
  65.1 1.4 %copy-start.1 = (bf16[4,800,208]{2,1,0:T(8,128)(2,1)S(1)}, bf16[4,800,208]{2,1,0:T(8,128)(2,1)}, u32[]{:S(2)}) copy-start(bf16[4,800,208]{2,1,0:T(8,128)(2,1)} %constant.74.clone.high_ref) | copy-start | bytes 3993604
  66.5 1.4 %copy-start.2 = (bf16[4,800,208]{2,1,0:T(8,128)(2,1)S(1)}, bf16[4,800,208]{2,1,0:T(8,128)(2,1)}, u32[]{:S(2)}) copy-start(bf16[4,800,208]{2,1,0:T(8,128)(2,1)} %constant.75.clone.low_ref) | copy-start | bytes 3993604
  67.9 1.0 %copy-start.9 = (f32[3,200,128]{2,1,0:T(8,128)S(1)}, f32[3,200,128]{2,1,0:T(8,128)}, u32[]{:S(2)}) copy-start(f32[3,200,128]{2,1,0:T(8,128)} %constant.76.clone.lat_ref) | copy-start | bytes 921604

commit v3 on v2

--- a/solution.py
+++ b/solution.py
@@ -1,3 +1,4 @@
+import functools
 import math
 
 import jax
@@ -15,7 +16,11 @@
 BLOCK = 40
 CHUNK = 40
 TOP = 32767.0
+WIND_STEP = 1.5 / TOP
 VMEM_BYTES = 24 * 2**20
+VMEM_SPEC = pl.BlockSpec(memory_space=pltpu.VMEM)
+SMEM_SPEC = pl.BlockSpec(memory_space=pltpu.SMEM)
+ANY_SPEC = pl.BlockSpec(memory_space=pl.ANY)
 
 
 def split_bf16(values):
@@ -27,7 +32,7 @@
 def table_bf16(table):
     high = table.astype(jnp.bfloat16)
     low = (table - high.astype(np.float64)).astype(jnp.bfloat16)
-    return high, low
+    return np.concatenate([high, low], axis=-1)
 
 
 def fourier_tables(pieces):
@@ -118,75 +123,153 @@
     return codes.astype(jnp.int32).astype(jnp.float32)
 
 
-def advect_kernel(tracer_ref, east_ref, north_ref, above_ref, below_ref, west_ref, east_edge_ref, out_ref):
-    levels, rows, lons = tracer_ref.shape
-    for level in range(levels):
-        field = tracer_ref[level].astype(jnp.float32)
-        west = jnp.concatenate([west_ref[level].astype(jnp.float32), field[:, :-1]], axis=1)
-        east = jnp.concatenate([field[:, 1:], east_edge_ref[level].astype(jnp.float32)], axis=1)
-        north = jnp.concatenate([above_ref[level].astype(jnp.float32), field[:-1]], axis=0)
-        south = jnp.concatenate([field[1:], below_ref[level].astype(jnp.float32)], axis=0)
+def partners(axis):
+    count = lax.axis_size(axis)
+    order = jnp.arange(count, dtype=jnp.int32)
+    return lax.axis_index(axis).astype(jnp.int32) ^ order if count == 4 else order
+
+
+def exchange(blocks, axis):
+    count = len(blocks)
+    if count != 4:
+        return list(lax.all_to_all(jnp.stack(blocks), axis, split_axis=0, concat_axis=0, tiled=True))
+    pairs = [[(i, i ^ step) for i in range(count)] for step in range(count)]
+    return [blocks[0]] + [lax.ppermute(blocks[step], axis, pairs[step]) for step in range(1, count)]
+
+
+def advect_kernel(order_ref, tracer_hbm, east_hbm, north_hbm, above_ref, below_ref, *rest):
+    levels, rows, lons = tracer_hbm.shape
+    outs, (tracer, east_wind, north_wind, sems) = rest[:levels], rest[levels:]
+    copies = []
+    for step in range(levels):
+        level = order_ref[step]
+        copies.append(
+            [
+                pltpu.make_async_copy(source.at[level], target.at[step], sems.at[step, kind])
+                for kind, (source, target) in enumerate(
+                    ((tracer_hbm, tracer), (east_hbm, east_wind), (north_hbm, north_wind))
+                )
+            ]
+        )
+        for copy in copies[-1]:
+            copy.start()
+    for step in range(levels):
+        level = order_ref[step]
+        for copy in copies[step]:
+            copy.wait()
+        field = tracer[step].astype(jnp.float32)
+        first, last = field[:, :1], field[:, lons - 1 :]
+        blank = jnp.zeros_like(first)
+        west = jnp.concatenate([blank, field[:, :-1]], axis=1)
+        east = jnp.concatenate([field[:, 1:], blank], axis=1)
+        above = above_ref[level].astype(jnp.float32)
+        below = below_ref[level].astype(jnp.float32)
+        north = jnp.concatenate([above, field[:-1]], axis=0)
+        south = jnp.concatenate([field[1:], below], axis=0)
+        eastward = 0.5 * east_wind[step].astype(jnp.float32)
         moved = (
             field
-            - 0.5 * east_ref[level].astype(jnp.float32) * (east - west)
-            - 0.5 * north_ref[level].astype(jnp.float32) * (south - north)
+            - eastward * (east - west)
+            - 0.5 * north_wind[step].astype(jnp.float32) * (south - north)
         )
-        code = scale_code(jnp.max(jnp.abs(moved), axis=1, keepdims=True))
-        steps = coded(moved, scale_of(code))
-        out_ref[level] = as_int16(jnp.concatenate([steps, code], axis=1))
-
-
-def advect(tracer, east_wind, north_wind):
+        biggest = jnp.maximum(jnp.abs(moved), jnp.abs(field))
+        code = scale_code(jnp.max(biggest, axis=1, keepdims=True))
+        scale = scale_of(code)
+        wind = jnp.concatenate([eastward[:, :1], eastward[:, lons - 1 :]], axis=1)
+        outs[step][...] = as_int16(
+            jnp.concatenate(
+                [
+                    coded(moved, scale),
+                    code,
+                    coded(first, scale),
+                    coded(last, scale),
+                    coded(wind, WIND_STEP),
+                ],
+                axis=1,
+            )
+        )
+
+
+def advect(tracer, east_wind, north_wind, order):
     levels, rows, lons = tracer.shape
     lat_count = lax.axis_size("lat")
-    ring = ("lev", "fld")
-    lon_count = lax.axis_size(ring)
     down = [(i, i + 1) for i in range(lat_count - 1)]
     up = [(i + 1, i) for i in range(lat_count - 1)]
-    right = [(i, (i + 1) % lon_count) for i in range(lon_count)]
-    left = [((i + 1) % lon_count, i) for i in range(lon_count)]
     above = lax.ppermute(tracer[:, rows - 1 :, :], "lat", down)
     below = lax.ppermute(tracer[:, :1, :], "lat", up)
-    west = lax.ppermute(tracer[:, :, -1:], ring, right)
-    east = lax.ppermute(tracer[:, :, :1], ring, left)
+    held = pltpu.VMEM((levels, rows, lons), jnp.bfloat16)
     return pl.pallas_call(
         advect_kernel,
-        out_shape=jax.ShapeDtypeStruct((levels, rows, lons + 1), jnp.int16),
-        in_specs=[pl.BlockSpec(memory_space=pltpu.VMEM)] * 7,
-        out_specs=pl.BlockSpec(memory_space=pltpu.VMEM),
+        out_shape=[jax.ShapeDtypeStruct((rows, lons + 5), jnp.int16)] * levels,
+        in_specs=[SMEM_SPEC] + [ANY_SPEC] * 3 + [VMEM_SPEC] * 2,
+        out_specs=[VMEM_SPEC] * levels,
+        scratch_shapes=[held, held, held, pltpu.SemaphoreType.DMA((levels, 3))],
         compiler_params=pltpu.CompilerParams(vmem_limit_bytes=VMEM_BYTES),
         cost_estimate=pl.CostEstimate(
             flops=20 * levels * rows * lons, bytes_accessed=8 * levels * rows * lons, transcendentals=0
         ),
-    )(tracer, east_wind, north_wind, above, below, west, east)
-
-
-def fourier_kernel(
-    grid_ref, t0h, t0l, t2h, t2l, tah, tal, tbh, tbl, place_ref, wave_ref, keep_ref, sine_ref, out_ref
-):
-    pieces, rows, width = grid_ref.shape
-    lons = width - 1
+    )(order, tracer, east_wind, north_wind, above, below)
+
+
+def fourier_kernel(pieces, targets, order_ref, *rest):
+    grids, rest = rest[:pieces], rest[pieces:]
+    tables_hbm, (place_ref, wave_ref, keep_ref, sine_ref), rest = rest[:4], rest[4:8], rest[8:]
+    outs, rest = rest[:targets], rest[targets:]
+    tables, (field, sems) = rest[:4], rest[4:]
+    _, rows, lons = field.shape
     share = pieces // 4
-
-    def product(value, high_ref, low_ref, spot):
+    copies = []
+    for kind in range(4):
+        copies.append(pltpu.make_async_copy(tables_hbm[kind], tables[kind], sems.at[kind]))
+        copies[-1].start()
+
+    edges = []
+    for piece in range(pieces):
+        values = from_int16(grids[piece][...])
+        code = values[:, lons : lons + 1]
+        field[order_ref[piece]] = values[:, :lons] * scale_of(code)
+        edges.append((scale_of(code), values[:, lons + 1 :]))
+    end = (lons - 1) // LANES * LANES
+    head = lax.broadcasted_iota(jnp.int32, (rows, LANES), 1) == 0
+    tail = lax.broadcasted_iota(jnp.int32, (rows, lons - end), 1) == lons - end - 1
+    for piece in range(pieces):
+        spot = order_ref[piece]
+        scale, ends = edges[piece]
+        first = scale * ends[:, 0:1]
+        last = scale * ends[:, 1:2]
+        for other in range(pieces):
+            if other == piece:
+                continue
+            after = order_ref[other] == lax.rem(spot + 1, pieces)
+            ahead = order_ref[other] == lax.rem(spot + pieces - 1, pieces)
+            winds = edges[other][1][:, 2:4] * WIND_STEP
+
+            @pl.when(after)
+            def _():
+                field[order_ref[other], :, :LANES] += jnp.where(head, winds[:, 0:1] * last, 0.0)
+
+            @pl.when(ahead)
+            def _():
+                field[order_ref[other], :, end:] -= jnp.where(tail, winds[:, 1:2] * first, 0.0)
+
+    def product(value, table, spot):
         high, low = split_bf16(value)
-        part = jnp.dot(high, high_ref[spot], preferred_element_type=jnp.float32)
-        part += jnp.dot(low, high_ref[spot], preferred_element_type=jnp.float32)
-        return part + jnp.dot(high, low_ref[spot], preferred_element_type=jnp.float32)
+        width = table.shape[2] // 2
+        both = jnp.dot(high, table[spot], preferred_element_type=jnp.float32)
+        part = jnp.dot(low, table[spot, :, :width], preferred_element_type=jnp.float32)
+        return part + both[:, :width] + both[:, width:]
 
     sums = [None, None, None]
     for spot in range(share):
-        quarters = []
-        for quarter in range(4):
-            values = from_int16(grid_ref[quarter * share + spot])
-            quarters.append(values[:, :lons] * scale_of(values[:, lons:]))
+        quarters = [field[quarter * share + spot] for quarter in range(4)]
         sum02, dif02 = quarters[0] + quarters[2], quarters[0] - quarters[2]
         sum13, dif13 = quarters[1] + quarters[3], quarters[1] - quarters[3]
-        parts = [
-            product(sum02 + sum13, t0h, t0l, spot),
-            product(sum02 - sum13, t2h, t2l, spot),
-            product(dif02, tah, tal, spot) + product(dif13, tbh, tbl, spot),
-        ]
+        parts = []
+        for kind, value in enumerate((sum02 + sum13, sum02 - sum13, dif02, dif13)):
+            if spot == 0:
+                copies[kind].wait()
+            parts.append(product(value, tables[kind], spot))
+        parts = [parts[0], parts[1], parts[2] + parts[3]]
         sums = [part if total is None else total + part for total, part in zip(sums, parts)]
     placed = None
     first = 0
@@ -200,34 +283,45 @@
     kept = jnp.where(wave_ref[...] < keep_ref[...], placed * sine_ref[...], 0.0)
     code = scale_code(jnp.max(jnp.abs(kept), axis=0, keepdims=True))
     steps = coded(kept, scale_of(code))
-    targets, padded_rows, span = out_ref.shape
+    padded_rows, span = outs[0].shape
     codes = jnp.broadcast_to(code, (padded_rows - rows, code.shape[1]))
     result = as_int16(jnp.concatenate([steps, codes], axis=0))
     for target in range(targets):
-        out_ref[target] = result[:, target * span : (target + 1) * span]
-
-
-def fourier(grid, places, wave_row, keep_col, sine_col, targets):
-    pieces, rows, _ = grid.shape
+        outs[target][...] = result[:, target * span : (target + 1) * span]
+
+
+def fourier(grids, order, places, wave_row, keep_col, sine_col, targets):
+    pieces = len(grids)
+    rows, width = grids[0].shape
+    lons = width - 5
     span = wave_row.shape[1] // targets
     padded_rows = -(-(rows + 1) // 16) * 16
-    tables = [part for table in fourier_tables(pieces) for part in table_bf16(table)]
+    tables = [table_bf16(table) for table in fourier_tables(pieces)]
     return pl.pallas_call(
-        fourier_kernel,
-        out_shape=jax.ShapeDtypeStruct((targets, padded_rows, span), jnp.int16),
-        in_specs=[pl.BlockSpec(memory_space=pltpu.VMEM)] * 13,
-        out_specs=pl.BlockSpec(memory_space=pltpu.VMEM),
+        functools.partial(fourier_kernel, pieces, targets),
+        out_shape=[jax.ShapeDtypeStruct((padded_rows, span), jnp.int16)] * targets,
+        in_specs=[SMEM_SPEC] + [VMEM_SPEC] * pieces + [ANY_SPEC] * 4 + [VMEM_SPEC] * 4,
+        out_specs=[VMEM_SPEC] * targets,
+        scratch_shapes=[pltpu.VMEM(table.shape, jnp.bfloat16) for table in tables]
+        + [pltpu.VMEM((pieces, rows, lons), jnp.float32), pltpu.SemaphoreType.DMA((4,))],
         compiler_params=pltpu.CompilerParams(vmem_limit_bytes=VMEM_BYTES),
         cost_estimate=pl.CostEstimate(
             flops=3 * rows * NLON * M, bytes_accessed=6 * 2**20, transcendentals=0
         ),
-    )(grid, *tables, places, wave_row, keep_col, sine_col)
-
-
-def legendre_kernel(
-    fields_ref, high_ref, low_ref, lat_ref, wave_ref, limit_ref, norm_ref,
-    out_ref, weight, before, current, level, sums, result, beta_ref, scale_ref, growth_ref,
-):
+    )(order, *grids, *tables, places, wave_row, keep_col, sine_col)
+
+
+def legendre_kernel(pieces, order_ref, *rest):
+    fields, rest = rest[:pieces], rest[pieces:]
+    table_hbm, lat_hbm, wave_ref, limit_ref, norm_ref, out_ref = rest[:6]
+    weight, before, current, level, sums, result, beta_ref, scale_ref, growth_ref = rest[6:15]
+    table, lat_ref, sems = rest[15:]
+    copies = [pltpu.make_async_copy(lat_hbm, lat_ref, sems.at[pieces])]
+    copies[0].start()
+    for piece in range(pieces):
+        source = table_hbm.at[order_ref[piece]]
+        copies.append(pltpu.make_async_copy(source, table.at[piece], sems.at[piece]))
+        copies[-1].start()
     half = lat_ref.shape[1]
     lanes = wave_ref.shape[1]
     slots = out_ref.shape[0]
@@ -253,26 +347,7 @@
         scale = scale * jnp.sqrt(square / spread)
     growth_ref[...] = scale
 
-    pieces, padded_rows, _ = fields_ref.shape
-    totals = [None] * 4
-    code_row = padded_rows - 1
-    for piece in range(pieces):
-        values = from_int16(fields_ref[piece])
-        values = values * scale_of(values[code_row:])
-        high, low = split_bf16(values)
-        for table in range(4):
-            rows = pl.ds(table * half, half)
-            value = jnp.dot(high_ref[piece, rows], high, preferred_element_type=jnp.float32)
-            value += jnp.dot(high_ref[piece, rows], low, preferred_element_type=jnp.float32)
-            value += jnp.dot(low_ref[piece, rows], high, preferred_element_type=jnp.float32)
-            totals[table] = value if piece == 0 else totals[table] + value
-    for parity in range(2):
-        for comp in range(2):
-            cols = slice(comp * lanes, (comp + 1) * lanes)
-            weight[2 * parity + comp] = jnp.where(
-                odd, totals[2 + parity][:, cols], totals[parity][:, cols]
-            )
-
+    copies[0].wait()
     for group in range(groups):
         cols = slice(group * LANES, (group + 1) * LANES)
         coarse = lat_ref[1] * wave[:, cols]
@@ -282,6 +357,26 @@
             (coarse - whole) + lat_ref[2] * wave[:, cols] + norm_ref[:, cols]
         )
         before[:, cols] = jnp.zeros((half, LANES), jnp.float32)
+
+    padded_rows = fields[0].shape[0]
+    totals = [None] * 4
+    for piece in range(pieces):
+        values = from_int16(fields[piece][...])
+        values = values * scale_of(values[padded_rows - 1 :])
+        high, low = split_bf16(values)
+        copies[1 + piece].wait()
+        for kind in range(4):
+            rows = pl.ds(kind * half, half)
+            value = jnp.dot(table[piece, 0, rows], high, preferred_element_type=jnp.float32)
+            value += jnp.dot(table[piece, 0, rows], low, preferred_element_type=jnp.float32)
+            value += jnp.dot(table[piece, 1, rows], high, preferred_element_type=jnp.float32)
+            totals[kind] = value if piece == 0 else totals[kind] + value
+    for parity in range(2):
+        for comp in range(2):
+            cols = slice(comp * lanes, (comp + 1) * lanes)
+            weight[2 * parity + comp] = jnp.where(
+                odd, totals[2 + parity][:, cols], totals[parity][:, cols]
+            )
 
     def step(block, carry):
         first = pl.multiple_of(block * BLOCK, 8)
@@ -327,9 +422,10 @@
         out_ref[:, comp, :] = result[comp].T[:slots]
 
 
-def legendre(fields, slot_wave, rows):
+def legendre(fields, order, slot_wave, rows):
     slots = slot_wave.shape[0]
-    pieces, padded_rows, span = fields.shape
+    pieces = len(fields)
+    padded_rows, span = fields[0].shape
     lanes = span // 2
     half = M // 2
     wave_row = jnp.pad(slot_wave, (0, lanes - slots), constant_values=2 * M)[None, :]
@@ -342,14 +438,16 @@
     )
     norm = 0.5 * (log_norm - 1.0)
     table = resample_table().reshape(2 * M, pieces, rows).transpose(1, 0, 2)
-    high, low = table_bf16(np.pad(table, ((0, 0), (0, 0), (0, padded_rows - rows))))
+    table = table_bf16(np.pad(table, ((0, 0), (0, 0), (0, padded_rows - rows))))
+    table = table.reshape(pieces, 2 * M, 2, padded_rows).transpose(0, 2, 1, 3)
+    latitudes = latitude_table()
     vector = pltpu.VMEM((half, lanes), jnp.float32)
     orders = pltpu.VMEM((M, lanes), jnp.float32)
     return pl.pallas_call(
-        legendre_kernel,
+        functools.partial(legendre_kernel, pieces),
         out_shape=jax.ShapeDtypeStruct((slots, 2, M), jnp.float32),
-        in_specs=[pl.BlockSpec(memory_space=pltpu.VMEM)] * 7,
-        out_specs=pl.BlockSpec(memory_space=pltpu.VMEM),
+        in_specs=[SMEM_SPEC] + [VMEM_SPEC] * pieces + [ANY_SPEC] * 2 + [VMEM_SPEC] * 3,
+        out_specs=VMEM_SPEC,
         scratch_shapes=[
             pltpu.VMEM((4, half, lanes), jnp.float32),
             vector,
@@ -360,12 +458,15 @@
             orders,
             orders,
             pltpu.VMEM((M // BLOCK, lanes), jnp.float32),
+            pltpu.VMEM(table.shape, jnp.bfloat16),
+            pltpu.VMEM(latitudes.shape, jnp.float32),
+            pltpu.SemaphoreType.DMA((pieces + 1,)),
         ],
         compiler_params=pltpu.CompilerParams(vmem_limit_bytes=VMEM_BYTES),
         cost_estimate=pl.CostEstimate(
             flops=7 * half * lanes * M, bytes_accessed=6 * 2**20, transcendentals=0
         ),
-    )(fields, high, low, latitude_table(), inside_wave, limit, norm)
+    )(order, *fields, table, latitudes, inside_wave, limit, norm)
 
 
 def shards(tracer, wind_east, wind_north, keep_m, slot_wave):
@@ -375,12 +476,13 @@
     lanes = -(-slots // LANES) * LANES
     lat_index = lax.axis_index("lat")
 
-    advected = advect(tracer, wind_east, wind_north)
-    grid = lax.all_to_all(advected, ("lev", "fld"), split_axis=0, concat_axis=0, tiled=True)
+    ring = ("lev", "fld")
+    level_order, lat_order = partners(ring), partners("lat")
+    grids = exchange(advect(tracer, wind_east, wind_north, level_order), ring)
 
     pad = ((0, 0), (0, 0), (0, lanes - slots))
     waves = jnp.pad(slot_wave.reshape(lat_count, 1, slots), pad, constant_values=2 * M)
-    waves = jnp.broadcast_to(waves, (lat_count, 2, lanes))
+    waves = jnp.broadcast_to(waves[lat_order], (lat_count, 2, lanes))
     table_rows = wave_rows()
     spots = np.full(4 * (-(-M // 2 // (2 * LANES)) * 2 * LANES), 4 * M, np.int32)
     for part in range(2):
@@ -390,11 +492,11 @@
     row_ids = (lat_index * rows + jnp.arange(rows, dtype=jnp.int32)).astype(jnp.float32)
     sines = jnp.sin(math.pi / NLAT * (row_ids + 0.5)) * math.sqrt(2.0 / NLAT)
     waved = fourier(
-        grid, places, waves.reshape(1, -1), keep_m[:, None], sines[:, None], lat_count
+        grids, level_order, places, waves.reshape(1, -1), keep_m[:, None], sines[:, None], lat_count
     )
-    fields = lax.all_to_all(waved, "lat", split_axis=0, concat_axis=0, tiled=True)
+    fields = exchange(waved, "lat")
     my_waves = lax.dynamic_slice_in_dim(slot_wave, lat_index * slots, slots)
-    return legendre(fields, my_waves, rows)[None]
+    return legendre(fields, lat_order, my_waves, rows)[None]
 
 
 def solution(mesh):

time: 83.2 us -> 74.3 us (0.89)
  Pallas kernels: 19.6 us -> 29 us
  local copies, waits for them, and re-layouts: 18.3 us -> 10.3 us
  waiting for transfers between devices: 25.4 us -> 18.1 us
  starting transfers between devices: 17.6 us -> 13.4 us
  other arithmetic: 1.26 us -> 2.67 us
    all_to_all x2 -> x0, waiting for transfers between devices: 22.8 us -> none  [the longest x1 11.4 us: shards(): lax.all_to_all(advected, ('lev', 'fld'), split_axis=0, concat_axis=0, til...]
    ppermute x2 -> x6, waiting for transfers between devices: 2.66 us -> 18.1 us  [exchange(): lax.ppermute(blocks[step], axis, pairs[step])]
    all_to_all x2 -> x0, starting transfers between devices: 9.57 us -> none  [the longest x1 5.94 us: shards(): lax.all_to_all(waved, 'lat', split_axis=0, concat_axis=0, tiled=True)]
    pallas_call x3, Pallas kernels: 19.6 us -> 29 us  [the longest x1 14.8 us: legendre(): pl.pallas_call(functools.partial(legendre_kernel, pieces), out_shape=jax....]
    unnamed x34 -> x24, local copies, waits for them, and re-layouts: 14 us -> 7.19 us
    ppermute x2 -> x6, starting transfers between devices: 1.79 us -> 7.16 us  [exchange(): lax.ppermute(blocks[step], axis, pairs[step])]
    slice x1 -> x0, local copies, waits for them, and re-layouts: 1.16 us -> none  [advect(): east = lax.ppermute(tracer[:, :, :1], ring, left)]
  transfers between devices with their start and end apart: 6 -> 8, of which waited for: 4 -> 4; matrix products, arithmetic and copies ran while one was open for 6% -> 7% of each run, Pallas kernels for 0% -> 0%
where the time goes in v3:
time: 74.3 us; the launch traced here: 73.8 us
  Pallas kernels  29 us (39%)
  waiting for transfers between devices  18.1 us (24%)
  starting transfers between devices  13.4 us (18%)
  local copies, waits for them, and re-layouts  10.3 us (14%)
  other arithmetic  2.67 us (4%)
    ppermute x6, waiting for transfers between devices, exchange(): lax.ppermute(blocks[step], axis, pairs[step])  18.1 us
    pallas_call x1, Pallas kernels, legendre(): pl.pallas_call(functools.partial(legendre_kernel, pieces), out_shape=jax....  14.8 us
    unnamed x24, local copies, waits for them, and re-layouts  7.19 us
    ppermute x6, starting transfers between devices, exchange(): lax.ppermute(blocks[step], axis, pairs[step])  7.16 us
    pallas_call x1, Pallas kernels, fourier(): pl.pallas_call(functools.partial(fourier_kernel, pieces, targets), out_sh...  7.14 us
    pallas_call x1, Pallas kernels, advect(): pl.pallas_call(advect_kernel, out_shape=[jax.ShapeDtypeStruct((rows, lons...  7.13 us
    ppermute x1, starting transfers between devices, advect(): above = lax.ppermute(tracer[:, rows - 1:, :], 'lat', down)  4.93 us
  transfers between devices with their start and end apart: 8, of which 4 were waited for; matrix products, arithmetic and copies ran while one was open for 7% of the time, Pallas kernels for 0%

profile of v3, /device:TPU:0, one launch (start us, length us, event | category | flops | bytes accessed | tf_op | source)
XLA Modules:
  0.0 73.8 jit_solution(15511005255401625000)
XLA Ops:
  0.0 0.9 %fusion.2 = (bf16[4,1,400]{2,1,0:T(2,128)(2,1)S(1)}, bf16[4,1,400]{2,1,0:T(2,128)(2,1)S(1)}) fusion(bf16[4,200,400]{2,1,0:T(8,128)(2,1)} %tracer_hbm.1), kind=kLoop, calls=%fused_computation.17 | loop fusion | bytes 12800 | tf_op jit(solution)/shard_map/slice | solution.py:199
  0.9 4.9 %collective-permute-start = (bf16[4,1,400]{2,1,0:T(2,128)(2,1)S(1)}, bf16[4,1,400]{2,1,0:T(2,128)(2,1)S(1)}, u32[]{:S(2)}, u32[]{:S(2)}) collective-permute-start(bf16[4,1,400]{2,1,0:T(2,128)(2,1)S(1)} %get-tuple-element.22), channel_id=1, source_target_pairs={{0,4},{4,8},{8,12},{1,5},{5,9},{9,13},{2,6},{6,10},{10,14},{3,7},{... | collective-permute-start | bytes 9608 | tf_op jit(solution)/shard_map/ppermute | solution.py:198
  5.8 1.3 %collective-permute-start.1 = (bf16[4,1,400]{2,1,0:T(2,128)(2,1)S(1)}, bf16[4,1,400]{2,1,0:T(2,128)(2,1)S(1)}, u32[]{:S(2)}, u32[]{:S(2)}) collective-permute-start(bf16[4,1,400]{2,1,0:T(2,128)(2,1)S(1)} %get-tuple-element.21), channel_id=1, source_target_pairs={{4,0},{8,4},{12,8},{5,1},{9,5},{13,9},{6,2},{10,6},{14,10},{7,3},{... | collective-permute-start | bytes 9608 | tf_op jit(solution)/shard_map/ppermute | solution.py:199
  7.2 0.8 %reshape.94 = s32[4,100]{1,0:T(4,128)S(1)} reshape(s32[400]{0:T(512)} %param.19) | data formatting | bytes 3200 | tf_op jit(solution)/shard_map/reshape | solution.py:484
  8.5 0.8 %dynamic_slice.3 = s32[100]{0:T(128)S(1)} dynamic-slice(s32[400]{0:T(512)} %param.19, s32[]{:T(128)S(6)} %select_n.18), dynamic_slice_sizes={100} | dynamic-slice | bytes 804 | tf_op jit(solution)/shard_map/dynamic_slice | solution.py:498
  9.3 0.9 %select_reduce_fusion = f32[128]{0:T(128)S(1)} fusion(f32[399]{0:T(512)} %constant.78, f32[128]{0:T(128)S(1)} %get-tuple-element.23, f32[399]{0:T(512)} %constant.77), kind=kLoop, calls=%fused_computation.2 | loop fusion | flops 153088 | bytes 4216 | tf_op jit(solution)/shard_map/reduce_sum | solution.py:436
  10.2 1.4 %and_convert_fusion.rest_8_ = bf16[1024,1024]{1,0:T(8,128)(2,1)S(1)} fusion(s32[1024]{0:T(1024)S(1)} %bitcast.19, s32[1024]{0:T(1024)} %constant.76, pred[1024]{0:T(1024)(128)(4,1)S(1)} %broadcast_compare_fusion), kind=kLoop, calls=%fused_computation.1 | loop fusion | flops 3145728 | bytes 2106368 | tf_op jit(solution)/shard_map/convert_element_type | solution.py:491
  11.6 1.1 %copy-done.1 = bf16[4,200,400]{2,1,0:T(8,128)(2,1)S(1)} copy-done((bf16[4,200,400]{2,1,0:T(8,128)(2,1)S(1)}, bf16[4,200,400]{2,1,0:T(8,128)(2,1)}, u32[]{:S(2)}) %copy-start.1) | copy-done | bytes 640024
  12.8 1.1 %copy-done.4 = bf16[4,200,400]{2,1,0:T(8,128)(2,1)S(1)} copy-done((bf16[4,200,400]{2,1,0:T(8,128)(2,1)S(1)}, bf16[4,200,400]{2,1,0:T(8,128)(2,1)}, u32[]{:S(2)}) %copy-start.4) | copy-done | bytes 640024
  13.9 1.1 %copy-done.5 = bf16[4,200,400]{2,1,0:T(8,128)(2,1)S(1)} copy-done((bf16[4,200,400]{2,1,0:T(8,128)(2,1)S(1)}, bf16[4,200,400]{2,1,0:T(8,128)(2,1)}, u32[]{:S(2)}) %copy-start.5) | copy-done | bytes 640024
  15.1 7.1 %shard_map.145 = (s16[200,405]{1,0:T(8,128)(2,1)S(1)}, s16[200,405]{1,0:T(8,128)(2,1)}, s16[200,405]{1,0:T(8,128)(2,1)}, s16[200,405]{1,0:T(8,128)(2,1)}) custom-call(s32[4]{0:T(128)S(1)} %iota_xor_fusion.order_ref, bf16[4,200,400]{2,1,0:T(8,128)(2,1)S(1)} %copy-done.1, bf16[4,200,400]{2,1,0:T(8,128)(2,1)S(1)} %copy-done.4, ...), custom_call_target="tpu_custom_call" | custom-call | flops 6400000 | bytes 2560000 | tf_op jit(solution)/shard_map/pallas_call | solution.py:201
  22.2 0.7 copy-done.9
  22.9 1.5 %collective-permute-start.3 = (s16[200,405]{1,0:T(8,128)(2,1)}, s16[200,405]{1,0:T(8,128)(2,1)}, u32[]{:S(2)}, u32[]{:S(2)}) collective-permute-start(s16[200,405]{1,0:T(8,128)(2,1)} %get-tuple-element.15), channel_id=1, source_target_pairs={{0,2},{1,3},{2,0},{3,1},{4,6},{5,7},{6,4},{7,5},{8,10},{9,11},{10,... | collective-permute-start | bytes 486008 | tf_op jit(solution)/shard_map/ppermute | solution.py:137
  25.3 5.8 %collective-permute-done.3.rest_2_ = s16[200,405]{1,0:T(8,128)(2,1)} collective-permute-done((s16[200,405]{1,0:T(8,128)(2,1)}, s16[200,405]{1,0:T(8,128)(2,1)}, u32[]{:S(2)}, u32[]{:S(2)}) %collective-permute-start.3) | collective-permute-done | bytes 162032 | tf_op jit(solution)/shard_map/ppermute | solution.py:137
  31.1 3.6 %collective-permute-done.4.rest_3_ = s16[200,405]{1,0:T(8,128)(2,1)} collective-permute-done((s16[200,405]{1,0:T(8,128)(2,1)}, s16[200,405]{1,0:T(8,128)(2,1)}, u32[]{:S(2)}, u32[]{:S(2)}) %collective-permute-start.4) | collective-permute-done | bytes 162032 | tf_op jit(solution)/shard_map/ppermute | solution.py:137
  34.7 1.1 %copy-done.3 = bf16[1,400,1024]{2,1,0:T(8,128)(2,1)S(1)} copy-done((bf16[1,400,1024]{2,1,0:T(8,128)(2,1)S(1)}, bf16[1,400,1024]{2,1,0:T(8,128)(2,1)}, u32[]{:S(2)}) %copy-start.3) | copy-done | bytes 819224
  35.8 1.0 %copy-done.7 = bf16[1,400,512]{2,1,0:T(8,128)(2,1)S(1)} copy-done((bf16[1,400,512]{2,1,0:T(8,128)(2,1)S(1)}, bf16[1,400,512]{2,1,0:T(8,128)(2,1)}, u32[]{:S(2)}) %copy-start.7) | copy-done | bytes 409624
  36.8 0.9 %copy-done.10 = s16[200,405]{1,0:T(8,128)(2,1)S(1)} copy-done((s16[200,405]{1,0:T(8,128)(2,1)S(1)}, s16[200,405]{1,0:T(8,128)(2,1)}, u32[]{:S(2)}) %copy-start.10) | copy-done | bytes 162024
  37.8 7.1 %shard_map.146 = (s16[208,256]{1,0:T(8,128)(2,1)S(1)}, s16[208,256]{1,0:T(8,128)(2,1)S(1)}, s16[208,256]{1,0:T(8,128)(2,1)S(1)}, s16[208,256]{1,0:T(8,128)(2,1)S(1)}) custom-call(s32[4]{0:T(128)S(1)} %iota_xor_fusion.order_ref, s16[200,405]{1,0:T(8,128)(2,1)S(1)} %copy-done.10, s16[200,405]{1,0:T(8,128)(2,1)} %collective-permute-done.2.rest_1_, ...), custom_call_target="tpu_custom_call" | custom-call | flops 384000000 | bytes 6291456 | tf_op jit(solution)/shard_map/pallas_call | solution.py:300
  44.9 2.7 %collective-permute-start.5 = (s16[208,256]{1,0:T(8,128)(2,1)S(1)}, s16[208,256]{1,0:T(8,128)(2,1)S(1)}, u32[]{:S(2)}, u32[]{:S(2)}) collective-permute-start(s16[208,256]{1,0:T(8,128)(2,1)S(1)} %get-tuple-element.18), channel_id=1, source_target_pairs={{0,4},{4,0},{8,12},{12,8},{1,5},{5,1},{9,13},{13,9},{2,6},{6,2},{1... | collective-permute-start | bytes 319496 | tf_op jit(solution)/shard_map/ppermute | solution.py:137
  47.6 2.6 %collective-permute-start.6 = (s16[208,256]{1,0:T(8,128)(2,1)S(1)}, s16[208,256]{1,0:T(8,128)(2,1)S(1)}, u32[]{:S(2)}, u32[]{:S(2)}) collective-permute-start(s16[208,256]{1,0:T(8,128)(2,1)S(1)} %get-tuple-element.19), channel_id=1, source_target_pairs={{0,8},{4,12},{8,0},{12,4},{1,9},{5,13},{9,1},{13,5},{2,10},{6,14},... | collective-permute-start | bytes 319496 | tf_op jit(solution)/shard_map/ppermute | solution.py:137
  50.2 0.8 %collective-permute-done.5.rest_1_ = s16[208,256]{1,0:T(8,128)(2,1)S(1)} collective-permute-done((s16[208,256]{1,0:T(8,128)(2,1)S(1)}, s16[208,256]{1,0:T(8,128)(2,1)S(1)}, u32[]{:S(2)}, u32[]{:S(2)}) %collective-permute-start.5) | collective-permute-done | bytes 106528 | tf_op jit(solution)/shard_map/ppermute | solution.py:137
  51.0 7.9 %collective-permute-done.6.rest_2_ = s16[208,256]{1,0:T(8,128)(2,1)S(1)} collective-permute-done((s16[208,256]{1,0:T(8,128)(2,1)S(1)}, s16[208,256]{1,0:T(8,128)(2,1)S(1)}, u32[]{:S(2)}, u32[]{:S(2)}) %collective-permute-start.6) | collective-permute-done | bytes 106528 | tf_op jit(solution)/shard_map/ppermute | solution.py:137
  58.9 14.8 %shard_map.147 = f32[100,2,400]{2,1,0:T(2,128)} custom-call(s32[4]{0:T(128)S(1)} %iota_xor_fusion.1.order_ref, s16[208,256]{1,0:T(8,128)(2,1)S(1)} %get-tuple-element.17.rest_0_, s16[208,256]{1,0:T(8,128)(2,1)S(1)} %collective-permute-done.5.rest_1_, s16[208,256]{1,0:T(8,128)(2,1)S(1)} %collective-permute-done.6.rest_2_, ...), custom_call_target="tpu_custom_call" | custom-call | flops 71680000 | bytes 6291456 | tf_op jit(solution)/shard_map/pallas_call | solution.py:446
  (38 shorter events, 1.5 us)
Async XLA Ops:
  0.0 34.7 %copy-start.6 = (bf16[1,400,512]{2,1,0:T(8,128)(2,1)S(1)}, bf16[1,400,512]{2,1,0:T(8,128)(2,1)}, u32[]{:S(2)}) copy-start(bf16[1,400,512]{2,1,0:T(8,128)(2,1)} %constant.64.clone.rest_4_) | copy-start | bytes 1228804
  0.0 34.7 %copy-start.2 = (bf16[1,400,1024]{2,1,0:T(8,128)(2,1)S(1)}, bf16[1,400,1024]{2,1,0:T(8,128)(2,1)}, u32[]{:S(2)}) copy-start(bf16[1,400,1024]{2,1,0:T(8,128)(2,1)} %constant.66.clone.rest_6_) | copy-start | bytes 2457604
  0.0 24.7 %copy-start.11 = (s32[200]{0:T(256)S(1)}, s32[200]{0:T(256)}, u32[]{:S(2)}) copy-start(s32[200]{0:T(256)} %param.18) | copy-start | bytes 2404
  0.9 10.7 %collective-permute-start = (bf16[4,1,400]{2,1,0:T(2,128)(2,1)S(1)}, bf16[4,1,400]{2,1,0:T(2,128)(2,1)S(1)}, u32[]{:S(2)}, u32[]{:S(2)}) collective-permute-start(bf16[4,1,400]{2,1,0:T(2,128)(2,1)S(1)} %get-tuple-element.22), channel_id=1, source_target_pairs={{0,4},{4,8},{8,12},{1,5},{5,9},{9,13},{2,6},{6,10},{10,14},{3,7},{... | collective-permute-start | bytes 9608 | tf_op jit(solution)/shard_map/ppermute | solution.py:198
  5.8 5.8 %collective-permute-start.1 = (bf16[4,1,400]{2,1,0:T(2,128)(2,1)S(1)}, bf16[4,1,400]{2,1,0:T(2,128)(2,1)S(1)}, u32[]{:S(2)}, u32[]{:S(2)}) collective-permute-start(bf16[4,1,400]{2,1,0:T(2,128)(2,1)S(1)} %get-tuple-element.21), channel_id=1, source_target_pairs={{4,0},{8,4},{12,8},{5,1},{9,5},{13,9},{6,2},{10,6},{14,10},{7,3},{... | collective-permute-start | bytes 9608 | tf_op jit(solution)/shard_map/ppermute | solution.py:199
  11.6 1.1 %copy-start.1 = (bf16[4,200,400]{2,1,0:T(8,128)(2,1)S(1)}, bf16[4,200,400]{2,1,0:T(8,128)(2,1)}, u32[]{:S(2)}) copy-start(bf16[4,200,400]{2,1,0:T(8,128)(2,1)} %tracer_hbm.1) | copy-start | bytes 1920004
  12.8 1.1 %copy-start.4 = (bf16[4,200,400]{2,1,0:T(8,128)(2,1)S(1)}, bf16[4,200,400]{2,1,0:T(8,128)(2,1)}, u32[]{:S(2)}) copy-start(bf16[4,200,400]{2,1,0:T(8,128)(2,1)} %east_hbm.1) | copy-start | bytes 1920004
  13.9 1.1 %copy-start.5 = (bf16[4,200,400]{2,1,0:T(8,128)(2,1)S(1)}, bf16[4,200,400]{2,1,0:T(8,128)(2,1)}, u32[]{:S(2)}) copy-start(bf16[4,200,400]{2,1,0:T(8,128)(2,1)} %north_hbm.1) | copy-start | bytes 1920004
  22.2 0.7 copy-start.9
  22.9 2.4 %collective-permute-start.2 = (s16[200,405]{1,0:T(8,128)(2,1)}, s16[200,405]{1,0:T(8,128)(2,1)}, u32[]{:S(2)}, u32[]{:S(2)}) collective-permute-start(s16[200,405]{1,0:T(8,128)(2,1)} %get-tuple-element.14), channel_id=1, source_target_pairs={{0,1},{1,0},{2,3},{3,2},{4,5},{5,4},{6,7},{7,6},{8,9},{9,8},{10,11... | collective-permute-start | bytes 486008 | tf_op jit(solution)/shard_map/ppermute | solution.py:137
  22.9 8.2 %collective-permute-start.3 = (s16[200,405]{1,0:T(8,128)(2,1)}, s16[200,405]{1,0:T(8,128)(2,1)}, u32[]{:S(2)}, u32[]{:S(2)}) collective-permute-start(s16[200,405]{1,0:T(8,128)(2,1)} %get-tuple-element.15), channel_id=1, source_target_pairs={{0,2},{1,3},{2,0},{3,1},{4,6},{5,7},{6,4},{7,5},{8,10},{9,11},{10,... | collective-permute-start | bytes 486008 | tf_op jit(solution)/shard_map/ppermute | solution.py:137
  24.4 10.3 %collective-permute-start.4 = (s16[200,405]{1,0:T(8,128)(2,1)}, s16[200,405]{1,0:T(8,128)(2,1)}, u32[]{:S(2)}, u32[]{:S(2)}) collective-permute-start(s16[200,405]{1,0:T(8,128)(2,1)} %get-tuple-element.16), channel_id=1, source_target_pairs={{0,3},{1,2},{2,1},{3,0},{4,7},{5,6},{6,5},{7,4},{8,11},{9,10},{10,... | collective-permute-start | bytes 486008 | tf_op jit(solution)/shard_map/ppermute | solution.py:137
  24.9 34.0 %copy-start = (bf16[4,2,800,208]{3,2,1,0:T(8,128)(2,1)S(1)}, bf16[4,2,800,208]{3,2,1,0:T(8,128)(2,1)}, u32[]{:S(2)}) copy-start(bf16[4,2,800,208]{3,2,1,0:T(8,128)(2,1)} %constant.70.clone.rest_4_) | copy-start | bytes 7987204
  34.7 1.1 %copy-start.3 = (bf16[1,400,1024]{2,1,0:T(8,128)(2,1)S(1)}, bf16[1,400,1024]{2,1,0:T(8,128)(2,1)}, u32[]{:S(2)}) copy-start(bf16[1,400,1024]{2,1,0:T(8,128)(2,1)} %constant.67.clone.rest_7_) | copy-start | bytes 2457604
  35.8 1.0 %copy-start.7 = (bf16[1,400,512]{2,1,0:T(8,128)(2,1)S(1)}, bf16[1,400,512]{2,1,0:T(8,128)(2,1)}, u32[]{:S(2)}) copy-start(bf16[1,400,512]{2,1,0:T(8,128)(2,1)} %constant.65.clone.rest_5_) | copy-start | bytes 1228804
  36.8 0.9 %copy-start.10 = (s16[200,405]{1,0:T(8,128)(2,1)S(1)}, s16[200,405]{1,0:T(8,128)(2,1)}, u32[]{:S(2)}) copy-start(s16[200,405]{1,0:T(8,128)(2,1)} %copy-done.9) | copy-start | bytes 486004
  37.8 21.1 %copy-start.8 = (f32[3,200,128]{2,1,0:T(8,128)S(1)}, f32[3,200,128]{2,1,0:T(8,128)}, u32[]{:S(2)}) copy-start(f32[3,200,128]{2,1,0:T(8,128)} %constant.71.clone.rest_5_) | copy-start | bytes 921604
  44.9 6.1 %collective-permute-start.5 = (s16[208,256]{1,0:T(8,128)(2,1)S(1)}, s16[208,256]{1,0:T(8,128)(2,1)S(1)}, u32[]{:S(2)}, u32[]{:S(2)}) collective-permute-start(s16[208,256]{1,0:T(8,128)(2,1)S(1)} %get-tuple-element.18), channel_id=1, source_target_pairs={{0,4},{4,0},{8,12},{12,8},{1,5},{5,1},{9,13},{13,9},{2,6},{6,2},{1... | collective-permute-start | bytes 319496 | tf_op jit(solution)/shard_map/ppermute | solution.py:137
  47.6 11.3 %collective-permute-start.6 = (s16[208,256]{1,0:T(8,128)(2,1)S(1)}, s16[208,256]{1,0:T(8,128)(2,1)S(1)}, u32[]{:S(2)}, u32[]{:S(2)}) collective-permute-start(s16[208,256]{1,0:T(8,128)(2,1)S(1)} %get-tuple-element.19), channel_id=1, source_target_pairs={{0,8},{4,12},{8,0},{12,4},{1,9},{5,13},{9,1},{13,5},{2,10},{6,14},... | collective-permute-start | bytes 319496 | tf_op jit(solution)/shard_map/ppermute | solution.py:137
  50.2 8.7 %collective-permute-start.7 = (s16[208,256]{1,0:T(8,128)(2,1)S(1)}, s16[208,256]{1,0:T(8,128)(2,1)S(1)}, u32[]{:S(2)}, u32[]{:S(2)}) collective-permute-start(s16[208,256]{1,0:T(8,128)(2,1)S(1)} %get-tuple-element.20), channel_id=1, source_target_pairs={{0,12},{4,8},{8,4},{12,0},{1,13},{5,9},{9,5},{13,1},{2,14},{6,10},... | collective-permute-start | bytes 319496 | tf_op jit(solution)/shard_map/ppermute | solution.py:137

commit v4 on v3

--- a/solution.py
+++ b/solution.py
@@ -20,7 +20,7 @@
 VMEM_BYTES = 24 * 2**20
 VMEM_SPEC = pl.BlockSpec(memory_space=pltpu.VMEM)
 SMEM_SPEC = pl.BlockSpec(memory_space=pltpu.SMEM)
-ANY_SPEC = pl.BlockSpec(memory_space=pl.ANY)
+HBM_SPEC = pl.BlockSpec(memory_space=pltpu.HBM)
 
 
 def split_bf16(values):
@@ -110,9 +110,8 @@
     return jnp.exp2(exponent) * (1.0 + rest * (1.0 / 128.0))
 
 
-def coded(values, scale):
-    steps = jnp.floor(values * (1.0 / scale) + 0.5)
-    return jnp.clip(steps, -TOP, TOP)
+def coded(values, inverse):
+    return jnp.floor(values * inverse + 0.5)
 
 
 def as_int16(values):
@@ -137,9 +136,10 @@
     return [blocks[0]] + [lax.ppermute(blocks[step], axis, pairs[step]) for step in range(1, count)]
 
 
-def advect_kernel(order_ref, tracer_hbm, east_hbm, north_hbm, above_ref, below_ref, *rest):
+def advect_kernel(order_ref, tracer_hbm, east_hbm, north_hbm, *rest):
     levels, rows, lons = tracer_hbm.shape
-    outs, (tracer, east_wind, north_wind, sems) = rest[:levels], rest[levels:]
+    outs, rest = rest[:levels], rest[levels:]
+    first_row, last_row, row_wind, tracer, east_wind, north_wind, sems = rest
     copies = []
     for step in range(levels):
         level = order_ref[step]
@@ -153,104 +153,119 @@
         )
         for copy in copies[-1]:
             copy.start()
+    end = (lons - 1) // LANES * LANES
+    spare = lons - end
+    lane = lax.broadcasted_iota(jnp.int32, (rows, LANES), 1)
     for step in range(levels):
         level = order_ref[step]
         for copy in copies[step]:
             copy.wait()
         field = tracer[step].astype(jnp.float32)
-        first, last = field[:, :1], field[:, lons - 1 :]
-        blank = jnp.zeros_like(first)
+        first_row[level] = field[:1]
+        last_row[level] = field[rows - 1 :]
+        blank = jnp.zeros((rows, 1), jnp.float32)
         west = jnp.concatenate([blank, field[:, :-1]], axis=1)
         east = jnp.concatenate([field[:, 1:], blank], axis=1)
-        above = above_ref[level].astype(jnp.float32)
-        below = below_ref[level].astype(jnp.float32)
-        north = jnp.concatenate([above, field[:-1]], axis=0)
-        south = jnp.concatenate([field[1:], below], axis=0)
+        blank = jnp.zeros((1, lons), jnp.float32)
+        north = jnp.concatenate([blank, field[:-1]], axis=0)
+        south = jnp.concatenate([field[1:], blank], axis=0)
         eastward = 0.5 * east_wind[step].astype(jnp.float32)
-        moved = (
-            field
-            - eastward * (east - west)
-            - 0.5 * north_wind[step].astype(jnp.float32) * (south - north)
-        )
-        biggest = jnp.maximum(jnp.abs(moved), jnp.abs(field))
-        code = scale_code(jnp.max(biggest, axis=1, keepdims=True))
-        scale = scale_of(code)
-        wind = jnp.concatenate([eastward[:, :1], eastward[:, lons - 1 :]], axis=1)
-        outs[step][...] = as_int16(
-            jnp.concatenate(
-                [
-                    coded(moved, scale),
-                    code,
-                    coded(first, scale),
-                    coded(last, scale),
-                    coded(wind, WIND_STEP),
-                ],
-                axis=1,
-            )
-        )
+        northward = 0.5 * north_wind[step].astype(jnp.float32)
+        row_wind[step, :1] = northward[:1]
+        row_wind[step, 1:2] = -northward[rows - 1 :]
+        moved = field - eastward * (east - west) - northward * (south - north)
+        first, last = field[:, :1], field[:, lons - 1 :]
+        biggest = jnp.max(jnp.abs(moved), axis=1, keepdims=True)
+        biggest = jnp.maximum(biggest, jnp.maximum(jnp.abs(first), jnp.abs(last)))
+        code = scale_code(biggest)
+        inverse = 1.0 / scale_of(code)
+        filler = jnp.zeros((rows, LANES - spare), jnp.float32)
+        tile = jnp.concatenate([moved[:, end:], filler], axis=1)
+        tile = jnp.where(lane == spare + 1, first, jnp.where(lane == spare + 2, last, tile))
+        tile = coded(tile, inverse)
+        tile = jnp.where(lane == spare, code, tile)
+        winds = jnp.where(lane == spare + 3, eastward[:, :1], eastward[:, lons - 1 :])
+        winds = coded(winds, 1.0 / WIND_STEP)
+        tile = jnp.where((lane == spare + 3) | (lane == spare + 4), winds, tile)
+        outs[step][:, :end] = as_int16(coded(moved[:, :end], inverse))
+        outs[step][:, end:] = as_int16(tile)
 
 
 def advect(tracer, east_wind, north_wind, order):
     levels, rows, lons = tracer.shape
-    lat_count = lax.axis_size("lat")
-    down = [(i, i + 1) for i in range(lat_count - 1)]
-    up = [(i + 1, i) for i in range(lat_count - 1)]
-    above = lax.ppermute(tracer[:, rows - 1 :, :], "lat", down)
-    below = lax.ppermute(tracer[:, :1, :], "lat", up)
+    width = (lons - 1) // LANES * LANES + LANES
     held = pltpu.VMEM((levels, rows, lons), jnp.bfloat16)
-    return pl.pallas_call(
+    row = jax.ShapeDtypeStruct((levels, 1, lons), jnp.float32)
+    result = pl.pallas_call(
         advect_kernel,
-        out_shape=[jax.ShapeDtypeStruct((rows, lons + 5), jnp.int16)] * levels,
-        in_specs=[SMEM_SPEC] + [ANY_SPEC] * 3 + [VMEM_SPEC] * 2,
-        out_specs=[VMEM_SPEC] * levels,
+        out_shape=[jax.ShapeDtypeStruct((rows, width), jnp.int16)] * levels
+        + [row, row, jax.ShapeDtypeStruct((levels, 2, lons), jnp.float32)],
+        in_specs=[SMEM_SPEC] + [HBM_SPEC] * 3,
+        out_specs=[VMEM_SPEC] * (levels + 3),
         scratch_shapes=[held, held, held, pltpu.SemaphoreType.DMA((levels, 3))],
         compiler_params=pltpu.CompilerParams(vmem_limit_bytes=VMEM_BYTES),
         cost_estimate=pl.CostEstimate(
             flops=20 * levels * rows * lons, bytes_accessed=8 * levels * rows * lons, transcendentals=0
         ),
-    )(order, tracer, east_wind, north_wind, above, below)
+    )(order, tracer, east_wind, north_wind)
+    return result[:levels], result[levels:]
+
+
+def halo_kernel(order_ref, above_ref, below_ref, row_wind, *outs):
+    for step, out_ref in enumerate(outs):
+        level = order_ref[step]
+        out_ref[:1] = row_wind[step, :1] * above_ref[level]
+        out_ref[1:] = row_wind[step, 1:2] * below_ref[level]
+
+
+def halo(order, first_row, last_row, row_wind):
+    levels, _, lons = first_row.shape
+    count = lax.axis_size("lat")
+    above = lax.ppermute(last_row, "lat", [(i, i + 1) for i in range(count - 1)])
+    below = lax.ppermute(first_row, "lat", [(i + 1, i) for i in range(count - 1)])
+    return pl.pallas_call(
+        halo_kernel,
+        out_shape=[jax.ShapeDtypeStruct((2, lons), jnp.float32)] * levels,
+        in_specs=[SMEM_SPEC] + [VMEM_SPEC] * 3,
+        out_specs=[VMEM_SPEC] * levels,
+    )(order, above, below, row_wind)
 
 
 def fourier_kernel(pieces, targets, order_ref, *rest):
-    grids, rest = rest[:pieces], rest[pieces:]
+    grids, halos, rest = rest[:pieces], rest[pieces : 2 * pieces], rest[2 * pieces :]
     tables_hbm, (place_ref, wave_ref, keep_ref, sine_ref), rest = rest[:4], rest[4:8], rest[8:]
     outs, rest = rest[:targets], rest[targets:]
     tables, (field, sems) = rest[:4], rest[4:]
-    _, rows, lons = field.shape
+    _, rows, width = field.shape
+    lons = tables[0].shape[1]
     share = pieces // 4
     copies = []
     for kind in range(4):
         copies.append(pltpu.make_async_copy(tables_hbm[kind], tables[kind], sems.at[kind]))
         copies[-1].start()
 
-    edges = []
-    for piece in range(pieces):
-        values = from_int16(grids[piece][...])
-        code = values[:, lons : lons + 1]
-        field[order_ref[piece]] = values[:, :lons] * scale_of(code)
-        edges.append((scale_of(code), values[:, lons + 1 :]))
-    end = (lons - 1) // LANES * LANES
-    head = lax.broadcasted_iota(jnp.int32, (rows, LANES), 1) == 0
-    tail = lax.broadcasted_iota(jnp.int32, (rows, lons - end), 1) == lons - end - 1
+    end = width - LANES
+    spare = lons - end
+    lane = lax.broadcasted_iota(jnp.int32, (rows, LANES), 1)
+    winds = (lane == spare + 3) | (lane == spare + 4)
     for piece in range(pieces):
         spot = order_ref[piece]
-        scale, ends = edges[piece]
-        first = scale * ends[:, 0:1]
-        last = scale * ends[:, 1:2]
-        for other in range(pieces):
-            if other == piece:
-                continue
-            after = order_ref[other] == lax.rem(spot + 1, pieces)
-            ahead = order_ref[other] == lax.rem(spot + pieces - 1, pieces)
-            winds = edges[other][1][:, 2:4] * WIND_STEP
-
-            @pl.when(after)
-            def _():
-                field[order_ref[other], :, :LANES] += jnp.where(head, winds[:, 0:1] * last, 0.0)
-
-            @pl.when(ahead)
-            def _():
-                field[order_ref[other], :, end:] -= jnp.where(tail, winds[:, 1:2] * first, 0.0)
+        values = from_int16(grids[piece][...])
+        tile = values[:, end:]
+        scale = scale_of(tile[:, spare : spare + 1])
+        field[spot, :, :end] = values[:, :end] * scale
+        field[spot, :, end:] = tile * jnp.where(winds, WIND_STEP, scale)
+        field[spot, :1, :lons] += halos[piece][:1]
+        field[spot, rows - 1 :, :lons] += halos[piece][1:]
+    for spot in range(pieces):
+        tile = field[spot, :, end:]
+        before = field[(spot - 1) % pieces, :, end:]
+        after = field[(spot + 1) % pieces, :, end:]
+        shift = LANES - spare
+        gain = pltpu.roll(tile, shift - 3, 1) * pltpu.roll(before, shift - 2, 1)
+        loss = pltpu.roll(tile, LANES - 5, 1) * pltpu.roll(after, LANES - 2, 1)
+        field[spot, :, end:] = tile - jnp.where(lane == spare - 1, loss, 0.0)
+        field[spot, :, :LANES] += jnp.where(lane == 0, gain, 0.0)
 
     def product(value, table, spot):
         high, low = split_bf16(value)
@@ -261,7 +276,7 @@
 
     sums = [None, None, None]
     for spot in range(share):
-        quarters = [field[quarter * share + spot] for quarter in range(4)]
+        quarters = [field[quarter * share + spot, :, :lons] for quarter in range(4)]
         sum02, dif02 = quarters[0] + quarters[2], quarters[0] - quarters[2]
         sum13, dif13 = quarters[1] + quarters[3], quarters[1] - quarters[3]
         parts = []
@@ -282,7 +297,7 @@
         first = last
     kept = jnp.where(wave_ref[...] < keep_ref[...], placed * sine_ref[...], 0.0)
     code = scale_code(jnp.max(jnp.abs(kept), axis=0, keepdims=True))
-    steps = coded(kept, scale_of(code))
+    steps = coded(kept, 1.0 / scale_of(code))
     padded_rows, span = outs[0].shape
     codes = jnp.broadcast_to(code, (padded_rows - rows, code.shape[1]))
     result = as_int16(jnp.concatenate([steps, codes], axis=0))
@@ -290,25 +305,25 @@
         outs[target][...] = result[:, target * span : (target + 1) * span]
 
 
-def fourier(grids, order, places, wave_row, keep_col, sine_col, targets):
+def fourier(grids, halos, order, places, wave_row, keep_col, sine_col, targets):
     pieces = len(grids)
     rows, width = grids[0].shape
-    lons = width - 5
+    lons = NLON // pieces
     span = wave_row.shape[1] // targets
     padded_rows = -(-(rows + 1) // 16) * 16
     tables = [table_bf16(table) for table in fourier_tables(pieces)]
     return pl.pallas_call(
         functools.partial(fourier_kernel, pieces, targets),
         out_shape=[jax.ShapeDtypeStruct((padded_rows, span), jnp.int16)] * targets,
-        in_specs=[SMEM_SPEC] + [VMEM_SPEC] * pieces + [ANY_SPEC] * 4 + [VMEM_SPEC] * 4,
+        in_specs=[SMEM_SPEC] + [VMEM_SPEC] * (2 * pieces) + [HBM_SPEC] * 4 + [VMEM_SPEC] * 4,
         out_specs=[VMEM_SPEC] * targets,
         scratch_shapes=[pltpu.VMEM(table.shape, jnp.bfloat16) for table in tables]
-        + [pltpu.VMEM((pieces, rows, lons), jnp.float32), pltpu.SemaphoreType.DMA((4,))],
+        + [pltpu.VMEM((pieces, rows, width), jnp.float32), pltpu.SemaphoreType.DMA((4,))],
         compiler_params=pltpu.CompilerParams(vmem_limit_bytes=VMEM_BYTES),
         cost_estimate=pl.CostEstimate(
             flops=3 * rows * NLON * M, bytes_accessed=6 * 2**20, transcendentals=0
         ),
-    )(order, *grids, *tables, places, wave_row, keep_col, sine_col)
+    )(order, *grids, *halos, *tables, places, wave_row, keep_col, sine_col)
 
 
 def legendre_kernel(pieces, order_ref, *rest):
@@ -446,7 +461,7 @@
     return pl.pallas_call(
         functools.partial(legendre_kernel, pieces),
         out_shape=jax.ShapeDtypeStruct((slots, 2, M), jnp.float32),
-        in_specs=[SMEM_SPEC] + [VMEM_SPEC] * pieces + [ANY_SPEC] * 2 + [VMEM_SPEC] * 3,
+        in_specs=[SMEM_SPEC] + [VMEM_SPEC] * pieces + [HBM_SPEC] * 2 + [VMEM_SPEC] * 3,
         out_specs=VMEM_SPEC,
         scratch_shapes=[
             pltpu.VMEM((4, half, lanes), jnp.float32),
@@ -478,7 +493,10 @@
 
     ring = ("lev", "fld")
     level_order, lat_order = partners(ring), partners("lat")
-    grids = exchange(advect(tracer, wind_east, wind_north, level_order), ring)
+    blocks, edges = advect(tracer, wind_east, wind_north, level_order)
+    blocks, slot_wave, keep_m = lax.optimization_barrier((blocks, slot_wave, keep_m))
+    grids = exchange(blocks, ring)
+    halos = exchange(halo(level_order, *edges), ring)
 
     pad = ((0, 0), (0, 0), (0, lanes - slots))
     waves = jnp.pad(slot_wave.reshape(lat_count, 1, slots), pad, constant_values=2 * M)
@@ -492,7 +510,7 @@
     row_ids = (lat_index * rows + jnp.arange(rows, dtype=jnp.int32)).astype(jnp.float32)
     sines = jnp.sin(math.pi / NLAT * (row_ids + 0.5)) * math.sqrt(2.0 / NLAT)
     waved = fourier(
-        grids, level_order, places, waves.reshape(1, -1), keep_m[:, None], sines[:, None], lat_count
+        grids, halos, level_order, places, waves.reshape(1, -1), keep_m[:, None], sines[:, None], lat_count
     )
     fields = exchange(waved, "lat")
     my_waves = lax.dynamic_slice_in_dim(slot_wave, lat_index * slots, slots)

time: 74.3 us -> 70.9 us (0.954)
  waiting for transfers between devices: 18.1 us -> 10.3 us
  local copies, waits for them, and re-layouts: 10.3 us -> 13.3 us
  starting transfers between devices: 13.4 us -> 15.2 us
    ppermute x6 -> x9, waiting for transfers between devices: 18.1 us -> 9.85 us  [exchange(): lax.ppermute(blocks[step], axis, pairs[step])]
    ppermute x6 -> x9, starting transfers between devices: 7.16 us -> 10.3 us  [exchange(): lax.ppermute(blocks[step], axis, pairs[step])]
    unnamed x24 -> x38, local copies, waits for them, and re-layouts: 7.19 us -> 9.11 us
    pallas_call x1 -> x2, Pallas kernels: 7.13 us -> 8.81 us  [the longest x1 7.4 us: advect(): pl.pallas_call(advect_kernel, out_shape=[jax.ShapeDtypeStruct((rows, widt...]
    pallas_call x1, Pallas kernels: 7.14 us -> 5.79 us  [fourier(): pl.pallas_call(functools.partial(fourier_kernel, pieces, targets), out_sh...]
    broadcast_in_dim x2, local copies, waits for them, and re-layouts: 0.01 us -> 1.28 us  [shards(): waves = jnp.broadcast_to(waves[lat_order], (lat_count, 2, lanes))]
    ppermute x2, starting transfers between devices: 6.22 us -> 4.98 us  [the longest x1 3.69 us: halo(): lax.ppermute(last_row, 'lat', [(i, i + 1) for i in range(count - 1)])]
    slice x1 -> x0, local copies, waits for them, and re-layouts: 0.9 us -> none  [advect(): below = lax.ppermute(tracer[:, :1, :], 'lat', up)]
  transfers between devices with their start and end apart: 8 -> 11, of which waited for: 4 -> 6; matrix products, arithmetic and copies ran while one was open for 7% -> 8% of each run, Pallas kernels for 0% -> 2%
where the time goes in v4:
time: 70.9 us; the launch traced here: 70.3 us
  Pallas kernels  29.4 us (41%)
  starting transfers between devices  15.2 us (21%)
  local copies, waits for them, and re-layouts  13.3 us (19%)
  waiting for transfers between devices  10.3 us (15%)
  other arithmetic  1.96 us (3%)
    pallas_call x1, Pallas kernels, legendre(): pl.pallas_call(functools.partial(legendre_kernel, pieces), out_shape=jax....  14.8 us
    ppermute x9, starting transfers between devices, exchange(): lax.ppermute(blocks[step], axis, pairs[step])  10.3 us
    ppermute x9, waiting for transfers between devices, exchange(): lax.ppermute(blocks[step], axis, pairs[step])  9.85 us
    unnamed x38, local copies, waits for them, and re-layouts  9.11 us
    pallas_call x1, Pallas kernels, advect(): pl.pallas_call(advect_kernel, out_shape=[jax.ShapeDtypeStruct((rows, widt...  7.4 us
    pallas_call x1, Pallas kernels, fourier(): pl.pallas_call(functools.partial(fourier_kernel, pieces, targets), out_sh...  5.79 us
    ppermute x1, starting transfers between devices, halo(): lax.ppermute(last_row, 'lat', [(i, i + 1) for i in range(count - 1)])  3.69 us
  transfers between devices with their start and end apart: 11, of which 6 were waited for; matrix products, arithmetic and copies ran while one was open for 8% of the time, Pallas kernels for 2%

profile of v4, /device:TPU:0, one launch (start us, length us, event | category | flops | bytes accessed | tf_op | source)
XLA Modules:
  0.0 70.3 jit_solution(16085869378588491876)
XLA Ops:
  0.0 1.2 %copy-done.3 = bf16[4,200,400]{2,1,0:T(8,128)(2,1)S(1)} copy-done((bf16[4,200,400]{2,1,0:T(8,128)(2,1)S(1)}, bf16[4,200,400]{2,1,0:T(8,128)(2,1)}, u32[]{:S(2)}) %copy-start.3) | copy-done | bytes 640024
  1.2 1.1 %copy-done.4 = bf16[4,200,400]{2,1,0:T(8,128)(2,1)S(1)} copy-done((bf16[4,200,400]{2,1,0:T(8,128)(2,1)S(1)}, bf16[4,200,400]{2,1,0:T(8,128)(2,1)}, u32[]{:S(2)}) %copy-start.4) | copy-done | bytes 640024
  2.4 1.1 %copy-done.5 = bf16[4,200,400]{2,1,0:T(8,128)(2,1)S(1)} copy-done((bf16[4,200,400]{2,1,0:T(8,128)(2,1)S(1)}, bf16[4,200,400]{2,1,0:T(8,128)(2,1)}, u32[]{:S(2)}) %copy-start.5) | copy-done | bytes 640024
  3.5 7.4 %shard_map.145 = (s16[200,512]{1,0:T(8,128)(2,1)S(1)}, s16[200,512]{1,0:T(8,128)(2,1)}, s16[200,512]{1,0:T(8,128)(2,1)}, s16[200,512]{1,0:T(8,128)(2,1)}, f32[4,...) custom-call(s32[4]{0:T(128)S(1)} %iota_xor_fusion.order_ref, ...), custom_call_target="tpu_custom_call" | custom-call | flops 6400000 | bytes 2560000 | tf_op jit(solution)/shard_map/pallas_call | solution.py:199
  12.1 2.5 %collective-permute-start.1 = (s16[200,512]{1,0:T(8,128)(2,1)}, s16[200,512]{1,0:T(8,128)(2,1)}, u32[]{:S(2)}, u32[]{:S(2)}) collective-permute-start(s16[200,512]{1,0:T(8,128)(2,1)} %get-tuple-element.32), channel_id=1, source_target_pairs={{0,2},{1,3},{2,0},{3,1},{4,6},{5,7},{6,4},{7,5},{8,10},{9,11},{10,... | collective-permute-start | bytes 614408 | tf_op jit(solution)/shard_map/ppermute | solution.py:136
  14.7 3.7 %collective-permute-start.3 = (f32[4,1,400]{2,1,0:T(1,128)S(1)}, f32[4,1,400]{2,1,0:T(1,128)S(1)}, u32[]{:S(2)}, u32[]{:S(2)}) collective-permute-start(f32[4,1,400]{2,1,0:T(1,128)S(1)} %get-tuple-element.34), channel_id=1, source_target_pairs={{0,4},{4,8},{8,12},{1,5},{5,9},{9,13},{2,6},{6,10},{10,14},{3,7},{... | collective-permute-start | bytes 19208 | tf_op jit(solution)/shard_map/ppermute | solution.py:224
  18.4 1.3 %collective-permute-start.4 = (f32[4,1,400]{2,1,0:T(1,128)S(1)}, f32[4,1,400]{2,1,0:T(1,128)S(1)}, u32[]{:S(2)}, u32[]{:S(2)}) collective-permute-start(f32[4,1,400]{2,1,0:T(1,128)S(1)} %get-tuple-element.35), channel_id=1, source_target_pairs={{4,0},{8,4},{12,8},{5,1},{9,5},{13,9},{6,2},{10,6},{14,10},{7,3},{... | collective-permute-start | bytes 19208 | tf_op jit(solution)/shard_map/ppermute | solution.py:225
  19.7 0.8 %reshape.94 = s32[4,100]{1,0:T(4,128)S(1)} reshape(s32[400]{0:T(512)} %param.19) | data formatting | bytes 3200 | tf_op jit(solution)/shard_map/reshape | solution.py:502
  21.1 0.8 %dynamic_slice.3 = s32[100]{0:T(128)S(1)} dynamic-slice(s32[400]{0:T(512)} %param.19, s32[]{:T(128)S(6)} %select_n.18), dynamic_slice_sizes={100} | dynamic-slice | bytes 804 | tf_op jit(solution)/shard_map/dynamic_slice | solution.py:516
  21.9 1.4 %and_convert_fusion.rest_12_ = bf16[1024,1024]{1,0:T(8,128)(2,1)S(1)} fusion(s32[1024]{0:T(1024)S(1)} %bitcast.19, s32[1024]{0:T(1024)} %constant.76, pred[1024]{0:T(1024)(128)(4,1)S(1)} %broadcast_compare_fusion), kind=kLoop, calls=%fused_computation.1 | loop fusion | flops 3145728 | bytes 2106368 | tf_op jit(solution)/shard_map/convert_element_type | solution.py:509
  24.6 1.4 %shard_map.146 = (f32[2,400]{1,0:T(2,128)}, f32[2,400]{1,0:T(2,128)}, f32[2,400]{1,0:T(2,128)}, f32[2,400]{1,0:T(2,128)}) custom-call(s32[4]{0:T(128)} %copy-done.12, f32[4,1,400]{2,1,0:T(1,128)} %copy-done.15, f32[4,1,400]{2,1,0:T(1,128)} %copy-done.16, f32[4,2,400]{2,1,0:T(2,128)} %copy-done.11), custom_call_target="tpu_custom_call" | custom-call | tf_op jit(solution)/shard_map/pallas_call | solution.py:226
  26.3 1.6 %collective-permute-start.6 = (f32[2,400]{1,0:T(2,128)}, f32[2,400]{1,0:T(2,128)S(1)}, u32[]{:S(2)}, u32[]{:S(2)}) collective-permute-start(f32[2,400]{1,0:T(2,128)} %get-tuple-element.39), channel_id=1, source_target_pairs={{0,2},{1,3},{2,0},{3,1},{4,6},{5,7},{6,4},{7,5},{8,10},{9,11},{10,... | collective-permute-start | bytes 9608 | tf_op jit(solution)/shard_map/ppermute | solution.py:136
  27.9 0.7 %collective-permute-start.7 = (f32[2,400]{1,0:T(2,128)}, f32[2,400]{1,0:T(2,128)S(1)}, u32[]{:S(2)}, u32[]{:S(2)}) collective-permute-start(f32[2,400]{1,0:T(2,128)} %get-tuple-element.40), channel_id=1, source_target_pairs={{0,3},{1,2},{2,1},{3,0},{4,7},{5,6},{6,5},{7,4},{8,11},{9,10},{10,... | collective-permute-start | bytes 9608 | tf_op jit(solution)/shard_map/ppermute | solution.py:136
  29.2 0.8 %copy.19.rest_14_ = s32[200,1]{1,0:T(8,128)S(1)} copy(s32[200,1]{0,1:T(1,128)} %bitcast.22) | data formatting | bytes 1600 | tf_op jit(solution)/shard_map/broadcast_in_dim | solution.py:513
  30.2 0.9 %collective-permute-done.7.rest_7_ = f32[2,400]{1,0:T(2,128)S(1)} collective-permute-done((f32[2,400]{1,0:T(2,128)}, f32[2,400]{1,0:T(2,128)S(1)}, u32[]{:S(2)}, u32[]{:S(2)}) %collective-permute-start.7) | collective-permute-done | bytes 3232 | tf_op jit(solution)/shard_map/ppermute | solution.py:136
  31.9 1.1 %copy-done.2 = bf16[1,400,1024]{2,1,0:T(8,128)(2,1)S(1)} copy-done((bf16[1,400,1024]{2,1,0:T(8,128)(2,1)S(1)}, bf16[1,400,1024]{2,1,0:T(8,128)(2,1)}, u32[]{:S(2)}) %copy-start.2) | copy-done | bytes 819224
  33.0 1.0 %copy-done.7 = bf16[1,400,512]{2,1,0:T(8,128)(2,1)S(1)} copy-done((bf16[1,400,512]{2,1,0:T(8,128)(2,1)S(1)}, bf16[1,400,512]{2,1,0:T(8,128)(2,1)}, u32[]{:S(2)}) %copy-start.7) | copy-done | bytes 409624
  34.0 0.9 %copy-done.10 = s16[200,512]{1,0:T(8,128)(2,1)S(1)} copy-done((s16[200,512]{1,0:T(8,128)(2,1)S(1)}, s16[200,512]{1,0:T(8,128)(2,1)}, u32[]{:S(2)}) %copy-start.10) | copy-done | bytes 204824
  36.2 5.8 %shard_map.147 = (s16[208,256]{1,0:T(8,128)(2,1)S(1)}, s16[208,256]{1,0:T(8,128)(2,1)S(1)}, s16[208,256]{1,0:T(8,128)(2,1)S(1)}, s16[208,256]{1,0:T(8,128)(2,1)S(1)}) custom-call(s32[4]{0:T(128)S(1)} %copy-done.13, s16[200,512]{1,0:T(8,128)(2,1)S(1)} %copy-done.10, s16[200,512]{1,0:T(8,128)(2,1)} %collective-permute-done.rest_1_, ...), custom_call_target="tpu_custom_call" | custom-call | flops 384000000 | bytes 6291456 | tf_op jit(solution)/shard_map/pallas_call | solution.py:315
  42.0 4.3 %collective-permute-start.10 = (s16[208,256]{1,0:T(8,128)(2,1)S(1)}, s16[208,256]{1,0:T(8,128)(2,1)S(1)}, u32[]{:S(2)}, u32[]{:S(2)}) collective-permute-start(s16[208,256]{1,0:T(8,128)(2,1)S(1)} %get-tuple-element.46), channel_id=1, source_target_pairs={{0,12},{4,8},{8,4},{12,0},{1,13},{5,9},{9,5},{13,1},{2,14},{6,10},... | collective-permute-start | bytes 319496 | tf_op jit(solution)/shard_map/ppermute | solution.py:136
  46.9 3.1 %collective-permute-done.10.rest_3_ = s16[208,256]{1,0:T(8,128)(2,1)S(1)} collective-permute-done((s16[208,256]{1,0:T(8,128)(2,1)S(1)}, s16[208,256]{1,0:T(8,128)(2,1)S(1)}, u32[]{:S(2)}, u32[]{:S(2)}) %collective-permute-start.10) | collective-permute-done | bytes 106528 | tf_op jit(solution)/shard_map/ppermute | solution.py:136
  50.0 3.0 %collective-permute-done.8.rest_1_ = s16[208,256]{1,0:T(8,128)(2,1)S(1)} collective-permute-done((s16[208,256]{1,0:T(8,128)(2,1)S(1)}, s16[208,256]{1,0:T(8,128)(2,1)S(1)}, u32[]{:S(2)}, u32[]{:S(2)}) %collective-permute-start.8) | collective-permute-done | bytes 106528 | tf_op jit(solution)/shard_map/ppermute | solution.py:136
  53.0 2.6 %collective-permute-done.9.rest_2_ = s16[208,256]{1,0:T(8,128)(2,1)S(1)} collective-permute-done((s16[208,256]{1,0:T(8,128)(2,1)S(1)}, s16[208,256]{1,0:T(8,128)(2,1)S(1)}, u32[]{:S(2)}, u32[]{:S(2)}) %collective-permute-start.9) | collective-permute-done | bytes 106528 | tf_op jit(solution)/shard_map/ppermute | solution.py:136
  55.6 14.8 %shard_map.148 = f32[100,2,400]{2,1,0:T(2,128)} custom-call(s32[4]{0:T(128)S(1)} %iota_xor_fusion.1.order_ref, s16[208,256]{1,0:T(8,128)(2,1)S(1)} %get-tuple-element.43.rest_0_, s16[208,256]{1,0:T(8,128)(2,1)S(1)} %collective-permute-done.8.rest_1_, s16[208,256]{1,0:T(8,128)(2,1)S(1)} %collective-permute-done.9.rest_2_, ...), custom_call_target="tpu_custom_call" | custom-call | flops 71680000 | bytes 6291456 | tf_op jit(solution)/shard_map/pallas_call | solution.py:461
  (58 shorter events, 7.0 us)
Async XLA Ops:
  0.0 23.2 %copy-start.17 = (f32[399]{0:T(512)S(1)}, f32[399]{0:T(512)}, u32[]{:S(2)}) copy-start(f32[399]{0:T(512)} %constant.77) | copy-start | bytes 4792
  0.0 23.2 %copy-start.18 = (f32[399]{0:T(512)S(1)}, f32[399]{0:T(512)}, u32[]{:S(2)}) copy-start(f32[399]{0:T(512)} %constant.78) | copy-start | bytes 4792
  0.0 31.8 %copy-start.1 = (bf16[1,400,1024]{2,1,0:T(8,128)(2,1)S(1)}, bf16[1,400,1024]{2,1,0:T(8,128)(2,1)}, u32[]{:S(2)}) copy-start(bf16[1,400,1024]{2,1,0:T(8,128)(2,1)} %constant.66.clone.rest_10_) | copy-start | bytes 2457604
  0.0 1.2 %copy-start.3 = (bf16[4,200,400]{2,1,0:T(8,128)(2,1)S(1)}, bf16[4,200,400]{2,1,0:T(8,128)(2,1)}, u32[]{:S(2)}) copy-start(bf16[4,200,400]{2,1,0:T(8,128)(2,1)} %tracer_hbm.1) | copy-start | bytes 1920004
  1.2 1.1 %copy-start.4 = (bf16[4,200,400]{2,1,0:T(8,128)(2,1)S(1)}, bf16[4,200,400]{2,1,0:T(8,128)(2,1)}, u32[]{:S(2)}) copy-start(bf16[4,200,400]{2,1,0:T(8,128)(2,1)} %east_hbm.1) | copy-start | bytes 1920004
  2.4 1.1 %copy-start.5 = (bf16[4,200,400]{2,1,0:T(8,128)(2,1)S(1)}, bf16[4,200,400]{2,1,0:T(8,128)(2,1)}, u32[]{:S(2)}) copy-start(bf16[4,200,400]{2,1,0:T(8,128)(2,1)} %north_hbm.1) | copy-start | bytes 1920004
  3.5 20.4 %copy-start.12 = (s32[4]{0:T(128)}, s32[4]{0:T(128)S(1)}, u32[]{:S(2)}) copy-start(s32[4]{0:T(128)S(1)} %iota_xor_fusion.order_ref) | copy-start | bytes 52
  3.5 28.3 %copy-start.6 = (bf16[1,400,512]{2,1,0:T(8,128)(2,1)S(1)}, bf16[1,400,512]{2,1,0:T(8,128)(2,1)}, u32[]{:S(2)}) copy-start(bf16[1,400,512]{2,1,0:T(8,128)(2,1)} %constant.64.clone.rest_8_) | copy-start | bytes 1228804
  11.6 12.4 %copy-start.11 = (f32[4,2,400]{2,1,0:T(2,128)}, f32[4,2,400]{2,1,0:T(2,128)S(1)}, u32[]{:S(2)}) copy-start(f32[4,2,400]{2,1,0:T(2,128)S(1)} %get-tuple-element.36.row_wind) | copy-start | bytes 38404
  11.6 19.5 %collective-permute-start = (s16[200,512]{1,0:T(8,128)(2,1)}, s16[200,512]{1,0:T(8,128)(2,1)}, u32[]{:S(2)}, u32[]{:S(2)}) collective-permute-start(s16[200,512]{1,0:T(8,128)(2,1)} %get-tuple-element.31), channel_id=1, source_target_pairs={{0,1},{1,0},{2,3},{3,2},{4,5},{5,4},{6,7},{7,6},{8,9},{9,8},{10,11... | collective-permute-start | bytes 614408 | tf_op jit(solution)/shard_map/ppermute | solution.py:136
  12.1 19.1 %collective-permute-start.1 = (s16[200,512]{1,0:T(8,128)(2,1)}, s16[200,512]{1,0:T(8,128)(2,1)}, u32[]{:S(2)}, u32[]{:S(2)}) collective-permute-start(s16[200,512]{1,0:T(8,128)(2,1)} %get-tuple-element.32), channel_id=1, source_target_pairs={{0,2},{1,3},{2,0},{3,1},{4,6},{5,7},{6,4},{7,5},{8,10},{9,11},{10,... | collective-permute-start | bytes 614408 | tf_op jit(solution)/shard_map/ppermute | solution.py:136
  14.6 16.6 %collective-permute-start.2 = (s16[200,512]{1,0:T(8,128)(2,1)}, s16[200,512]{1,0:T(8,128)(2,1)}, u32[]{:S(2)}, u32[]{:S(2)}) collective-permute-start(s16[200,512]{1,0:T(8,128)(2,1)} %get-tuple-element.33), channel_id=1, source_target_pairs={{0,3},{1,2},{2,1},{3,0},{4,7},{5,6},{6,5},{7,4},{8,11},{9,10},{10,... | collective-permute-start | bytes 614408 | tf_op jit(solution)/shard_map/ppermute | solution.py:136
  14.7 8.7 %collective-permute-start.3 = (f32[4,1,400]{2,1,0:T(1,128)S(1)}, f32[4,1,400]{2,1,0:T(1,128)S(1)}, u32[]{:S(2)}, u32[]{:S(2)}) collective-permute-start(f32[4,1,400]{2,1,0:T(1,128)S(1)} %get-tuple-element.34), channel_id=1, source_target_pairs={{0,4},{4,8},{8,12},{1,5},{5,9},{9,13},{2,6},{6,10},{10,14},{3,7},{... | collective-permute-start | bytes 19208 | tf_op jit(solution)/shard_map/ppermute | solution.py:224
  18.4 5.5 %collective-permute-start.4 = (f32[4,1,400]{2,1,0:T(1,128)S(1)}, f32[4,1,400]{2,1,0:T(1,128)S(1)}, u32[]{:S(2)}, u32[]{:S(2)}) collective-permute-start(f32[4,1,400]{2,1,0:T(1,128)S(1)} %get-tuple-element.35), channel_id=1, source_target_pairs={{4,0},{8,4},{12,8},{5,1},{9,5},{13,9},{6,2},{10,6},{14,10},{7,3},{... | collective-permute-start | bytes 19208 | tf_op jit(solution)/shard_map/ppermute | solution.py:225
  26.0 1.9 %collective-permute-start.5 = (f32[2,400]{1,0:T(2,128)}, f32[2,400]{1,0:T(2,128)S(1)}, u32[]{:S(2)}, u32[]{:S(2)}) collective-permute-start(f32[2,400]{1,0:T(2,128)} %get-tuple-element.38), channel_id=1, source_target_pairs={{0,1},{1,0},{2,3},{3,2},{4,5},{5,4},{6,7},{7,6},{8,9},{9,8},{10,11... | collective-permute-start | bytes 9608 | tf_op jit(solution)/shard_map/ppermute | solution.py:136
  26.3 3.9 %collective-permute-start.6 = (f32[2,400]{1,0:T(2,128)}, f32[2,400]{1,0:T(2,128)S(1)}, u32[]{:S(2)}, u32[]{:S(2)}) collective-permute-start(f32[2,400]{1,0:T(2,128)} %get-tuple-element.39), channel_id=1, source_target_pairs={{0,2},{1,3},{2,0},{3,1},{4,6},{5,7},{6,4},{7,5},{8,10},{9,11},{10,... | collective-permute-start | bytes 9608 | tf_op jit(solution)/shard_map/ppermute | solution.py:136
  27.9 3.2 %collective-permute-start.7 = (f32[2,400]{1,0:T(2,128)}, f32[2,400]{1,0:T(2,128)S(1)}, u32[]{:S(2)}, u32[]{:S(2)}) collective-permute-start(f32[2,400]{1,0:T(2,128)} %get-tuple-element.40), channel_id=1, source_target_pairs={{0,3},{1,2},{2,1},{3,0},{4,7},{5,6},{6,5},{7,4},{8,11},{9,10},{10,... | collective-permute-start | bytes 9608 | tf_op jit(solution)/shard_map/ppermute | solution.py:136
  30.0 25.6 %copy-start = (bf16[4,2,800,208]{3,2,1,0:T(8,128)(2,1)S(1)}, bf16[4,2,800,208]{3,2,1,0:T(8,128)(2,1)}, u32[]{:S(2)}) copy-start(bf16[4,2,800,208]{3,2,1,0:T(8,128)(2,1)} %constant.70.clone.rest_4_) | copy-start | bytes 7987204
  31.9 1.1 %copy-start.2 = (bf16[1,400,1024]{2,1,0:T(8,128)(2,1)S(1)}, bf16[1,400,1024]{2,1,0:T(8,128)(2,1)}, u32[]{:S(2)}) copy-start(bf16[1,400,1024]{2,1,0:T(8,128)(2,1)} %constant.67.clone.rest_11_) | copy-start | bytes 2457604
  33.0 1.0 %copy-start.7 = (bf16[1,400,512]{2,1,0:T(8,128)(2,1)S(1)}, bf16[1,400,512]{2,1,0:T(8,128)(2,1)}, u32[]{:S(2)}) copy-start(bf16[1,400,512]{2,1,0:T(8,128)(2,1)} %constant.65.clone.rest_9_) | copy-start | bytes 1228804
  36.2 19.4 %copy-start.8 = (f32[3,200,128]{2,1,0:T(8,128)S(1)}, f32[3,200,128]{2,1,0:T(8,128)}, u32[]{:S(2)}) copy-start(f32[3,200,128]{2,1,0:T(8,128)} %constant.71.clone.rest_5_) | copy-start | bytes 921604
  42.0 8.0 %collective-permute-start.10 = (s16[208,256]{1,0:T(8,128)(2,1)S(1)}, s16[208,256]{1,0:T(8,128)(2,1)S(1)}, u32[]{:S(2)}, u32[]{:S(2)}) collective-permute-start(s16[208,256]{1,0:T(8,128)(2,1)S(1)} %get-tuple-element.46), channel_id=1, source_target_pairs={{0,12},{4,8},{8,4},{12,0},{1,13},{5,9},{9,5},{13,1},{2,14},{6,10},... | collective-permute-start | bytes 319496 | tf_op jit(solution)/shard_map/ppermute | solution.py:136
  46.2 6.8 %collective-permute-start.8 = (s16[208,256]{1,0:T(8,128)(2,1)S(1)}, s16[208,256]{1,0:T(8,128)(2,1)S(1)}, u32[]{:S(2)}, u32[]{:S(2)}) collective-permute-start(s16[208,256]{1,0:T(8,128)(2,1)S(1)} %get-tuple-element.44), channel_id=1, source_target_pairs={{0,4},{4,0},{8,12},{12,8},{1,5},{5,1},{9,13},{13,9},{2,6},{6,2},{1... | collective-permute-start | bytes 319496 | tf_op jit(solution)/shard_map/ppermute | solution.py:136
  46.2 9.4 %collective-permute-start.9 = (s16[208,256]{1,0:T(8,128)(2,1)S(1)}, s16[208,256]{1,0:T(8,128)(2,1)S(1)}, u32[]{:S(2)}, u32[]{:S(2)}) collective-permute-start(s16[208,256]{1,0:T(8,128)(2,1)S(1)} %get-tuple-element.45), channel_id=1, source_target_pairs={{0,8},{4,12},{8,0},{12,4},{1,9},{5,13},{9,1},{13,5},{2,10},{6,14},... | collective-permute-start | bytes 319496 | tf_op jit(solution)/shard_map/ppermute | solution.py:136
  (6 other events, 4.0 us)

commit v5 on v4

--- a/solution.py
+++ b/solution.py
@@ -17,7 +17,7 @@
 CHUNK = 40
 TOP = 32767.0
 WIND_STEP = 1.5 / TOP
-VMEM_BYTES = 24 * 2**20
+VMEM_BYTES = 60 * 2**20
 VMEM_SPEC = pl.BlockSpec(memory_space=pltpu.VMEM)
 SMEM_SPEC = pl.BlockSpec(memory_space=pltpu.SMEM)
 HBM_SPEC = pl.BlockSpec(memory_space=pltpu.HBM)

time: 70.9 us -> 66.6 us (0.939)
  local copies, waits for them, and re-layouts: 13.3 us -> 4.89 us
  other arithmetic: 1.96 us -> 6.04 us
    unnamed x38 -> x28, local copies, waits for them, and re-layouts: 9.11 us -> 1.36 us
    pallas_call x1, Pallas kernels: 7.4 us -> 5.47 us  [advect(): pl.pallas_call(advect_kernel, out_shape=[jax.ShapeDtypeStruct((rows, widt...]
    convert_element_type x1, other arithmetic: 1.36 us -> 2.69 us  [shards(): ((spots[:, None] == columns) & (columns < 2 * M)).astype(jnp.bfloat16)]
    xor x2, other arithmetic: 0.01 us -> 1.03 us  [partners(): lax.axis_index(axis).astype(jnp.int32) ^ order]
    pallas_call x1, Pallas kernels: 14.8 us -> 15.7 us  [legendre(): pl.pallas_call(functools.partial(legendre_kernel, pieces), out_shape=jax....]
    pallas_call x1, Pallas kernels: 5.79 us -> 6.67 us  [fourier(): pl.pallas_call(functools.partial(fourier_kernel, pieces, targets), out_sh...]
    ppermute x9, waiting for transfers between devices: 9.85 us -> 10.6 us  [exchange(): lax.ppermute(blocks[step], axis, pairs[step])]
  transfers between devices with their start and end apart: 11 -> 11, of which waited for: 6 -> 5; matrix products, arithmetic and copies ran while one was open for 8% -> 13% of each run, Pallas kernels for 2% -> 2%
where the time goes in v5:
time: 66.6 us; the launch traced here: 66.2 us
  Pallas kernels  29.3 us (44%)
  starting transfers between devices  15.3 us (23%)
  waiting for transfers between devices  10.6 us (16%)
  other arithmetic  6.04 us (9%)
  local copies, waits for them, and re-layouts  4.89 us (7%)
    pallas_call x1, Pallas kernels, legendre(): pl.pallas_call(functools.partial(legendre_kernel, pieces), out_shape=jax....  15.7 us
    ppermute x9, waiting for transfers between devices, exchange(): lax.ppermute(blocks[step], axis, pairs[step])  10.6 us
    ppermute x9, starting transfers between devices, exchange(): lax.ppermute(blocks[step], axis, pairs[step])  10.3 us
    pallas_call x1, Pallas kernels, fourier(): pl.pallas_call(functools.partial(fourier_kernel, pieces, targets), out_sh...  6.67 us
    pallas_call x1, Pallas kernels, advect(): pl.pallas_call(advect_kernel, out_shape=[jax.ShapeDtypeStruct((rows, widt...  5.47 us
    ppermute x1, starting transfers between devices, halo(): lax.ppermute(last_row, 'lat', [(i, i + 1) for i in range(count - 1)])  3.7 us
    convert_element_type x1, other arithmetic, shards(): ((spots[:, None] == columns) & (columns < 2 * M)).astype(jnp.bfloat16)  2.69 us
    pallas_call x1, Pallas kernels, halo(): pl.pallas_call(halo_kernel, out_shape=[jax.ShapeDtypeStruct((2, lons), jn...  1.44 us
  transfers between devices with their start and end apart: 11, of which 5 were waited for; matrix products, arithmetic and copies ran while one was open for 13% of the time, Pallas kernels for 2%

profile of v5, /device:TPU:0, one launch (start us, length us, event | category | flops | bytes accessed | tf_op | source)
XLA Modules:
  0.0 66.2 jit_solution(6083764744732729591)
XLA Ops:
  0.5 5.5 %shard_map.145 = (s16[200,512]{1,0:T(8,128)(2,1)}, s16[200,512]{1,0:T(8,128)(2,1)}, s16[200,512]{1,0:T(8,128)(2,1)}, s16[200,512]{1,0:T(8,128)(2,1)}, f32[4,1,40...) custom-call(s32[4]{0:T(128)} %iota_xor_fusion.order_ref, bf16[4,200,400]{2,1,0:T(8,128)(2,1)} %tracer_hbm.1, ...), custom_call_target="tpu_custom_call" | custom-call | flops 6400000 | bytes 2560000 | tf_op jit(solution)/shard_map/pallas_call | solution.py:199
  6.5 2.6 %collective-permute-start.1 = (s16[200,512]{1,0:T(8,128)(2,1)}, s16[200,512]{1,0:T(8,128)(2,1)S(1)}, u32[]{:S(2)}, u32[]{:S(2)}) collective-permute-start(s16[200,512]{1,0:T(8,128)(2,1)} %get-tuple-element.32), channel_id=1, source_target_pairs={{0,2},{1,3},{2,0},{3,1},{4,6},{5,7},{6,4},{7,5},{8,10},{9,11},{10,... | collective-permute-start | bytes 614408 | tf_op jit(solution)/shard_map/ppermute | solution.py:136
  9.2 3.7 %collective-permute-start.3 = (f32[4,1,400]{2,1,0:T(1,128)}, f32[4,1,400]{2,1,0:T(1,128)S(1)}, u32[]{:S(2)}, u32[]{:S(2)}) collective-permute-start(f32[4,1,400]{2,1,0:T(1,128)} %get-tuple-element.34), channel_id=1, source_target_pairs={{0,4},{4,8},{8,12},{1,5},{5,9},{9,13},{2,6},{6,10},{10,14},{3,7},{... | collective-permute-start | bytes 19208 | tf_op jit(solution)/shard_map/ppermute | solution.py:224
  12.9 1.3 %collective-permute-start.4 = (f32[4,1,400]{2,1,0:T(1,128)}, f32[4,1,400]{2,1,0:T(1,128)S(1)}, u32[]{:S(2)}, u32[]{:S(2)}) collective-permute-start(f32[4,1,400]{2,1,0:T(1,128)} %get-tuple-element.35), channel_id=1, source_target_pairs={{4,0},{8,4},{12,8},{5,1},{9,5},{13,9},{6,2},{10,6},{14,10},{7,3},{... | collective-permute-start | bytes 19208 | tf_op jit(solution)/shard_map/ppermute | solution.py:225
  14.2 0.8 %reshape.94 = s32[4,100]{1,0:T(4,128)S(1)} reshape(s32[400]{0:T(512)} %param.19) | data formatting | bytes 3200 | tf_op jit(solution)/shard_map/reshape | solution.py:502
  15.0 0.6 gather_fusion
  15.6 0.8 %dynamic_slice.3 = s32[100]{0:T(128)S(1)} dynamic-slice(s32[400]{0:T(512)} %param.19, s32[]{:T(128)S(6)} %select_n.18), dynamic_slice_sizes={100} | dynamic-slice | bytes 804 | tf_op jit(solution)/shard_map/dynamic_slice | solution.py:516
  16.9 2.7 %and_convert_fusion.rest_12_ = bf16[1024,1024]{1,0:T(8,128)(2,1)} fusion(s32[1024]{0:T(1024)S(1)} %bitcast.18, s32[1024]{0:T(1024)} %constant.76, pred[1024]{0:T(1024)(128)(4,1)S(1)} %broadcast_compare_fusion), kind=kLoop, calls=%fused_computation.1 | loop fusion | flops 3145728 | bytes 2106368 | tf_op jit(solution)/shard_map/convert_element_type | solution.py:509
  20.3 0.6 copy-done.6
  20.9 1.4 %shard_map.146 = (f32[2,400]{1,0:T(2,128)}, f32[2,400]{1,0:T(2,128)}, f32[2,400]{1,0:T(2,128)}, f32[2,400]{1,0:T(2,128)}) custom-call(s32[4]{0:T(128)} %iota_xor_fusion.order_ref, f32[4,1,400]{2,1,0:T(1,128)} %copy-done.6, f32[4,1,400]{2,1,0:T(1,128)} %copy-done.7, f32[4,2,400]{2,1,0:T(2,128)} %get-tuple-element.36.row_wind), custom_call_target="tpu_custom_call" | custom-call | tf_op jit(solution)/shard_map/pallas_call | solution.py:226
  22.4 1.0 %sine_multiply_fusion.rest_15_ = f32[200,1]{1,0:T(8,128)} fusion(s32[]{:T(128)S(6)} %mul.53), kind=kLoop, calls=%fused_computation.3 | loop fusion | flops 1000 | bytes 804 | tf_op jit(solution)/shard_map/mul | solution.py:511
  23.4 1.5 %collective-permute-start.6 = (f32[2,400]{1,0:T(2,128)}, f32[2,400]{1,0:T(2,128)S(1)}, u32[]{:S(2)}, u32[]{:S(2)}) collective-permute-start(f32[2,400]{1,0:T(2,128)} %get-tuple-element.39), channel_id=1, source_target_pairs={{0,2},{1,3},{2,0},{3,1},{4,6},{5,7},{6,4},{7,5},{8,10},{9,11},{10,... | collective-permute-start | bytes 9608 | tf_op jit(solution)/shard_map/ppermute | solution.py:136
  25.2 0.8 %copy.19.rest_14_ = s32[200,1]{1,0:T(8,128)} copy(s32[200,1]{0,1:T(1,128)S(1)} %bitcast.22) | data formatting | bytes 1600 | tf_op jit(solution)/shard_map/broadcast_in_dim | solution.py:513
  26.0 1.2 %collective-permute-done.6.rest_6_ = f32[2,400]{1,0:T(2,128)S(1)} collective-permute-done((f32[2,400]{1,0:T(2,128)}, f32[2,400]{1,0:T(2,128)S(1)}, u32[]{:S(2)}, u32[]{:S(2)}) %collective-permute-start.6) | collective-permute-done | bytes 3232 | tf_op jit(solution)/shard_map/ppermute | solution.py:136
  27.2 0.9 %collective-permute-done.7.rest_7_ = f32[2,400]{1,0:T(2,128)S(1)} collective-permute-done((f32[2,400]{1,0:T(2,128)}, f32[2,400]{1,0:T(2,128)S(1)}, u32[]{:S(2)}, u32[]{:S(2)}) %collective-permute-start.7) | collective-permute-done | bytes 3232 | tf_op jit(solution)/shard_map/ppermute | solution.py:136
  28.2 0.7 %broadcast_in_dim.36 = s32[4,2,128]{2,1,0:T(2,128)} broadcast(s32[4,128]{1,0:T(4,128)S(1)} %pad_bitcast_fusion), dimensions={0,2} | broadcast | bytes 6144 | tf_op jit(solution)/shard_map/broadcast_in_dim | solution.py:503
  29.0 6.7 %shard_map.147 = (s16[208,256]{1,0:T(8,128)(2,1)}, s16[208,256]{1,0:T(8,128)(2,1)}, s16[208,256]{1,0:T(8,128)(2,1)}, s16[208,256]{1,0:T(8,128)(2,1)}) custom-call(s32[4]{0:T(128)} %iota_xor_fusion.order_ref, s16[200,512]{1,0:T(8,128)(2,1)} %get-tuple-element.30.rest_0_, s16[200,512]{1,0:T(8,128)(2,1)} %copy-done, s16[200,512]{1,0:T(8,128)(2,1)} %copy-done.1, ...), custom_call_target="tpu_custom_call" | custom-call | flops 384000000 | bytes 6291456 | tf_op jit(solution)/shard_map/pallas_call | solution.py:315
  35.7 4.7 %collective-permute-start.10 = (s16[208,256]{1,0:T(8,128)(2,1)}, s16[208,256]{1,0:T(8,128)(2,1)S(1)}, u32[]{:S(2)}, u32[]{:S(2)}) collective-permute-start(s16[208,256]{1,0:T(8,128)(2,1)} %get-tuple-element.46), channel_id=1, source_target_pairs={{0,12},{4,8},{8,4},{12,0},{1,13},{5,9},{9,5},{13,1},{2,14},{6,10},... | collective-permute-start | bytes 319496 | tf_op jit(solution)/shard_map/ppermute | solution.py:136
  40.4 0.6 collective-permute-start.9
  41.5 2.8 %collective-permute-done.10.rest_3_ = s16[208,256]{1,0:T(8,128)(2,1)S(1)} collective-permute-done((s16[208,256]{1,0:T(8,128)(2,1)}, s16[208,256]{1,0:T(8,128)(2,1)S(1)}, u32[]{:S(2)}, u32[]{:S(2)}) %collective-permute-start.10) | collective-permute-done | bytes 106528 | tf_op jit(solution)/shard_map/ppermute | solution.py:136
  44.4 2.9 %collective-permute-done.8.rest_1_ = s16[208,256]{1,0:T(8,128)(2,1)S(1)} collective-permute-done((s16[208,256]{1,0:T(8,128)(2,1)}, s16[208,256]{1,0:T(8,128)(2,1)S(1)}, u32[]{:S(2)}, u32[]{:S(2)}) %collective-permute-start.8) | collective-permute-done | bytes 106528 | tf_op jit(solution)/shard_map/ppermute | solution.py:136
  47.3 2.6 %collective-permute-done.9.rest_2_ = s16[208,256]{1,0:T(8,128)(2,1)S(1)} collective-permute-done((s16[208,256]{1,0:T(8,128)(2,1)}, s16[208,256]{1,0:T(8,128)(2,1)S(1)}, u32[]{:S(2)}, u32[]{:S(2)}) %collective-permute-start.9) | collective-permute-done | bytes 106528 | tf_op jit(solution)/shard_map/ppermute | solution.py:136
  49.9 0.6 copy-done.5
  50.5 15.7 %shard_map.148 = f32[100,2,400]{2,1,0:T(2,128)} custom-call(s32[4]{0:T(128)} %iota_xor_fusion.1.order_ref, s16[208,256]{1,0:T(8,128)(2,1)} %get-tuple-element.43.rest_0_, s16[208,256]{1,0:T(8,128)(2,1)} %copy-done.4, s16[208,256]{1,0:T(8,128)(2,1)} %copy-done.5, s16[208,256]{1,0:T(8,128)(2,1)} %copy-done.3, bf16[4,2,800,208]{3,2,1,0:T(8,128)(2,1)} %constant.70.clone.rest_4_, ...), custom_call_target="tpu_custom_call" | custom-call | flops 71680000 | bytes 6291456 | tf_op jit(solution)/shard_map/pallas_call | solution.py:461
  (48 shorter events, 3.5 us)
Async XLA Ops:
  0.0 19.6 %copy-start.11 = (f32[399]{0:T(512)S(1)}, f32[399]{0:T(512)}, u32[]{:S(2)}) copy-start(f32[399]{0:T(512)} %constant.77) | copy-start | bytes 4792
  0.0 19.6 %copy-start.12 = (f32[399]{0:T(512)S(1)}, f32[399]{0:T(512)}, u32[]{:S(2)}) copy-start(f32[399]{0:T(512)} %constant.78) | copy-start | bytes 4792
  0.0 25.2 %copy-start.13 = (s32[200]{0:T(256)S(1)}, s32[200]{0:T(256)}, u32[]{:S(2)}) copy-start(s32[200]{0:T(256)} %param.18) | copy-start | bytes 2404
  6.0 22.2 %collective-permute-start = (s16[200,512]{1,0:T(8,128)(2,1)}, s16[200,512]{1,0:T(8,128)(2,1)S(1)}, u32[]{:S(2)}, u32[]{:S(2)}) collective-permute-start(s16[200,512]{1,0:T(8,128)(2,1)} %get-tuple-element.31), channel_id=1, source_target_pairs={{0,1},{1,0},{2,3},{3,2},{4,5},{5,4},{6,7},{7,6},{8,9},{9,8},{10,11... | collective-permute-start | bytes 614408 | tf_op jit(solution)/shard_map/ppermute | solution.py:136
  6.5 21.6 %collective-permute-start.1 = (s16[200,512]{1,0:T(8,128)(2,1)}, s16[200,512]{1,0:T(8,128)(2,1)S(1)}, u32[]{:S(2)}, u32[]{:S(2)}) collective-permute-start(s16[200,512]{1,0:T(8,128)(2,1)} %get-tuple-element.32), channel_id=1, source_target_pairs={{0,2},{1,3},{2,0},{3,1},{4,6},{5,7},{6,4},{7,5},{8,10},{9,11},{10,... | collective-permute-start | bytes 614408 | tf_op jit(solution)/shard_map/ppermute | solution.py:136
  9.1 19.1 %collective-permute-start.2 = (s16[200,512]{1,0:T(8,128)(2,1)}, s16[200,512]{1,0:T(8,128)(2,1)S(1)}, u32[]{:S(2)}, u32[]{:S(2)}) collective-permute-start(s16[200,512]{1,0:T(8,128)(2,1)} %get-tuple-element.33), channel_id=1, source_target_pairs={{0,3},{1,2},{2,1},{3,0},{4,7},{5,6},{6,5},{7,4},{8,11},{9,10},{10,... | collective-permute-start | bytes 614408 | tf_op jit(solution)/shard_map/ppermute | solution.py:136
  9.2 11.1 %collective-permute-start.3 = (f32[4,1,400]{2,1,0:T(1,128)}, f32[4,1,400]{2,1,0:T(1,128)S(1)}, u32[]{:S(2)}, u32[]{:S(2)}) collective-permute-start(f32[4,1,400]{2,1,0:T(1,128)} %get-tuple-element.34), channel_id=1, source_target_pairs={{0,4},{4,8},{8,12},{1,5},{5,9},{9,13},{2,6},{6,10},{10,14},{3,7},{... | collective-permute-start | bytes 19208 | tf_op jit(solution)/shard_map/ppermute | solution.py:224
  12.9 7.4 %collective-permute-start.4 = (f32[4,1,400]{2,1,0:T(1,128)}, f32[4,1,400]{2,1,0:T(1,128)S(1)}, u32[]{:S(2)}, u32[]{:S(2)}) collective-permute-start(f32[4,1,400]{2,1,0:T(1,128)} %get-tuple-element.35), channel_id=1, source_target_pairs={{4,0},{8,4},{12,8},{5,1},{9,5},{13,9},{6,2},{10,6},{14,10},{7,3},{... | collective-permute-start | bytes 19208 | tf_op jit(solution)/shard_map/ppermute | solution.py:225
  20.3 0.6 copy-start.7
  22.4 2.6 %collective-permute-start.5 = (f32[2,400]{1,0:T(2,128)}, f32[2,400]{1,0:T(2,128)S(1)}, u32[]{:S(2)}, u32[]{:S(2)}) collective-permute-start(f32[2,400]{1,0:T(2,128)} %get-tuple-element.38), channel_id=1, source_target_pairs={{0,1},{1,0},{2,3},{3,2},{4,5},{5,4},{6,7},{7,6},{8,9},{9,8},{10,11... | collective-permute-start | bytes 9608 | tf_op jit(solution)/shard_map/ppermute | solution.py:136
  23.4 3.8 %collective-permute-start.6 = (f32[2,400]{1,0:T(2,128)}, f32[2,400]{1,0:T(2,128)S(1)}, u32[]{:S(2)}, u32[]{:S(2)}) collective-permute-start(f32[2,400]{1,0:T(2,128)} %get-tuple-element.39), channel_id=1, source_target_pairs={{0,2},{1,3},{2,0},{3,1},{4,6},{5,7},{6,4},{7,5},{8,10},{9,11},{10,... | collective-permute-start | bytes 9608 | tf_op jit(solution)/shard_map/ppermute | solution.py:136
  24.9 4.0 %copy-start.8 = (f32[2,400]{1,0:T(2,128)}, f32[2,400]{1,0:T(2,128)S(1)}, u32[]{:S(2)}) copy-start(f32[2,400]{1,0:T(2,128)S(1)} %collective-permute-done.5.rest_5_) | copy-start | bytes 9604
  24.9 3.2 %collective-permute-start.7 = (f32[2,400]{1,0:T(2,128)}, f32[2,400]{1,0:T(2,128)S(1)}, u32[]{:S(2)}, u32[]{:S(2)}) collective-permute-start(f32[2,400]{1,0:T(2,128)} %get-tuple-element.40), channel_id=1, source_target_pairs={{0,3},{1,2},{2,1},{3,0},{4,7},{5,6},{6,5},{7,4},{8,11},{9,10},{10,... | collective-permute-start | bytes 9608 | tf_op jit(solution)/shard_map/ppermute | solution.py:136
  27.2 1.6 %copy-start.9 = (f32[2,400]{1,0:T(2,128)}, f32[2,400]{1,0:T(2,128)S(1)}, u32[]{:S(2)}) copy-start(f32[2,400]{1,0:T(2,128)S(1)} %collective-permute-done.6.rest_6_) | copy-start | bytes 9604
  28.2 0.7 %copy-start.10 = (f32[2,400]{1,0:T(2,128)}, f32[2,400]{1,0:T(2,128)S(1)}, u32[]{:S(2)}) copy-start(f32[2,400]{1,0:T(2,128)S(1)} %collective-permute-done.7.rest_7_) | copy-start | bytes 9604
  28.2 0.7 %copy-start = (s16[200,512]{1,0:T(8,128)(2,1)}, s16[200,512]{1,0:T(8,128)(2,1)S(1)}, u32[]{:S(2)}) copy-start(s16[200,512]{1,0:T(8,128)(2,1)S(1)} %collective-permute-done.rest_1_) | copy-start | bytes 614404
  28.2 0.8 %copy-start.1 = (s16[200,512]{1,0:T(8,128)(2,1)}, s16[200,512]{1,0:T(8,128)(2,1)S(1)}, u32[]{:S(2)}) copy-start(s16[200,512]{1,0:T(8,128)(2,1)S(1)} %collective-permute-done.1.rest_2_) | copy-start | bytes 614404
  28.2 0.8 %copy-start.2 = (s16[200,512]{1,0:T(8,128)(2,1)}, s16[200,512]{1,0:T(8,128)(2,1)S(1)}, u32[]{:S(2)}) copy-start(s16[200,512]{1,0:T(8,128)(2,1)S(1)} %collective-permute-done.2.rest_3_) | copy-start | bytes 614404
  35.7 8.7 %collective-permute-start.10 = (s16[208,256]{1,0:T(8,128)(2,1)}, s16[208,256]{1,0:T(8,128)(2,1)S(1)}, u32[]{:S(2)}, u32[]{:S(2)}) collective-permute-start(s16[208,256]{1,0:T(8,128)(2,1)} %get-tuple-element.46), channel_id=1, source_target_pairs={{0,12},{4,8},{8,4},{12,0},{1,13},{5,9},{9,5},{13,1},{2,14},{6,10},... | collective-permute-start | bytes 319496 | tf_op jit(solution)/shard_map/ppermute | solution.py:136
  40.4 6.9 %collective-permute-start.8 = (s16[208,256]{1,0:T(8,128)(2,1)}, s16[208,256]{1,0:T(8,128)(2,1)S(1)}, u32[]{:S(2)}, u32[]{:S(2)}) collective-permute-start(s16[208,256]{1,0:T(8,128)(2,1)} %get-tuple-element.44), channel_id=1, source_target_pairs={{0,4},{4,0},{8,12},{12,8},{1,5},{5,1},{9,13},{13,9},{2,6},{6,2},{1... | collective-permute-start | bytes 319496 | tf_op jit(solution)/shard_map/ppermute | solution.py:136
  40.4 9.6 %collective-permute-start.9 = (s16[208,256]{1,0:T(8,128)(2,1)}, s16[208,256]{1,0:T(8,128)(2,1)S(1)}, u32[]{:S(2)}, u32[]{:S(2)}) collective-permute-start(s16[208,256]{1,0:T(8,128)(2,1)} %get-tuple-element.45), channel_id=1, source_target_pairs={{0,8},{4,12},{8,0},{12,4},{1,9},{5,13},{9,1},{13,5},{2,10},{6,14},... | collective-permute-start | bytes 319496 | tf_op jit(solution)/shard_map/ppermute | solution.py:136
  44.4 5.6 %copy-start.3 = (s16[208,256]{1,0:T(8,128)(2,1)}, s16[208,256]{1,0:T(8,128)(2,1)S(1)}, u32[]{:S(2)}) copy-start(s16[208,256]{1,0:T(8,128)(2,1)S(1)} %collective-permute-done.10.rest_3_) | copy-start | bytes 319492
  47.3 2.6 %copy-start.4 = (s16[208,256]{1,0:T(8,128)(2,1)}, s16[208,256]{1,0:T(8,128)(2,1)S(1)}, u32[]{:S(2)}) copy-start(s16[208,256]{1,0:T(8,128)(2,1)S(1)} %collective-permute-done.8.rest_1_) | copy-start | bytes 319492
  49.9 0.6 copy-start.5
  (1 other events, 0.6 us)

commit v6 on v5

--- a/solution.py
+++ b/solution.py
@@ -494,9 +494,11 @@
     ring = ("lev", "fld")
     level_order, lat_order = partners(ring), partners("lat")
     blocks, edges = advect(tracer, wind_east, wind_north, level_order)
-    blocks, slot_wave, keep_m = lax.optimization_barrier((blocks, slot_wave, keep_m))
     grids = exchange(blocks, ring)
-    halos = exchange(halo(level_order, *edges), ring)
+    ends, slot_wave, keep_m = lax.optimization_barrier(
+        (halo(level_order, *edges), slot_wave, keep_m)
+    )
+    halos = exchange(ends, ring)
 
     pad = ((0, 0), (0, 0), (0, lanes - slots))
     waves = jnp.pad(slot_wave.reshape(lat_count, 1, slots), pad, constant_values=2 * M)

time: 66.6 us -> 67 us (level)
  waiting for transfers between devices: 10.6 us -> 11.4 us
    ppermute x9, starting transfers between devices: 10.3 us -> 8.63 us  [exchange(): lax.ppermute(blocks[step], axis, pairs[step])]
    ppermute x1, starting transfers between devices: 3.7 us -> 4.94 us  [halo(): lax.ppermute(last_row, 'lat', [(i, i + 1) for i in range(count - 1)])]
    ppermute x1, waiting for transfers between devices: 0.01 us -> 0.94 us  [halo(): lax.ppermute(first_row, 'lat', [(i + 1, i) for i in range(count - 1)])]
where the time goes in v6:
time: 67 us; the launch traced here: 66.6 us
  Pallas kernels  29.3 us (44%)
  starting transfers between devices  14.9 us (22%)
  waiting for transfers between devices  11.4 us (17%)
  other arithmetic  6.08 us (9%)
  local copies, waits for them, and re-layouts  4.88 us (7%)
    pallas_call x1, Pallas kernels, legendre(): pl.pallas_call(functools.partial(legendre_kernel, pieces), out_shape=jax....  15.7 us
    ppermute x9, waiting for transfers between devices, exchange(): lax.ppermute(blocks[step], axis, pairs[step])  10.4 us
    ppermute x9, starting transfers between devices, exchange(): lax.ppermute(blocks[step], axis, pairs[step])  8.63 us
    pallas_call x1, Pallas kernels, fourier(): pl.pallas_call(functools.partial(fourier_kernel, pieces, targets), out_sh...  6.67 us
    pallas_call x1, Pallas kernels, advect(): pl.pallas_call(advect_kernel, out_shape=[jax.ShapeDtypeStruct((rows, widt...  5.47 us
    ppermute x1, starting transfers between devices, halo(): lax.ppermute(last_row, 'lat', [(i, i + 1) for i in range(count - 1)])  4.94 us
    convert_element_type x1, other arithmetic, shards(): ((spots[:, None] == columns) & (columns < 2 * M)).astype(jnp.bfloat16)  2.69 us
    pallas_call x1, Pallas kernels, halo(): pl.pallas_call(halo_kernel, out_shape=[jax.ShapeDtypeStruct((2, lons), jn...  1.44 us
  transfers between devices with their start and end apart: 11, of which 5 were waited for; matrix products, arithmetic and copies ran while one was open for 13% of the time, Pallas kernels for 2%

profile of v6, /device:TPU:0, one launch (start us, length us, event | category | flops | bytes accessed | tf_op | source)
XLA Modules:
  0.0 66.6 jit_solution(761542048853413754)
XLA Ops:
  0.5 5.5 %shard_map.145 = (s16[200,512]{1,0:T(8,128)(2,1)}, s16[200,512]{1,0:T(8,128)(2,1)}, s16[200,512]{1,0:T(8,128)(2,1)}, s16[200,512]{1,0:T(8,128)(2,1)}, f32[4,1,40...) custom-call(s32[4]{0:T(128)} %iota_xor_fusion.order_ref, bf16[4,200,400]{2,1,0:T(8,128)(2,1)} %tracer_hbm.1, ...), custom_call_target="tpu_custom_call" | custom-call | flops 6400000 | bytes 2560000 | tf_op jit(solution)/shard_map/pallas_call | solution.py:199
  6.0 4.9 %collective-permute-start.3 = (f32[4,1,400]{2,1,0:T(1,128)}, f32[4,1,400]{2,1,0:T(1,128)S(1)}, u32[]{:S(2)}, u32[]{:S(2)}) collective-permute-start(f32[4,1,400]{2,1,0:T(1,128)} %get-tuple-element.30), channel_id=1, source_target_pairs={{0,4},{4,8},{8,12},{1,5},{5,9},{9,13},{2,6},{6,10},{10,14},{3,7},{... | collective-permute-start | bytes 19208 | tf_op jit(solution)/shard_map/ppermute | solution.py:224
  11.0 1.3 %collective-permute-start.4 = (f32[4,1,400]{2,1,0:T(1,128)}, f32[4,1,400]{2,1,0:T(1,128)S(1)}, u32[]{:S(2)}, u32[]{:S(2)}) collective-permute-start(f32[4,1,400]{2,1,0:T(1,128)} %get-tuple-element.31), channel_id=1, source_target_pairs={{4,0},{8,4},{12,8},{5,1},{9,5},{13,9},{6,2},{10,6},{14,10},{7,3},{... | collective-permute-start | bytes 19208 | tf_op jit(solution)/shard_map/ppermute | solution.py:225
  12.3 1.6 %collective-permute-start.1 = (s16[200,512]{1,0:T(8,128)(2,1)}, s16[200,512]{1,0:T(8,128)(2,1)S(1)}, u32[]{:S(2)}, u32[]{:S(2)}) collective-permute-start(s16[200,512]{1,0:T(8,128)(2,1)} %get-tuple-element.28), channel_id=1, source_target_pairs={{0,2},{1,3},{2,0},{3,1},{4,6},{5,7},{6,4},{7,5},{8,10},{9,11},{10,... | collective-permute-start | bytes 614408 | tf_op jit(solution)/shard_map/ppermute | solution.py:136
  14.2 1.0 %sine_multiply_fusion.rest_15_ = f32[200,1]{1,0:T(8,128)} fusion(s32[]{:T(128)S(6)} %mul.53), kind=kLoop, calls=%fused_computation.3 | loop fusion | flops 1000 | bytes 804 | tf_op jit(solution)/shard_map/mul | solution.py:513
  15.8 0.9 %collective-permute-done.4.below_ref = f32[4,1,400]{2,1,0:T(1,128)S(1)} collective-permute-done((f32[4,1,400]{2,1,0:T(1,128)}, f32[4,1,400]{2,1,0:T(1,128)S(1)}, u32[]{:S(2)}, u32[]{:S(2)}) %collective-permute-start.4) | collective-permute-done | bytes 6432 | tf_op jit(solution)/shard_map/ppermute | solution.py:225
  16.7 0.6 copy-done.7
  17.3 1.4 %shard_map.146 = (f32[2,400]{1,0:T(2,128)}, f32[2,400]{1,0:T(2,128)}, f32[2,400]{1,0:T(2,128)}, f32[2,400]{1,0:T(2,128)}) custom-call(s32[4]{0:T(128)} %iota_xor_fusion.order_ref, f32[4,1,400]{2,1,0:T(1,128)} %copy-done.6, f32[4,1,400]{2,1,0:T(1,128)} %copy-done.7, f32[4,2,400]{2,1,0:T(2,128)} %get-tuple-element.32.row_wind), custom_call_target="tpu_custom_call" | custom-call | tf_op jit(solution)/shard_map/pallas_call | solution.py:226
  18.8 0.8 %reshape.94 = s32[4,100]{1,0:T(4,128)S(1)} reshape(s32[400]{0:T(512)} %param.19) | data formatting | bytes 3200 | tf_op jit(solution)/shard_map/reshape | solution.py:504
  19.5 0.6 gather_fusion
  20.2 1.6 %collective-permute-start.6 = (f32[2,400]{1,0:T(2,128)}, f32[2,400]{1,0:T(2,128)S(1)}, u32[]{:S(2)}, u32[]{:S(2)}) collective-permute-start(f32[2,400]{1,0:T(2,128)} %get-tuple-element.39), channel_id=1, source_target_pairs={{0,2},{1,3},{2,0},{3,1},{4,6},{5,7},{6,4},{7,5},{8,10},{9,11},{10,... | collective-permute-start | bytes 9608 | tf_op jit(solution)/shard_map/ppermute | solution.py:136
  21.7 0.8 %dynamic_slice.3 = s32[100]{0:T(128)S(1)} dynamic-slice(s32[400]{0:T(512)} %param.19, s32[]{:T(128)S(6)} %select_n.18), dynamic_slice_sizes={100} | dynamic-slice | bytes 804 | tf_op jit(solution)/shard_map/dynamic_slice | solution.py:518
  23.1 2.7 %and_convert_fusion.rest_12_ = bf16[1024,1024]{1,0:T(8,128)(2,1)} fusion(s32[1024]{0:T(1024)S(1)} %bitcast.18, s32[1024]{0:T(1024)} %constant.76, pred[1024]{0:T(1024)(128)(4,1)S(1)} %broadcast_compare_fusion), kind=kLoop, calls=%fused_computation.1 | loop fusion | flops 3145728 | bytes 2106368 | tf_op jit(solution)/shard_map/convert_element_type | solution.py:511
  26.3 0.8 %copy.19.rest_14_ = s32[200,1]{1,0:T(8,128)} copy(s32[200,1]{0,1:T(1,128)S(1)} %bitcast.22) | data formatting | bytes 1600 | tf_op jit(solution)/shard_map/broadcast_in_dim | solution.py:515
  27.1 2.2 %collective-permute-done.7.rest_7_ = f32[2,400]{1,0:T(2,128)S(1)} collective-permute-done((f32[2,400]{1,0:T(2,128)}, f32[2,400]{1,0:T(2,128)S(1)}, u32[]{:S(2)}, u32[]{:S(2)}) %collective-permute-start.7) | collective-permute-done | bytes 3232 | tf_op jit(solution)/shard_map/ppermute | solution.py:136
  29.3 0.7 %broadcast_in_dim.36 = s32[4,2,128]{2,1,0:T(2,128)} broadcast(s32[4,128]{1,0:T(4,128)S(1)} %pad_bitcast_fusion), dimensions={0,2} | broadcast | bytes 6144 | tf_op jit(solution)/shard_map/broadcast_in_dim | solution.py:505
  30.1 6.7 %shard_map.147 = (s16[208,256]{1,0:T(8,128)(2,1)}, s16[208,256]{1,0:T(8,128)(2,1)}, s16[208,256]{1,0:T(8,128)(2,1)}, s16[208,256]{1,0:T(8,128)(2,1)}) custom-call(s32[4]{0:T(128)} %iota_xor_fusion.order_ref, s16[200,512]{1,0:T(8,128)(2,1)} %get-tuple-element.26.rest_0_, s16[200,512]{1,0:T(8,128)(2,1)} %copy-done, s16[200,512]{1,0:T(8,128)(2,1)} %copy-done.1, ...), custom_call_target="tpu_custom_call" | custom-call | flops 384000000 | bytes 6291456 | tf_op jit(solution)/shard_map/pallas_call | solution.py:315
  36.8 4.1 %collective-permute-start.10 = (s16[208,256]{1,0:T(8,128)(2,1)}, s16[208,256]{1,0:T(8,128)(2,1)S(1)}, u32[]{:S(2)}, u32[]{:S(2)}) collective-permute-start(s16[208,256]{1,0:T(8,128)(2,1)} %get-tuple-element.46), channel_id=1, source_target_pairs={{0,12},{4,8},{8,4},{12,0},{1,13},{5,9},{9,5},{13,1},{2,14},{6,10},... | collective-permute-start | bytes 319496 | tf_op jit(solution)/shard_map/ppermute | solution.py:136
  40.8 0.6 collective-permute-start.9
  42.0 2.8 %collective-permute-done.10.rest_3_ = s16[208,256]{1,0:T(8,128)(2,1)S(1)} collective-permute-done((s16[208,256]{1,0:T(8,128)(2,1)}, s16[208,256]{1,0:T(8,128)(2,1)S(1)}, u32[]{:S(2)}, u32[]{:S(2)}) %collective-permute-start.10) | collective-permute-done | bytes 106528 | tf_op jit(solution)/shard_map/ppermute | solution.py:136
  44.9 2.8 %collective-permute-done.8.rest_1_ = s16[208,256]{1,0:T(8,128)(2,1)S(1)} collective-permute-done((s16[208,256]{1,0:T(8,128)(2,1)}, s16[208,256]{1,0:T(8,128)(2,1)S(1)}, u32[]{:S(2)}, u32[]{:S(2)}) %collective-permute-start.8) | collective-permute-done | bytes 106528 | tf_op jit(solution)/shard_map/ppermute | solution.py:136
  47.7 2.6 %collective-permute-done.9.rest_2_ = s16[208,256]{1,0:T(8,128)(2,1)S(1)} collective-permute-done((s16[208,256]{1,0:T(8,128)(2,1)}, s16[208,256]{1,0:T(8,128)(2,1)S(1)}, u32[]{:S(2)}, u32[]{:S(2)}) %collective-permute-start.9) | collective-permute-done | bytes 106528 | tf_op jit(solution)/shard_map/ppermute | solution.py:136
  50.3 0.6 copy-done.5
  50.9 15.7 %shard_map.148 = f32[100,2,400]{2,1,0:T(2,128)} custom-call(s32[4]{0:T(128)} %iota_xor_fusion.1.order_ref, s16[208,256]{1,0:T(8,128)(2,1)} %get-tuple-element.43.rest_0_, s16[208,256]{1,0:T(8,128)(2,1)} %copy-done.4, s16[208,256]{1,0:T(8,128)(2,1)} %copy-done.5, s16[208,256]{1,0:T(8,128)(2,1)} %copy-done.3, bf16[4,2,800,208]{3,2,1,0:T(8,128)(2,1)} %constant.70.clone.rest_4_, ...), custom_call_target="tpu_custom_call" | custom-call | flops 71680000 | bytes 6291456 | tf_op jit(solution)/shard_map/pallas_call | solution.py:461
  (48 shorter events, 3.4 us)
Async XLA Ops:
  0.0 25.7 %copy-start.11 = (f32[399]{0:T(512)S(1)}, f32[399]{0:T(512)}, u32[]{:S(2)}) copy-start(f32[399]{0:T(512)} %constant.77) | copy-start | bytes 4792
  0.0 25.7 %copy-start.12 = (f32[399]{0:T(512)S(1)}, f32[399]{0:T(512)}, u32[]{:S(2)}) copy-start(f32[399]{0:T(512)} %constant.78) | copy-start | bytes 4792
  0.0 26.3 %copy-start.13 = (s32[200]{0:T(256)S(1)}, s32[200]{0:T(256)}, u32[]{:S(2)}) copy-start(s32[200]{0:T(256)} %param.18) | copy-start | bytes 2404
  6.0 9.8 %collective-permute-start.3 = (f32[4,1,400]{2,1,0:T(1,128)}, f32[4,1,400]{2,1,0:T(1,128)S(1)}, u32[]{:S(2)}, u32[]{:S(2)}) collective-permute-start(f32[4,1,400]{2,1,0:T(1,128)} %get-tuple-element.30), channel_id=1, source_target_pairs={{0,4},{4,8},{8,12},{1,5},{5,9},{9,13},{2,6},{6,10},{10,14},{3,7},{... | collective-permute-start | bytes 19208 | tf_op jit(solution)/shard_map/ppermute | solution.py:224
  11.0 5.8 %collective-permute-start.4 = (f32[4,1,400]{2,1,0:T(1,128)}, f32[4,1,400]{2,1,0:T(1,128)S(1)}, u32[]{:S(2)}, u32[]{:S(2)}) collective-permute-start(f32[4,1,400]{2,1,0:T(1,128)} %get-tuple-element.31), channel_id=1, source_target_pairs={{4,0},{8,4},{12,8},{5,1},{9,5},{13,9},{6,2},{10,6},{14,10},{7,3},{... | collective-permute-start | bytes 19208 | tf_op jit(solution)/shard_map/ppermute | solution.py:225
  12.3 17.0 %collective-permute-start = (s16[200,512]{1,0:T(8,128)(2,1)}, s16[200,512]{1,0:T(8,128)(2,1)S(1)}, u32[]{:S(2)}, u32[]{:S(2)}) collective-permute-start(s16[200,512]{1,0:T(8,128)(2,1)} %get-tuple-element.27), channel_id=1, source_target_pairs={{0,1},{1,0},{2,3},{3,2},{4,5},{5,4},{6,7},{7,6},{8,9},{9,8},{10,11... | collective-permute-start | bytes 614408 | tf_op jit(solution)/shard_map/ppermute | solution.py:136
  12.3 16.9 %collective-permute-start.1 = (s16[200,512]{1,0:T(8,128)(2,1)}, s16[200,512]{1,0:T(8,128)(2,1)S(1)}, u32[]{:S(2)}, u32[]{:S(2)}) collective-permute-start(s16[200,512]{1,0:T(8,128)(2,1)} %get-tuple-element.28), channel_id=1, source_target_pairs={{0,2},{1,3},{2,0},{3,1},{4,6},{5,7},{6,4},{7,5},{8,10},{9,11},{10,... | collective-permute-start | bytes 614408 | tf_op jit(solution)/shard_map/ppermute | solution.py:136
  13.9 15.4 %collective-permute-start.2 = (s16[200,512]{1,0:T(8,128)(2,1)}, s16[200,512]{1,0:T(8,128)(2,1)S(1)}, u32[]{:S(2)}, u32[]{:S(2)}) collective-permute-start(s16[200,512]{1,0:T(8,128)(2,1)} %get-tuple-element.29), channel_id=1, source_target_pairs={{0,3},{1,2},{2,1},{3,0},{4,7},{5,6},{6,5},{7,4},{8,11},{9,10},{10,... | collective-permute-start | bytes 614408 | tf_op jit(solution)/shard_map/ppermute | solution.py:136
  15.8 1.0 %copy-start.6 = (f32[4,1,400]{2,1,0:T(1,128)}, f32[4,1,400]{2,1,0:T(1,128)S(1)}, u32[]{:S(2)}) copy-start(f32[4,1,400]{2,1,0:T(1,128)S(1)} %collective-permute-done.3.above_ref) | copy-start | bytes 19204
  20.1 5.8 %collective-permute-start.5 = (f32[2,400]{1,0:T(2,128)}, f32[2,400]{1,0:T(2,128)S(1)}, u32[]{:S(2)}, u32[]{:S(2)}) collective-permute-start(f32[2,400]{1,0:T(2,128)} %get-tuple-element.38), channel_id=1, source_target_pairs={{0,1},{1,0},{2,3},{3,2},{4,5},{5,4},{6,7},{7,6},{8,9},{9,8},{10,11... | collective-permute-start | bytes 9608 | tf_op jit(solution)/shard_map/ppermute | solution.py:136
  20.2 6.9 %collective-permute-start.6 = (f32[2,400]{1,0:T(2,128)}, f32[2,400]{1,0:T(2,128)S(1)}, u32[]{:S(2)}, u32[]{:S(2)}) collective-permute-start(f32[2,400]{1,0:T(2,128)} %get-tuple-element.39), channel_id=1, source_target_pairs={{0,2},{1,3},{2,0},{3,1},{4,6},{5,7},{6,4},{7,5},{8,10},{9,11},{10,... | collective-permute-start | bytes 9608 | tf_op jit(solution)/shard_map/ppermute | solution.py:136
  25.9 4.0 %copy-start.8 = (f32[2,400]{1,0:T(2,128)}, f32[2,400]{1,0:T(2,128)S(1)}, u32[]{:S(2)}) copy-start(f32[2,400]{1,0:T(2,128)S(1)} %collective-permute-done.5.rest_5_) | copy-start | bytes 9604
  26.0 3.3 %collective-permute-start.7 = (f32[2,400]{1,0:T(2,128)}, f32[2,400]{1,0:T(2,128)S(1)}, u32[]{:S(2)}, u32[]{:S(2)}) collective-permute-start(f32[2,400]{1,0:T(2,128)} %get-tuple-element.40), channel_id=1, source_target_pairs={{0,3},{1,2},{2,1},{3,0},{4,7},{5,6},{6,5},{7,4},{8,11},{9,10},{10,... | collective-permute-start | bytes 9608 | tf_op jit(solution)/shard_map/ppermute | solution.py:136
  27.1 2.9 %copy-start.9 = (f32[2,400]{1,0:T(2,128)}, f32[2,400]{1,0:T(2,128)S(1)}, u32[]{:S(2)}) copy-start(f32[2,400]{1,0:T(2,128)S(1)} %collective-permute-done.6.rest_6_) | copy-start | bytes 9604
  29.3 0.7 %copy-start.10 = (f32[2,400]{1,0:T(2,128)}, f32[2,400]{1,0:T(2,128)S(1)}, u32[]{:S(2)}) copy-start(f32[2,400]{1,0:T(2,128)S(1)} %collective-permute-done.7.rest_7_) | copy-start | bytes 9604
  29.3 0.7 %copy-start = (s16[200,512]{1,0:T(8,128)(2,1)}, s16[200,512]{1,0:T(8,128)(2,1)S(1)}, u32[]{:S(2)}) copy-start(s16[200,512]{1,0:T(8,128)(2,1)S(1)} %collective-permute-done.rest_1_) | copy-start | bytes 614404
  29.3 0.8 %copy-start.1 = (s16[200,512]{1,0:T(8,128)(2,1)}, s16[200,512]{1,0:T(8,128)(2,1)S(1)}, u32[]{:S(2)}) copy-start(s16[200,512]{1,0:T(8,128)(2,1)S(1)} %collective-permute-done.1.rest_2_) | copy-start | bytes 614404
  29.3 0.8 %copy-start.2 = (s16[200,512]{1,0:T(8,128)(2,1)}, s16[200,512]{1,0:T(8,128)(2,1)S(1)}, u32[]{:S(2)}) copy-start(s16[200,512]{1,0:T(8,128)(2,1)S(1)} %collective-permute-done.2.rest_3_) | copy-start | bytes 614404
  36.8 8.1 %collective-permute-start.10 = (s16[208,256]{1,0:T(8,128)(2,1)}, s16[208,256]{1,0:T(8,128)(2,1)S(1)}, u32[]{:S(2)}, u32[]{:S(2)}) collective-permute-start(s16[208,256]{1,0:T(8,128)(2,1)} %get-tuple-element.46), channel_id=1, source_target_pairs={{0,12},{4,8},{8,4},{12,0},{1,13},{5,9},{9,5},{13,1},{2,14},{6,10},... | collective-permute-start | bytes 319496 | tf_op jit(solution)/shard_map/ppermute | solution.py:136
  40.8 6.8 %collective-permute-start.8 = (s16[208,256]{1,0:T(8,128)(2,1)}, s16[208,256]{1,0:T(8,128)(2,1)S(1)}, u32[]{:S(2)}, u32[]{:S(2)}) collective-permute-start(s16[208,256]{1,0:T(8,128)(2,1)} %get-tuple-element.44), channel_id=1, source_target_pairs={{0,4},{4,0},{8,12},{12,8},{1,5},{5,1},{9,13},{13,9},{2,6},{6,2},{1... | collective-permute-start | bytes 319496 | tf_op jit(solution)/shard_map/ppermute | solution.py:136
  40.8 9.5 %collective-permute-start.9 = (s16[208,256]{1,0:T(8,128)(2,1)}, s16[208,256]{1,0:T(8,128)(2,1)S(1)}, u32[]{:S(2)}, u32[]{:S(2)}) collective-permute-start(s16[208,256]{1,0:T(8,128)(2,1)} %get-tuple-element.45), channel_id=1, source_target_pairs={{0,8},{4,12},{8,0},{12,4},{1,9},{5,13},{9,1},{13,5},{2,10},{6,14},... | collective-permute-start | bytes 319496 | tf_op jit(solution)/shard_map/ppermute | solution.py:136
  44.9 5.4 %copy-start.3 = (s16[208,256]{1,0:T(8,128)(2,1)}, s16[208,256]{1,0:T(8,128)(2,1)S(1)}, u32[]{:S(2)}) copy-start(s16[208,256]{1,0:T(8,128)(2,1)S(1)} %collective-permute-done.10.rest_3_) | copy-start | bytes 319492
  47.7 2.6 %copy-start.4 = (s16[208,256]{1,0:T(8,128)(2,1)}, s16[208,256]{1,0:T(8,128)(2,1)S(1)}, u32[]{:S(2)}) copy-start(s16[208,256]{1,0:T(8,128)(2,1)S(1)} %collective-permute-done.8.rest_1_) | copy-start | bytes 319492
  50.3 0.6 copy-start.5
  (1 other events, 0.6 us)

commit v7 on v6

--- a/solution.py
+++ b/solution.py
@@ -13,8 +13,9 @@
 NLAT = 800
 NLON = 1600
 LANES = 128
-BLOCK = 40
-CHUNK = 40
+BLOCK = 32
+CHUNKS = (40, 32, 32)
+SIDE = LANES // 2
 TOP = 32767.0
 WIND_STEP = 1.5 / TOP
 VMEM_BYTES = 60 * 2**20
@@ -62,16 +63,15 @@
     return result
 
 
-def wave_rows():
-    quarter_width = -(-M // 2 // (2 * LANES)) * 2 * LANES
+def column_waves():
+    width = -(-M // 2 // (2 * LANES)) * 2 * LANES
+    spots = np.full(4 * width, -1.0, np.float32)
     waves = np.arange(M)
-    quarter_count, half_count = M // 4, M // 2
-    rows = []
     for part in range(2):
-        even = np.where(waves % 4 == 0, 0, quarter_width) + part * quarter_count + waves // 4
-        odd = 2 * quarter_width + part * half_count + waves // 2
-        rows.append(np.where(waves % 2 == 0, even, odd))
-    return np.stack(rows).astype(np.int32)
+        even = np.where(waves % 4 == 0, 0, width) + part * (M // 4) + waves // 4
+        odd = 2 * width + part * (M // 2) + waves // 2
+        spots[np.where(waves % 2 == 0, even, odd)] = 2 * waves + part
+    return spots[:, None]
 
 
 def resample_table():
@@ -85,7 +85,8 @@
     rows = []
     for full in (even, odd):
         for sign in (1.0, -1.0):
-            rows.append(full[:half] + sign * full[::-1][:half])
+            folded = (full[:half] + sign * full[::-1][:half]).reshape(2, half // 2, NLAT)
+            rows.append(np.pad(folded, ((0, 0), (0, -half // 2 % 8), (0, 0))).reshape(-1, NLAT))
     return np.concatenate(rows, axis=0)
 
 
@@ -94,8 +95,9 @@
     angles = math.pi / M * (np.arange(half) + 0.5)
     log_sine = np.log2(np.sin(angles))
     coarse = np.round(log_sine * 1024.0) / 1024.0
-    rows = np.stack([2.0 * np.cos(angles), coarse, log_sine - coarse])
-    return np.broadcast_to(rows[:, :, None], (3, half, LANES)).astype(np.float32)
+    rows = np.stack([2.0 * np.cos(angles), coarse, log_sine - coarse]).reshape(3, 2, half // 2)
+    rows = np.pad(rows, ((0, 0), (0, 0), (0, -half // 2 % 8)))
+    return np.repeat(rows.transpose(0, 2, 1), SIDE, axis=2).astype(np.float32)
 
 
 def scale_code(biggest):
@@ -233,15 +235,15 @@
 
 def fourier_kernel(pieces, targets, order_ref, *rest):
     grids, halos, rest = rest[:pieces], rest[pieces : 2 * pieces], rest[2 * pieces :]
-    tables_hbm, (place_ref, wave_ref, keep_ref, sine_ref), rest = rest[:4], rest[4:8], rest[8:]
+    tables_hbm, (wave_ref, keep_ref, sine_ref), rest = rest[:5], rest[5:8], rest[8:]
     outs, rest = rest[:targets], rest[targets:]
-    tables, (field, sems) = rest[:4], rest[4:]
+    tables, place_ref, (field, sems) = rest[:4], rest[4], rest[5:]
     _, rows, width = field.shape
     lons = tables[0].shape[1]
     share = pieces // 4
     copies = []
-    for kind in range(4):
-        copies.append(pltpu.make_async_copy(tables_hbm[kind], tables[kind], sems.at[kind]))
+    for kind, target in enumerate((*tables, place_ref)):
+        copies.append(pltpu.make_async_copy(tables_hbm[kind], target, sems.at[kind]))
         copies[-1].start()
 
     end = width - LANES
@@ -288,6 +290,7 @@
         sums = [part if total is None else total + part for total, part in zip(sums, parts)]
     placed = None
     first = 0
+    copies[4].wait()
     for total in sums:
         last = first + total.shape[1]
         high, low = split_bf16(total)
@@ -315,10 +318,11 @@
     return pl.pallas_call(
         functools.partial(fourier_kernel, pieces, targets),
         out_shape=[jax.ShapeDtypeStruct((padded_rows, span), jnp.int16)] * targets,
-        in_specs=[SMEM_SPEC] + [VMEM_SPEC] * (2 * pieces) + [HBM_SPEC] * 4 + [VMEM_SPEC] * 4,
+        in_specs=[SMEM_SPEC] + [VMEM_SPEC] * (2 * pieces) + [HBM_SPEC] * 5 + [VMEM_SPEC] * 3,
         out_specs=[VMEM_SPEC] * targets,
         scratch_shapes=[pltpu.VMEM(table.shape, jnp.bfloat16) for table in tables]
-        + [pltpu.VMEM((pieces, rows, width), jnp.float32), pltpu.SemaphoreType.DMA((4,))],
+        + [pltpu.VMEM(places.shape, jnp.bfloat16)]
+        + [pltpu.VMEM((pieces, rows, width), jnp.float32), pltpu.SemaphoreType.DMA((5,))],
         compiler_params=pltpu.CompilerParams(vmem_limit_bytes=VMEM_BYTES),
         cost_estimate=pl.CostEstimate(
             flops=3 * rows * NLON * M, bytes_accessed=6 * 2**20, transcendentals=0
@@ -326,52 +330,167 @@
     )(order, *grids, *halos, *tables, places, wave_row, keep_col, sine_col)
 
 
+def places_kernel(
+    order_ref, lat_ref, slot_ref, keep_ref, sine_ref, spot_ref,
+    place_ref, wave_ref, mine_ref, back_ref, keep_col, sine_col, sorted_rows,
+):
+    groups, _, rows = sine_ref.shape
+    slots = slot_ref.shape[1] // groups
+    paired = (slots + 1) // 2
+    shape = (LANES, LANES)
+    down = lax.broadcasted_iota(jnp.int32, shape, 0)
+    across = lax.broadcasted_iota(jnp.int32, shape, 1)
+    filler = jnp.full((1, LANES - slots), 2.0 * M, jnp.float32)
+    for group in range(groups):
+        row = slot_ref[:, group * slots : (group + 1) * slots].astype(jnp.float32)
+        row = jnp.broadcast_to(jnp.concatenate([row, filler], axis=1), shape)
+        column = jnp.sum(jnp.where(down == across, row, 0.0), axis=1, keepdims=True)
+        ahead = (row < column) | ((row == column) & (across < down))
+        rank = jnp.sum(jnp.where(ahead, 1.0, 0.0), axis=1, keepdims=True)
+        place = jnp.where(rank < paired, rank, SIDE + slots - 1.0 - rank)
+        place = jnp.where(rank < slots, place, -1.0)
+        hot = jnp.where(place == across.astype(jnp.float32), 1.0, 0.0)
+        filled = jnp.sum(hot, axis=0, keepdims=True)
+        values = jnp.sum(hot * column, axis=0, keepdims=True)
+        values = jnp.where(filled > 0.5, values, 2.0 * M)
+        sorted_rows[group] = jnp.broadcast_to(values, sorted_rows.shape[1:])
+
+        @pl.when(group == lat_ref[0])
+        def _():
+            mine_ref[...] = values
+            back_ref[...] = hot.astype(jnp.bfloat16)
+
+    spots = spot_ref[...]
+    for step in range(groups):
+        row = sorted_rows[order_ref[step], :1]
+        for part in range(2):
+            cols = slice((2 * step + part) * LANES, (2 * step + part + 1) * LANES)
+            wave_ref[:, cols] = row
+            hit = spots == 2.0 * row + part
+            place_ref[:, cols] = jnp.where(hit, 1.0, 0.0).astype(jnp.bfloat16)
+
+    shape = (rows, rows)
+    same = lax.broadcasted_iota(jnp.int32, shape, 0) == lax.broadcasted_iota(jnp.int32, shape, 1)
+    kept = jnp.broadcast_to(keep_ref[...].astype(jnp.float32), shape)
+    keep_col[...] = jnp.sum(jnp.where(same, kept, 0.0), axis=1, keepdims=True)
+    sine = jnp.broadcast_to(sine_ref[lat_ref[0]], shape)
+    sine_col[...] = jnp.sum(jnp.where(same, sine, 0.0), axis=1, keepdims=True)
+
+
+def prepare_places(order, lat_index, slot_wave, keep_m, groups):
+    rows = keep_m.shape[0]
+    sines = np.sin(math.pi / NLAT * (np.arange(NLAT) + 0.5)) * math.sqrt(2.0 / NLAT)
+    spots = column_waves()
+    width = 2 * groups * LANES
+    return pl.pallas_call(
+        places_kernel,
+        out_shape=[
+            jax.ShapeDtypeStruct((spots.shape[0], width), jnp.bfloat16),
+            jax.ShapeDtypeStruct((1, width), jnp.float32),
+            jax.ShapeDtypeStruct((1, LANES), jnp.float32),
+            jax.ShapeDtypeStruct((LANES, LANES), jnp.bfloat16),
+            jax.ShapeDtypeStruct((rows, 1), jnp.float32),
+            jax.ShapeDtypeStruct((rows, 1), jnp.float32),
+        ],
+        in_specs=[SMEM_SPEC] * 2 + [VMEM_SPEC] * 4,
+        out_specs=[VMEM_SPEC] * 6,
+        scratch_shapes=[pltpu.VMEM((groups, 8, LANES), jnp.float32)],
+        compiler_params=pltpu.CompilerParams(vmem_limit_bytes=VMEM_BYTES),
+    )(
+        order, lat_index[None], slot_wave[None], keep_m[None],
+        sines.reshape(groups, 1, rows).astype(np.float32), spots,
+    )
+
+
+def lane_pairs(row):
+    lane = lax.broadcasted_iota(jnp.int32, row.shape, 1)
+    other = pltpu.roll(row, SIDE, 1)
+    return jnp.where(lane < SIDE, row, other), jnp.where(lane < SIDE, other, row)
+
+
+def block_count(wave):
+    return jnp.floor((jnp.maximum(M - wave, 0.0) + (BLOCK - 1)) * (1.0 / BLOCK))
+
+
+def recurrence_kernel(mine_ref, lat_ref, term_ref, beta_ref, scale_ref, growth_ref, start_ref):
+    pair = lane_pairs(jnp.broadcast_to(mine_ref[...], (8, LANES)))
+    one, two = pair[0][:1], pair[1][:1]
+    blocks = growth_ref.shape[0]
+    turn = block_count(one)
+    block = lax.broadcasted_iota(jnp.int32, (blocks, LANES), 0).astype(jnp.float32)
+    second = block >= turn
+    wave = jnp.where(second, two, one)
+    limit = M - wave
+    wave = jnp.minimum(wave, M - 1.0)
+    first = (block - jnp.where(second, turn, 0.0)) * BLOCK
+
+    scale = jnp.ones((blocks, LANES), jnp.float32)
+    for index in range(BLOCK + 1):
+        order = first + index
+        degree = wave + order
+        square = 4.0 * degree * degree - 1.0
+        spread = 4.0 * order * (degree + wave)
+        if index > 0:
+            scale = scale * jnp.sqrt(square / spread)
+        if index < BLOCK:
+            beta_ref[pl.ds(index, blocks, stride=BLOCK)] = spread / jnp.maximum(square, 1.0)
+            scale_ref[pl.ds(index, blocks, stride=BLOCK)] = jnp.where(order < limit, scale, 0.0)
+    growth_ref[...] = scale
+
+    for kind, wave in enumerate((one, two)):
+        wave = jnp.minimum(wave, M - 1.0)
+        counter = lax.broadcasted_iota(jnp.int32, term_ref.shape, 0).astype(jnp.float32)
+        norm = jnp.sum(jnp.where(counter <= wave, term_ref[...], 0.0), axis=0, keepdims=True)
+        coarse = lat_ref[1] * wave
+        whole = jnp.floor(coarse)
+        start_ref[2 * kind] = jnp.exp2(
+            (coarse - whole) + lat_ref[2] * wave + 0.5 * (norm - 1.0)
+        )
+        start_ref[2 * kind + 1] = whole
+
+
+def prepare_recurrence(mine):
+    latitudes = latitude_table()
+    points = latitudes.shape[1]
+    blocks = 2 * -(-M // BLOCK)
+    counter = np.arange(M)
+    terms = np.log1p(0.5 / np.maximum(counter, 1)) * (counter > 0) / math.log(2.0)
+    terms = np.broadcast_to(terms[:, None], (M, LANES)).astype(np.float32)
+    orders = jax.ShapeDtypeStruct((blocks * BLOCK, LANES), jnp.float32)
+    return pl.pallas_call(
+        recurrence_kernel,
+        out_shape=[
+            orders,
+            orders,
+            jax.ShapeDtypeStruct((blocks, LANES), jnp.float32),
+            jax.ShapeDtypeStruct((4, points, LANES), jnp.float32),
+        ],
+        in_specs=[VMEM_SPEC] * 3,
+        out_specs=[VMEM_SPEC] * 4,
+        compiler_params=pltpu.CompilerParams(vmem_limit_bytes=VMEM_BYTES),
+    )(mine, latitudes, terms)
+
+
 def legendre_kernel(pieces, order_ref, *rest):
     fields, rest = rest[:pieces], rest[pieces:]
-    table_hbm, lat_hbm, wave_ref, limit_ref, norm_ref, out_ref = rest[:6]
-    weight, before, current, level, sums, result, beta_ref, scale_ref, growth_ref = rest[6:15]
-    table, lat_ref, sems = rest[15:]
-    copies = [pltpu.make_async_copy(lat_hbm, lat_ref, sems.at[pieces])]
-    copies[0].start()
+    hbm, (mine_ref, back_ref, out_ref), rest = rest[:6], rest[6:9], rest[9:]
+    held, (weights, before, current, level, sums, result, final, sems) = rest[:6], rest[6:]
+    table, lat_ref, beta_ref, scale_ref, growth_ref, start_ref = held
+    copies = []
     for piece in range(pieces):
-        source = table_hbm.at[order_ref[piece]]
+        source = hbm[0].at[order_ref[piece]]
         copies.append(pltpu.make_async_copy(source, table.at[piece], sems.at[piece]))
         copies[-1].start()
-    half = lat_ref.shape[1]
-    lanes = wave_ref.shape[1]
+    for kind in range(1, 6):
+        copies.append(pltpu.make_async_copy(hbm[kind], held[kind], sems.at[pieces + kind - 1]))
+        copies[-1].start()
+    points = lat_ref.shape[1]
     slots = out_ref.shape[0]
-    groups = lanes // LANES
-    wave = wave_ref[...]
-    odd = wave - 2.0 * jnp.floor(wave * 0.5) > 0.5
-
-    def squares(order):
-        degree = wave + order
-        return 4.0 * degree * degree - 1.0, 4.0 * order * (degree + wave)
-
-    square, spread = squares(
-        lax.broadcasted_iota(jnp.int32, (M, lanes), 0).astype(jnp.float32)
-    )
-    beta_ref[...] = spread / jnp.maximum(square, 1.0)
-    blocks = M // BLOCK
-    first_order = lax.broadcasted_iota(jnp.int32, (blocks, lanes), 0).astype(jnp.float32) * BLOCK
-    scale = jnp.ones((blocks, lanes), jnp.float32)
-    for index in range(BLOCK):
-        inside = first_order + index < limit_ref[...]
-        scale_ref[pl.ds(index, blocks, stride=BLOCK)] = jnp.where(inside, scale, 0.0)
-        square, spread = squares(first_order + (index + 1))
-        scale = scale * jnp.sqrt(square / spread)
-    growth_ref[...] = scale
-
-    copies[0].wait()
-    for group in range(groups):
-        cols = slice(group * LANES, (group + 1) * LANES)
-        coarse = lat_ref[1] * wave[:, cols]
-        whole = jnp.floor(coarse)
-        level[:, cols] = whole
-        current[:, cols] = jnp.exp2(
-            (coarse - whole) + lat_ref[2] * wave[:, cols] + norm_ref[:, cols]
-        )
-        before[:, cols] = jnp.zeros((half, LANES), jnp.float32)
+    mine = mine_ref[...]
+    odd = mine - 2.0 * jnp.floor(mine * 0.5) > 0.5
+    pair = lane_pairs(jnp.broadcast_to(mine, (8, LANES)))
+    turn = block_count(pair[0][:1])
+    block_total = jnp.max(turn + block_count(pair[1][:1])).astype(jnp.int32)
 
     padded_rows = fields[0].shape[0]
     totals = [None] * 4
@@ -379,144 +498,155 @@
         values = from_int16(fields[piece][...])
         values = values * scale_of(values[padded_rows - 1 :])
         high, low = split_bf16(values)
-        copies[1 + piece].wait()
+        copies[piece].wait()
         for kind in range(4):
-            rows = pl.ds(kind * half, half)
+            rows = pl.ds(kind * 2 * points, 2 * points)
             value = jnp.dot(table[piece, 0, rows], high, preferred_element_type=jnp.float32)
             value += jnp.dot(table[piece, 0, rows], low, preferred_element_type=jnp.float32)
             value += jnp.dot(table[piece, 1, rows], high, preferred_element_type=jnp.float32)
             totals[kind] = value if piece == 0 else totals[kind] + value
+    left = lax.broadcasted_iota(jnp.int32, (points, LANES), 1) < SIDE
     for parity in range(2):
         for comp in range(2):
-            cols = slice(comp * lanes, (comp + 1) * lanes)
-            weight[2 * parity + comp] = jnp.where(
-                odd, totals[2 + parity][:, cols], totals[parity][:, cols]
+            cols = slice(comp * LANES, (comp + 1) * LANES)
+            value = jnp.where(odd, totals[2 + parity][:, cols], totals[parity][:, cols])
+            top, bottom = value[:points], value[points:]
+            kind = 2 * parity + comp
+            weights[0, kind] = jnp.where(left, top, pltpu.roll(bottom, SIDE, 1))
+            weights[1, kind] = jnp.where(left, pltpu.roll(top, SIDE, 1), bottom)
+    for copy in copies[pieces:]:
+        copy.wait()
+    current[...] = start_ref[0]
+    level[...] = start_ref[1]
+    before[...] = jnp.zeros_like(before)
+
+    def step(block, carry):
+        base = pl.multiple_of(block * BLOCK, BLOCK)
+        now = block.astype(jnp.float32)
+        second, begins = now >= turn, now == turn
+        grow = growth_ref[pl.ds(block, 1)]
+        first = 0
+        for chunk in CHUNKS:
+            rows = slice(first, first + chunk)
+            height = jnp.where(begins, start_ref[3, rows], level[rows])
+            factor = jnp.exp2(height)
+            scaled = [
+                jnp.where(second, weights[1, k, rows], weights[0, k, rows]) * factor for k in range(4)
+            ]
+            cosine = lat_ref[0, rows]
+            old = jnp.where(begins, 0.0, before[rows])
+            new = jnp.where(begins, start_ref[2, rows], current[rows])
+            for order in range(BLOCK):
+                for comp in range(2):
+                    product = new * scaled[2 * (order % 2) + comp]
+                    partial = product.reshape(chunk // 8, 8, LANES).sum(axis=0)
+                    place = pl.ds((order * 2 + comp) * 8, 8)
+                    if first == 0:
+                        sums[place] = partial
+                    else:
+                        sums[place] += partial
+                beta = beta_ref[pl.ds(base + order, 1)]
+                old, new = new, cosine * new - beta * old
+            biggest = jnp.maximum(jnp.abs(old), jnp.abs(new)) * grow
+            shift = jnp.floor(jnp.log(biggest) * (1.0 / math.log(2.0)))
+            factor = grow * jnp.exp2(-shift)
+            before[rows] = old * factor
+            current[rows] = new * factor
+            level[rows] = height + shift
+            first += chunk
+        for comp in range(2):
+            total = sums[pl.ds(comp * 8, BLOCK, stride=16)]
+            for lane in range(1, 8):
+                total += sums[pl.ds(comp * 8 + lane, BLOCK, stride=16)]
+            total = total * scale_ref[pl.ds(base, BLOCK)]
+            result[comp, pl.ds(base, BLOCK)] = total + pltpu.roll(total, SIDE, 1)
+        return carry
+
+    lax.fori_loop(0, block_total, step, 0)
+
+    left = lax.broadcasted_iota(jnp.int32, (BLOCK, LANES), 1) < SIDE
+    for place in range(-(-M // BLOCK)):
+        rows = pl.ds(place * BLOCK, BLOCK)
+
+        def pick(block, found):
+            chosen = block.astype(jnp.float32) - place == turn
+            base = pl.multiple_of(block * BLOCK, BLOCK)
+            return tuple(
+                jnp.where(chosen, result[comp, pl.ds(base, BLOCK)], found[comp]) for comp in range(2)
             )
 
-    def step(block, carry):
-        first = pl.multiple_of(block * BLOCK, 8)
-        for group in range(groups):
-            cols = slice(group * LANES, (group + 1) * LANES)
-            grow = growth_ref[pl.ds(block, 1), cols]
-            for chunk in range(half // CHUNK):
-                rows = slice(chunk * CHUNK, (chunk + 1) * CHUNK)
-                height = level[rows, cols]
-                factor = jnp.exp2(height)
-                weights = [weight[k, rows, cols] * factor for k in range(4)]
-                cosine = lat_ref[0, rows]
-                old = before[rows, cols]
-                new = current[rows, cols]
-                for order in range(BLOCK):
-                    for comp in range(2):
-                        product = new * weights[2 * (order % 2) + comp]
-                        partial = product.reshape(CHUNK // 8, 8, LANES).sum(axis=0)
-                        place = pl.ds((order * 2 + comp) * 8, 8)
-                        if chunk == 0:
-                            sums[place] = partial
-                        else:
-                            sums[place] += partial
-                    beta = beta_ref[pl.ds(first + order, 1), cols]
-                    old, new = new, cosine * new - beta * old
-                biggest = jnp.maximum(jnp.abs(old), jnp.abs(new)) * grow
-                shift = jnp.floor(jnp.log(biggest) * (1.0 / math.log(2.0)))
-                factor = grow * jnp.exp2(-shift)
-                before[rows, cols] = old * factor
-                current[rows, cols] = new * factor
-                level[rows, cols] = height + shift
-            for comp in range(2):
-                total = sums[pl.ds(comp * 8, BLOCK, stride=16)]
-                for lane in range(1, 8):
-                    total += sums[pl.ds(comp * 8 + lane, BLOCK, stride=16)]
-                result[comp, pl.ds(first, BLOCK), cols] = (
-                    total * scale_ref[pl.ds(first, BLOCK), cols]
-                )
-        return carry
-
-    lax.fori_loop(0, M // BLOCK, step, 0)
+        blank = jnp.zeros((BLOCK, LANES), jnp.float32)
+        later = lax.fori_loop(place, block_total, pick, (blank, blank))
+        for comp in range(2):
+            early = jnp.where(turn > place, result[comp, rows], 0.0)
+            final[comp, rows] = jnp.where(left, early, later[comp])
+    back = back_ref[...]
+    dims = (((1,), (1,)), ((), ()))
     for comp in range(2):
-        out_ref[:, comp, :] = result[comp].T[:slots]
-
-
-def legendre(fields, order, slot_wave, rows):
-    slots = slot_wave.shape[0]
+        high, low = split_bf16(final[comp])
+        value = lax.dot_general(back, high, dims, preferred_element_type=jnp.float32)
+        value += lax.dot_general(back, low, dims, preferred_element_type=jnp.float32)
+        out_ref[:, comp, :] = value[:slots, :M]
+
+
+def legendre(fields, order, mine, back, prepared, rows, slots):
     pieces = len(fields)
-    padded_rows, span = fields[0].shape
-    lanes = span // 2
-    half = M // 2
-    wave_row = jnp.pad(slot_wave, (0, lanes - slots), constant_values=2 * M)[None, :]
-    inside_wave = jnp.minimum(wave_row, M - 1).astype(jnp.float32)
-    limit = (M - wave_row).astype(jnp.float32)
-    counter = np.arange(1, M)[:, None]
-    log_terms = (np.log1p(0.5 / counter) / math.log(2.0)).astype(np.float32)
-    log_norm = jnp.sum(
-        jnp.where(counter.astype(np.float32) <= inside_wave, log_terms, 0.0), axis=0, keepdims=True
-    )
-    norm = 0.5 * (log_norm - 1.0)
-    table = resample_table().reshape(2 * M, pieces, rows).transpose(1, 0, 2)
+    padded_rows = fields[0].shape[0]
+    latitudes = latitude_table()
+    points = latitudes.shape[1]
+    table = resample_table().reshape(8 * points, pieces, rows).transpose(1, 0, 2)
     table = table_bf16(np.pad(table, ((0, 0), (0, 0), (0, padded_rows - rows))))
-    table = table.reshape(pieces, 2 * M, 2, padded_rows).transpose(0, 2, 1, 3)
-    latitudes = latitude_table()
-    vector = pltpu.VMEM((half, lanes), jnp.float32)
-    orders = pltpu.VMEM((M, lanes), jnp.float32)
+    table = table.reshape(pieces, 8 * points, 2, padded_rows).transpose(0, 2, 1, 3)
+    tables = (table, latitudes, *prepared)
+    vector = pltpu.VMEM((points, LANES), jnp.float32)
+    block_rows = -(-M // BLOCK) * BLOCK
     return pl.pallas_call(
         functools.partial(legendre_kernel, pieces),
         out_shape=jax.ShapeDtypeStruct((slots, 2, M), jnp.float32),
-        in_specs=[SMEM_SPEC] + [VMEM_SPEC] * pieces + [HBM_SPEC] * 2 + [VMEM_SPEC] * 3,
+        in_specs=[SMEM_SPEC] + [VMEM_SPEC] * pieces + [HBM_SPEC] * 6 + [VMEM_SPEC] * 2,
         out_specs=VMEM_SPEC,
-        scratch_shapes=[
-            pltpu.VMEM((4, half, lanes), jnp.float32),
+        scratch_shapes=[pltpu.VMEM(array.shape, array.dtype) for array in tables]
+        + [
+            pltpu.VMEM((2, 4, points, LANES), jnp.float32),
             vector,
             vector,
             vector,
             pltpu.VMEM((BLOCK * 16, LANES), jnp.float32),
-            pltpu.VMEM((2, M, lanes), jnp.float32),
-            orders,
-            orders,
-            pltpu.VMEM((M // BLOCK, lanes), jnp.float32),
-            pltpu.VMEM(table.shape, jnp.bfloat16),
-            pltpu.VMEM(latitudes.shape, jnp.float32),
-            pltpu.SemaphoreType.DMA((pieces + 1,)),
+            pltpu.VMEM((2, 2 * block_rows, LANES), jnp.float32),
+            pltpu.VMEM((2, block_rows, LANES), jnp.float32),
+            pltpu.SemaphoreType.DMA((pieces + 5,)),
         ],
         compiler_params=pltpu.CompilerParams(vmem_limit_bytes=VMEM_BYTES),
         cost_estimate=pl.CostEstimate(
-            flops=7 * half * lanes * M, bytes_accessed=6 * 2**20, transcendentals=0
+            flops=7 * points * LANES * M, bytes_accessed=6 * 2**20, transcendentals=0
         ),
-    )(order, *fields, table, latitudes, inside_wave, limit, norm)
+    )(order, *fields, *tables, mine, back)
 
 
 def shards(tracer, wind_east, wind_north, keep_m, slot_wave):
     rows = tracer.shape[1]
     lat_count = lax.axis_size("lat")
     slots = slot_wave.shape[0] // lat_count
-    lanes = -(-slots // LANES) * LANES
-    lat_index = lax.axis_index("lat")
-
+    lat_index = lax.axis_index("lat").astype(jnp.int32)
     ring = ("lev", "fld")
     level_order, lat_order = partners(ring), partners("lat")
+
     blocks, edges = advect(tracer, wind_east, wind_north, level_order)
     grids = exchange(blocks, ring)
     ends, slot_wave, keep_m = lax.optimization_barrier(
         (halo(level_order, *edges), slot_wave, keep_m)
     )
     halos = exchange(ends, ring)
-
-    pad = ((0, 0), (0, 0), (0, lanes - slots))
-    waves = jnp.pad(slot_wave.reshape(lat_count, 1, slots), pad, constant_values=2 * M)
-    waves = jnp.broadcast_to(waves[lat_order], (lat_count, 2, lanes))
-    table_rows = wave_rows()
-    spots = np.full(4 * (-(-M // 2 // (2 * LANES)) * 2 * LANES), 4 * M, np.int32)
-    for part in range(2):
-        spots[table_rows[part]] = np.arange(M) * 2 + part
-    columns = (waves * 2 + jnp.array([0, 1], jnp.int32)[None, :, None]).reshape(1, -1)
-    places = ((spots[:, None] == columns) & (columns < 2 * M)).astype(jnp.bfloat16)
-    row_ids = (lat_index * rows + jnp.arange(rows, dtype=jnp.int32)).astype(jnp.float32)
-    sines = jnp.sin(math.pi / NLAT * (row_ids + 0.5)) * math.sqrt(2.0 / NLAT)
+    places, wave_row, mine, back, keep_col, sine_col = prepare_places(
+        lat_order, lat_index, slot_wave, keep_m, lat_count
+    )
     waved = fourier(
-        grids, halos, level_order, places, waves.reshape(1, -1), keep_m[:, None], sines[:, None], lat_count
+        grids, halos, level_order, places, wave_row, keep_col, sine_col, lat_count
     )
+    waved, mine = lax.optimization_barrier((list(waved), mine))
     fields = exchange(waved, "lat")
-    my_waves = lax.dynamic_slice_in_dim(slot_wave, lat_index * slots, slots)
-    return legendre(fields, lat_order, my_waves, rows)[None]
+    prepared = prepare_recurrence(mine)
+    return legendre(fields, lat_order, mine, back, prepared, rows, slots)[None]
 
 
 def solution(mesh):

time: 67 us -> 63.6 us (0.949)
  other arithmetic: 6.08 us -> 1.06 us
  Pallas kernels: 29.3 us -> 34.3 us
  local copies, waits for them, and re-layouts: 4.88 us -> 2.05 us
  waiting for transfers between devices: 11.4 us -> 10.1 us
    pallas_call x0 -> x2, Pallas kernels: none -> 7.05 us  [the longest x1 3.95 us: prepare_places(): pl.pallas_call(places_kernel, out_shape=[jax.ShapeDtypeStruct((spots.shap...]
    ppermute x9, waiting for transfers between devices: 10.4 us -> 5.64 us  [exchange(): lax.ppermute(blocks[step], axis, pairs[step])]
    ppermute x1, waiting for transfers between devices: 0.94 us -> 4.19 us  [halo(): lax.ppermute(first_row, 'lat', [(i + 1, i) for i in range(count - 1)])]
    convert_element_type x2 -> x0, other arithmetic: 3.24 us -> none  [the longest x1 2.69 us: shards(): ((spots[:, None] == columns) & (columns < 2 * M)).astype(jnp.bfloat16)]
    ppermute x9, starting transfers between devices: 8.63 us -> 10.2 us  [exchange(): lax.ppermute(blocks[step], axis, pairs[step])]
    mul x3 -> x0, other arithmetic: 1.54 us -> none  [the longest x1 1 us: shards(): sines = jnp.sin(math.pi / NLAT * (row_ids + 0.5)) * math.sqrt(2.0 / NLAT)]
    broadcast_in_dim x3 -> x0, local copies, waits for them, and re-layouts: 1.45 us -> none  [the longest x1 0.77 us: shards(): keep_m[:, None]]
    pallas_call x1, Pallas kernels: 15.7 us -> 14.3 us  [legendre(): pl.pallas_call(functools.partial(legendre_kernel, pieces), out_shape=jax....]
  transfers between devices with their start and end apart: 11 -> 11, of which waited for: 5 -> 3; matrix products, arithmetic and copies ran while one was open for 13% -> 1% of each run, Pallas kernels for 2% -> 13%
where the time goes in v7:
time: 63.6 us; the launch traced here: 62.9 us
  Pallas kernels  34.3 us (54%)
  starting transfers between devices  15.2 us (24%)
  waiting for transfers between devices  10.1 us (16%)
  local copies, waits for them, and re-layouts  2.05 us (3%)
  other arithmetic  1.06 us (2%)
    pallas_call x1, Pallas kernels, legendre(): pl.pallas_call(functools.partial(legendre_kernel, pieces), out_shape=jax....  14.3 us
    ppermute x9, starting transfers between devices, exchange(): lax.ppermute(blocks[step], axis, pairs[step])  10.2 us
    pallas_call x1, Pallas kernels, fourier(): pl.pallas_call(functools.partial(fourier_kernel, pieces, targets), out_sh...  6.13 us
    ppermute x9, waiting for transfers between devices, exchange(): lax.ppermute(blocks[step], axis, pairs[step])  5.64 us
    pallas_call x1, Pallas kernels, advect(): pl.pallas_call(advect_kernel, out_shape=[jax.ShapeDtypeStruct((rows, widt...  5.47 us
    ppermute x1, waiting for transfers between devices, halo(): lax.ppermute(first_row, 'lat', [(i + 1, i) for i in range(count - 1)])  4.19 us
    pallas_call x1, Pallas kernels, prepare_places(): pl.pallas_call(places_kernel, out_shape=[jax.ShapeDtypeStruct((spots.shap...  3.95 us
    ppermute x1, starting transfers between devices, halo(): lax.ppermute(last_row, 'lat', [(i, i + 1) for i in range(count - 1)])  3.7 us
  transfers between devices with their start and end apart: 11, of which 3 were waited for; matrix products, arithmetic and copies ran while one was open for 1% of the time, Pallas kernels for 13%

profile of v7, /device:TPU:0, one launch (start us, length us, event | category | flops | bytes accessed | tf_op | source)
XLA Modules:
  0.0 62.9 jit_solution(13780504380898666238)
XLA Ops:
  0.0 0.5 iota_xor_fusion.order_ref
  0.5 5.5 %shard_map.145 = (s16[200,512]{1,0:T(8,128)(2,1)}, s16[200,512]{1,0:T(8,128)(2,1)}, s16[200,512]{1,0:T(8,128)(2,1)}, s16[200,512]{1,0:T(8,128)(2,1)}, f32[4,1,40...) custom-call(s32[4]{0:T(128)} %iota_xor_fusion.order_ref, bf16[4,200,400]{2,1,0:T(8,128)(2,1)} %tracer_hbm.1, ...), custom_call_target="tpu_custom_call" | custom-call | flops 6400000 | bytes 2560000 | tf_op jit(solution)/shard_map/pallas_call | solution.py:201
  6.0 0.5 collective-permute-start
  6.5 2.6 %collective-permute-start.1 = (s16[200,512]{1,0:T(8,128)(2,1)}, s16[200,512]{1,0:T(8,128)(2,1)S(1)}, u32[]{:S(2)}, u32[]{:S(2)}) collective-permute-start(s16[200,512]{1,0:T(8,128)(2,1)} %get-tuple-element.43), channel_id=1, source_target_pairs={{0,2},{1,3},{2,0},{3,1},{4,6},{5,7},{6,4},{7,5},{8,10},{9,11},{10,... | collective-permute-start | bytes 614408 | tf_op jit(solution)/shard_map/ppermute | solution.py:138
  9.1 3.7 %collective-permute-start.3 = (f32[4,1,400]{2,1,0:T(1,128)}, f32[4,1,400]{2,1,0:T(1,128)S(1)}, u32[]{:S(2)}, u32[]{:S(2)}) collective-permute-start(f32[4,1,400]{2,1,0:T(1,128)} %get-tuple-element.45), channel_id=1, source_target_pairs={{0,4},{4,8},{8,12},{1,5},{5,9},{9,13},{2,6},{6,10},{10,14},{3,7},{... | collective-permute-start | bytes 19208 | tf_op jit(solution)/shard_map/ppermute | solution.py:226
  12.9 1.3 %collective-permute-start.4 = (f32[4,1,400]{2,1,0:T(1,128)}, f32[4,1,400]{2,1,0:T(1,128)S(1)}, u32[]{:S(2)}, u32[]{:S(2)}) collective-permute-start(f32[4,1,400]{2,1,0:T(1,128)} %get-tuple-element.46), channel_id=1, source_target_pairs={{4,0},{8,4},{12,8},{5,1},{9,5},{13,9},{6,2},{10,6},{14,10},{7,3},{... | collective-permute-start | bytes 19208 | tf_op jit(solution)/shard_map/ppermute | solution.py:227
  14.2 0.3 collective-permute-done.3.above_ref
  14.4 4.2 %collective-permute-done.4.below_ref = f32[4,1,400]{2,1,0:T(1,128)S(1)} collective-permute-done((f32[4,1,400]{2,1,0:T(1,128)}, f32[4,1,400]{2,1,0:T(1,128)S(1)}, u32[]{:S(2)}, u32[]{:S(2)}) %collective-permute-start.4) | collective-permute-done | bytes 6432 | tf_op jit(solution)/shard_map/ppermute | solution.py:227
  18.6 0.6 copy-done.7
  19.2 1.4 %shard_map.146 = (f32[2,400]{1,0:T(2,128)}, f32[2,400]{1,0:T(2,128)}, f32[2,400]{1,0:T(2,128)}, f32[2,400]{1,0:T(2,128)}) custom-call(s32[4]{0:T(128)} %iota_xor_fusion.order_ref, f32[4,1,400]{2,1,0:T(1,128)} %copy-done.6, f32[4,1,400]{2,1,0:T(1,128)} %copy-done.7, f32[4,2,400]{2,1,0:T(2,128)} %get-tuple-element.47.row_wind), custom_call_target="tpu_custom_call" | custom-call | tf_op jit(solution)/shard_map/pallas_call | solution.py:228
  20.6 1.5 %collective-permute-start.6 = (f32[2,400]{1,0:T(2,128)}, f32[2,400]{1,0:T(2,128)S(1)}, u32[]{:S(2)}, u32[]{:S(2)}) collective-permute-start(f32[2,400]{1,0:T(2,128)} %get-tuple-element.54), channel_id=1, source_target_pairs={{0,2},{1,3},{2,0},{3,1},{4,6},{5,7},{6,4},{7,5},{8,10},{9,11},{10,... | collective-permute-start | bytes 9608 | tf_op jit(solution)/shard_map/ppermute | solution.py:138
  22.2 1.1 %collective-permute-start.7 = (f32[2,400]{1,0:T(2,128)}, f32[2,400]{1,0:T(2,128)S(1)}, u32[]{:S(2)}, u32[]{:S(2)}) collective-permute-start(f32[2,400]{1,0:T(2,128)} %get-tuple-element.55), channel_id=1, source_target_pairs={{0,3},{1,2},{2,1},{3,0},{4,7},{5,6},{6,5},{7,4},{8,11},{9,10},{10,... | collective-permute-start | bytes 9608 | tf_op jit(solution)/shard_map/ppermute | solution.py:138
  23.3 0.5 iota_xor_fusion.1.order_ref
  23.8 4.0 %shard_map.147 = (bf16[1024,1024]{1,0:T(8,128)(2,1)}, f32[1,1024]{1,0:T(1,128)}, f32[1,128]{1,0:T(1,128)}, bf16[128,128]{1,0:T(8,128)(2,1)}, f32[200,1]{1,0:T(8,128)}, /*index=5*/f32[200,1]{1,0:T(8,128)}) custom-call(s32[4]{0:T(128)} %iota_xor_fusion.1.order_ref, s32[1]{0:T(128)} %bitcast.lat_ref, s32[1,400]{1,0:T(1,128)} %bitcast.4, s32[1,200]{1,0:T(1,128)} %bitcast.5, ...), custom_call_target="tpu_custom_call" | custom-call | tf_op jit(solution)/shard_map/pallas_call | solution.py:385
  27.9 0.5 copy-done.9
  28.4 0.1 copy-done
  28.6 6.1 %shard_map.148 = (s16[208,256]{1,0:T(8,128)(2,1)}, s16[208,256]{1,0:T(8,128)(2,1)}, s16[208,256]{1,0:T(8,128)(2,1)}, s16[208,256]{1,0:T(8,128)(2,1)}) custom-call(s32[4]{0:T(128)} %iota_xor_fusion.order_ref, s16[200,512]{1,0:T(8,128)(2,1)} %get-tuple-element.41.rest_0_, s16[200,512]{1,0:T(8,128)(2,1)} %copy-done, s16[200,512]{1,0:T(8,128)(2,1)} %copy-done.1, ...), custom_call_target="tpu_custom_call" | custom-call | flops 384000000 | bytes 6291456 | tf_op jit(solution)/shard_map/pallas_call | solution.py:318
  34.8 1.6 %collective-permute-start.8 = (s16[208,256]{1,0:T(8,128)(2,1)}, s16[208,256]{1,0:T(8,128)(2,1)S(1)}, u32[]{:S(2)}, u32[]{:S(2)}) collective-permute-start(s16[208,256]{1,0:T(8,128)(2,1)} %get-tuple-element.68), channel_id=1, source_target_pairs={{0,4},{4,0},{8,12},{12,8},{1,5},{5,1},{9,13},{13,9},{2,6},{6,2},{1... | collective-permute-start | bytes 319496 | tf_op jit(solution)/shard_map/ppermute | solution.py:138
  36.4 1.1 %collective-permute-start.9 = (s16[208,256]{1,0:T(8,128)(2,1)}, s16[208,256]{1,0:T(8,128)(2,1)S(1)}, u32[]{:S(2)}, u32[]{:S(2)}) collective-permute-start(s16[208,256]{1,0:T(8,128)(2,1)} %get-tuple-element.69), channel_id=1, source_target_pairs={{0,8},{4,12},{8,0},{12,4},{1,9},{5,13},{9,1},{13,5},{2,10},{6,14},... | collective-permute-start | bytes 319496 | tf_op jit(solution)/shard_map/ppermute | solution.py:138
  37.5 1.7 %collective-permute-start.10 = (s16[208,256]{1,0:T(8,128)(2,1)}, s16[208,256]{1,0:T(8,128)(2,1)S(1)}, u32[]{:S(2)}, u32[]{:S(2)}) collective-permute-start(s16[208,256]{1,0:T(8,128)(2,1)} %get-tuple-element.70), channel_id=1, source_target_pairs={{0,12},{4,8},{8,4},{12,0},{1,13},{5,9},{9,5},{13,1},{2,14},{6,10},... | collective-permute-start | bytes 319496 | tf_op jit(solution)/shard_map/ppermute | solution.py:138
  39.2 3.1 %shard_map.149 = (f32[832,128]{1,0:T(8,128)}, f32[832,128]{1,0:T(8,128)}, f32[26,128]{1,0:T(8,128)}, f32[4,104,128]{2,1,0:T(8,128)}) custom-call(f32[1,128]{1,0:T(1,128)} %get-tuple-element.71.mine_ref.rest_10_, f32[3,104,128]{2,1,0:T(8,128)} %constant.37.clone.lat_ref.rest_5_, f32[400,128]{1,0:T(8,128)} %constant.38.clone.term_ref), custom_call_target="tpu_custom_call" | custom-call | tf_op jit(solution)/shard_map/pallas_call | solution.py:460
  42.3 5.6 %collective-permute-done.9.rest_2_ = s16[208,256]{1,0:T(8,128)(2,1)S(1)} collective-permute-done((s16[208,256]{1,0:T(8,128)(2,1)}, s16[208,256]{1,0:T(8,128)(2,1)S(1)}, u32[]{:S(2)}, u32[]{:S(2)}) %collective-permute-start.9) | collective-permute-done | bytes 106528 | tf_op jit(solution)/shard_map/ppermute | solution.py:138
  47.9 0.6 copy-done.4
  48.6 14.3 %shard_map.150 = f32[100,2,400]{2,1,0:T(2,128)} custom-call(s32[4]{0:T(128)} %iota_xor_fusion.1.order_ref, s16[208,256]{1,0:T(8,128)(2,1)} %get-tuple-element.67.rest_0_, s16[208,256]{1,0:T(8,128)(2,1)} %copy-done.3, s16[208,256]{1,0:T(8,128)(2,1)} %copy-done.4, s16[208,256]{1,0:T(8,128)(2,1)} %copy-done.5, bf16[4,2,832,208]{3,2,1,0:T(8,128)(2,1)} %constant.39.clone.rest_4_, ...), custom_call_target="tpu_custom_call" | custom-call | flops 37273600 | bytes 6291456 | tf_op jit(solution)/shard_map/pallas_call | solution.py:603
  (28 shorter events, 0.3 us)
Async XLA Ops:
  6.0 21.8 %collective-permute-start = (s16[200,512]{1,0:T(8,128)(2,1)}, s16[200,512]{1,0:T(8,128)(2,1)S(1)}, u32[]{:S(2)}, u32[]{:S(2)}) collective-permute-start(s16[200,512]{1,0:T(8,128)(2,1)} %get-tuple-element.42), channel_id=1, source_target_pairs={{0,1},{1,0},{2,3},{3,2},{4,5},{5,4},{6,7},{7,6},{8,9},{9,8},{10,11... | collective-permute-start | bytes 614408 | tf_op jit(solution)/shard_map/ppermute | solution.py:138
  6.5 21.3 %collective-permute-start.1 = (s16[200,512]{1,0:T(8,128)(2,1)}, s16[200,512]{1,0:T(8,128)(2,1)S(1)}, u32[]{:S(2)}, u32[]{:S(2)}) collective-permute-start(s16[200,512]{1,0:T(8,128)(2,1)} %get-tuple-element.43), channel_id=1, source_target_pairs={{0,2},{1,3},{2,0},{3,1},{4,6},{5,7},{6,4},{7,5},{8,10},{9,11},{10,... | collective-permute-start | bytes 614408 | tf_op jit(solution)/shard_map/ppermute | solution.py:138
  9.1 18.8 %collective-permute-start.2 = (s16[200,512]{1,0:T(8,128)(2,1)}, s16[200,512]{1,0:T(8,128)(2,1)S(1)}, u32[]{:S(2)}, u32[]{:S(2)}) collective-permute-start(s16[200,512]{1,0:T(8,128)(2,1)} %get-tuple-element.44), channel_id=1, source_target_pairs={{0,3},{1,2},{2,1},{3,0},{4,7},{5,6},{6,5},{7,4},{8,11},{9,10},{10,... | collective-permute-start | bytes 614408 | tf_op jit(solution)/shard_map/ppermute | solution.py:138
  9.1 5.3 %collective-permute-start.3 = (f32[4,1,400]{2,1,0:T(1,128)}, f32[4,1,400]{2,1,0:T(1,128)S(1)}, u32[]{:S(2)}, u32[]{:S(2)}) collective-permute-start(f32[4,1,400]{2,1,0:T(1,128)} %get-tuple-element.45), channel_id=1, source_target_pairs={{0,4},{4,8},{8,12},{1,5},{5,9},{9,13},{2,6},{6,10},{10,14},{3,7},{... | collective-permute-start | bytes 19208 | tf_op jit(solution)/shard_map/ppermute | solution.py:226
  12.9 5.8 %collective-permute-start.4 = (f32[4,1,400]{2,1,0:T(1,128)}, f32[4,1,400]{2,1,0:T(1,128)S(1)}, u32[]{:S(2)}, u32[]{:S(2)}) collective-permute-start(f32[4,1,400]{2,1,0:T(1,128)} %get-tuple-element.46), channel_id=1, source_target_pairs={{4,0},{8,4},{12,8},{5,1},{9,5},{13,9},{6,2},{10,6},{14,10},{7,3},{... | collective-permute-start | bytes 19208 | tf_op jit(solution)/shard_map/ppermute | solution.py:227
  14.4 4.2 %copy-start.6 = (f32[4,1,400]{2,1,0:T(1,128)}, f32[4,1,400]{2,1,0:T(1,128)S(1)}, u32[]{:S(2)}) copy-start(f32[4,1,400]{2,1,0:T(1,128)S(1)} %collective-permute-done.3.above_ref) | copy-start | bytes 19204
  18.6 0.6 copy-start.7
  20.6 1.6 %collective-permute-start.5 = (f32[2,400]{1,0:T(2,128)}, f32[2,400]{1,0:T(2,128)S(1)}, u32[]{:S(2)}, u32[]{:S(2)}) collective-permute-start(f32[2,400]{1,0:T(2,128)} %get-tuple-element.53), channel_id=1, source_target_pairs={{0,1},{1,0},{2,3},{3,2},{4,5},{5,4},{6,7},{7,6},{8,9},{9,8},{10,11... | collective-permute-start | bytes 9608 | tf_op jit(solution)/shard_map/ppermute | solution.py:138
  20.6 7.1 %collective-permute-start.6 = (f32[2,400]{1,0:T(2,128)}, f32[2,400]{1,0:T(2,128)S(1)}, u32[]{:S(2)}, u32[]{:S(2)}) collective-permute-start(f32[2,400]{1,0:T(2,128)} %get-tuple-element.54), channel_id=1, source_target_pairs={{0,2},{1,3},{2,0},{3,1},{4,6},{5,7},{6,4},{7,5},{8,10},{9,11},{10,... | collective-permute-start | bytes 9608 | tf_op jit(solution)/shard_map/ppermute | solution.py:138
  22.2 5.7 %copy-start.8 = (f32[2,400]{1,0:T(2,128)}, f32[2,400]{1,0:T(2,128)S(1)}, u32[]{:S(2)}) copy-start(f32[2,400]{1,0:T(2,128)S(1)} %collective-permute-done.5.rest_5_) | copy-start | bytes 9604
  22.2 5.6 %collective-permute-start.7 = (f32[2,400]{1,0:T(2,128)}, f32[2,400]{1,0:T(2,128)S(1)}, u32[]{:S(2)}, u32[]{:S(2)}) collective-permute-start(f32[2,400]{1,0:T(2,128)} %get-tuple-element.55), channel_id=1, source_target_pairs={{0,3},{1,2},{2,1},{3,0},{4,7},{5,6},{6,5},{7,4},{8,11},{9,10},{10,... | collective-permute-start | bytes 9608 | tf_op jit(solution)/shard_map/ppermute | solution.py:138
  27.8 0.6 copy-start.9
  27.8 0.6 copy-start.10
  27.8 0.7 %copy-start = (s16[200,512]{1,0:T(8,128)(2,1)}, s16[200,512]{1,0:T(8,128)(2,1)S(1)}, u32[]{:S(2)}) copy-start(s16[200,512]{1,0:T(8,128)(2,1)S(1)} %collective-permute-done.rest_1_) | copy-start | bytes 614404
  27.8 0.7 %copy-start.1 = (s16[200,512]{1,0:T(8,128)(2,1)}, s16[200,512]{1,0:T(8,128)(2,1)S(1)}, u32[]{:S(2)}) copy-start(s16[200,512]{1,0:T(8,128)(2,1)S(1)} %collective-permute-done.1.rest_2_) | copy-start | bytes 614404
  27.8 0.8 %copy-start.2 = (s16[200,512]{1,0:T(8,128)(2,1)}, s16[200,512]{1,0:T(8,128)(2,1)S(1)}, u32[]{:S(2)}) copy-start(s16[200,512]{1,0:T(8,128)(2,1)S(1)} %collective-permute-done.2.rest_3_) | copy-start | bytes 614404
  34.8 7.6 %collective-permute-start.8 = (s16[208,256]{1,0:T(8,128)(2,1)}, s16[208,256]{1,0:T(8,128)(2,1)S(1)}, u32[]{:S(2)}, u32[]{:S(2)}) collective-permute-start(s16[208,256]{1,0:T(8,128)(2,1)} %get-tuple-element.68), channel_id=1, source_target_pairs={{0,4},{4,0},{8,12},{12,8},{1,5},{5,1},{9,13},{13,9},{2,6},{6,2},{1... | collective-permute-start | bytes 319496 | tf_op jit(solution)/shard_map/ppermute | solution.py:138
  36.4 11.5 %collective-permute-start.9 = (s16[208,256]{1,0:T(8,128)(2,1)}, s16[208,256]{1,0:T(8,128)(2,1)S(1)}, u32[]{:S(2)}, u32[]{:S(2)}) collective-permute-start(s16[208,256]{1,0:T(8,128)(2,1)} %get-tuple-element.69), channel_id=1, source_target_pairs={{0,8},{4,12},{8,0},{12,4},{1,9},{5,13},{9,1},{13,5},{2,10},{6,14},... | collective-permute-start | bytes 319496 | tf_op jit(solution)/shard_map/ppermute | solution.py:138
  37.5 10.4 %collective-permute-start.10 = (s16[208,256]{1,0:T(8,128)(2,1)}, s16[208,256]{1,0:T(8,128)(2,1)S(1)}, u32[]{:S(2)}, u32[]{:S(2)}) collective-permute-start(s16[208,256]{1,0:T(8,128)(2,1)} %get-tuple-element.70), channel_id=1, source_target_pairs={{0,12},{4,8},{8,4},{12,0},{1,13},{5,9},{9,5},{13,1},{2,14},{6,10},... | collective-permute-start | bytes 319496 | tf_op jit(solution)/shard_map/ppermute | solution.py:138
  42.3 5.6 %copy-start.3 = (s16[208,256]{1,0:T(8,128)(2,1)}, s16[208,256]{1,0:T(8,128)(2,1)S(1)}, u32[]{:S(2)}) copy-start(s16[208,256]{1,0:T(8,128)(2,1)S(1)} %collective-permute-done.8.rest_1_) | copy-start | bytes 319492
  47.9 0.6 %copy-start.4 = (s16[208,256]{1,0:T(8,128)(2,1)}, s16[208,256]{1,0:T(8,128)(2,1)S(1)}, u32[]{:S(2)}) copy-start(s16[208,256]{1,0:T(8,128)(2,1)S(1)} %collective-permute-done.9.rest_2_) | copy-start | bytes 319492
  47.9 0.7 %copy-start.5 = (s16[208,256]{1,0:T(8,128)(2,1)}, s16[208,256]{1,0:T(8,128)(2,1)S(1)}, u32[]{:S(2)}) copy-start(s16[208,256]{1,0:T(8,128)(2,1)S(1)} %collective-permute-done.10.rest_3_) | copy-start | bytes 319492

commit v8 on v7

--- a/solution.py
+++ b/solution.py
@@ -19,6 +19,7 @@
 TOP = 32767.0
 WIND_STEP = 1.5 / TOP
 VMEM_BYTES = 60 * 2**20
+LATE_BYTES = 24 * 2**20
 VMEM_SPEC = pl.BlockSpec(memory_space=pltpu.VMEM)
 SMEM_SPEC = pl.BlockSpec(memory_space=pltpu.SMEM)
 HBM_SPEC = pl.BlockSpec(memory_space=pltpu.HBM)
@@ -138,16 +139,15 @@
     return [blocks[0]] + [lax.ppermute(blocks[step], axis, pairs[step]) for step in range(1, count)]
 
 
-def advect_kernel(order_ref, tracer_hbm, east_hbm, north_hbm, *rest):
-    levels, rows, lons = tracer_hbm.shape
-    outs, rest = rest[:levels], rest[levels:]
-    first_row, last_row, row_wind, tracer, east_wind, north_wind, sems = rest
+def advect_kernel(steps, order_ref, tracer_hbm, east_hbm, north_hbm, above_ref, below_ref, *rest):
+    _, rows, lons = tracer_hbm.shape
+    outs, (tracer, east_wind, north_wind, sems) = rest[: len(steps)], rest[len(steps) :]
     copies = []
-    for step in range(levels):
+    for spot, step in enumerate(steps):
         level = order_ref[step]
         copies.append(
             [
-                pltpu.make_async_copy(source.at[level], target.at[step], sems.at[step, kind])
+                pltpu.make_async_copy(source.at[level], target.at[spot], sems.at[spot, kind])
                 for kind, (source, target) in enumerate(
                     ((tracer_hbm, tracer), (east_hbm, east_wind), (north_hbm, north_wind))
                 )
@@ -158,23 +158,18 @@
     end = (lons - 1) // LANES * LANES
     spare = lons - end
     lane = lax.broadcasted_iota(jnp.int32, (rows, LANES), 1)
-    for step in range(levels):
+    for spot, step in enumerate(steps):
         level = order_ref[step]
-        for copy in copies[step]:
+        for copy in copies[spot]:
             copy.wait()
-        field = tracer[step].astype(jnp.float32)
-        first_row[level] = field[:1]
-        last_row[level] = field[rows - 1 :]
+        field = tracer[spot].astype(jnp.float32)
         blank = jnp.zeros((rows, 1), jnp.float32)
         west = jnp.concatenate([blank, field[:, :-1]], axis=1)
         east = jnp.concatenate([field[:, 1:], blank], axis=1)
-        blank = jnp.zeros((1, lons), jnp.float32)
-        north = jnp.concatenate([blank, field[:-1]], axis=0)
-        south = jnp.concatenate([field[1:], blank], axis=0)
-        eastward = 0.5 * east_wind[step].astype(jnp.float32)
-        northward = 0.5 * north_wind[step].astype(jnp.float32)
-        row_wind[step, :1] = northward[:1]
-        row_wind[step, 1:2] = -northward[rows - 1 :]
+        north = jnp.concatenate([above_ref[level].astype(jnp.float32), field[:-1]], axis=0)
+        south = jnp.concatenate([field[1:], below_ref[level].astype(jnp.float32)], axis=0)
+        eastward = 0.5 * east_wind[spot].astype(jnp.float32)
+        northward = 0.5 * north_wind[spot].astype(jnp.float32)
         moved = field - eastward * (east - west) - northward * (south - north)
         first, last = field[:, :1], field[:, lons - 1 :]
         biggest = jnp.max(jnp.abs(moved), axis=1, keepdims=True)
@@ -189,52 +184,30 @@
         winds = jnp.where(lane == spare + 3, eastward[:, :1], eastward[:, lons - 1 :])
         winds = coded(winds, 1.0 / WIND_STEP)
         tile = jnp.where((lane == spare + 3) | (lane == spare + 4), winds, tile)
-        outs[step][:, :end] = as_int16(coded(moved[:, :end], inverse))
-        outs[step][:, end:] = as_int16(tile)
-
-
-def advect(tracer, east_wind, north_wind, order):
+        outs[spot][:, :end] = as_int16(coded(moved[:, :end], inverse))
+        outs[spot][:, end:] = as_int16(tile)
+
+
+def advect(tracer, east_wind, north_wind, above, below, order, steps):
     levels, rows, lons = tracer.shape
     width = (lons - 1) // LANES * LANES + LANES
-    held = pltpu.VMEM((levels, rows, lons), jnp.bfloat16)
-    row = jax.ShapeDtypeStruct((levels, 1, lons), jnp.float32)
-    result = pl.pallas_call(
-        advect_kernel,
-        out_shape=[jax.ShapeDtypeStruct((rows, width), jnp.int16)] * levels
-        + [row, row, jax.ShapeDtypeStruct((levels, 2, lons), jnp.float32)],
-        in_specs=[SMEM_SPEC] + [HBM_SPEC] * 3,
-        out_specs=[VMEM_SPEC] * (levels + 3),
-        scratch_shapes=[held, held, held, pltpu.SemaphoreType.DMA((levels, 3))],
+    count = len(steps)
+    held = pltpu.VMEM((count, rows, lons), jnp.bfloat16)
+    return pl.pallas_call(
+        functools.partial(advect_kernel, steps),
+        out_shape=[jax.ShapeDtypeStruct((rows, width), jnp.int16)] * count,
+        in_specs=[SMEM_SPEC] + [HBM_SPEC] * 3 + [VMEM_SPEC] * 2,
+        out_specs=[VMEM_SPEC] * count,
+        scratch_shapes=[held, held, held, pltpu.SemaphoreType.DMA((count, 3))],
         compiler_params=pltpu.CompilerParams(vmem_limit_bytes=VMEM_BYTES),
         cost_estimate=pl.CostEstimate(
-            flops=20 * levels * rows * lons, bytes_accessed=8 * levels * rows * lons, transcendentals=0
+            flops=20 * count * rows * lons, bytes_accessed=8 * count * rows * lons, transcendentals=0
         ),
-    )(order, tracer, east_wind, north_wind)
-    return result[:levels], result[levels:]
-
-
-def halo_kernel(order_ref, above_ref, below_ref, row_wind, *outs):
-    for step, out_ref in enumerate(outs):
-        level = order_ref[step]
-        out_ref[:1] = row_wind[step, :1] * above_ref[level]
-        out_ref[1:] = row_wind[step, 1:2] * below_ref[level]
-
-
-def halo(order, first_row, last_row, row_wind):
-    levels, _, lons = first_row.shape
-    count = lax.axis_size("lat")
-    above = lax.ppermute(last_row, "lat", [(i, i + 1) for i in range(count - 1)])
-    below = lax.ppermute(first_row, "lat", [(i + 1, i) for i in range(count - 1)])
-    return pl.pallas_call(
-        halo_kernel,
-        out_shape=[jax.ShapeDtypeStruct((2, lons), jnp.float32)] * levels,
-        in_specs=[SMEM_SPEC] + [VMEM_SPEC] * 3,
-        out_specs=[VMEM_SPEC] * levels,
-    )(order, above, below, row_wind)
+    )(order, tracer, east_wind, north_wind, above, below)
 
 
 def fourier_kernel(pieces, targets, order_ref, *rest):
-    grids, halos, rest = rest[:pieces], rest[pieces : 2 * pieces], rest[2 * pieces :]
+    grids, rest = rest[:pieces], rest[pieces:]
     tables_hbm, (wave_ref, keep_ref, sine_ref), rest = rest[:5], rest[5:8], rest[8:]
     outs, rest = rest[:targets], rest[targets:]
     tables, place_ref, (field, sems) = rest[:4], rest[4], rest[5:]
@@ -257,8 +230,6 @@
         scale = scale_of(tile[:, spare : spare + 1])
         field[spot, :, :end] = values[:, :end] * scale
         field[spot, :, end:] = tile * jnp.where(winds, WIND_STEP, scale)
-        field[spot, :1, :lons] += halos[piece][:1]
-        field[spot, rows - 1 :, :lons] += halos[piece][1:]
     for spot in range(pieces):
         tile = field[spot, :, end:]
         before = field[(spot - 1) % pieces, :, end:]
@@ -308,7 +279,7 @@
         outs[target][...] = result[:, target * span : (target + 1) * span]
 
 
-def fourier(grids, halos, order, places, wave_row, keep_col, sine_col, targets):
+def fourier(grids, order, places, wave_row, keep_col, sine_col, targets):
     pieces = len(grids)
     rows, width = grids[0].shape
     lons = NLON // pieces
@@ -318,7 +289,7 @@
     return pl.pallas_call(
         functools.partial(fourier_kernel, pieces, targets),
         out_shape=[jax.ShapeDtypeStruct((padded_rows, span), jnp.int16)] * targets,
-        in_specs=[SMEM_SPEC] + [VMEM_SPEC] * (2 * pieces) + [HBM_SPEC] * 5 + [VMEM_SPEC] * 3,
+        in_specs=[SMEM_SPEC] + [VMEM_SPEC] * pieces + [HBM_SPEC] * 5 + [VMEM_SPEC] * 3,
         out_specs=[VMEM_SPEC] * targets,
         scratch_shapes=[pltpu.VMEM(table.shape, jnp.bfloat16) for table in tables]
         + [pltpu.VMEM(places.shape, jnp.bfloat16)]
@@ -327,7 +298,7 @@
         cost_estimate=pl.CostEstimate(
             flops=3 * rows * NLON * M, bytes_accessed=6 * 2**20, transcendentals=0
         ),
-    )(order, *grids, *halos, *tables, places, wave_row, keep_col, sine_col)
+    )(order, *grids, *tables, places, wave_row, keep_col, sine_col)
 
 
 def places_kernel(
@@ -467,23 +438,47 @@
         ],
         in_specs=[VMEM_SPEC] * 3,
         out_specs=[VMEM_SPEC] * 4,
-        compiler_params=pltpu.CompilerParams(vmem_limit_bytes=VMEM_BYTES),
+        compiler_params=pltpu.CompilerParams(vmem_limit_bytes=LATE_BYTES),
     )(mine, latitudes, terms)
 
 
-def legendre_kernel(pieces, order_ref, *rest):
-    fields, rest = rest[:pieces], rest[pieces:]
-    hbm, (mine_ref, back_ref, out_ref), rest = rest[:6], rest[6:9], rest[9:]
-    held, (weights, before, current, level, sums, result, final, sems) = rest[:6], rest[6:]
-    table, lat_ref, beta_ref, scale_ref, growth_ref, start_ref = held
-    copies = []
-    for piece in range(pieces):
-        source = hbm[0].at[order_ref[piece]]
-        copies.append(pltpu.make_async_copy(source, table.at[piece], sems.at[piece]))
-        copies[-1].start()
-    for kind in range(1, 6):
-        copies.append(pltpu.make_async_copy(hbm[kind], held[kind], sems.at[pieces + kind - 1]))
-        copies[-1].start()
+def resampled(first, order_ref, fields, table, total):
+    for piece, field in enumerate(fields):
+        values = from_int16(field[...])
+        values = values * scale_of(values[field.shape[0] - 1 :])
+        high, low = split_bf16(values)
+        spot = order_ref[first + piece]
+        both = jnp.concatenate([high, low], axis=1)
+        part = jnp.dot(table[spot, 0], both, preferred_element_type=jnp.float32)
+        part = part[:, : high.shape[1]] + part[:, high.shape[1] :]
+        part += jnp.dot(table[spot, 1], high, preferred_element_type=jnp.float32)
+        total = part if total is None else total + part
+    return total
+
+
+def resample_kernel(order_ref, table_ref, *rest):
+    rest[-1][...] = resampled(0, order_ref, rest[:-1], table_ref, None)
+
+
+def resample(fields, order, table):
+    count, _, height, _ = table.shape
+    span = fields[0].shape[1]
+    return pl.pallas_call(
+        resample_kernel,
+        out_shape=jax.ShapeDtypeStruct((height, span), jnp.float32),
+        in_specs=[SMEM_SPEC] + [VMEM_SPEC] * (1 + len(fields)),
+        out_specs=VMEM_SPEC,
+        compiler_params=pltpu.CompilerParams(vmem_limit_bytes=LATE_BYTES),
+        cost_estimate=pl.CostEstimate(
+            flops=6 * height * span * NLAT // count * len(fields), bytes_accessed=4 * 2**20, transcendentals=0
+        ),
+    )(order, table, *fields)
+
+
+def legendre_kernel(early, order_ref, *rest):
+    table, lat_ref, beta_ref, scale_ref, growth_ref, start_ref, total_ref, mine_ref, back_ref = rest[:9]
+    fields, rest = rest[9:-8], rest[-8:]
+    out_ref, weights, before, current, level, sums, result, final = rest
     points = lat_ref.shape[1]
     slots = out_ref.shape[0]
     mine = mine_ref[...]
@@ -492,19 +487,8 @@
     turn = block_count(pair[0][:1])
     block_total = jnp.max(turn + block_count(pair[1][:1])).astype(jnp.int32)
 
-    padded_rows = fields[0].shape[0]
-    totals = [None] * 4
-    for piece in range(pieces):
-        values = from_int16(fields[piece][...])
-        values = values * scale_of(values[padded_rows - 1 :])
-        high, low = split_bf16(values)
-        copies[piece].wait()
-        for kind in range(4):
-            rows = pl.ds(kind * 2 * points, 2 * points)
-            value = jnp.dot(table[piece, 0, rows], high, preferred_element_type=jnp.float32)
-            value += jnp.dot(table[piece, 0, rows], low, preferred_element_type=jnp.float32)
-            value += jnp.dot(table[piece, 1, rows], high, preferred_element_type=jnp.float32)
-            totals[kind] = value if piece == 0 else totals[kind] + value
+    total = resampled(early, order_ref, fields, table, total_ref[...])
+    totals = [total[2 * points * kind : 2 * points * (kind + 1)] for kind in range(4)]
     left = lax.broadcasted_iota(jnp.int32, (points, LANES), 1) < SIDE
     for parity in range(2):
         for comp in range(2):
@@ -514,8 +498,7 @@
             kind = 2 * parity + comp
             weights[0, kind] = jnp.where(left, top, pltpu.roll(bottom, SIDE, 1))
             weights[1, kind] = jnp.where(left, pltpu.roll(top, SIDE, 1), bottom)
-    for copy in copies[pieces:]:
-        copy.wait()
+    result[...] = jnp.zeros_like(result)
     current[...] = start_ref[0]
     level[...] = start_ref[1]
     before[...] = jnp.zeros_like(before)
@@ -565,21 +548,19 @@
     lax.fori_loop(0, block_total, step, 0)
 
     left = lax.broadcasted_iota(jnp.int32, (BLOCK, LANES), 1) < SIDE
-    for place in range(-(-M // BLOCK)):
-        rows = pl.ds(place * BLOCK, BLOCK)
-
-        def pick(block, found):
-            chosen = block.astype(jnp.float32) - place == turn
-            base = pl.multiple_of(block * BLOCK, BLOCK)
-            return tuple(
-                jnp.where(chosen, result[comp, pl.ds(base, BLOCK)], found[comp]) for comp in range(2)
-            )
-
-        blank = jnp.zeros((BLOCK, LANES), jnp.float32)
-        later = lax.fori_loop(place, block_total, pick, (blank, blank))
+    spots = -(-M // BLOCK)
+    chosen = [jnp.broadcast_to(turn, (8, LANES)) == value for value in range(spots + 1)]
+    chosen = [jnp.concatenate([mask] * (BLOCK // 8), axis=0) for mask in chosen]
+    for place in range(spots):
+        rows = slice(place * BLOCK, (place + 1) * BLOCK)
         for comp in range(2):
-            early = jnp.where(turn > place, result[comp, rows], 0.0)
-            final[comp, rows] = jnp.where(left, early, later[comp])
+            early_part = jnp.where(turn > place, result[comp, rows], 0.0)
+            later = jnp.zeros((BLOCK, LANES), jnp.float32)
+            for value in range(spots + 1):
+                base = (place + value) * BLOCK
+                if base < result.shape[1]:
+                    later = jnp.where(chosen[value], result[comp, base : base + BLOCK], later)
+            final[comp, rows] = jnp.where(left, early_part, later)
     back = back_ref[...]
     dims = (((1,), (1,)), ((), ()))
     for comp in range(2):
@@ -589,24 +570,28 @@
         out_ref[:, comp, :] = value[:slots, :M]
 
 
+def resample_pieces(pieces, rows, padded_rows):
+    full = resample_table()
+    table = full.reshape(full.shape[0], pieces, rows).transpose(1, 0, 2)
+    table = table_bf16(np.pad(table, ((0, 0), (0, 0), (0, padded_rows - rows))))
+    return table.reshape(pieces, full.shape[0], 2, padded_rows).transpose(0, 2, 1, 3)
+
+
 def legendre(fields, order, mine, back, prepared, rows, slots):
     pieces = len(fields)
-    padded_rows = fields[0].shape[0]
+    early = pieces // 2
     latitudes = latitude_table()
     points = latitudes.shape[1]
-    table = resample_table().reshape(8 * points, pieces, rows).transpose(1, 0, 2)
-    table = table_bf16(np.pad(table, ((0, 0), (0, 0), (0, padded_rows - rows))))
-    table = table.reshape(pieces, 8 * points, 2, padded_rows).transpose(0, 2, 1, 3)
-    tables = (table, latitudes, *prepared)
+    table = jnp.asarray(resample_pieces(pieces, rows, fields[0].shape[0]))
+    total = resample(fields[:early], order, table)
     vector = pltpu.VMEM((points, LANES), jnp.float32)
     block_rows = -(-M // BLOCK) * BLOCK
     return pl.pallas_call(
-        functools.partial(legendre_kernel, pieces),
+        functools.partial(legendre_kernel, early),
         out_shape=jax.ShapeDtypeStruct((slots, 2, M), jnp.float32),
-        in_specs=[SMEM_SPEC] + [VMEM_SPEC] * pieces + [HBM_SPEC] * 6 + [VMEM_SPEC] * 2,
+        in_specs=[SMEM_SPEC] + [VMEM_SPEC] * (9 + pieces - early),
         out_specs=VMEM_SPEC,
-        scratch_shapes=[pltpu.VMEM(array.shape, array.dtype) for array in tables]
-        + [
+        scratch_shapes=[
             pltpu.VMEM((2, 4, points, LANES), jnp.float32),
             vector,
             vector,
@@ -614,13 +599,12 @@
             pltpu.VMEM((BLOCK * 16, LANES), jnp.float32),
             pltpu.VMEM((2, 2 * block_rows, LANES), jnp.float32),
             pltpu.VMEM((2, block_rows, LANES), jnp.float32),
-            pltpu.SemaphoreType.DMA((pieces + 5,)),
         ],
-        compiler_params=pltpu.CompilerParams(vmem_limit_bytes=VMEM_BYTES),
+        compiler_params=pltpu.CompilerParams(vmem_limit_bytes=LATE_BYTES),
         cost_estimate=pl.CostEstimate(
             flops=7 * points * LANES * M, bytes_accessed=6 * 2**20, transcendentals=0
         ),
-    )(order, *fields, *tables, mine, back)
+    )(order, table, latitudes, *prepared, total, mine, back, *fields[early:])
 
 
 def shards(tracer, wind_east, wind_north, keep_m, slot_wave):
@@ -631,17 +615,20 @@
     ring = ("lev", "fld")
     level_order, lat_order = partners(ring), partners("lat")
 
-    blocks, edges = advect(tracer, wind_east, wind_north, level_order)
-    grids = exchange(blocks, ring)
-    ends, slot_wave, keep_m = lax.optimization_barrier(
-        (halo(level_order, *edges), slot_wave, keep_m)
-    )
-    halos = exchange(ends, ring)
+    count = lax.axis_size("lat")
+    above = lax.ppermute(tracer[:, rows - 1 :], "lat", [(i, i + 1) for i in range(count - 1)])
+    below = lax.ppermute(tracer[:, :1], "lat", [(i + 1, i) for i in range(count - 1)])
+    fields = (tracer, wind_east, wind_north, above, below, level_order)
+    levels = tracer.shape[0]
+    far = advect(*fields, tuple(range(levels // 2, levels)))
+    near = advect(*fields, tuple(range(levels // 2)))
+    near, slot_wave, keep_m = lax.optimization_barrier((list(near), slot_wave, keep_m))
+    grids = exchange([*near, *far], ring)
     places, wave_row, mine, back, keep_col, sine_col = prepare_places(
         lat_order, lat_index, slot_wave, keep_m, lat_count
     )
     waved = fourier(
-        grids, halos, level_order, places, wave_row, keep_col, sine_col, lat_count
+        grids, level_order, places, wave_row, keep_col, sine_col, lat_count
     )
     waved, mine = lax.optimization_barrier((list(waved), mine))
     fields = exchange(waved, "lat")

time: 63.6 us -> 57 us (0.90)
  waiting for transfers between devices: 10.1 us -> 5.98 us
  Pallas kernels: 34.3 us -> 32.9 us
  starting transfers between devices: 15.2 us -> 14.2 us
    ppermute x2, waiting for transfers between devices: 4.45 us -> 0.76 us  [the longest x1 0.75 us: shards(): lax.ppermute(tracer[:, rows - 1:], 'lat', [(i, i + 1) for i in range(coun...]
    ppermute x9 -> x6, starting transfers between devices: 10.2 us -> 7.32 us  [exchange(): lax.ppermute(blocks[step], axis, pairs[step])]
    pallas_call x1, Pallas kernels: 3.1 us -> 1.22 us  [prepare_recurrence(): pl.pallas_call(recurrence_kernel, out_shape=[orders, orders, jax.ShapeDty...]
    ppermute x2, starting transfers between devices: 5 us -> 6.85 us  [the longest x1 5.56 us: shards(): lax.ppermute(tracer[:, rows - 1:], 'lat', [(i, i + 1) for i in range(coun...]
    slice x0 -> x1, local copies, waits for them, and re-layouts: none -> 0.79 us  [shards(): tracer[:, :1]]
    unnamed x22 -> x18, local copies, waits for them, and re-layouts: 2.05 us -> 1.51 us
    ppermute x9 -> x6, waiting for transfers between devices: 5.64 us -> 5.23 us  [exchange(): lax.ppermute(blocks[step], axis, pairs[step])]
    pallas_call x3 -> x4, Pallas kernels: 21.2 us -> 21.3 us  [the longest x1 11.9 us: legendre(): pl.pallas_call(functools.partial(legendre_kernel, early), out_shape=jax.S...]
  transfers between devices with their start and end apart: 11 -> 8, of which waited for: 3 -> 2; matrix products, arithmetic and copies ran while one was open for 1% -> 2% of each run, Pallas kernels for 13% -> 19%
where the time goes in v8:
time: 57 us; the launch traced here: 56.7 us
  Pallas kernels  32.9 us (58%)
  starting transfers between devices  14.2 us (25%)
  waiting for transfers between devices  5.98 us (10%)
  local copies, waits for them, and re-layouts  2.3 us (4%)
  other arithmetic  1.15 us (2%)
    pallas_call x1, Pallas kernels, legendre(): pl.pallas_call(functools.partial(legendre_kernel, early), out_shape=jax.S...  11.9 us
    pallas_call x2, Pallas kernels, advect(): pl.pallas_call(functools.partial(advect_kernel, steps), out_shape=[jax.Sh...  8.06 us
    ppermute x6, starting transfers between devices, exchange(): lax.ppermute(blocks[step], axis, pairs[step])  7.32 us
    pallas_call x1, Pallas kernels, fourier(): pl.pallas_call(functools.partial(fourier_kernel, pieces, targets), out_sh...  6.08 us
    ppermute x1, starting transfers between devices, shards(): lax.ppermute(tracer[:, rows - 1:], 'lat', [(i, i + 1) for i in range(coun...  5.56 us
    ppermute x6, waiting for transfers between devices, exchange(): lax.ppermute(blocks[step], axis, pairs[step])  5.23 us
    pallas_call x1, Pallas kernels, prepare_places(): pl.pallas_call(places_kernel, out_shape=[jax.ShapeDtypeStruct((spots.shap...  4.32 us
    unnamed x18, local copies, waits for them, and re-layouts  1.51 us
  transfers between devices with their start and end apart: 8, of which 2 were waited for; matrix products, arithmetic and copies ran while one was open for 2% of the time, Pallas kernels for 19%

profile of v8, /device:TPU:0, one launch (start us, length us, event | category | flops | bytes accessed | tf_op | source)
XLA Modules:
  0.0 56.7 jit_solution(17791981556244106469)
XLA Ops:
  0.0 0.8 %fusion = (bf16[4,1,400]{2,1,0:T(2,128)(2,1)S(1)}, bf16[4,1,400]{2,1,0:T(2,128)(2,1)S(1)}) fusion(bf16[4,200,400]{2,1,0:T(8,128)(2,1)} %tracer_hbm.3), kind=kLoop, calls=%fused_computation.2 | loop fusion | bytes 12800 | tf_op jit(solution)/shard_map/slice | solution.py:620
  0.8 1.3 %collective-permute-start.1 = (bf16[4,1,400]{2,1,0:T(2,128)(2,1)S(1)}, bf16[4,1,400]{2,1,0:T(2,128)(2,1)S(1)}, u32[]{:S(2)}, u32[]{:S(2)}) collective-permute-start(bf16[4,1,400]{2,1,0:T(2,128)(2,1)S(1)} %get-tuple-element.59), channel_id=1, source_target_pairs={{4,0},{8,4},{12,8},{5,1},{9,5},{13,9},{6,2},{10,6},{14,10},{7,3},{... | collective-permute-start | bytes 9608 | tf_op jit(solution)/shard_map/ppermute | solution.py:620
  2.1 5.6 %collective-permute-start = (bf16[4,1,400]{2,1,0:T(2,128)(2,1)S(1)}, bf16[4,1,400]{2,1,0:T(2,128)(2,1)S(1)}, u32[]{:S(2)}, u32[]{:S(2)}) collective-permute-start(bf16[4,1,400]{2,1,0:T(2,128)(2,1)S(1)} %get-tuple-element.60), channel_id=1, source_target_pairs={{0,4},{4,8},{8,12},{1,5},{5,9},{9,13},{2,6},{6,10},{10,14},{3,7},{... | collective-permute-start | bytes 9608 | tf_op jit(solution)/shard_map/ppermute | solution.py:619
  7.7 0.6 %iota_xor_fusion.order_ref = s32[4]{0:T(128)} fusion(s32[]{:T(128)S(6)} %add.3), kind=kLoop, calls=%fused_computation | loop fusion | flops 4 | bytes 20 | tf_op jit(solution)/shard_map/xor | solution.py:131
  8.2 0.0 collective-permute-done.1.below_ref
  8.3 0.8 %collective-permute-done.above_ref = bf16[4,1,400]{2,1,0:T(2,128)(2,1)S(1)} collective-permute-done((bf16[4,1,400]{2,1,0:T(2,128)(2,1)S(1)}, bf16[4,1,400]{2,1,0:T(2,128)(2,1)S(1)}, u32[]{:S(2)}, u32[]{:S(2)}) %collective-permute-start) | collective-permute-done | bytes 3232 | tf_op jit(solution)/shard_map/ppermute | solution.py:619
  9.0 0.6 %copy-done.8 = bf16[4,1,400]{2,1,0:T(2,128)(2,1)} copy-done((bf16[4,1,400]{2,1,0:T(2,128)(2,1)}, bf16[4,1,400]{2,1,0:T(2,128)(2,1)S(1)}, u32[]{:S(2)}) %copy-start.8) | copy-done | bytes 3224
  9.6 4.0 %shard_map.146 = (s16[200,512]{1,0:T(8,128)(2,1)}, s16[200,512]{1,0:T(8,128)(2,1)}) custom-call(s32[4]{0:T(128)} %iota_xor_fusion.order_ref, bf16[4,200,400]{2,1,0:T(8,128)(2,1)} %tracer_hbm.3, bf16[4,200,400]{2,1,0:T(8,128)(2,1)} %east_hbm.3, bf16[4,200,400]{2,1,0:T(8,128)(2,1)} %north_hbm.3, bf16[4,1,400]{2,1,0:T(2,128)(2,1)} %copy-done.8, ...), custom_call_target="tpu_custom_call" | custom-call | flops 3200000 | bytes 1280000 | tf_op jit(solution)/shard_map/pallas_call | solution.py:196
  13.6 2.0 %collective-permute-start.3 = (s16[200,512]{1,0:T(8,128)(2,1)}, s16[200,512]{1,0:T(8,128)(2,1)}, u32[]{:S(2)}, u32[]{:S(2)}) collective-permute-start(s16[200,512]{1,0:T(8,128)(2,1)} %get-tuple-element.36), channel_id=1, source_target_pairs={{0,2},{1,3},{2,0},{3,1},{4,6},{5,7},{6,4},{7,5},{8,10},{9,11},{10,... | collective-permute-start | bytes 614408 | tf_op jit(solution)/shard_map/ppermute | solution.py:139
  15.6 0.0 collective-permute-start.4
  15.6 4.0 %shard_map.145 = (s16[200,512]{1,0:T(8,128)(2,1)}, s16[200,512]{1,0:T(8,128)(2,1)}) custom-call(s32[4]{0:T(128)} %iota_xor_fusion.order_ref, bf16[4,200,400]{2,1,0:T(8,128)(2,1)} %tracer_hbm.3, bf16[4,200,400]{2,1,0:T(8,128)(2,1)} %east_hbm.3, bf16[4,200,400]{2,1,0:T(8,128)(2,1)} %north_hbm.3, bf16[4,1,400]{2,1,0:T(2,128)(2,1)} %copy-done.8, ...), custom_call_target="tpu_custom_call" | custom-call | flops 3200000 | bytes 1280000 | tf_op jit(solution)/shard_map/pallas_call | solution.py:196
  19.7 0.0 copy-start
  19.7 0.3 collective-permute-start.2
  20.0 0.6 iota_xor_fusion.1.order_ref
  20.5 4.3 %shard_map.147 = (bf16[1024,1024]{1,0:T(8,128)(2,1)}, f32[1,1024]{1,0:T(1,128)}, f32[1,128]{1,0:T(1,128)}, bf16[128,128]{1,0:T(8,128)(2,1)}, f32[200,1]{1,0:T(8,128)}, /*index=5*/f32[200,1]{1,0:T(8,128)}) custom-call(s32[4]{0:T(128)} %iota_xor_fusion.1.order_ref, s32[1]{0:T(128)} %bitcast.lat_ref, s32[1,400]{1,0:T(1,128)} %bitcast.4, s32[1,200]{1,0:T(1,128)} %bitcast.5, ...), custom_call_target="tpu_custom_call" | custom-call | tf_op jit(solution)/shard_map/pallas_call | solution.py:356
  24.8 0.0 collective-permute-done.3.rest_2_
  24.9 6.1 %shard_map.148 = (s16[208,256]{1,0:T(8,128)(2,1)}, s16[208,256]{1,0:T(8,128)(2,1)}, s16[208,256]{1,0:T(8,128)(2,1)}, s16[208,256]{1,0:T(8,128)(2,1)}) custom-call(s32[4]{0:T(128)} %iota_xor_fusion.order_ref, s16[200,512]{1,0:T(8,128)(2,1)} %get-tuple-element.34.rest_0_, s16[200,512]{1,0:T(8,128)(2,1)} %collective-permute-done.2.rest_1_, ...), custom_call_target="tpu_custom_call" | custom-call | flops 384000000 | bytes 6291456 | tf_op jit(solution)/shard_map/pallas_call | solution.py:289
  31.0 2.3 %collective-permute-start.5 = (s16[208,256]{1,0:T(8,128)(2,1)}, s16[208,256]{1,0:T(8,128)(2,1)S(1)}, u32[]{:S(2)}, u32[]{:S(2)}) collective-permute-start(s16[208,256]{1,0:T(8,128)(2,1)} %get-tuple-element.55), channel_id=1, source_target_pairs={{0,4},{4,0},{8,12},{12,8},{1,5},{5,1},{9,13},{13,9},{2,6},{6,2},{1... | collective-permute-start | bytes 319496 | tf_op jit(solution)/shard_map/ppermute | solution.py:139
  33.3 2.7 %collective-permute-start.6 = (s16[208,256]{1,0:T(8,128)(2,1)}, s16[208,256]{1,0:T(8,128)(2,1)S(1)}, u32[]{:S(2)}, u32[]{:S(2)}) collective-permute-start(s16[208,256]{1,0:T(8,128)(2,1)} %get-tuple-element.57), channel_id=1, source_target_pairs={{0,8},{4,12},{8,0},{12,4},{1,9},{5,13},{9,1},{13,5},{2,10},{6,14},... | collective-permute-start | bytes 319496 | tf_op jit(solution)/shard_map/ppermute | solution.py:139
  36.0 1.2 %shard_map.149 = (f32[832,128]{1,0:T(8,128)S(1)}, f32[832,128]{1,0:T(8,128)S(1)}, f32[26,128]{1,0:T(8,128)S(1)}, f32[4,104,128]{2,1,0:T(8,128)S(1)}) custom-call(f32[1,128]{1,0:T(1,128)S(1)} %copy-done.6, f32[3,104,128]{2,1,0:T(8,128)S(1)} %copy-done.1, f32[400,128]{1,0:T(8,128)S(1)} %copy-done.2), custom_call_target="tpu_custom_call" | custom-call | tf_op jit(solution)/shard_map/pallas_call | solution.py:431
  37.3 0.9 %copy-done.3 = s16[208,256]{1,0:T(8,128)(2,1)S(1)} copy-done((s16[208,256]{1,0:T(8,128)(2,1)S(1)}, s16[208,256]{1,0:T(8,128)(2,1)}, u32[]{:S(2)}) %copy-start.3) | copy-done | bytes 106520
  38.2 1.4 %shard_map.150.rest_6_ = f32[832,256]{1,0:T(8,128)S(1)} custom-call(s32[4]{0:T(128)S(1)} %copy-done.5, bf16[4,2,832,208]{3,2,1,0:T(8,128)(2,1)S(1)} %copy-done, s16[208,256]{1,0:T(8,128)(2,1)S(1)} %copy-done.3, s16[208,256]{1,0:T(8,128)(2,1)S(1)} %collective-permute-done.5.rest_1_), custom_call_target="tpu_custom_call" | custom-call | flops 511180800 | bytes 4194304 | tf_op jit(solution)/shard_map/pallas_call | solution.py:466
  39.6 5.2 %collective-permute-done.6.rest_9_ = s16[208,256]{1,0:T(8,128)(2,1)S(1)} collective-permute-done((s16[208,256]{1,0:T(8,128)(2,1)}, s16[208,256]{1,0:T(8,128)(2,1)S(1)}, u32[]{:S(2)}, u32[]{:S(2)}) %collective-permute-start.6) | collective-permute-done | bytes 106528 | tf_op jit(solution)/shard_map/ppermute | solution.py:139
  44.8 11.9 %shard_map.151 = f32[100,2,400]{2,1,0:T(2,128)} custom-call(s32[4]{0:T(128)S(1)} %copy-done.5, bf16[4,2,832,208]{3,2,1,0:T(8,128)(2,1)S(1)} %copy-done, f32[3,104,128]{2,1,0:T(8,128)S(1)} %copy-done.1, f32[832,128]{1,0:T(8,128)S(1)} %get-tuple-element.50.rest_2_, f32[832,128]{1,0:T(8,128)S(1)} %get-tuple-element.51.rest_3_, ...), custom_call_target="tpu_custom_call" | custom-call | flops 37273600 | bytes 6291456 | tf_op jit(solution)/shard_map/pallas_call | solution.py:589
  (20 shorter events, 0.0 us)
Async XLA Ops:
  0.8 7.5 %collective-permute-start.1 = (bf16[4,1,400]{2,1,0:T(2,128)(2,1)S(1)}, bf16[4,1,400]{2,1,0:T(2,128)(2,1)S(1)}, u32[]{:S(2)}, u32[]{:S(2)}) collective-permute-start(bf16[4,1,400]{2,1,0:T(2,128)(2,1)S(1)} %get-tuple-element.59), channel_id=1, source_target_pairs={{4,0},{8,4},{12,8},{5,1},{9,5},{13,9},{6,2},{10,6},{14,10},{7,3},{... | collective-permute-start | bytes 9608 | tf_op jit(solution)/shard_map/ppermute | solution.py:620
  2.1 6.9 %collective-permute-start = (bf16[4,1,400]{2,1,0:T(2,128)(2,1)S(1)}, bf16[4,1,400]{2,1,0:T(2,128)(2,1)S(1)}, u32[]{:S(2)}, u32[]{:S(2)}) collective-permute-start(bf16[4,1,400]{2,1,0:T(2,128)(2,1)S(1)} %get-tuple-element.60), channel_id=1, source_target_pairs={{0,4},{4,8},{8,12},{1,5},{5,9},{9,13},{2,6},{6,10},{10,14},{3,7},{... | collective-permute-start | bytes 9608 | tf_op jit(solution)/shard_map/ppermute | solution.py:619
  8.3 0.8 %copy-start.7 = (bf16[4,1,400]{2,1,0:T(2,128)(2,1)}, bf16[4,1,400]{2,1,0:T(2,128)(2,1)S(1)}, u32[]{:S(2)}) copy-start(bf16[4,1,400]{2,1,0:T(2,128)(2,1)S(1)} %collective-permute-done.1.below_ref) | copy-start | bytes 9604
  9.0 0.6 %copy-start.8 = (bf16[4,1,400]{2,1,0:T(2,128)(2,1)}, bf16[4,1,400]{2,1,0:T(2,128)(2,1)S(1)}, u32[]{:S(2)}) copy-start(bf16[4,1,400]{2,1,0:T(2,128)(2,1)S(1)} %collective-permute-done.above_ref) | copy-start | bytes 9604
  13.6 11.2 %collective-permute-start.3 = (s16[200,512]{1,0:T(8,128)(2,1)}, s16[200,512]{1,0:T(8,128)(2,1)}, u32[]{:S(2)}, u32[]{:S(2)}) collective-permute-start(s16[200,512]{1,0:T(8,128)(2,1)} %get-tuple-element.36), channel_id=1, source_target_pairs={{0,2},{1,3},{2,0},{3,1},{4,6},{5,7},{6,4},{7,5},{8,10},{9,11},{10,... | collective-permute-start | bytes 614408 | tf_op jit(solution)/shard_map/ppermute | solution.py:139
  15.6 9.2 %collective-permute-start.4 = (s16[200,512]{1,0:T(8,128)(2,1)}, s16[200,512]{1,0:T(8,128)(2,1)}, u32[]{:S(2)}, u32[]{:S(2)}) collective-permute-start(s16[200,512]{1,0:T(8,128)(2,1)} %get-tuple-element.37), channel_id=1, source_target_pairs={{0,3},{1,2},{2,1},{3,0},{4,7},{5,6},{6,5},{7,4},{8,11},{9,10},{10,... | collective-permute-start | bytes 614408 | tf_op jit(solution)/shard_map/ppermute | solution.py:139
  19.7 17.6 %copy-start = (bf16[4,2,832,208]{3,2,1,0:T(8,128)(2,1)S(1)}, bf16[4,2,832,208]{3,2,1,0:T(8,128)(2,1)}, u32[]{:S(2)}) copy-start(bf16[4,2,832,208]{3,2,1,0:T(8,128)(2,1)} %constant.39.clone.table_ref.rest_0_) | copy-start | bytes 8306692
  19.7 5.2 %collective-permute-start.2 = (s16[200,512]{1,0:T(8,128)(2,1)}, s16[200,512]{1,0:T(8,128)(2,1)}, u32[]{:S(2)}, u32[]{:S(2)}) collective-permute-start(s16[200,512]{1,0:T(8,128)(2,1)} %get-tuple-element.35), channel_id=1, source_target_pairs={{0,1},{1,0},{2,3},{3,2},{4,5},{5,4},{6,7},{7,6},{8,9},{9,8},{10,11... | collective-permute-start | bytes 614408 | tf_op jit(solution)/shard_map/ppermute | solution.py:139
  20.0 16.1 %copy-start.1 = (f32[3,104,128]{2,1,0:T(8,128)S(1)}, f32[3,104,128]{2,1,0:T(8,128)}, u32[]{:S(2)}) copy-start(f32[3,104,128]{2,1,0:T(8,128)} %constant.37.clone.lat_ref.rest_1_) | copy-start | bytes 479236
  20.0 16.1 %copy-start.2 = (f32[400,128]{1,0:T(8,128)S(1)}, f32[400,128]{1,0:T(8,128)}, u32[]{:S(2)}) copy-start(f32[400,128]{1,0:T(8,128)} %constant.38.clone.term_ref) | copy-start | bytes 614404
  20.5 16.8 %copy-start.5 = (s32[4]{0:T(128)S(1)}, s32[4]{0:T(128)}, u32[]{:S(2)}) copy-start(s32[4]{0:T(128)} %iota_xor_fusion.1.order_ref) | copy-start | bytes 52
  24.8 11.2 %copy-start.6 = (f32[1,128]{1,0:T(1,128)S(1)}, f32[1,128]{1,0:T(1,128)}, u32[]{:S(2)}) copy-start(f32[1,128]{1,0:T(1,128)} %get-tuple-element.49.mine_ref.rest_7_) | copy-start | bytes 1540
  31.0 13.8 %copy-start.4 = (bf16[128,128]{1,0:T(8,128)(2,1)S(1)}, bf16[128,128]{1,0:T(8,128)(2,1)}, u32[]{:S(2)}) copy-start(bf16[128,128]{1,0:T(8,128)(2,1)} %get-tuple-element.56.rest_8_) | copy-start | bytes 98308
  31.0 6.3 %collective-permute-start.5 = (s16[208,256]{1,0:T(8,128)(2,1)}, s16[208,256]{1,0:T(8,128)(2,1)S(1)}, u32[]{:S(2)}, u32[]{:S(2)}) collective-permute-start(s16[208,256]{1,0:T(8,128)(2,1)} %get-tuple-element.55), channel_id=1, source_target_pairs={{0,4},{4,0},{8,12},{12,8},{1,5},{5,1},{9,13},{13,9},{2,6},{6,2},{1... | collective-permute-start | bytes 319496 | tf_op jit(solution)/shard_map/ppermute | solution.py:139
  33.3 11.5 %collective-permute-start.6 = (s16[208,256]{1,0:T(8,128)(2,1)}, s16[208,256]{1,0:T(8,128)(2,1)S(1)}, u32[]{:S(2)}, u32[]{:S(2)}) collective-permute-start(s16[208,256]{1,0:T(8,128)(2,1)} %get-tuple-element.57), channel_id=1, source_target_pairs={{0,8},{4,12},{8,0},{12,4},{1,9},{5,13},{9,1},{13,5},{2,10},{6,14},... | collective-permute-start | bytes 319496 | tf_op jit(solution)/shard_map/ppermute | solution.py:139
  36.0 8.8 %collective-permute-start.7 = (s16[208,256]{1,0:T(8,128)(2,1)}, s16[208,256]{1,0:T(8,128)(2,1)S(1)}, u32[]{:S(2)}, u32[]{:S(2)}) collective-permute-start(s16[208,256]{1,0:T(8,128)(2,1)} %get-tuple-element.58), channel_id=1, source_target_pairs={{0,12},{4,8},{8,4},{12,0},{1,13},{5,9},{9,5},{13,1},{2,14},{6,10},... | collective-permute-start | bytes 319496 | tf_op jit(solution)/shard_map/ppermute | solution.py:139
  37.3 0.9 %copy-start.3 = (s16[208,256]{1,0:T(8,128)(2,1)S(1)}, s16[208,256]{1,0:T(8,128)(2,1)}, u32[]{:S(2)}) copy-start(s16[208,256]{1,0:T(8,128)(2,1)} %get-tuple-element.54.rest_0_) | copy-start | bytes 319492

commit v9 on v8

--- a/solution.py
+++ b/solution.py
@@ -46,33 +46,27 @@
         angles = 2.0 * math.pi / NLON * (spots * waves[None, :] % NLON)
         return factor * np.cos(angles), factor * np.sin(angles)
 
+    def shaped(columns):
+        pad = [(0, 0), (0, -columns[0].shape[1] % LANES)]
+        table = np.concatenate([np.pad(part, pad) for part in columns], axis=1)
+        return table.reshape(share, quarter // share, -1)
+
+    share = pieces // 4
     tables = []
     for first in (0, 2):
         cosine, sine = parts(np.arange(first, M, 4))
-        tables.append([cosine, -sine])
+        tables.append(shaped([cosine, -sine]))
     waves = np.arange(1, M, 2)
     sign = np.where(waves % 4 == 1, 1.0, -1.0)[None, :]
     cosine, sine = parts(waves)
-    tables.append([cosine, -sine])
-    tables.append([-sign * sine, -sign * cosine])
-    share = pieces // 4
-    result = []
-    for columns in tables:
-        table = np.concatenate(columns, axis=1)
-        table = np.pad(table, ((0, 0), (0, -table.shape[1] % (2 * LANES))))
-        result.append(table.reshape(share, quarter // share, table.shape[1]))
-    return result
+    return [*tables, shaped([cosine, -sine]), shaped([-sign * sine, -sign * cosine])]
 
 
 def column_waves():
-    width = -(-M // 2 // (2 * LANES)) * 2 * LANES
-    spots = np.full(4 * width, -1.0, np.float32)
-    waves = np.arange(M)
-    for part in range(2):
-        even = np.where(waves % 4 == 0, 0, width) + part * (M // 4) + waves // 4
-        odd = 2 * width + part * (M // 2) + waves // 2
-        spots[np.where(waves % 2 == 0, even, odd)] = 2 * waves + part
-    return spots[:, None]
+    columns = []
+    for waves in (np.arange(0, M, 4), np.arange(2, M, 4), np.arange(1, M, 2)):
+        columns.append(np.pad(waves, (0, -len(waves) % LANES), constant_values=-1))
+    return np.concatenate(columns).astype(np.float32)[:, None]
 
 
 def resample_table():
@@ -125,10 +119,14 @@
     return codes.astype(jnp.int32).astype(jnp.float32)
 
 
-def partners(axis):
-    count = lax.axis_size(axis)
-    order = jnp.arange(count, dtype=jnp.int32)
-    return lax.axis_index(axis).astype(jnp.int32) ^ order if count == 4 else order
+def partner(axes, sizes, step):
+    count = math.prod(sizes)
+    if count != 4:
+        return step
+    index = lax.axis_index(axes[0])
+    for axis, size in zip(axes[1:], sizes[1:]):
+        index = index * size + lax.axis_index(axis)
+    return index ^ step
 
 
 def exchange(blocks, axis):
@@ -139,15 +137,15 @@
     return [blocks[0]] + [lax.ppermute(blocks[step], axis, pairs[step]) for step in range(1, count)]
 
 
-def advect_kernel(steps, order_ref, tracer_hbm, east_hbm, north_hbm, above_ref, below_ref, *rest):
-    _, rows, lons = tracer_hbm.shape
-    outs, (tracer, east_wind, north_wind, sems) = rest[: len(steps)], rest[len(steps) :]
+def advect_kernel(ring, lat_count, tracer_hbm, east_hbm, north_hbm, *rest):
+    levels, rows, lons = tracer_hbm.shape
+    outs, (edge_ref, tracer, east_wind, north_wind, sems) = rest[:levels], rest[levels:]
+    chosen = [partner(*ring, step) for step in range(levels)]
     copies = []
-    for spot, step in enumerate(steps):
-        level = order_ref[step]
+    for step, level in enumerate(chosen):
         copies.append(
             [
-                pltpu.make_async_copy(source.at[level], target.at[spot], sems.at[spot, kind])
+                pltpu.make_async_copy(source.at[level], target.at[step], sems.at[step, kind])
                 for kind, (source, target) in enumerate(
                     ((tracer_hbm, tracer), (east_hbm, east_wind), (north_hbm, north_wind))
                 )
@@ -155,21 +153,33 @@
         )
         for copy in copies[-1]:
             copy.start()
+    padded_rows = outs[0].shape[0]
     end = (lons - 1) // LANES * LANES
     spare = lons - end
     lane = lax.broadcasted_iota(jnp.int32, (rows, LANES), 1)
-    for spot, step in enumerate(steps):
-        level = order_ref[step]
-        for copy in copies[spot]:
+    lat_index = lax.axis_index("lat")
+    edge_ref[...] = jnp.zeros_like(edge_ref)
+    for step, level in enumerate(chosen):
+        for copy in copies[step]:
             copy.wait()
-        field = tracer[spot].astype(jnp.float32)
+        field = tracer[step].astype(jnp.float32)
+
+        @pl.when(lat_index < lat_count - 1)
+        def _():
+            edge_ref[(lat_index + 1) * levels + level] = field[rows - 1 :]
+
+        @pl.when(lat_index > 0)
+        def _():
+            edge_ref[(lat_index - 1) * levels + level] = field[:1]
+
         blank = jnp.zeros((rows, 1), jnp.float32)
         west = jnp.concatenate([blank, field[:, :-1]], axis=1)
         east = jnp.concatenate([field[:, 1:], blank], axis=1)
-        north = jnp.concatenate([above_ref[level].astype(jnp.float32), field[:-1]], axis=0)
-        south = jnp.concatenate([field[1:], below_ref[level].astype(jnp.float32)], axis=0)
-        eastward = 0.5 * east_wind[spot].astype(jnp.float32)
-        northward = 0.5 * north_wind[spot].astype(jnp.float32)
+        blank = jnp.zeros((1, lons), jnp.float32)
+        north = jnp.concatenate([blank, field[:-1]], axis=0)
+        south = jnp.concatenate([field[1:], blank], axis=0)
+        eastward = 0.5 * east_wind[step].astype(jnp.float32)
+        northward = 0.5 * north_wind[step].astype(jnp.float32)
         moved = field - eastward * (east - west) - northward * (south - north)
         first, last = field[:, :1], field[:, lons - 1 :]
         biggest = jnp.max(jnp.abs(moved), axis=1, keepdims=True)
@@ -184,32 +194,41 @@
         winds = jnp.where(lane == spare + 3, eastward[:, :1], eastward[:, lons - 1 :])
         winds = coded(winds, 1.0 / WIND_STEP)
         tile = jnp.where((lane == spare + 3) | (lane == spare + 4), winds, tile)
-        outs[spot][:, :end] = as_int16(coded(moved[:, :end], inverse))
-        outs[spot][:, end:] = as_int16(tile)
-
-
-def advect(tracer, east_wind, north_wind, above, below, order, steps):
+        wind_rows = jnp.concatenate([northward[:1], northward[rows - 1 :]], axis=0)
+        wind_rows = coded(wind_rows, 1.0 / WIND_STEP)
+        blank = jnp.zeros((padded_rows - rows - 2, lons), jnp.float32)
+        wind_rows = jnp.concatenate([wind_rows, blank], axis=0)
+        filler = jnp.zeros((padded_rows - rows, LANES - spare), jnp.float32)
+        wind_tile = jnp.concatenate([wind_rows[:, end:], filler], axis=1)
+        steps = jnp.concatenate([coded(moved[:, :end], inverse), wind_rows[:, :end]], axis=0)
+        outs[step][:, :end] = as_int16(steps)
+        outs[step][:, end:] = as_int16(jnp.concatenate([tile, wind_tile], axis=0))
+
+
+def advect(tracer, east_wind, north_wind, ring):
     levels, rows, lons = tracer.shape
+    lat_count = lax.axis_size("lat")
     width = (lons - 1) // LANES * LANES + LANES
-    count = len(steps)
-    held = pltpu.VMEM((count, rows, lons), jnp.bfloat16)
-    return pl.pallas_call(
-        functools.partial(advect_kernel, steps),
-        out_shape=[jax.ShapeDtypeStruct((rows, width), jnp.int16)] * count,
-        in_specs=[SMEM_SPEC] + [HBM_SPEC] * 3 + [VMEM_SPEC] * 2,
-        out_specs=[VMEM_SPEC] * count,
-        scratch_shapes=[held, held, held, pltpu.SemaphoreType.DMA((count, 3))],
+    padded_rows = -(-(rows + 2) // 16) * 16
+    held = pltpu.VMEM((levels, rows, lons), jnp.bfloat16)
+    result = pl.pallas_call(
+        functools.partial(advect_kernel, ring, lat_count),
+        out_shape=[jax.ShapeDtypeStruct((padded_rows, width), jnp.int16)] * levels
+        + [jax.ShapeDtypeStruct((lat_count * levels, 1, lons), jnp.float32)],
+        in_specs=[HBM_SPEC] * 3,
+        out_specs=[VMEM_SPEC] * (levels + 1),
+        scratch_shapes=[held, held, held, pltpu.SemaphoreType.DMA((levels, 3))],
         compiler_params=pltpu.CompilerParams(vmem_limit_bytes=VMEM_BYTES),
         cost_estimate=pl.CostEstimate(
-            flops=20 * count * rows * lons, bytes_accessed=8 * count * rows * lons, transcendentals=0
+            flops=20 * levels * rows * lons, bytes_accessed=8 * levels * rows * lons, transcendentals=0
         ),
-    )(order, tracer, east_wind, north_wind, above, below)
-
-
-def fourier_kernel(pieces, targets, order_ref, *rest):
-    grids, rest = rest[:pieces], rest[pieces:]
-    tables_hbm, (wave_ref, keep_ref, sine_ref), rest = rest[:5], rest[5:8], rest[8:]
-    outs, rest = rest[:targets], rest[targets:]
+    )(tracer, east_wind, north_wind)
+    return list(result[:levels]), result[levels]
+
+
+def fourier_kernel(ring, lat_count, pieces, *rest):
+    grids, (edge_ref, *tables_hbm, wave_ref, keep_ref, sine_ref) = rest[:pieces], rest[pieces : pieces + 9]
+    outs, rest = rest[pieces + 9 :][:lat_count], rest[pieces + 9 + lat_count :]
     tables, place_ref, (field, sems) = rest[:4], rest[4], rest[5:]
     _, rows, width = field.shape
     lons = tables[0].shape[1]
@@ -223,13 +242,26 @@
     spare = lons - end
     lane = lax.broadcasted_iota(jnp.int32, (rows, LANES), 1)
     winds = (lane == spare + 3) | (lane == spare + 4)
+    lat_index = lax.axis_index("lat")
     for piece in range(pieces):
-        spot = order_ref[piece]
+        spot = partner(*ring, piece)
         values = from_int16(grids[piece][...])
-        tile = values[:, end:]
+        tile = values[:rows, end:]
         scale = scale_of(tile[:, spare : spare + 1])
-        field[spot, :, :end] = values[:, :end] * scale
+        field[spot, :, :end] = values[:rows, :end] * scale
         field[spot, :, end:] = tile * jnp.where(winds, WIND_STEP, scale)
+        wind_rows = values[rows : rows + 2, :lons] * WIND_STEP
+
+        @pl.when(lat_index > 0)
+        def _():
+            above = edge_ref[(lat_index - 1) * pieces + spot]
+            field[spot, :1, :lons] += wind_rows[:1] * above
+
+        @pl.when(lat_index < lat_count - 1)
+        def _():
+            below = edge_ref[(lat_index + 1) * pieces + spot]
+            field[spot, rows - 1 :, :lons] -= wind_rows[1:] * below
+
     for spot in range(pieces):
         tile = field[spot, :, end:]
         before = field[(spot - 1) % pieces, :, end:]
@@ -259,38 +291,38 @@
             parts.append(product(value, tables[kind], spot))
         parts = [parts[0], parts[1], parts[2] + parts[3]]
         sums = [part if total is None else total + part for total, part in zip(sums, parts)]
-    placed = None
-    first = 0
     copies[4].wait()
-    for total in sums:
-        last = first + total.shape[1]
-        high, low = split_bf16(total)
-        part = jnp.dot(high, place_ref[first:last], preferred_element_type=jnp.float32)
-        part += jnp.dot(low, place_ref[first:last], preferred_element_type=jnp.float32)
-        placed = part if placed is None else placed + part
-        first = last
-    kept = jnp.where(wave_ref[...] < keep_ref[...], placed * sine_ref[...], 0.0)
-    code = scale_code(jnp.max(jnp.abs(kept), axis=0, keepdims=True))
-    steps = coded(kept, 1.0 / scale_of(code))
-    padded_rows, span = outs[0].shape
-    codes = jnp.broadcast_to(code, (padded_rows - rows, code.shape[1]))
-    result = as_int16(jnp.concatenate([steps, codes], axis=0))
-    for target in range(targets):
-        outs[target][...] = result[:, target * span : (target + 1) * span]
-
-
-def fourier(grids, order, places, wave_row, keep_col, sine_col, targets):
+    placed = []
+    for part in range(2):
+        columns = []
+        for total in sums:
+            half = total.shape[1] // 2
+            columns.append(total[:, part * half : (part + 1) * half])
+        high, low = split_bf16(jnp.concatenate(columns, axis=1))
+        value = jnp.dot(high, place_ref[...], preferred_element_type=jnp.float32)
+        value += jnp.dot(low, place_ref[...], preferred_element_type=jnp.float32)
+        kept = jnp.where(wave_ref[...] < keep_ref[...], value * sine_ref[...], 0.0)
+        code = scale_code(jnp.max(jnp.abs(kept), axis=0, keepdims=True))
+        steps = coded(kept, 1.0 / scale_of(code))
+        codes = jnp.broadcast_to(code, (outs[0].shape[0] - rows, code.shape[1]))
+        placed.append(as_int16(jnp.concatenate([steps, codes], axis=0)))
+    for target in range(lat_count):
+        for part in range(2):
+            cols = slice(target * LANES, (target + 1) * LANES)
+            outs[target][:, part * LANES : (part + 1) * LANES] = placed[part][:, cols]
+
+
+def fourier(grids, edges, ring, places, wave_row, keep_col, sine_col, lat_count):
     pieces = len(grids)
-    rows, width = grids[0].shape
-    lons = NLON // pieces
-    span = wave_row.shape[1] // targets
+    rows = keep_col.shape[0]
+    width = grids[0].shape[1]
     padded_rows = -(-(rows + 1) // 16) * 16
     tables = [table_bf16(table) for table in fourier_tables(pieces)]
     return pl.pallas_call(
-        functools.partial(fourier_kernel, pieces, targets),
-        out_shape=[jax.ShapeDtypeStruct((padded_rows, span), jnp.int16)] * targets,
-        in_specs=[SMEM_SPEC] + [VMEM_SPEC] * pieces + [HBM_SPEC] * 5 + [VMEM_SPEC] * 3,
-        out_specs=[VMEM_SPEC] * targets,
+        functools.partial(fourier_kernel, ring, lat_count, pieces),
+        out_shape=[jax.ShapeDtypeStruct((padded_rows, 2 * LANES), jnp.int16)] * lat_count,
+        in_specs=[VMEM_SPEC] * (pieces + 1) + [HBM_SPEC] * 5 + [VMEM_SPEC] * 3,
+        out_specs=[VMEM_SPEC] * lat_count,
         scratch_shapes=[pltpu.VMEM(table.shape, jnp.bfloat16) for table in tables]
         + [pltpu.VMEM(places.shape, jnp.bfloat16)]
         + [pltpu.VMEM((pieces, rows, width), jnp.float32), pltpu.SemaphoreType.DMA((5,))],
@@ -298,14 +330,15 @@
         cost_estimate=pl.CostEstimate(
             flops=3 * rows * NLON * M, bytes_accessed=6 * 2**20, transcendentals=0
         ),
-    )(order, *grids, *tables, places, wave_row, keep_col, sine_col)
+    )(*grids, edges, *tables, places, wave_row, keep_col, sine_col)
 
 
 def places_kernel(
-    order_ref, lat_ref, slot_ref, keep_ref, sine_ref, spot_ref,
+    slot_ref, keep_ref, sine_ref, spot_ref,
     place_ref, wave_ref, mine_ref, back_ref, keep_col, sine_col, sorted_rows,
 ):
     groups, _, rows = sine_ref.shape
+    lat_index = lax.axis_index("lat")
     slots = slot_ref.shape[1] // groups
     paired = (slots + 1) // 2
     shape = (LANES, LANES)
@@ -326,33 +359,31 @@
         values = jnp.where(filled > 0.5, values, 2.0 * M)
         sorted_rows[group] = jnp.broadcast_to(values, sorted_rows.shape[1:])
 
-        @pl.when(group == lat_ref[0])
+        @pl.when(group == lat_index)
         def _():
             mine_ref[...] = values
             back_ref[...] = hot.astype(jnp.bfloat16)
 
-    spots = spot_ref[...]
+    spots = jnp.broadcast_to(spot_ref[...], (spot_ref.shape[0], LANES))
     for step in range(groups):
-        row = sorted_rows[order_ref[step], :1]
-        for part in range(2):
-            cols = slice((2 * step + part) * LANES, (2 * step + part + 1) * LANES)
-            wave_ref[:, cols] = row
-            hit = spots == 2.0 * row + part
-            place_ref[:, cols] = jnp.where(hit, 1.0, 0.0).astype(jnp.bfloat16)
+        row = sorted_rows[partner(("lat",), (groups,), step), :1]
+        cols = slice(step * LANES, (step + 1) * LANES)
+        wave_ref[:, cols] = row
+        place_ref[:, cols] = jnp.where(spots == row, 1.0, 0.0).astype(jnp.bfloat16)
 
     shape = (rows, rows)
     same = lax.broadcasted_iota(jnp.int32, shape, 0) == lax.broadcasted_iota(jnp.int32, shape, 1)
     kept = jnp.broadcast_to(keep_ref[...].astype(jnp.float32), shape)
     keep_col[...] = jnp.sum(jnp.where(same, kept, 0.0), axis=1, keepdims=True)
-    sine = jnp.broadcast_to(sine_ref[lat_ref[0]], shape)
+    sine = jnp.broadcast_to(sine_ref[lat_index], shape)
     sine_col[...] = jnp.sum(jnp.where(same, sine, 0.0), axis=1, keepdims=True)
 
 
-def prepare_places(order, lat_index, slot_wave, keep_m, groups):
+def prepare_places(slot_wave, keep_m, groups):
     rows = keep_m.shape[0]
     sines = np.sin(math.pi / NLAT * (np.arange(NLAT) + 0.5)) * math.sqrt(2.0 / NLAT)
     spots = column_waves()
-    width = 2 * groups * LANES
+    width = groups * LANES
     return pl.pallas_call(
         places_kernel,
         out_shape=[
@@ -363,12 +394,12 @@
             jax.ShapeDtypeStruct((rows, 1), jnp.float32),
             jax.ShapeDtypeStruct((rows, 1), jnp.float32),
         ],
-        in_specs=[SMEM_SPEC] * 2 + [VMEM_SPEC] * 4,
+        in_specs=[VMEM_SPEC] * 4,
         out_specs=[VMEM_SPEC] * 6,
         scratch_shapes=[pltpu.VMEM((groups, 8, LANES), jnp.float32)],
         compiler_params=pltpu.CompilerParams(vmem_limit_bytes=VMEM_BYTES),
     )(
-        order, lat_index[None], slot_wave[None], keep_m[None],
+        slot_wave[None], keep_m[None],
         sines.reshape(groups, 1, rows).astype(np.float32), spots,
     )
 
@@ -442,12 +473,12 @@
     )(mine, latitudes, terms)
 
 
-def resampled(first, order_ref, fields, table, total):
+def resampled(first, fields, table, total):
     for piece, field in enumerate(fields):
         values = from_int16(field[...])
         values = values * scale_of(values[field.shape[0] - 1 :])
         high, low = split_bf16(values)
-        spot = order_ref[first + piece]
+        spot = partner(("lat",), table.shape[:1], first + piece)
         both = jnp.concatenate([high, low], axis=1)
         part = jnp.dot(table[spot, 0], both, preferred_element_type=jnp.float32)
         part = part[:, : high.shape[1]] + part[:, high.shape[1] :]
@@ -456,26 +487,26 @@
     return total
 
 
-def resample_kernel(order_ref, table_ref, *rest):
-    rest[-1][...] = resampled(0, order_ref, rest[:-1], table_ref, None)
-
-
-def resample(fields, order, table):
+def resample_kernel(table_ref, *rest):
+    rest[-1][...] = resampled(0, rest[:-1], table_ref, None)
+
+
+def resample(fields, table):
     count, _, height, _ = table.shape
     span = fields[0].shape[1]
     return pl.pallas_call(
         resample_kernel,
         out_shape=jax.ShapeDtypeStruct((height, span), jnp.float32),
-        in_specs=[SMEM_SPEC] + [VMEM_SPEC] * (1 + len(fields)),
+        in_specs=[VMEM_SPEC] * (1 + len(fields)),
         out_specs=VMEM_SPEC,
         compiler_params=pltpu.CompilerParams(vmem_limit_bytes=LATE_BYTES),
         cost_estimate=pl.CostEstimate(
             flops=6 * height * span * NLAT // count * len(fields), bytes_accessed=4 * 2**20, transcendentals=0
         ),
-    )(order, table, *fields)
-
-
-def legendre_kernel(early, order_ref, *rest):
+    )(table, *fields)
+
+
+def legendre_kernel(early, *rest):
     table, lat_ref, beta_ref, scale_ref, growth_ref, start_ref, total_ref, mine_ref, back_ref = rest[:9]
     fields, rest = rest[9:-8], rest[-8:]
     out_ref, weights, before, current, level, sums, result, final = rest
@@ -487,7 +518,7 @@
     turn = block_count(pair[0][:1])
     block_total = jnp.max(turn + block_count(pair[1][:1])).astype(jnp.int32)
 
-    total = resampled(early, order_ref, fields, table, total_ref[...])
+    total = resampled(early, fields, table, total_ref[...])
     totals = [total[2 * points * kind : 2 * points * (kind + 1)] for kind in range(4)]
     left = lax.broadcasted_iota(jnp.int32, (points, LANES), 1) < SIDE
     for parity in range(2):
@@ -577,19 +608,19 @@
     return table.reshape(pieces, full.shape[0], 2, padded_rows).transpose(0, 2, 1, 3)
 
 
-def legendre(fields, order, mine, back, prepared, rows, slots):
+def legendre(fields, mine, back, prepared, rows, slots):
     pieces = len(fields)
     early = pieces // 2
     latitudes = latitude_table()
     points = latitudes.shape[1]
     table = jnp.asarray(resample_pieces(pieces, rows, fields[0].shape[0]))
-    total = resample(fields[:early], order, table)
+    total = resample(fields[:early], table)
     vector = pltpu.VMEM((points, LANES), jnp.float32)
     block_rows = -(-M // BLOCK) * BLOCK
     return pl.pallas_call(
         functools.partial(legendre_kernel, early),
         out_shape=jax.ShapeDtypeStruct((slots, 2, M), jnp.float32),
-        in_specs=[SMEM_SPEC] + [VMEM_SPEC] * (9 + pieces - early),
+        in_specs=[VMEM_SPEC] * (9 + pieces - early),
         out_specs=VMEM_SPEC,
         scratch_shapes=[
             pltpu.VMEM((2, 4, points, LANES), jnp.float32),
@@ -604,36 +635,26 @@
         cost_estimate=pl.CostEstimate(
             flops=7 * points * LANES * M, bytes_accessed=6 * 2**20, transcendentals=0
         ),
-    )(order, table, latitudes, *prepared, total, mine, back, *fields[early:])
+    )(table, latitudes, *prepared, total, mine, back, *fields[early:])
 
 
 def shards(tracer, wind_east, wind_north, keep_m, slot_wave):
     rows = tracer.shape[1]
     lat_count = lax.axis_size("lat")
     slots = slot_wave.shape[0] // lat_count
-    lat_index = lax.axis_index("lat").astype(jnp.int32)
-    ring = ("lev", "fld")
-    level_order, lat_order = partners(ring), partners("lat")
-
-    count = lax.axis_size("lat")
-    above = lax.ppermute(tracer[:, rows - 1 :], "lat", [(i, i + 1) for i in range(count - 1)])
-    below = lax.ppermute(tracer[:, :1], "lat", [(i + 1, i) for i in range(count - 1)])
-    fields = (tracer, wind_east, wind_north, above, below, level_order)
-    levels = tracer.shape[0]
-    far = advect(*fields, tuple(range(levels // 2, levels)))
-    near = advect(*fields, tuple(range(levels // 2)))
-    near, slot_wave, keep_m = lax.optimization_barrier((list(near), slot_wave, keep_m))
-    grids = exchange([*near, *far], ring)
-    places, wave_row, mine, back, keep_col, sine_col = prepare_places(
-        lat_order, lat_index, slot_wave, keep_m, lat_count
-    )
-    waved = fourier(
-        grids, level_order, places, wave_row, keep_col, sine_col, lat_count
-    )
+    axes = ("lev", "fld")
+    ring = (axes, tuple(lax.axis_size(axis) for axis in axes))
+
+    blocks, edges = advect(tracer, wind_east, wind_north, ring)
+    blocks, slot_wave, keep_m = lax.optimization_barrier((blocks, slot_wave, keep_m))
+    grids = exchange(blocks, axes)
+    edges = lax.all_to_all(edges, ("lat", *axes), split_axis=0, concat_axis=0, tiled=True)
+    places, wave_row, mine, back, keep_col, sine_col = prepare_places(slot_wave, keep_m, lat_count)
+    waved = fourier(grids, edges, ring, places, wave_row, keep_col, sine_col, lat_count)
     waved, mine = lax.optimization_barrier((list(waved), mine))
     fields = exchange(waved, "lat")
     prepared = prepare_recurrence(mine)
-    return legendre(fields, lat_order, mine, back, prepared, rows, slots)[None]
+    return legendre(fields, mine, back, prepared, rows, slots)[None]
 
 
 def solution(mesh):

time: 57 us -> 50.9 us (0.89); the launches traced: 56.7 us -> 51.2 us
  Pallas kernels: 32.9 us -> 27.9 us
  waiting for transfers between devices: 5.98 us -> 7.97 us
  other arithmetic: 1.15 us -> 0 us
  local copies, waits for them, and re-layouts: 2.3 us -> 1.49 us
    ppermute x2 -> x0, starting transfers between devices: 6.85 us -> none  [the longest x1 5.56 us: shards(): lax.ppermute(tracer[:, rows - 1:], 'lat', [(i, i + 1) for i in range(coun...]
    all_to_all x0 -> x1, starting transfers between devices: none -> 6.15 us  [shards(): lax.all_to_all(edges, ('lat', *axes), split_axis=0, concat_axis=0, tiled=...]
    all_to_all x0 -> x1, waiting for transfers between devices: none -> 3.57 us  [shards(): lax.all_to_all(edges, ('lat', *axes), split_axis=0, concat_axis=0, tiled=...]
    pallas_call x3 -> x2, Pallas kernels: 14.1 us -> 10.9 us  [the longest x1 5.84 us: fourier(): pl.pallas_call(functools.partial(fourier_kernel, ring, lat_count, pieces)...]
    pallas_call x1, Pallas kernels: 4.32 us -> 3.06 us  [prepare_places(): pl.pallas_call(places_kernel, out_shape=[jax.ShapeDtypeStruct((spots.shap...]
    xor x2 -> x0, other arithmetic: 1.15 us -> none  [partners(): lax.axis_index(axis).astype(jnp.int32) ^ order]
    ppermute x6, waiting for transfers between devices: 5.23 us -> 4.4 us  [exchange(): lax.ppermute(blocks[step], axis, pairs[step])]
    slice x1 -> x0, local copies, waits for them, and re-layouts: 0.79 us -> none  [shards(): tracer[:, :1]]
  transfers between devices with their start and end apart: 8 -> 7, of which waited for: 2 -> 3; matrix products, arithmetic and copies ran while one was open for 2% -> 0% of each run, Pallas kernels for 19% -> 10%
where the time goes in v9:
time: 50.9 us; the launch traced here: 51.2 us
  Pallas kernels  27.9 us (55%)
  starting transfers between devices  13.8 us (27%)
  waiting for transfers between devices  7.97 us (16%)
  local copies, waits for them, and re-layouts  1.49 us (3%)
    pallas_call x1, Pallas kernels, legendre(): pl.pallas_call(functools.partial(legendre_kernel, early), out_shape=jax.S...  11.9 us
    ppermute x6, starting transfers between devices, exchange(): lax.ppermute(blocks[step], axis, pairs[step])  7.6 us
    all_to_all x1, starting transfers between devices, shards(): lax.all_to_all(edges, ('lat', *axes), split_axis=0, concat_axis=0, tiled=...  6.15 us
    pallas_call x1, Pallas kernels, fourier(): pl.pallas_call(functools.partial(fourier_kernel, ring, lat_count, pieces)...  5.84 us
    pallas_call x1, Pallas kernels, advect(): pl.pallas_call(functools.partial(advect_kernel, ring, lat_count), out_sha...  5.09 us
    ppermute x6, waiting for transfers between devices, exchange(): lax.ppermute(blocks[step], axis, pairs[step])  4.4 us
    all_to_all x1, waiting for transfers between devices, shards(): lax.all_to_all(edges, ('lat', *axes), split_axis=0, concat_axis=0, tiled=...  3.57 us
    pallas_call x1, Pallas kernels, prepare_places(): pl.pallas_call(places_kernel, out_shape=[jax.ShapeDtypeStruct((spots.shap...  3.06 us
  transfers between devices with their start and end apart: 7, of which 3 were waited for; matrix products, arithmetic and copies ran while one was open for 0% of the time, Pallas kernels for 10%

profile of v9, /device:TPU:0, one launch (start us, length us, event | category | flops | bytes accessed | tf_op | source)
XLA Modules:
  0.0 51.2 jit_solution(15476662732596660013)
XLA Ops:
  0.0 5.1 %shard_map.145 = (s16[208,512]{1,0:T(8,128)(2,1)}, s16[208,512]{1,0:T(8,128)(2,1)}, s16[208,512]{1,0:T(8,128)(2,1)}, s16[208,512]{1,0:T(8,128)(2,1)}, f32[16,1,400]{2,1,0:T(1,128)}) custom-call(bf16[4,200,400]{2,1,0:T(8,128)(2,1)} %tracer_hbm.1, bf16[4,200,400]{2,1,0:T(8,128)(2,1)} %east_hbm.1, bf16[4,200,400]{2,1,0:T(8,128)(2,1)} %north_hbm.1), custom_call_target="tpu_custom_call" | custom-call | flops 6400000 | bytes 2560000 | tf_op jit(solution)/shard_map/pallas_call | solution.py:214
  5.1 0.5 %collective-permute-start = (s16[208,512]{1,0:T(8,128)(2,1)}, s16[208,512]{1,0:T(8,128)(2,1)}, u32[]{:S(2)}, u32[]{:S(2)}) collective-permute-start(s16[208,512]{1,0:T(8,128)(2,1)} %get-tuple-element.40), channel_id=1, source_target_pairs={{0,1},{1,0},{2,3},{3,2},{4,5},{5,4},{6,7},{7,6},{8,9},{9,8},{10,11... | collective-permute-start | bytes 638984 | tf_op jit(solution)/shard_map/ppermute | solution.py:137
  5.6 2.6 %collective-permute-start.1 = (s16[208,512]{1,0:T(8,128)(2,1)}, s16[208,512]{1,0:T(8,128)(2,1)}, u32[]{:S(2)}, u32[]{:S(2)}) collective-permute-start(s16[208,512]{1,0:T(8,128)(2,1)} %get-tuple-element.41), channel_id=1, source_target_pairs={{0,2},{1,3},{2,0},{3,1},{4,6},{5,7},{6,4},{7,5},{8,10},{9,11},{10,... | collective-permute-start | bytes 638984 | tf_op jit(solution)/shard_map/ppermute | solution.py:137
  8.2 0.1 collective-permute-start.2
  8.3 6.2 %all-to-all-start = ((f32[16,1,400]{2,1,0:T(1,128)}), f32[16,1,400]{2,1,0:T(1,128)S(1)}, u32[]{:S(2)}, u32[]{:S(2)}) async-start(f32[16,1,400]{2,1,0:T(1,128)} %get-tuple-element.43), calls=%async_computation | async-start | bytes 65536 | tf_op jit(solution)/shard_map/all_to_all | solution.py:651
  14.4 3.1 %shard_map.146 = (bf16[512,512]{1,0:T(8,128)(2,1)}, f32[1,512]{1,0:T(1,128)}, f32[1,128]{1,0:T(1,128)}, bf16[128,128]{1,0:T(8,128)(2,1)}, f32[200,1]{1,0:T(8,128)}, /*index=5*/f32[200,1]{1,0:T(8,128)}) custom-call(s32[1,400]{1,0:T(1,128)} %bitcast.3, s32[1,200]{1,0:T(1,128)} %bitcast.4, f32[4,1,200]{2,1,0:T(1,128)} %constant.18.clone.sine_ref, ...), custom_call_target="tpu_custom_call" | custom-call | tf_op jit(solution)/shard_map/pallas_call | solution.py:387
  17.5 3.6 %all-to-all-done.rest_4_ = f32[16,1,400]{2,1,0:T(1,128)S(1)} async-done(((f32[16,1,400]{2,1,0:T(1,128)}), f32[16,1,400]{2,1,0:T(1,128)S(1)}, u32[]{:S(2)}, u32[]{:S(2)}) %all-to-all-start) | async-done | bytes 25632 | tf_op jit(solution)/shard_map/all_to_all | solution.py:651
  21.1 0.0 collective-permute-done.rest_1_
  21.1 0.0 collective-permute-done.1.rest_2_
  21.1 0.0 collective-permute-done.2.rest_3_
  21.1 0.6 %copy-done.6 = f32[16,1,400]{2,1,0:T(1,128)} copy-done((f32[16,1,400]{2,1,0:T(1,128)}, f32[16,1,400]{2,1,0:T(1,128)S(1)}, u32[]{:S(2)}) %copy-start.6) | copy-done | bytes 25624
  21.7 5.8 %shard_map.147 = (s16[208,256]{1,0:T(8,128)(2,1)}, s16[208,256]{1,0:T(8,128)(2,1)}, s16[208,256]{1,0:T(8,128)(2,1)}, s16[208,256]{1,0:T(8,128)(2,1)}) custom-call(s16[208,512]{1,0:T(8,128)(2,1)} %get-tuple-element.39.rest_0_, s16[208,512]{1,0:T(8,128)(2,1)} %collective-permute-done.rest_1_, s16[208,512]{1,0:T(8,128)(2,1)} %collective-permute-done.1.rest_2_, ...), custom_call_target="tpu_custom_call" | custom-call | flops 384000000 | bytes 6291456 | tf_op jit(solution)/shard_map/pallas_call | solution.py:321
  27.5 0.4 collective-permute-start.3
  27.9 2.1 %collective-permute-start.4 = (s16[208,256]{1,0:T(8,128)(2,1)}, s16[208,256]{1,0:T(8,128)(2,1)S(1)}, u32[]{:S(2)}, u32[]{:S(2)}) collective-permute-start(s16[208,256]{1,0:T(8,128)(2,1)} %get-tuple-element.63), channel_id=1, source_target_pairs={{0,8},{4,12},{8,0},{12,4},{1,9},{5,13},{9,1},{13,5},{2,10},{6,14},... | collective-permute-start | bytes 319496 | tf_op jit(solution)/shard_map/ppermute | solution.py:137
  30.1 1.9 %collective-permute-start.5 = (s16[208,256]{1,0:T(8,128)(2,1)}, s16[208,256]{1,0:T(8,128)(2,1)S(1)}, u32[]{:S(2)}, u32[]{:S(2)}) collective-permute-start(s16[208,256]{1,0:T(8,128)(2,1)} %get-tuple-element.64), channel_id=1, source_target_pairs={{0,12},{4,8},{8,4},{12,0},{1,13},{5,9},{9,5},{13,1},{2,14},{6,10},... | collective-permute-start | bytes 319496 | tf_op jit(solution)/shard_map/ppermute | solution.py:137
  32.0 0.0 copy-done.2
  32.0 1.2 %shard_map.148 = (f32[832,128]{1,0:T(8,128)S(1)}, f32[832,128]{1,0:T(8,128)S(1)}, f32[26,128]{1,0:T(8,128)S(1)}, f32[4,104,128]{2,1,0:T(8,128)S(1)}) custom-call(f32[1,128]{1,0:T(1,128)S(1)} %copy-done.5, f32[3,104,128]{2,1,0:T(8,128)S(1)} %copy-done.1, f32[400,128]{1,0:T(8,128)S(1)} %copy-done.2), custom_call_target="tpu_custom_call" | custom-call | tf_op jit(solution)/shard_map/pallas_call | solution.py:462
  33.2 0.8 %collective-permute-done.3.rest_1_ = s16[208,256]{1,0:T(8,128)(2,1)S(1)} collective-permute-done((s16[208,256]{1,0:T(8,128)(2,1)}, s16[208,256]{1,0:T(8,128)(2,1)S(1)}, u32[]{:S(2)}, u32[]{:S(2)}) %collective-permute-start.3) | collective-permute-done | bytes 106528 | tf_op jit(solution)/shard_map/ppermute | solution.py:137
  34.0 0.9 %copy-done.3 = s16[208,256]{1,0:T(8,128)(2,1)S(1)} copy-done((s16[208,256]{1,0:T(8,128)(2,1)S(1)}, s16[208,256]{1,0:T(8,128)(2,1)}, u32[]{:S(2)}) %copy-start.3) | copy-done | bytes 106520
  34.9 0.8 %shard_map.149.rest_6_ = f32[832,256]{1,0:T(8,128)S(1)} custom-call(bf16[4,2,832,208]{3,2,1,0:T(8,128)(2,1)S(1)} %copy-done, s16[208,256]{1,0:T(8,128)(2,1)S(1)} %copy-done.3, s16[208,256]{1,0:T(8,128)(2,1)S(1)} %collective-permute-done.3.rest_1_), custom_call_target="tpu_custom_call" | custom-call | flops 511180800 | bytes 4194304 | tf_op jit(solution)/shard_map/pallas_call | solution.py:497
  35.7 3.6 %collective-permute-done.4.rest_9_ = s16[208,256]{1,0:T(8,128)(2,1)S(1)} collective-permute-done((s16[208,256]{1,0:T(8,128)(2,1)}, s16[208,256]{1,0:T(8,128)(2,1)S(1)}, u32[]{:S(2)}, u32[]{:S(2)}) %collective-permute-start.4) | collective-permute-done | bytes 106528 | tf_op jit(solution)/shard_map/ppermute | solution.py:137
  39.3 0.0 collective-permute-done.5.rest_10_
  39.3 0.0 copy-done.4
  39.3 11.9 %shard_map.150 = f32[100,2,400]{2,1,0:T(2,128)} custom-call(bf16[4,2,832,208]{3,2,1,0:T(8,128)(2,1)S(1)} %copy-done, f32[3,104,128]{2,1,0:T(8,128)S(1)} %copy-done.1, f32[832,128]{1,0:T(8,128)S(1)} %get-tuple-element.56.rest_2_, f32[832,128]{1,0:T(8,128)S(1)} %get-tuple-element.57.rest_3_, f32[26,128]{1,0:T(8,128)S(1)} %get-tuple-element.58.rest_4_, ...), custom_call_target="tpu_custom_call" | custom-call | flops 37273600 | bytes 6291456 | tf_op jit(solution)/shard_map/pallas_call | solution.py:620
  (10 shorter events, 0.0 us)
Async XLA Ops:
  0.0 34.0 %copy-start = (bf16[4,2,832,208]{3,2,1,0:T(8,128)(2,1)S(1)}, bf16[4,2,832,208]{3,2,1,0:T(8,128)(2,1)}, u32[]{:S(2)}) copy-start(bf16[4,2,832,208]{3,2,1,0:T(8,128)(2,1)} %constant.26.clone.table_ref.rest_0_) | copy-start | bytes 8306692
  5.1 16.0 %collective-permute-start = (s16[208,512]{1,0:T(8,128)(2,1)}, s16[208,512]{1,0:T(8,128)(2,1)}, u32[]{:S(2)}, u32[]{:S(2)}) collective-permute-start(s16[208,512]{1,0:T(8,128)(2,1)} %get-tuple-element.40), channel_id=1, source_target_pairs={{0,1},{1,0},{2,3},{3,2},{4,5},{5,4},{6,7},{7,6},{8,9},{9,8},{10,11... | collective-permute-start | bytes 638984 | tf_op jit(solution)/shard_map/ppermute | solution.py:137
  5.6 15.4 %collective-permute-start.1 = (s16[208,512]{1,0:T(8,128)(2,1)}, s16[208,512]{1,0:T(8,128)(2,1)}, u32[]{:S(2)}, u32[]{:S(2)}) collective-permute-start(s16[208,512]{1,0:T(8,128)(2,1)} %get-tuple-element.41), channel_id=1, source_target_pairs={{0,2},{1,3},{2,0},{3,1},{4,6},{5,7},{6,4},{7,5},{8,10},{9,11},{10,... | collective-permute-start | bytes 638984 | tf_op jit(solution)/shard_map/ppermute | solution.py:137
  8.2 12.9 %collective-permute-start.2 = (s16[208,512]{1,0:T(8,128)(2,1)}, s16[208,512]{1,0:T(8,128)(2,1)}, u32[]{:S(2)}, u32[]{:S(2)}) collective-permute-start(s16[208,512]{1,0:T(8,128)(2,1)} %get-tuple-element.42), channel_id=1, source_target_pairs={{0,3},{1,2},{2,1},{3,0},{4,7},{5,6},{6,5},{7,4},{8,11},{9,10},{10,... | collective-permute-start | bytes 638984 | tf_op jit(solution)/shard_map/ppermute | solution.py:137
  8.3 12.8 %all-to-all-start = ((f32[16,1,400]{2,1,0:T(1,128)}), f32[16,1,400]{2,1,0:T(1,128)S(1)}, u32[]{:S(2)}, u32[]{:S(2)}) async-start(f32[16,1,400]{2,1,0:T(1,128)} %get-tuple-element.43), calls=%async_computation | async-start | bytes 65536 | tf_op jit(solution)/shard_map/all_to_all | solution.py:651
  17.5 14.5 %copy-start.5 = (f32[1,128]{1,0:T(1,128)S(1)}, f32[1,128]{1,0:T(1,128)}, u32[]{:S(2)}) copy-start(f32[1,128]{1,0:T(1,128)} %get-tuple-element.55.mine_ref.rest_7_) | copy-start | bytes 1540
  21.0 0.6 %copy-start.6 = (f32[16,1,400]{2,1,0:T(1,128)}, f32[16,1,400]{2,1,0:T(1,128)S(1)}, u32[]{:S(2)}) copy-start(f32[16,1,400]{2,1,0:T(1,128)S(1)} %all-to-all-done.rest_4_) | copy-start | bytes 76804
  21.0 10.9 %copy-start.1 = (f32[3,104,128]{2,1,0:T(8,128)S(1)}, f32[3,104,128]{2,1,0:T(8,128)}, u32[]{:S(2)}) copy-start(f32[3,104,128]{2,1,0:T(8,128)} %constant.24.clone.lat_ref.rest_1_) | copy-start | bytes 479236
  21.1 10.9 %copy-start.2 = (f32[400,128]{1,0:T(8,128)S(1)}, f32[400,128]{1,0:T(8,128)}, u32[]{:S(2)}) copy-start(f32[400,128]{1,0:T(8,128)} %constant.25.clone.term_ref) | copy-start | bytes 614404
  27.5 11.8 %copy-start.4 = (bf16[128,128]{1,0:T(8,128)(2,1)S(1)}, bf16[128,128]{1,0:T(8,128)(2,1)}, u32[]{:S(2)}) copy-start(bf16[128,128]{1,0:T(8,128)(2,1)} %get-tuple-element.62.rest_8_) | copy-start | bytes 98308
  27.5 6.5 %collective-permute-start.3 = (s16[208,256]{1,0:T(8,128)(2,1)}, s16[208,256]{1,0:T(8,128)(2,1)S(1)}, u32[]{:S(2)}, u32[]{:S(2)}) collective-permute-start(s16[208,256]{1,0:T(8,128)(2,1)} %get-tuple-element.61), channel_id=1, source_target_pairs={{0,4},{4,0},{8,12},{12,8},{1,5},{5,1},{9,13},{13,9},{2,6},{6,2},{1... | collective-permute-start | bytes 319496 | tf_op jit(solution)/shard_map/ppermute | solution.py:137
  27.9 11.4 %collective-permute-start.4 = (s16[208,256]{1,0:T(8,128)(2,1)}, s16[208,256]{1,0:T(8,128)(2,1)S(1)}, u32[]{:S(2)}, u32[]{:S(2)}) collective-permute-start(s16[208,256]{1,0:T(8,128)(2,1)} %get-tuple-element.63), channel_id=1, source_target_pairs={{0,8},{4,12},{8,0},{12,4},{1,9},{5,13},{9,1},{13,5},{2,10},{6,14},... | collective-permute-start | bytes 319496 | tf_op jit(solution)/shard_map/ppermute | solution.py:137
  30.1 9.3 %collective-permute-start.5 = (s16[208,256]{1,0:T(8,128)(2,1)}, s16[208,256]{1,0:T(8,128)(2,1)S(1)}, u32[]{:S(2)}, u32[]{:S(2)}) collective-permute-start(s16[208,256]{1,0:T(8,128)(2,1)} %get-tuple-element.64), channel_id=1, source_target_pairs={{0,12},{4,8},{8,4},{12,0},{1,13},{5,9},{9,5},{13,1},{2,14},{6,10},... | collective-permute-start | bytes 319496 | tf_op jit(solution)/shard_map/ppermute | solution.py:137
  34.0 0.9 %copy-start.3 = (s16[208,256]{1,0:T(8,128)(2,1)S(1)}, s16[208,256]{1,0:T(8,128)(2,1)}, u32[]{:S(2)}) copy-start(s16[208,256]{1,0:T(8,128)(2,1)} %get-tuple-element.60.rest_0_) | copy-start | bytes 319492

commit v10 on v9

--- a/solution.py
+++ b/solution.py
@@ -119,14 +119,15 @@
     return codes.astype(jnp.int32).astype(jnp.float32)
 
 
-def partner(axes, sizes, step):
-    count = math.prod(sizes)
-    if count != 4:
-        return step
+def group_index(axes, sizes):
     index = lax.axis_index(axes[0])
     for axis, size in zip(axes[1:], sizes[1:]):
         index = index * size + lax.axis_index(axis)
-    return index ^ step
+    return index
+
+
+def partner(axes, sizes, step):
+    return group_index(axes, sizes) ^ step if math.prod(sizes) == 4 else step
 
 
 def exchange(blocks, axis):
@@ -137,9 +138,9 @@
     return [blocks[0]] + [lax.ppermute(blocks[step], axis, pairs[step]) for step in range(1, count)]
 
 
-def advect_kernel(ring, lat_count, tracer_hbm, east_hbm, north_hbm, *rest):
+def advect_kernel(ring, tracer_hbm, east_hbm, north_hbm, *rest):
     levels, rows, lons = tracer_hbm.shape
-    outs, (edge_ref, tracer, east_wind, north_wind, sems) = rest[:levels], rest[levels:]
+    outs, (tracer, east_wind, north_wind, sems) = rest[:levels], rest[levels:]
     chosen = [partner(*ring, step) for step in range(levels)]
     copies = []
     for step, level in enumerate(chosen):
@@ -157,21 +158,10 @@
     end = (lons - 1) // LANES * LANES
     spare = lons - end
     lane = lax.broadcasted_iota(jnp.int32, (rows, LANES), 1)
-    lat_index = lax.axis_index("lat")
-    edge_ref[...] = jnp.zeros_like(edge_ref)
-    for step, level in enumerate(chosen):
+    for step in range(levels):
         for copy in copies[step]:
             copy.wait()
         field = tracer[step].astype(jnp.float32)
-
-        @pl.when(lat_index < lat_count - 1)
-        def _():
-            edge_ref[(lat_index + 1) * levels + level] = field[rows - 1 :]
-
-        @pl.when(lat_index > 0)
-        def _():
-            edge_ref[(lat_index - 1) * levels + level] = field[:1]
-
         blank = jnp.zeros((rows, 1), jnp.float32)
         west = jnp.concatenate([blank, field[:, :-1]], axis=1)
         east = jnp.concatenate([field[:, 1:], blank], axis=1)
@@ -207,23 +197,20 @@
 
 def advect(tracer, east_wind, north_wind, ring):
     levels, rows, lons = tracer.shape
-    lat_count = lax.axis_size("lat")
     width = (lons - 1) // LANES * LANES + LANES
     padded_rows = -(-(rows + 2) // 16) * 16
     held = pltpu.VMEM((levels, rows, lons), jnp.bfloat16)
-    result = pl.pallas_call(
-        functools.partial(advect_kernel, ring, lat_count),
-        out_shape=[jax.ShapeDtypeStruct((padded_rows, width), jnp.int16)] * levels
-        + [jax.ShapeDtypeStruct((lat_count * levels, 1, lons), jnp.float32)],
+    return pl.pallas_call(
+        functools.partial(advect_kernel, ring),
+        out_shape=[jax.ShapeDtypeStruct((padded_rows, width), jnp.int16)] * levels,
         in_specs=[HBM_SPEC] * 3,
-        out_specs=[VMEM_SPEC] * (levels + 1),
+        out_specs=[VMEM_SPEC] * levels,
         scratch_shapes=[held, held, held, pltpu.SemaphoreType.DMA((levels, 3))],
         compiler_params=pltpu.CompilerParams(vmem_limit_bytes=VMEM_BYTES),
         cost_estimate=pl.CostEstimate(
             flops=20 * levels * rows * lons, bytes_accessed=8 * levels * rows * lons, transcendentals=0
         ),
     )(tracer, east_wind, north_wind)
-    return list(result[:levels]), result[levels]
 
 
 def fourier_kernel(ring, lat_count, pieces, *rest):
@@ -243,6 +230,7 @@
     lane = lax.broadcasted_iota(jnp.int32, (rows, LANES), 1)
     winds = (lane == spare + 3) | (lane == spare + 4)
     lat_index = lax.axis_index("lat")
+    level = group_index(*ring)
     for piece in range(pieces):
         spot = partner(*ring, piece)
         values = from_int16(grids[piece][...])
@@ -254,12 +242,12 @@
 
         @pl.when(lat_index > 0)
         def _():
-            above = edge_ref[(lat_index - 1) * pieces + spot]
+            above = edge_ref[(lat_index - 1) * pieces + spot, pl.ds(pieces + level, 1)]
             field[spot, :1, :lons] += wind_rows[:1] * above
 
         @pl.when(lat_index < lat_count - 1)
         def _():
-            below = edge_ref[(lat_index + 1) * pieces + spot]
+            below = edge_ref[(lat_index + 1) * pieces + spot, pl.ds(level, 1)]
             field[spot, rows - 1 :, :lons] -= wind_rows[1:] * below
 
     for spot in range(pieces):
@@ -645,10 +633,11 @@
     axes = ("lev", "fld")
     ring = (axes, tuple(lax.axis_size(axis) for axis in axes))
 
-    blocks, edges = advect(tracer, wind_east, wind_north, ring)
-    blocks, slot_wave, keep_m = lax.optimization_barrier((blocks, slot_wave, keep_m))
+    edges = jnp.concatenate([tracer[:, 0], tracer[:, rows - 1]], axis=0).astype(jnp.float32)
+    edges = lax.all_gather(edges, ("lat", *axes))
+    blocks = advect(tracer, wind_east, wind_north, ring)
+    blocks, slot_wave, keep_m = lax.optimization_barrier((list(blocks), slot_wave, keep_m))
     grids = exchange(blocks, axes)
-    edges = lax.all_to_all(edges, ("lat", *axes), split_axis=0, concat_axis=0, tiled=True)
     places, wave_row, mine, back, keep_col, sine_col = prepare_places(slot_wave, keep_m, lat_count)
     waved = fourier(grids, edges, ring, places, wave_row, keep_col, sine_col, lat_count)
     waved, mine = lax.optimization_barrier((list(waved), mine))

time: 50.9 us -> 65.7 us (1.29)
  blocking collectives: 0 us -> 24.3 us
  starting transfers between devices: 13.8 us -> 7.6 us
  waiting for transfers between devices: 7.97 us -> 4.22 us
  local copies, waits for them, and re-layouts: 1.49 us -> 2.37 us
  Pallas kernels: 27.9 us -> 27.2 us
    all_gather x0 -> x1, blocking collectives: none -> 24.3 us  [shards(): edges = lax.all_gather(edges, ('lat', *axes))]
    all_to_all x1 -> x0, starting transfers between devices: 6.15 us -> none  [shards(): lax.all_to_all(edges, ('lat', *axes), split_axis=0, concat_axis=0, tiled=...]
    all_to_all x1 -> x0, waiting for transfers between devices: 3.57 us -> none  [shards(): lax.all_to_all(edges, ('lat', *axes), split_axis=0, concat_axis=0, tiled=...]
    slice x0 -> x1, local copies, waits for them, and re-layouts: none -> 0.79 us  [shards(): tracer[:, 0]]
    pallas_call x1, Pallas kernels: 11.9 us -> 11.2 us  [legendre(): pl.pallas_call(functools.partial(legendre_kernel, early), out_shape=jax.S...]
  transfers between devices with their start and end apart: 7 -> 6, of which waited for: 3 -> 2; matrix products, arithmetic and copies ran while one was open for 0% -> 1% of each run, Pallas kernels for 10% -> 8%
where the time goes in v10:
time: 65.7 us
  Pallas kernels  27.2 us (41%)
  blocking collectives  24.3 us (37%)
  starting transfers between devices  7.6 us (12%)
  waiting for transfers between devices  4.22 us (6%)
  local copies, waits for them, and re-layouts  2.37 us (4%)
    all_gather x1, blocking collectives, shards(): edges = lax.all_gather(edges, ('lat', *axes))  24.3 us
    pallas_call x1, Pallas kernels, legendre(): pl.pallas_call(functools.partial(legendre_kernel, early), out_shape=jax.S...  11.2 us
    ppermute x6, starting transfers between devices, exchange(): lax.ppermute(blocks[step], axis, pairs[step])  7.6 us
    pallas_call x1, Pallas kernels, fourier(): pl.pallas_call(functools.partial(fourier_kernel, ring, lat_count, pieces)...  5.9 us
    pallas_call x1, Pallas kernels, advect(): pl.pallas_call(functools.partial(advect_kernel, ring), out_shape=[jax.Sha...  4.95 us
    ppermute x6, waiting for transfers between devices, exchange(): lax.ppermute(blocks[step], axis, pairs[step])  4.22 us
    pallas_call x1, Pallas kernels, prepare_places(): pl.pallas_call(places_kernel, out_shape=[jax.ShapeDtypeStruct((spots.shap...  3.04 us
    unnamed x14, local copies, waits for them, and re-layouts  1.58 us
  transfers between devices with their start and end apart: 6, of which 2 were waited for; matrix products, arithmetic and copies ran while one was open for 1% of the time, Pallas kernels for 8%

profile of v10, /device:TPU:0, one launch (start us, length us, event | category | flops | bytes accessed | tf_op | source)
XLA Modules:
  0.0 65.7 jit_solution(8048189406312438386)
XLA Ops:
  0.0 5.0 %shard_map.145 = (s16[208,512]{1,0:T(8,128)(2,1)}, s16[208,512]{1,0:T(8,128)(2,1)}, s16[208,512]{1,0:T(8,128)(2,1)}, s16[208,512]{1,0:T(8,128)(2,1)}) custom-call(bf16[4,200,400]{2,1,0:T(8,128)(2,1)} %tracer_hbm.1, bf16[4,200,400]{2,1,0:T(8,128)(2,1)} %east_hbm.1, bf16[4,200,400]{2,1,0:T(8,128)(2,1)} %north_hbm.1), custom_call_target="tpu_custom_call" | custom-call | flops 6400000 | bytes 2560000 | tf_op jit(solution)/shard_map/pallas_call | solution.py:203
  5.0 0.5 collective-permute-start
  5.5 2.6 %collective-permute-start.1 = (s16[208,512]{1,0:T(8,128)(2,1)}, s16[208,512]{1,0:T(8,128)(2,1)}, u32[]{:S(2)}, u32[]{:S(2)}) collective-permute-start(s16[208,512]{1,0:T(8,128)(2,1)} %get-tuple-element.40), channel_id=1, source_target_pairs={{0,2},{1,3},{2,0},{3,1},{4,6},{5,7},{6,4},{7,5},{8,10},{9,11},{10,... | collective-permute-start | bytes 638984 | tf_op jit(solution)/shard_map/ppermute | solution.py:138
  8.1 0.1 collective-permute-start.2
  8.1 0.8 %fusion = (bf16[4,1,400]{2,1,0:T(2,128)(2,1)S(1)}, bf16[4,1,400]{2,1,0:T(2,128)(2,1)S(1)}) fusion(bf16[4,200,400]{2,1,0:T(8,128)(2,1)} %tracer_hbm.1), kind=kLoop, calls=%fused_computation.3 | loop fusion | bytes 12800 | tf_op jit(solution)/shard_map/slice | solution.py:636
  8.9 3.0 %shard_map.146 = (bf16[512,512]{1,0:T(8,128)(2,1)}, f32[1,512]{1,0:T(1,128)}, f32[1,128]{1,0:T(1,128)}, bf16[128,128]{1,0:T(8,128)(2,1)}, f32[200,1]{1,0:T(8,128)}, /*index=5*/f32[200,1]{1,0:T(8,128)}) custom-call(s32[1,400]{1,0:T(1,128)} %bitcast.7, s32[1,200]{1,0:T(1,128)} %bitcast.8, f32[4,1,200]{2,1,0:T(1,128)} %constant.18.clone.sine_ref, ...), custom_call_target="tpu_custom_call" | custom-call | tf_op jit(solution)/shard_map/pallas_call | solution.py:375
  12.0 24.3 %all_gather.4.rest_4_ = f32[16,8,400]{2,1,0:T(8,128)} all-gather(f32[1,8,400]{2,1,0:T(8,128)S(1)} %maximum_convert_fusion), channel_id=1, replica_groups=mesh['member'=2,'lat'=4,'lev'=2,'fld'=2] {'lat','lev','fld'}, dimensions={0}, use_global_device_ids=true | all-gather | bytes 217600 | tf_op jit(solution)/shard_map/all_gather | solution.py:637
  36.3 0.0 collective-permute-done.rest_1_
  36.3 0.0 collective-permute-done.1.rest_2_
  36.3 0.0 collective-permute-done.2.rest_3_
  36.3 0.7 %copy-done.6 = s16[208,512]{1,0:T(8,128)(2,1)} copy-done((s16[208,512]{1,0:T(8,128)(2,1)}, s16[208,512]{1,0:T(8,128)(2,1)S(1)}, u32[]{:S(2)}) %copy-start.6) | copy-done | bytes 213016
  37.0 5.9 %shard_map.147 = (s16[208,256]{1,0:T(8,128)(2,1)}, s16[208,256]{1,0:T(8,128)(2,1)}, s16[208,256]{1,0:T(8,128)(2,1)}, s16[208,256]{1,0:T(8,128)(2,1)}) custom-call(s16[208,512]{1,0:T(8,128)(2,1)} %get-tuple-element.38.rest_0_, s16[208,512]{1,0:T(8,128)(2,1)} %copy-done.6, s16[208,512]{1,0:T(8,128)(2,1)} %collective-permute-done.1.rest_2_, ...), custom_call_target="tpu_custom_call" | custom-call | flops 384000000 | bytes 6291456 | tf_op jit(solution)/shard_map/pallas_call | solution.py:309
  42.9 0.0 copy-start.4
  42.9 0.1 collective-permute-start.3
  43.0 0.1 collective-permute-start.4
  43.0 4.3 %collective-permute-start.5 = (s16[208,256]{1,0:T(8,128)(2,1)}, s16[208,256]{1,0:T(8,128)(2,1)S(1)}, u32[]{:S(2)}, u32[]{:S(2)}) collective-permute-start(s16[208,256]{1,0:T(8,128)(2,1)} %get-tuple-element.62), channel_id=1, source_target_pairs={{0,12},{4,8},{8,4},{12,0},{1,13},{5,9},{9,5},{13,1},{2,14},{6,10},... | collective-permute-start | bytes 319496 | tf_op jit(solution)/shard_map/ppermute | solution.py:138
  47.3 0.0 copy-done.1
  47.3 1.2 %shard_map.148 = (f32[832,128]{1,0:T(8,128)S(1)}, f32[832,128]{1,0:T(8,128)S(1)}, f32[26,128]{1,0:T(8,128)S(1)}, f32[4,104,128]{2,1,0:T(8,128)S(1)}) custom-call(f32[1,128]{1,0:T(1,128)S(1)} %copy-done.5, f32[3,104,128]{2,1,0:T(8,128)S(1)} %copy-done.1, f32[400,128]{1,0:T(8,128)S(1)} %copy-done.2), custom_call_target="tpu_custom_call" | custom-call | tf_op jit(solution)/shard_map/pallas_call | solution.py:450
  48.6 1.0 %collective-permute-done.3.rest_1_ = s16[208,256]{1,0:T(8,128)(2,1)S(1)} collective-permute-done((s16[208,256]{1,0:T(8,128)(2,1)}, s16[208,256]{1,0:T(8,128)(2,1)S(1)}, u32[]{:S(2)}, u32[]{:S(2)}) %collective-permute-start.3) | collective-permute-done | bytes 106528 | tf_op jit(solution)/shard_map/ppermute | solution.py:138
  49.5 0.9 %copy-done.3 = s16[208,256]{1,0:T(8,128)(2,1)S(1)} copy-done((s16[208,256]{1,0:T(8,128)(2,1)S(1)}, s16[208,256]{1,0:T(8,128)(2,1)}, u32[]{:S(2)}) %copy-start.3) | copy-done | bytes 106520
  50.4 0.9 %shard_map.149.rest_6_ = f32[832,256]{1,0:T(8,128)S(1)} custom-call(bf16[4,2,832,208]{3,2,1,0:T(8,128)(2,1)S(1)} %copy-done, s16[208,256]{1,0:T(8,128)(2,1)S(1)} %copy-done.3, s16[208,256]{1,0:T(8,128)(2,1)S(1)} %collective-permute-done.3.rest_1_), custom_call_target="tpu_custom_call" | custom-call | flops 511180800 | bytes 4194304 | tf_op jit(solution)/shard_map/pallas_call | solution.py:485
  51.3 3.2 %collective-permute-done.4.rest_9_ = s16[208,256]{1,0:T(8,128)(2,1)S(1)} collective-permute-done((s16[208,256]{1,0:T(8,128)(2,1)}, s16[208,256]{1,0:T(8,128)(2,1)S(1)}, u32[]{:S(2)}, u32[]{:S(2)}) %collective-permute-start.4) | collective-permute-done | bytes 106528 | tf_op jit(solution)/shard_map/ppermute | solution.py:138
  54.5 0.0 collective-permute-done.5.rest_10_
  54.5 11.2 %shard_map.150 = f32[100,2,400]{2,1,0:T(2,128)} custom-call(bf16[4,2,832,208]{3,2,1,0:T(8,128)(2,1)S(1)} %copy-done, f32[3,104,128]{2,1,0:T(8,128)S(1)} %copy-done.1, f32[832,128]{1,0:T(8,128)S(1)} %get-tuple-element.54.rest_2_, f32[832,128]{1,0:T(8,128)S(1)} %get-tuple-element.55.rest_3_, f32[26,128]{1,0:T(8,128)S(1)} %get-tuple-element.56.rest_4_, ...), custom_call_target="tpu_custom_call" | custom-call | flops 37273600 | bytes 6291456 | tf_op jit(solution)/shard_map/pallas_call | solution.py:608
  (12 shorter events, 0.0 us)
Async XLA Ops:
  0.0 47.3 %copy-start.1 = (f32[3,104,128]{2,1,0:T(8,128)S(1)}, f32[3,104,128]{2,1,0:T(8,128)}, u32[]{:S(2)}) copy-start(f32[3,104,128]{2,1,0:T(8,128)} %constant.24.clone.lat_ref.rest_1_) | copy-start | bytes 479236
  0.0 47.3 %copy-start.2 = (f32[400,128]{1,0:T(8,128)S(1)}, f32[400,128]{1,0:T(8,128)}, u32[]{:S(2)}) copy-start(f32[400,128]{1,0:T(8,128)} %constant.25.clone.term_ref) | copy-start | bytes 614404
  0.0 49.5 %copy-start = (bf16[4,2,832,208]{3,2,1,0:T(8,128)(2,1)S(1)}, bf16[4,2,832,208]{3,2,1,0:T(8,128)(2,1)}, u32[]{:S(2)}) copy-start(bf16[4,2,832,208]{3,2,1,0:T(8,128)(2,1)} %constant.26.clone.table_ref.rest_0_) | copy-start | bytes 8306692
  5.0 31.3 %collective-permute-start = (s16[208,512]{1,0:T(8,128)(2,1)}, s16[208,512]{1,0:T(8,128)(2,1)S(1)}, u32[]{:S(2)}, u32[]{:S(2)}) collective-permute-start(s16[208,512]{1,0:T(8,128)(2,1)} %get-tuple-element.39), channel_id=1, source_target_pairs={{0,1},{1,0},{2,3},{3,2},{4,5},{5,4},{6,7},{7,6},{8,9},{9,8},{10,11... | collective-permute-start | bytes 638984 | tf_op jit(solution)/shard_map/ppermute | solution.py:138
  5.5 30.8 %collective-permute-start.1 = (s16[208,512]{1,0:T(8,128)(2,1)}, s16[208,512]{1,0:T(8,128)(2,1)}, u32[]{:S(2)}, u32[]{:S(2)}) collective-permute-start(s16[208,512]{1,0:T(8,128)(2,1)} %get-tuple-element.40), channel_id=1, source_target_pairs={{0,2},{1,3},{2,0},{3,1},{4,6},{5,7},{6,4},{7,5},{8,10},{9,11},{10,... | collective-permute-start | bytes 638984 | tf_op jit(solution)/shard_map/ppermute | solution.py:138
  8.1 28.2 %collective-permute-start.2 = (s16[208,512]{1,0:T(8,128)(2,1)}, s16[208,512]{1,0:T(8,128)(2,1)}, u32[]{:S(2)}, u32[]{:S(2)}) collective-permute-start(s16[208,512]{1,0:T(8,128)(2,1)} %get-tuple-element.41), channel_id=1, source_target_pairs={{0,3},{1,2},{2,1},{3,0},{4,7},{5,6},{6,5},{7,4},{8,11},{9,10},{10,... | collective-permute-start | bytes 638984 | tf_op jit(solution)/shard_map/ppermute | solution.py:138
  12.0 35.4 %copy-start.5 = (f32[1,128]{1,0:T(1,128)S(1)}, f32[1,128]{1,0:T(1,128)}, u32[]{:S(2)}) copy-start(f32[1,128]{1,0:T(1,128)} %get-tuple-element.53.mine_ref.rest_7_) | copy-start | bytes 1540
  36.3 0.7 %copy-start.6 = (s16[208,512]{1,0:T(8,128)(2,1)}, s16[208,512]{1,0:T(8,128)(2,1)S(1)}, u32[]{:S(2)}) copy-start(s16[208,512]{1,0:T(8,128)(2,1)S(1)} %collective-permute-done.rest_1_) | copy-start | bytes 638980
  42.9 11.7 %copy-start.4 = (bf16[128,128]{1,0:T(8,128)(2,1)S(1)}, bf16[128,128]{1,0:T(8,128)(2,1)}, u32[]{:S(2)}) copy-start(bf16[128,128]{1,0:T(8,128)(2,1)} %get-tuple-element.60.rest_8_) | copy-start | bytes 98308
  42.9 6.7 %collective-permute-start.3 = (s16[208,256]{1,0:T(8,128)(2,1)}, s16[208,256]{1,0:T(8,128)(2,1)S(1)}, u32[]{:S(2)}, u32[]{:S(2)}) collective-permute-start(s16[208,256]{1,0:T(8,128)(2,1)} %get-tuple-element.59), channel_id=1, source_target_pairs={{0,4},{4,0},{8,12},{12,8},{1,5},{5,1},{9,13},{13,9},{2,6},{6,2},{1... | collective-permute-start | bytes 319496 | tf_op jit(solution)/shard_map/ppermute | solution.py:138
  43.0 11.6 %collective-permute-start.4 = (s16[208,256]{1,0:T(8,128)(2,1)}, s16[208,256]{1,0:T(8,128)(2,1)S(1)}, u32[]{:S(2)}, u32[]{:S(2)}) collective-permute-start(s16[208,256]{1,0:T(8,128)(2,1)} %get-tuple-element.61), channel_id=1, source_target_pairs={{0,8},{4,12},{8,0},{12,4},{1,9},{5,13},{9,1},{13,5},{2,10},{6,14},... | collective-permute-start | bytes 319496 | tf_op jit(solution)/shard_map/ppermute | solution.py:138
  43.0 11.5 %collective-permute-start.5 = (s16[208,256]{1,0:T(8,128)(2,1)}, s16[208,256]{1,0:T(8,128)(2,1)S(1)}, u32[]{:S(2)}, u32[]{:S(2)}) collective-permute-start(s16[208,256]{1,0:T(8,128)(2,1)} %get-tuple-element.62), channel_id=1, source_target_pairs={{0,12},{4,8},{8,4},{12,0},{1,13},{5,9},{9,5},{13,1},{2,14},{6,10},... | collective-permute-start | bytes 319496 | tf_op jit(solution)/shard_map/ppermute | solution.py:138
  49.5 0.9 %copy-start.3 = (s16[208,256]{1,0:T(8,128)(2,1)S(1)}, s16[208,256]{1,0:T(8,128)(2,1)}, u32[]{:S(2)}) copy-start(s16[208,256]{1,0:T(8,128)(2,1)} %get-tuple-element.58.rest_0_) | copy-start | bytes 319492

commit v11 on v9

--- a/solution.py
+++ b/solution.py
@@ -15,11 +15,12 @@
 LANES = 128
 BLOCK = 32
 CHUNKS = (40, 32, 32)
+HELD = -(-M // BLOCK)
 SIDE = LANES // 2
 TOP = 32767.0
 WIND_STEP = 1.5 / TOP
 VMEM_BYTES = 60 * 2**20
-LATE_BYTES = 24 * 2**20
+LATE_BYTES = 30 * 2**20
 VMEM_SPEC = pl.BlockSpec(memory_space=pltpu.VMEM)
 SMEM_SPEC = pl.BlockSpec(memory_space=pltpu.SMEM)
 HBM_SPEC = pl.BlockSpec(memory_space=pltpu.HBM)
@@ -414,7 +415,9 @@
     return jnp.floor((jnp.maximum(M - wave, 0.0) + (BLOCK - 1)) * (1.0 / BLOCK))
 
 
-def recurrence_kernel(mine_ref, lat_ref, term_ref, beta_ref, scale_ref, growth_ref, start_ref):
+def sweep_kernel(
+    mine_ref, lat_ref, term_ref, beta_ref, scale_ref, growth_ref, start_ref, state_ref, values_ref
+):
     pair = lane_pairs(jnp.broadcast_to(mine_ref[...], (8, LANES)))
     one, two = pair[0][:1], pair[1][:1]
     blocks = growth_ref.shape[0]
@@ -450,6 +453,47 @@
         )
         start_ref[2 * kind + 1] = whole
 
+    state_ref[0] = jnp.zeros_like(state_ref[0])
+    state_ref[1] = start_ref[0]
+    state_ref[2] = start_ref[1]
+    points = lat_ref.shape[1]
+
+    def step(block, carry):
+        first = 0
+        for chunk in (points // 16 * 8, points - points // 16 * 8):
+            rows = slice(first, first + chunk)
+
+            def keep(order, value):
+                values_ref[block, order, rows] = value
+
+            sweep_block(block, turn, rows, lat_ref, beta_ref, growth_ref, start_ref, state_ref, keep)
+            first += chunk
+        return carry
+
+    total = jnp.max(turn + block_count(two)).astype(jnp.int32)
+    lax.fori_loop(0, jnp.minimum(total, HELD), step, 0)
+
+
+def sweep_block(block, turn, rows, lat_ref, beta_ref, growth_ref, start_ref, state_ref, use):
+    base = pl.multiple_of(block * BLOCK, BLOCK)
+    begins = block.astype(jnp.float32) == turn
+    grow = growth_ref[pl.ds(block, 1)]
+    cosine = lat_ref[0, rows]
+    height = jnp.where(begins, start_ref[3, rows], state_ref[2, rows])
+    factor = jnp.exp2(height)
+    old = jnp.where(begins, 0.0, state_ref[0, rows])
+    new = jnp.where(begins, start_ref[2, rows], state_ref[1, rows])
+    for order in range(BLOCK):
+        use(order, new * factor)
+        beta = beta_ref[pl.ds(base + order, 1)]
+        old, new = new, cosine * new - beta * old
+    biggest = jnp.maximum(jnp.abs(old), jnp.abs(new)) * grow
+    shift = jnp.floor(jnp.log(biggest) * (1.0 / math.log(2.0)))
+    factor = grow * jnp.exp2(-shift)
+    state_ref[0, rows] = old * factor
+    state_ref[1, rows] = new * factor
+    state_ref[2, rows] = height + shift
+
 
 def prepare_recurrence(mine):
     latitudes = latitude_table()
@@ -460,15 +504,17 @@
     terms = np.broadcast_to(terms[:, None], (M, LANES)).astype(np.float32)
     orders = jax.ShapeDtypeStruct((blocks * BLOCK, LANES), jnp.float32)
     return pl.pallas_call(
-        recurrence_kernel,
+        sweep_kernel,
         out_shape=[
             orders,
             orders,
             jax.ShapeDtypeStruct((blocks, LANES), jnp.float32),
             jax.ShapeDtypeStruct((4, points, LANES), jnp.float32),
+            jax.ShapeDtypeStruct((3, points, LANES), jnp.float32),
+            jax.ShapeDtypeStruct((HELD, BLOCK, points, LANES), jnp.float32),
         ],
         in_specs=[VMEM_SPEC] * 3,
-        out_specs=[VMEM_SPEC] * 4,
+        out_specs=[VMEM_SPEC] * 6,
         compiler_params=pltpu.CompilerParams(vmem_limit_bytes=LATE_BYTES),
     )(mine, latitudes, terms)
 
@@ -507,9 +553,9 @@
 
 
 def legendre_kernel(early, *rest):
-    table, lat_ref, beta_ref, scale_ref, growth_ref, start_ref, total_ref, mine_ref, back_ref = rest[:9]
-    fields, rest = rest[9:-8], rest[-8:]
-    out_ref, weights, before, current, level, sums, result, final = rest
+    table, lat_ref, beta_ref, scale_ref, growth_ref, start_ref, left_ref, values_ref = rest[:8]
+    total_ref, mine_ref, back_ref = rest[8:11]
+    fields, (out_ref, weights, state_ref, sums, result, final) = rest[11:-6], rest[-6:]
     points = lat_ref.shape[1]
     slots = out_ref.shape[0]
     mine = mine_ref[...]
@@ -530,53 +576,56 @@
             weights[0, kind] = jnp.where(left, top, pltpu.roll(bottom, SIDE, 1))
             weights[1, kind] = jnp.where(left, pltpu.roll(top, SIDE, 1), bottom)
     result[...] = jnp.zeros_like(result)
-    current[...] = start_ref[0]
-    level[...] = start_ref[1]
-    before[...] = jnp.zeros_like(before)
+    state_ref[...] = left_ref[...]
+
+    def reduced(block):
+        base = pl.multiple_of(block * BLOCK, BLOCK)
+        for comp in range(2):
+            total = sums[pl.ds(comp * 8, BLOCK, stride=16)]
+            for lane in range(1, 8):
+                total += sums[pl.ds(comp * 8 + lane, BLOCK, stride=16)]
+            total = total * scale_ref[pl.ds(base, BLOCK)]
+            result[comp, pl.ds(base, BLOCK)] = total + pltpu.roll(total, SIDE, 1)
+
+    def held_step(block, carry):
+        second = block.astype(jnp.float32) >= turn
+        for parity in range(2):
+            scaled = [
+                jnp.where(second, weights[1, 2 * parity + comp], weights[0, 2 * parity + comp])
+                for comp in range(2)
+            ]
+            for order in range(parity, BLOCK, 2):
+                value = values_ref[block, order]
+                for comp in range(2):
+                    product = (value * scaled[comp]).reshape(points // 8, 8, LANES)
+                    sums[pl.ds((order * 2 + comp) * 8, 8)] = product.sum(axis=0)
+        reduced(block)
+        return carry
 
     def step(block, carry):
-        base = pl.multiple_of(block * BLOCK, BLOCK)
-        now = block.astype(jnp.float32)
-        second, begins = now >= turn, now == turn
-        grow = growth_ref[pl.ds(block, 1)]
+        second = block.astype(jnp.float32) >= turn
         first = 0
         for chunk in CHUNKS:
             rows = slice(first, first + chunk)
-            height = jnp.where(begins, start_ref[3, rows], level[rows])
-            factor = jnp.exp2(height)
-            scaled = [
-                jnp.where(second, weights[1, k, rows], weights[0, k, rows]) * factor for k in range(4)
-            ]
-            cosine = lat_ref[0, rows]
-            old = jnp.where(begins, 0.0, before[rows])
-            new = jnp.where(begins, start_ref[2, rows], current[rows])
-            for order in range(BLOCK):
+            scaled = [jnp.where(second, weights[1, k, rows], weights[0, k, rows]) for k in range(4)]
+
+            def add(order, value):
                 for comp in range(2):
-                    product = new * scaled[2 * (order % 2) + comp]
+                    product = value * scaled[2 * (order % 2) + comp]
                     partial = product.reshape(chunk // 8, 8, LANES).sum(axis=0)
                     place = pl.ds((order * 2 + comp) * 8, 8)
                     if first == 0:
                         sums[place] = partial
                     else:
                         sums[place] += partial
-                beta = beta_ref[pl.ds(base + order, 1)]
-                old, new = new, cosine * new - beta * old
-            biggest = jnp.maximum(jnp.abs(old), jnp.abs(new)) * grow
-            shift = jnp.floor(jnp.log(biggest) * (1.0 / math.log(2.0)))
-            factor = grow * jnp.exp2(-shift)
-            before[rows] = old * factor
-            current[rows] = new * factor
-            level[rows] = height + shift
+
+            sweep_block(block, turn, rows, lat_ref, beta_ref, growth_ref, start_ref, state_ref, add)
             first += chunk
-        for comp in range(2):
-            total = sums[pl.ds(comp * 8, BLOCK, stride=16)]
-            for lane in range(1, 8):
-                total += sums[pl.ds(comp * 8 + lane, BLOCK, stride=16)]
-            total = total * scale_ref[pl.ds(base, BLOCK)]
-            result[comp, pl.ds(base, BLOCK)] = total + pltpu.roll(total, SIDE, 1)
+        reduced(block)
         return carry
 
-    lax.fori_loop(0, block_total, step, 0)
+    lax.fori_loop(0, jnp.minimum(block_total, HELD), held_step, 0)
+    lax.fori_loop(HELD, block_total, step, 0)
 
     left = lax.broadcasted_iota(jnp.int32, (BLOCK, LANES), 1) < SIDE
     spots = -(-M // BLOCK)
@@ -615,18 +664,15 @@
     points = latitudes.shape[1]
     table = jnp.asarray(resample_pieces(pieces, rows, fields[0].shape[0]))
     total = resample(fields[:early], table)
-    vector = pltpu.VMEM((points, LANES), jnp.float32)
     block_rows = -(-M // BLOCK) * BLOCK
     return pl.pallas_call(
         functools.partial(legendre_kernel, early),
         out_shape=jax.ShapeDtypeStruct((slots, 2, M), jnp.float32),
-        in_specs=[VMEM_SPEC] * (9 + pieces - early),
+        in_specs=[VMEM_SPEC] * (11 + pieces - early),
         out_specs=VMEM_SPEC,
         scratch_shapes=[
             pltpu.VMEM((2, 4, points, LANES), jnp.float32),
-            vector,
-            vector,
-            vector,
+            pltpu.VMEM((3, points, LANES), jnp.float32),
             pltpu.VMEM((BLOCK * 16, LANES), jnp.float32),
             pltpu.VMEM((2, 2 * block_rows, LANES), jnp.float32),
             pltpu.VMEM((2, block_rows, LANES), jnp.float32),

time: 50.9 us -> 71.3 us (1.40); the launches traced: 51.2 us -> 70.8 us
  local copies, waits for them, and re-layouts: 1.49 us -> 17.8 us
  Pallas kernels: 27.9 us -> 35.6 us
  waiting for transfers between devices: 7.97 us -> 3.59 us
    unnamed x14 -> x28, local copies, waits for them, and re-layouts: 1.49 us -> 17.8 us
    ppermute x6, waiting for transfers between devices: 4.4 us -> 0.02 us  [exchange(): lax.ppermute(blocks[step], axis, pairs[step])]
    pallas_call x1, Pallas kernels: 11.9 us -> 15.8 us  [legendre(): pl.pallas_call(functools.partial(legendre_kernel, early), out_shape=jax.S...]
    pallas_call x1, Pallas kernels: 1.22 us -> 5.04 us  [prepare_recurrence(): pl.pallas_call(sweep_kernel, out_shape=[orders, orders, jax.ShapeDtypeStr...]
  transfers between devices with their start and end apart: 7 -> 7, of which waited for: 3 -> 1; matrix products, arithmetic and copies ran while one was open for 0% -> 0% of each run, Pallas kernels for 10% -> 13%
where the time goes in v11:
time: 71.3 us; the launch traced here: 70.8 us
  Pallas kernels  35.6 us (50%)
  local copies, waits for them, and re-layouts  17.8 us (25%)
  starting transfers between devices  13.8 us (19%)
  waiting for transfers between devices  3.59 us (5%)
    unnamed x28, local copies, waits for them, and re-layouts  17.8 us
    pallas_call x1, Pallas kernels, legendre(): pl.pallas_call(functools.partial(legendre_kernel, early), out_shape=jax.S...  15.8 us
    ppermute x6, starting transfers between devices, exchange(): lax.ppermute(blocks[step], axis, pairs[step])  7.61 us
    all_to_all x1, starting transfers between devices, shards(): lax.all_to_all(edges, ('lat', *axes), split_axis=0, concat_axis=0, tiled=...  6.15 us
    pallas_call x1, Pallas kernels, fourier(): pl.pallas_call(functools.partial(fourier_kernel, ring, lat_count, pieces)...  5.84 us
    pallas_call x1, Pallas kernels, prepare_recurrence(): pl.pallas_call(sweep_kernel, out_shape=[orders, orders, jax.ShapeDtypeStr...  5.04 us
    pallas_call x1, Pallas kernels, advect(): pl.pallas_call(functools.partial(advect_kernel, ring, lat_count), out_sha...  4.93 us
    all_to_all x1, waiting for transfers between devices, shards(): lax.all_to_all(edges, ('lat', *axes), split_axis=0, concat_axis=0, tiled=...  3.57 us
  transfers between devices with their start and end apart: 7, of which 1 were waited for; matrix products, arithmetic and copies ran while one was open for 0% of the time, Pallas kernels for 13%

profile of v11, /device:TPU:0, one launch (start us, length us, event | category | flops | bytes accessed | tf_op | source)
XLA Modules:
  0.0 70.8 jit_solution(10765277183038693057)
XLA Ops:
  0.0 4.9 %shard_map.145 = (s16[208,512]{1,0:T(8,128)(2,1)}, s16[208,512]{1,0:T(8,128)(2,1)}, s16[208,512]{1,0:T(8,128)(2,1)}, s16[208,512]{1,0:T(8,128)(2,1)}, f32[16,1,400]{2,1,0:T(1,128)}) custom-call(bf16[4,200,400]{2,1,0:T(8,128)(2,1)} %tracer_hbm.1, bf16[4,200,400]{2,1,0:T(8,128)(2,1)} %east_hbm.1, bf16[4,200,400]{2,1,0:T(8,128)(2,1)} %north_hbm.1), custom_call_target="tpu_custom_call" | custom-call | flops 6400000 | bytes 2560000 | tf_op jit(solution)/shard_map/pallas_call | solution.py:215
  4.9 0.5 collective-permute-start
  5.5 2.6 %collective-permute-start.1 = (s16[208,512]{1,0:T(8,128)(2,1)}, s16[208,512]{1,0:T(8,128)(2,1)S(1)}, u32[]{:S(2)}, u32[]{:S(2)}) collective-permute-start(s16[208,512]{1,0:T(8,128)(2,1)} %get-tuple-element.43), channel_id=1, source_target_pairs={{0,2},{1,3},{2,0},{3,1},{4,6},{5,7},{6,4},{7,5},{8,10},{9,11},{10,... | collective-permute-start | bytes 638984 | tf_op jit(solution)/shard_map/ppermute | solution.py:138
  8.1 6.2 %all-to-all-start = ((f32[16,1,400]{2,1,0:T(1,128)}), f32[16,1,400]{2,1,0:T(1,128)S(1)}, u32[]{:S(2)}, u32[]{:S(2)}) async-start(f32[16,1,400]{2,1,0:T(1,128)} %get-tuple-element.45), calls=%async_computation | async-start | bytes 65536 | tf_op jit(solution)/shard_map/all_to_all | solution.py:697
  14.3 3.1 %shard_map.146 = (bf16[512,512]{1,0:T(8,128)(2,1)}, f32[1,512]{1,0:T(1,128)}, f32[1,128]{1,0:T(1,128)}, bf16[128,128]{1,0:T(8,128)(2,1)}, f32[200,1]{1,0:T(8,128)}, /*index=5*/f32[200,1]{1,0:T(8,128)}) custom-call(s32[1,400]{1,0:T(1,128)} %bitcast.3, s32[1,200]{1,0:T(1,128)} %bitcast.4, f32[4,1,200]{2,1,0:T(1,128)} %constant.18.clone.sine_ref, ...), custom_call_target="tpu_custom_call" | custom-call | tf_op jit(solution)/shard_map/pallas_call | solution.py:388
  17.3 3.6 %all-to-all-done.rest_4_ = f32[16,1,400]{2,1,0:T(1,128)S(1)} async-done(((f32[16,1,400]{2,1,0:T(1,128)}), f32[16,1,400]{2,1,0:T(1,128)S(1)}, u32[]{:S(2)}, u32[]{:S(2)}) %all-to-all-start) | async-done | bytes 25632 | tf_op jit(solution)/shard_map/all_to_all | solution.py:697
  20.9 0.6 copy-done.13
  21.8 5.8 %shard_map.147 = (s16[208,256]{1,0:T(8,128)(2,1)}, s16[208,256]{1,0:T(8,128)(2,1)}, s16[208,256]{1,0:T(8,128)(2,1)}, s16[208,256]{1,0:T(8,128)(2,1)}) custom-call(s16[208,512]{1,0:T(8,128)(2,1)} %get-tuple-element.41.rest_0_, s16[208,512]{1,0:T(8,128)(2,1)} %copy-done.10, s16[208,512]{1,0:T(8,128)(2,1)} %copy-done.11, s16[208,512]{1,0:T(8,128)(2,1)} %copy-done.12, ...), custom_call_target="tpu_custom_call" | custom-call | flops 384000000 | bytes 6291456 | tf_op jit(solution)/shard_map/pallas_call | solution.py:322
  27.6 0.4 collective-permute-start.3
  28.0 2.1 %collective-permute-start.4 = (s16[208,256]{1,0:T(8,128)(2,1)}, s16[208,256]{1,0:T(8,128)(2,1)S(1)}, u32[]{:S(2)}, u32[]{:S(2)}) collective-permute-start(s16[208,256]{1,0:T(8,128)(2,1)} %get-tuple-element.67), channel_id=1, source_target_pairs={{0,8},{4,12},{8,0},{12,4},{1,9},{5,13},{9,1},{13,5},{2,10},{6,14},... | collective-permute-start | bytes 319496 | tf_op jit(solution)/shard_map/ppermute | solution.py:138
  30.2 1.9 %collective-permute-start.5 = (s16[208,256]{1,0:T(8,128)(2,1)}, s16[208,256]{1,0:T(8,128)(2,1)S(1)}, u32[]{:S(2)}, u32[]{:S(2)}) collective-permute-start(s16[208,256]{1,0:T(8,128)(2,1)} %get-tuple-element.68), channel_id=1, source_target_pairs={{0,12},{4,8},{8,4},{12,0},{1,13},{5,9},{9,5},{13,1},{2,14},{6,10},... | collective-permute-start | bytes 319496 | tf_op jit(solution)/shard_map/ppermute | solution.py:138
  32.1 0.9 %copy-done.3 = f32[3,104,128]{2,1,0:T(8,128)S(1)} copy-done((f32[3,104,128]{2,1,0:T(8,128)S(1)}, f32[3,104,128]{2,1,0:T(8,128)}, u32[]{:S(2)}) %copy-start.3) | copy-done | bytes 159768
  33.0 0.9 %copy-done.5 = f32[400,128]{1,0:T(8,128)S(1)} copy-done((f32[400,128]{1,0:T(8,128)S(1)}, f32[400,128]{1,0:T(8,128)}, u32[]{:S(2)}) %copy-start.5) | copy-done | bytes 204824
  33.9 0.6 copy-done.8
  34.5 5.0 %shard_map.148 = (f32[832,128]{1,0:T(8,128)S(1)}, f32[832,128]{1,0:T(8,128)S(1)}, f32[26,128]{1,0:T(8,128)S(1)}, f32[4,104,128]{2,1,0:T(8,128)S(1)}, f32[3,104,1...) custom-call(f32[1,128]{1,0:T(1,128)S(1)} %copy-done.8, f32[3,104,128]{2,1,0:T(8,128)S(1)} %copy-done.3, ...), custom_call_target="tpu_custom_call" | custom-call | tf_op jit(solution)/shard_map/pallas_call | solution.py:506
  39.6 7.4 %copy-done = f32[13,32,104,128]{3,2,1,0:T(8,128)} copy-done((f32[13,32,104,128]{3,2,1,0:T(8,128)}, f32[13,32,104,128]{3,2,1,0:T(8,128)S(1)}, u32[]{:S(2)}) %copy-start) | copy-done | bytes 22151192
  47.0 2.0 %copy-done.1 = bf16[4,2,832,208]{3,2,1,0:T(8,128)(2,1)S(1)} copy-done((bf16[4,2,832,208]{3,2,1,0:T(8,128)(2,1)S(1)}, bf16[4,2,832,208]{3,2,1,0:T(8,128)(2,1)}, u32[]{:S(2)}) %copy-start.1) | copy-done | bytes 2768920
  48.9 0.9 %copy-done.6 = s16[208,256]{1,0:T(8,128)(2,1)S(1)} copy-done((s16[208,256]{1,0:T(8,128)(2,1)S(1)}, s16[208,256]{1,0:T(8,128)(2,1)}, u32[]{:S(2)}) %copy-start.6) | copy-done | bytes 106520
  49.8 0.9 %shard_map.149.rest_8_ = f32[832,256]{1,0:T(8,128)S(1)} custom-call(bf16[4,2,832,208]{3,2,1,0:T(8,128)(2,1)S(1)} %copy-done.1, s16[208,256]{1,0:T(8,128)(2,1)S(1)} %copy-done.6, s16[208,256]{1,0:T(8,128)(2,1)S(1)} %collective-permute-done.3.rest_1_), custom_call_target="tpu_custom_call" | custom-call | flops 511180800 | bytes 4194304 | tf_op jit(solution)/shard_map/pallas_call | solution.py:543
  50.7 2.0 %copy-done.2 = bf16[4,2,832,208]{3,2,1,0:T(8,128)(2,1)S(1)} copy-done((bf16[4,2,832,208]{3,2,1,0:T(8,128)(2,1)S(1)}, bf16[4,2,832,208]{3,2,1,0:T(8,128)(2,1)}, u32[]{:S(2)}) %copy-start.2) | copy-done | bytes 2768920
  52.7 0.9 %copy-done.4 = f32[3,104,128]{2,1,0:T(8,128)S(1)} copy-done((f32[3,104,128]{2,1,0:T(8,128)S(1)}, f32[3,104,128]{2,1,0:T(8,128)}, u32[]{:S(2)}) %copy-start.4) | copy-done | bytes 159768
  53.6 0.8 %copy-done.7 = bf16[128,128]{1,0:T(8,128)(2,1)S(1)} copy-done((bf16[128,128]{1,0:T(8,128)(2,1)S(1)}, bf16[128,128]{1,0:T(8,128)(2,1)}, u32[]{:S(2)}) %copy-start.7) | copy-done | bytes 32792
  54.3 0.6 copy-done.9
  55.0 15.8 %shard_map.150 = f32[100,2,400]{2,1,0:T(2,128)} custom-call(bf16[4,2,832,208]{3,2,1,0:T(8,128)(2,1)S(1)} %copy-done.2, f32[3,104,128]{2,1,0:T(8,128)S(1)} %copy-done.4, f32[832,128]{1,0:T(8,128)S(1)} %get-tuple-element.58.rest_2_, f32[832,128]{1,0:T(8,128)S(1)} %get-tuple-element.59.rest_3_, f32[26,128]{1,0:T(8,128)S(1)} %get-tuple-element.60.rest_4_, ...), custom_call_target="tpu_custom_call" | custom-call | flops 37273600 | bytes 6291456 | tf_op jit(solution)/shard_map/pallas_call | solution.py:668
  (24 shorter events, 0.4 us)
Async XLA Ops:
  4.9 16.0 %collective-permute-start = (s16[208,512]{1,0:T(8,128)(2,1)}, s16[208,512]{1,0:T(8,128)(2,1)S(1)}, u32[]{:S(2)}, u32[]{:S(2)}) collective-permute-start(s16[208,512]{1,0:T(8,128)(2,1)} %get-tuple-element.42), channel_id=1, source_target_pairs={{0,1},{1,0},{2,3},{3,2},{4,5},{5,4},{6,7},{7,6},{8,9},{9,8},{10,11... | collective-permute-start | bytes 638984 | tf_op jit(solution)/shard_map/ppermute | solution.py:138
  5.5 15.4 %collective-permute-start.1 = (s16[208,512]{1,0:T(8,128)(2,1)}, s16[208,512]{1,0:T(8,128)(2,1)S(1)}, u32[]{:S(2)}, u32[]{:S(2)}) collective-permute-start(s16[208,512]{1,0:T(8,128)(2,1)} %get-tuple-element.43), channel_id=1, source_target_pairs={{0,2},{1,3},{2,0},{3,1},{4,6},{5,7},{6,4},{7,5},{8,10},{9,11},{10,... | collective-permute-start | bytes 638984 | tf_op jit(solution)/shard_map/ppermute | solution.py:138
  8.0 12.9 %collective-permute-start.2 = (s16[208,512]{1,0:T(8,128)(2,1)}, s16[208,512]{1,0:T(8,128)(2,1)S(1)}, u32[]{:S(2)}, u32[]{:S(2)}) collective-permute-start(s16[208,512]{1,0:T(8,128)(2,1)} %get-tuple-element.44), channel_id=1, source_target_pairs={{0,3},{1,2},{2,1},{3,0},{4,7},{5,6},{6,5},{7,4},{8,11},{9,10},{10,... | collective-permute-start | bytes 638984 | tf_op jit(solution)/shard_map/ppermute | solution.py:138
  8.1 12.8 %all-to-all-start = ((f32[16,1,400]{2,1,0:T(1,128)}), f32[16,1,400]{2,1,0:T(1,128)S(1)}, u32[]{:S(2)}, u32[]{:S(2)}) async-start(f32[16,1,400]{2,1,0:T(1,128)} %get-tuple-element.45), calls=%async_computation | async-start | bytes 65536 | tf_op jit(solution)/shard_map/all_to_all | solution.py:697
  20.9 0.6 copy-start.13
  20.9 0.7 copy-start.10
  20.9 0.8 %copy-start.11 = (s16[208,512]{1,0:T(8,128)(2,1)}, s16[208,512]{1,0:T(8,128)(2,1)S(1)}, u32[]{:S(2)}) copy-start(s16[208,512]{1,0:T(8,128)(2,1)S(1)} %collective-permute-done.1.rest_2_) | copy-start | bytes 638980
  20.9 0.8 %copy-start.12 = (s16[208,512]{1,0:T(8,128)(2,1)}, s16[208,512]{1,0:T(8,128)(2,1)S(1)}, u32[]{:S(2)}) copy-start(s16[208,512]{1,0:T(8,128)(2,1)S(1)} %collective-permute-done.2.rest_3_) | copy-start | bytes 638980
  27.6 19.4 %collective-permute-start.3 = (s16[208,256]{1,0:T(8,128)(2,1)}, s16[208,256]{1,0:T(8,128)(2,1)S(1)}, u32[]{:S(2)}, u32[]{:S(2)}) collective-permute-start(s16[208,256]{1,0:T(8,128)(2,1)} %get-tuple-element.65), channel_id=1, source_target_pairs={{0,4},{4,0},{8,12},{12,8},{1,5},{5,1},{9,13},{13,9},{2,6},{6,2},{1... | collective-permute-start | bytes 319496 | tf_op jit(solution)/shard_map/ppermute | solution.py:138
  28.0 22.7 %collective-permute-start.4 = (s16[208,256]{1,0:T(8,128)(2,1)}, s16[208,256]{1,0:T(8,128)(2,1)S(1)}, u32[]{:S(2)}, u32[]{:S(2)}) collective-permute-start(s16[208,256]{1,0:T(8,128)(2,1)} %get-tuple-element.67), channel_id=1, source_target_pairs={{0,8},{4,12},{8,0},{12,4},{1,9},{5,13},{9,1},{13,5},{2,10},{6,14},... | collective-permute-start | bytes 319496 | tf_op jit(solution)/shard_map/ppermute | solution.py:138
  30.2 20.5 %collective-permute-start.5 = (s16[208,256]{1,0:T(8,128)(2,1)}, s16[208,256]{1,0:T(8,128)(2,1)S(1)}, u32[]{:S(2)}, u32[]{:S(2)}) collective-permute-start(s16[208,256]{1,0:T(8,128)(2,1)} %get-tuple-element.68), channel_id=1, source_target_pairs={{0,12},{4,8},{8,4},{12,0},{1,13},{5,9},{9,5},{13,1},{2,14},{6,10},... | collective-permute-start | bytes 319496 | tf_op jit(solution)/shard_map/ppermute | solution.py:138
  32.1 0.9 %copy-start.3 = (f32[3,104,128]{2,1,0:T(8,128)S(1)}, f32[3,104,128]{2,1,0:T(8,128)}, u32[]{:S(2)}) copy-start(f32[3,104,128]{2,1,0:T(8,128)} %constant.24.clone.lat_ref.rest_1_) | copy-start | bytes 479236
  33.0 0.9 %copy-start.5 = (f32[400,128]{1,0:T(8,128)S(1)}, f32[400,128]{1,0:T(8,128)}, u32[]{:S(2)}) copy-start(f32[400,128]{1,0:T(8,128)} %constant.25.clone.term_ref) | copy-start | bytes 614404
  33.9 0.6 copy-start.8
  39.6 7.4 %copy-start = (f32[13,32,104,128]{3,2,1,0:T(8,128)}, f32[13,32,104,128]{3,2,1,0:T(8,128)S(1)}, u32[]{:S(2)}) copy-start(f32[13,32,104,128]{3,2,1,0:T(8,128)S(1)} %get-tuple-element.63.rest_7_) | copy-start | bytes 66453508
  47.0 2.0 %copy-start.1 = (bf16[4,2,832,208]{3,2,1,0:T(8,128)(2,1)S(1)}, bf16[4,2,832,208]{3,2,1,0:T(8,128)(2,1)}, u32[]{:S(2)}) copy-start(bf16[4,2,832,208]{3,2,1,0:T(8,128)(2,1)} %constant.26.clone.table_ref.rest_0_) | copy-start | bytes 8306692
  48.9 0.9 %copy-start.6 = (s16[208,256]{1,0:T(8,128)(2,1)S(1)}, s16[208,256]{1,0:T(8,128)(2,1)}, u32[]{:S(2)}) copy-start(s16[208,256]{1,0:T(8,128)(2,1)} %get-tuple-element.64.rest_0_) | copy-start | bytes 319492
  50.7 2.0 %copy-start.2 = (bf16[4,2,832,208]{3,2,1,0:T(8,128)(2,1)S(1)}, bf16[4,2,832,208]{3,2,1,0:T(8,128)(2,1)}, u32[]{:S(2)}) copy-start(bf16[4,2,832,208]{3,2,1,0:T(8,128)(2,1)} %constant.26.clone.table_ref.rest_0_) | copy-start | bytes 8306692
  52.7 0.9 %copy-start.4 = (f32[3,104,128]{2,1,0:T(8,128)S(1)}, f32[3,104,128]{2,1,0:T(8,128)}, u32[]{:S(2)}) copy-start(f32[3,104,128]{2,1,0:T(8,128)} %constant.24.clone.lat_ref.rest_1_) | copy-start | bytes 479236
  53.6 0.8 %copy-start.7 = (bf16[128,128]{1,0:T(8,128)(2,1)S(1)}, bf16[128,128]{1,0:T(8,128)(2,1)}, u32[]{:S(2)}) copy-start(bf16[128,128]{1,0:T(8,128)(2,1)} %get-tuple-element.66.rest_10_) | copy-start | bytes 98308
  54.3 0.6 copy-start.9

commit v12 on v11

--- a/solution.py
+++ b/solution.py
@@ -20,7 +20,7 @@
 TOP = 32767.0
 WIND_STEP = 1.5 / TOP
 VMEM_BYTES = 60 * 2**20
-LATE_BYTES = 30 * 2**20
+LATE_BYTES = 20 * 2**20
 VMEM_SPEC = pl.BlockSpec(memory_space=pltpu.VMEM)
 SMEM_SPEC = pl.BlockSpec(memory_space=pltpu.SMEM)
 HBM_SPEC = pl.BlockSpec(memory_space=pltpu.HBM)
@@ -495,7 +495,7 @@
     state_ref[2, rows] = height + shift
 
 
-def prepare_recurrence(mine):
+def prepare_recurrence(mine, pieces):
     latitudes = latitude_table()
     points = latitudes.shape[1]
     blocks = 2 * -(-M // BLOCK)
@@ -515,7 +515,7 @@
         ],
         in_specs=[VMEM_SPEC] * 3,
         out_specs=[VMEM_SPEC] * 6,
-        compiler_params=pltpu.CompilerParams(vmem_limit_bytes=LATE_BYTES),
+        compiler_params=pltpu.CompilerParams(vmem_limit_bytes=late_bytes(pieces)),
     )(mine, latitudes, terms)
 
 
@@ -537,6 +537,10 @@
     rest[-1][...] = resampled(0, rest[:-1], table_ref, None)
 
 
+def late_bytes(pieces):
+    return LATE_BYTES if pieces <= 4 else VMEM_BYTES
+
+
 def resample(fields, table):
     count, _, height, _ = table.shape
     span = fields[0].shape[1]
@@ -545,7 +549,7 @@
         out_shape=jax.ShapeDtypeStruct((height, span), jnp.float32),
         in_specs=[VMEM_SPEC] * (1 + len(fields)),
         out_specs=VMEM_SPEC,
-        compiler_params=pltpu.CompilerParams(vmem_limit_bytes=LATE_BYTES),
+        compiler_params=pltpu.CompilerParams(vmem_limit_bytes=late_bytes(count)),
         cost_estimate=pl.CostEstimate(
             flops=6 * height * span * NLAT // count * len(fields), bytes_accessed=4 * 2**20, transcendentals=0
         ),
@@ -677,7 +681,7 @@
             pltpu.VMEM((2, 2 * block_rows, LANES), jnp.float32),
             pltpu.VMEM((2, block_rows, LANES), jnp.float32),
         ],
-        compiler_params=pltpu.CompilerParams(vmem_limit_bytes=LATE_BYTES),
+        compiler_params=pltpu.CompilerParams(vmem_limit_bytes=late_bytes(pieces)),
         cost_estimate=pl.CostEstimate(
             flops=7 * points * LANES * M, bytes_accessed=6 * 2**20, transcendentals=0
         ),
@@ -699,7 +703,7 @@
     waved = fourier(grids, edges, ring, places, wave_row, keep_col, sine_col, lat_count)
     waved, mine = lax.optimization_barrier((list(waved), mine))
     fields = exchange(waved, "lat")
-    prepared = prepare_recurrence(mine)
+    prepared = prepare_recurrence(mine, lat_count)
     return legendre(fields, mine, back, prepared, rows, slots)[None]
 
 

time: 71.3 us -> 71.6 us (level)
  local copies, waits for them, and re-layouts: 17.8 us -> 25 us
  Pallas kernels: 35.6 us -> 28.9 us
    unnamed x28 -> x30, local copies, waits for them, and re-layouts: 17.8 us -> 25 us
    pallas_call x1, Pallas kernels: 15.8 us -> 9.18 us  [legendre(): pl.pallas_call(functools.partial(legendre_kernel, early), out_shape=jax.S...]
where the time goes in v12:
time: 71.6 us; the launch traced here: 71.4 us
  Pallas kernels  28.9 us (40%)
  local copies, waits for them, and re-layouts  25 us (35%)
  starting transfers between devices  13.8 us (19%)
  waiting for transfers between devices  3.6 us (5%)
    unnamed x30, local copies, waits for them, and re-layouts  25 us
    pallas_call x1, Pallas kernels, legendre(): pl.pallas_call(functools.partial(legendre_kernel, early), out_shape=jax.S...  9.18 us
    ppermute x6, starting transfers between devices, exchange(): lax.ppermute(blocks[step], axis, pairs[step])  7.61 us
    all_to_all x1, starting transfers between devices, shards(): lax.all_to_all(edges, ('lat', *axes), split_axis=0, concat_axis=0, tiled=...  6.15 us
    pallas_call x1, Pallas kernels, fourier(): pl.pallas_call(functools.partial(fourier_kernel, ring, lat_count, pieces)...  5.85 us
    pallas_call x1, Pallas kernels, prepare_recurrence(): pl.pallas_call(sweep_kernel, out_shape=[orders, orders, jax.ShapeDtypeStr...  5.04 us
    pallas_call x1, Pallas kernels, advect(): pl.pallas_call(functools.partial(advect_kernel, ring, lat_count), out_sha...  4.94 us
    all_to_all x1, waiting for transfers between devices, shards(): lax.all_to_all(edges, ('lat', *axes), split_axis=0, concat_axis=0, tiled=...  3.58 us
  transfers between devices with their start and end apart: 7, of which 1 were waited for; matrix products, arithmetic and copies ran while one was open for 0% of the time, Pallas kernels for 13%

profile of v12, /device:TPU:0, one launch (start us, length us, event | category | flops | bytes accessed | tf_op | source)
XLA Modules:
  0.0 71.4 jit_solution(17511903307153611141)
XLA Ops:
  0.0 4.9 %shard_map.145 = (s16[208,512]{1,0:T(8,128)(2,1)}, s16[208,512]{1,0:T(8,128)(2,1)}, s16[208,512]{1,0:T(8,128)(2,1)}, s16[208,512]{1,0:T(8,128)(2,1)}, f32[16,1,400]{2,1,0:T(1,128)}) custom-call(bf16[4,200,400]{2,1,0:T(8,128)(2,1)} %tracer_hbm.1, bf16[4,200,400]{2,1,0:T(8,128)(2,1)} %east_hbm.1, bf16[4,200,400]{2,1,0:T(8,128)(2,1)} %north_hbm.1), custom_call_target="tpu_custom_call" | custom-call | flops 6400000 | bytes 2560000 | tf_op jit(solution)/shard_map/pallas_call | solution.py:215
  4.9 0.5 collective-permute-start
  5.5 2.6 %collective-permute-start.1 = (s16[208,512]{1,0:T(8,128)(2,1)}, s16[208,512]{1,0:T(8,128)(2,1)S(1)}, u32[]{:S(2)}, u32[]{:S(2)}) collective-permute-start(s16[208,512]{1,0:T(8,128)(2,1)} %get-tuple-element.43), channel_id=1, source_target_pairs={{0,2},{1,3},{2,0},{3,1},{4,6},{5,7},{6,4},{7,5},{8,10},{9,11},{10,... | collective-permute-start | bytes 638984 | tf_op jit(solution)/shard_map/ppermute | solution.py:138
  8.1 6.2 %all-to-all-start = ((f32[16,1,400]{2,1,0:T(1,128)}), f32[16,1,400]{2,1,0:T(1,128)S(1)}, u32[]{:S(2)}, u32[]{:S(2)}) async-start(f32[16,1,400]{2,1,0:T(1,128)} %get-tuple-element.45), calls=%async_computation | async-start | bytes 65536 | tf_op jit(solution)/shard_map/all_to_all | solution.py:701
  14.3 3.1 %shard_map.146 = (bf16[512,512]{1,0:T(8,128)(2,1)}, f32[1,512]{1,0:T(1,128)}, f32[1,128]{1,0:T(1,128)}, bf16[128,128]{1,0:T(8,128)(2,1)}, f32[200,1]{1,0:T(8,128)}, /*index=5*/f32[200,1]{1,0:T(8,128)}) custom-call(s32[1,400]{1,0:T(1,128)} %bitcast.3, s32[1,200]{1,0:T(1,128)} %bitcast.4, f32[4,1,200]{2,1,0:T(1,128)} %constant.18.clone.sine_ref, ...), custom_call_target="tpu_custom_call" | custom-call | tf_op jit(solution)/shard_map/pallas_call | solution.py:388
  17.3 3.6 %all-to-all-done.rest_4_ = f32[16,1,400]{2,1,0:T(1,128)S(1)} async-done(((f32[16,1,400]{2,1,0:T(1,128)}), f32[16,1,400]{2,1,0:T(1,128)S(1)}, u32[]{:S(2)}, u32[]{:S(2)}) %all-to-all-start) | async-done | bytes 25632 | tf_op jit(solution)/shard_map/all_to_all | solution.py:701
  20.9 0.6 copy-done.14
  21.8 5.8 %shard_map.147 = (s16[208,256]{1,0:T(8,128)(2,1)}, s16[208,256]{1,0:T(8,128)(2,1)}, s16[208,256]{1,0:T(8,128)(2,1)}, s16[208,256]{1,0:T(8,128)(2,1)}) custom-call(s16[208,512]{1,0:T(8,128)(2,1)} %get-tuple-element.41.rest_0_, s16[208,512]{1,0:T(8,128)(2,1)} %copy-done.11, s16[208,512]{1,0:T(8,128)(2,1)} %copy-done.12, s16[208,512]{1,0:T(8,128)(2,1)} %copy-done.13, ...), custom_call_target="tpu_custom_call" | custom-call | flops 384000000 | bytes 6291456 | tf_op jit(solution)/shard_map/pallas_call | solution.py:322
  28.0 2.1 %collective-permute-start.4 = (s16[208,256]{1,0:T(8,128)(2,1)}, s16[208,256]{1,0:T(8,128)(2,1)S(1)}, u32[]{:S(2)}, u32[]{:S(2)}) collective-permute-start(s16[208,256]{1,0:T(8,128)(2,1)} %get-tuple-element.67), channel_id=1, source_target_pairs={{0,8},{4,12},{8,0},{12,4},{1,9},{5,13},{9,1},{13,5},{2,10},{6,14},... | collective-permute-start | bytes 319496 | tf_op jit(solution)/shard_map/ppermute | solution.py:138
  30.2 1.9 %collective-permute-start.5 = (s16[208,256]{1,0:T(8,128)(2,1)}, s16[208,256]{1,0:T(8,128)(2,1)S(1)}, u32[]{:S(2)}, u32[]{:S(2)}) collective-permute-start(s16[208,256]{1,0:T(8,128)(2,1)} %get-tuple-element.68), channel_id=1, source_target_pairs={{0,12},{4,8},{8,4},{12,0},{1,13},{5,9},{9,5},{13,1},{2,14},{6,10},... | collective-permute-start | bytes 319496 | tf_op jit(solution)/shard_map/ppermute | solution.py:138
  32.1 0.9 %copy-done.4 = f32[3,104,128]{2,1,0:T(8,128)S(1)} copy-done((f32[3,104,128]{2,1,0:T(8,128)S(1)}, f32[3,104,128]{2,1,0:T(8,128)}, u32[]{:S(2)}) %copy-start.4) | copy-done | bytes 159768
  33.0 0.9 %copy-done.6 = f32[400,128]{1,0:T(8,128)S(1)} copy-done((f32[400,128]{1,0:T(8,128)S(1)}, f32[400,128]{1,0:T(8,128)}, u32[]{:S(2)}) %copy-start.6) | copy-done | bytes 204824
  33.9 0.6 copy-done.9
  34.5 5.0 %shard_map.148 = (f32[832,128]{1,0:T(8,128)S(1)}, f32[832,128]{1,0:T(8,128)S(1)}, f32[26,128]{1,0:T(8,128)S(1)}, f32[4,104,128]{2,1,0:T(8,128)S(1)}, f32[3,104,1...) custom-call(f32[1,128]{1,0:T(1,128)S(1)} %copy-done.9, f32[3,104,128]{2,1,0:T(8,128)S(1)} %copy-done.4, ...), custom_call_target="tpu_custom_call" | custom-call | tf_op jit(solution)/shard_map/pallas_call | solution.py:506
  39.6 7.4 %copy-done = f32[13,32,104,128]{3,2,1,0:T(8,128)} copy-done((f32[13,32,104,128]{3,2,1,0:T(8,128)}, f32[13,32,104,128]{3,2,1,0:T(8,128)S(1)}, u32[]{:S(2)}) %copy-start) | copy-done | bytes 22151192
  47.0 2.0 %copy-done.2 = bf16[4,2,832,208]{3,2,1,0:T(8,128)(2,1)S(1)} copy-done((bf16[4,2,832,208]{3,2,1,0:T(8,128)(2,1)S(1)}, bf16[4,2,832,208]{3,2,1,0:T(8,128)(2,1)}, u32[]{:S(2)}) %copy-start.2) | copy-done | bytes 2768920
  48.9 0.9 %copy-done.7 = s16[208,256]{1,0:T(8,128)(2,1)S(1)} copy-done((s16[208,256]{1,0:T(8,128)(2,1)S(1)}, s16[208,256]{1,0:T(8,128)(2,1)}, u32[]{:S(2)}) %copy-start.7) | copy-done | bytes 106520
  49.8 0.9 %shard_map.149.rest_8_ = f32[832,256]{1,0:T(8,128)S(1)} custom-call(bf16[4,2,832,208]{3,2,1,0:T(8,128)(2,1)S(1)} %copy-done.2, s16[208,256]{1,0:T(8,128)(2,1)S(1)} %copy-done.7, s16[208,256]{1,0:T(8,128)(2,1)S(1)} %collective-permute-done.3.rest_1_), custom_call_target="tpu_custom_call" | custom-call | flops 511180800 | bytes 4194304 | tf_op jit(solution)/shard_map/pallas_call | solution.py:547
  50.7 7.3 %copy-done.1 = f32[13,32,104,128]{3,2,1,0:T(8,128)S(1)} copy-done((f32[13,32,104,128]{3,2,1,0:T(8,128)S(1)}, f32[13,32,104,128]{3,2,1,0:T(8,128)}, u32[]{:S(2)}) %copy-start.1) | copy-done | bytes 22151192
  58.0 2.0 %copy-done.3 = bf16[4,2,832,208]{3,2,1,0:T(8,128)(2,1)S(1)} copy-done((bf16[4,2,832,208]{3,2,1,0:T(8,128)(2,1)S(1)}, bf16[4,2,832,208]{3,2,1,0:T(8,128)(2,1)}, u32[]{:S(2)}) %copy-start.3) | copy-done | bytes 2768920
  60.0 0.9 %copy-done.5 = f32[3,104,128]{2,1,0:T(8,128)S(1)} copy-done((f32[3,104,128]{2,1,0:T(8,128)S(1)}, f32[3,104,128]{2,1,0:T(8,128)}, u32[]{:S(2)}) %copy-start.5) | copy-done | bytes 159768
  60.9 0.8 %copy-done.8 = bf16[128,128]{1,0:T(8,128)(2,1)S(1)} copy-done((bf16[128,128]{1,0:T(8,128)(2,1)S(1)}, bf16[128,128]{1,0:T(8,128)(2,1)}, u32[]{:S(2)}) %copy-start.8) | copy-done | bytes 32792
  61.6 0.6 copy-done.10
  62.2 9.2 %shard_map.150 = f32[100,2,400]{2,1,0:T(2,128)} custom-call(bf16[4,2,832,208]{3,2,1,0:T(8,128)(2,1)S(1)} %copy-done.3, f32[3,104,128]{2,1,0:T(8,128)S(1)} %copy-done.5, f32[832,128]{1,0:T(8,128)S(1)} %get-tuple-element.58.rest_2_, f32[832,128]{1,0:T(8,128)S(1)} %get-tuple-element.59.rest_3_, f32[26,128]{1,0:T(8,128)S(1)} %get-tuple-element.60.rest_4_, ...), custom_call_target="tpu_custom_call" | custom-call | flops 37273600 | bytes 6291456 | tf_op jit(solution)/shard_map/pallas_call | solution.py:672
  (26 shorter events, 0.8 us)
Async XLA Ops:
  4.9 16.0 %collective-permute-start = (s16[208,512]{1,0:T(8,128)(2,1)}, s16[208,512]{1,0:T(8,128)(2,1)S(1)}, u32[]{:S(2)}, u32[]{:S(2)}) collective-permute-start(s16[208,512]{1,0:T(8,128)(2,1)} %get-tuple-element.42), channel_id=1, source_target_pairs={{0,1},{1,0},{2,3},{3,2},{4,5},{5,4},{6,7},{7,6},{8,9},{9,8},{10,11... | collective-permute-start | bytes 638984 | tf_op jit(solution)/shard_map/ppermute | solution.py:138
  5.5 15.4 %collective-permute-start.1 = (s16[208,512]{1,0:T(8,128)(2,1)}, s16[208,512]{1,0:T(8,128)(2,1)S(1)}, u32[]{:S(2)}, u32[]{:S(2)}) collective-permute-start(s16[208,512]{1,0:T(8,128)(2,1)} %get-tuple-element.43), channel_id=1, source_target_pairs={{0,2},{1,3},{2,0},{3,1},{4,6},{5,7},{6,4},{7,5},{8,10},{9,11},{10,... | collective-permute-start | bytes 638984 | tf_op jit(solution)/shard_map/ppermute | solution.py:138
  8.0 12.9 %collective-permute-start.2 = (s16[208,512]{1,0:T(8,128)(2,1)}, s16[208,512]{1,0:T(8,128)(2,1)S(1)}, u32[]{:S(2)}, u32[]{:S(2)}) collective-permute-start(s16[208,512]{1,0:T(8,128)(2,1)} %get-tuple-element.44), channel_id=1, source_target_pairs={{0,3},{1,2},{2,1},{3,0},{4,7},{5,6},{6,5},{7,4},{8,11},{9,10},{10,... | collective-permute-start | bytes 638984 | tf_op jit(solution)/shard_map/ppermute | solution.py:138
  8.1 12.8 %all-to-all-start = ((f32[16,1,400]{2,1,0:T(1,128)}), f32[16,1,400]{2,1,0:T(1,128)S(1)}, u32[]{:S(2)}, u32[]{:S(2)}) async-start(f32[16,1,400]{2,1,0:T(1,128)} %get-tuple-element.45), calls=%async_computation | async-start | bytes 65536 | tf_op jit(solution)/shard_map/all_to_all | solution.py:701
  20.9 0.6 copy-start.14
  20.9 0.7 copy-start.11
  20.9 0.8 %copy-start.12 = (s16[208,512]{1,0:T(8,128)(2,1)}, s16[208,512]{1,0:T(8,128)(2,1)S(1)}, u32[]{:S(2)}) copy-start(s16[208,512]{1,0:T(8,128)(2,1)S(1)} %collective-permute-done.1.rest_2_) | copy-start | bytes 638980
  20.9 0.8 %copy-start.13 = (s16[208,512]{1,0:T(8,128)(2,1)}, s16[208,512]{1,0:T(8,128)(2,1)S(1)}, u32[]{:S(2)}) copy-start(s16[208,512]{1,0:T(8,128)(2,1)S(1)} %collective-permute-done.2.rest_3_) | copy-start | bytes 638980
  27.6 19.3 %collective-permute-start.3 = (s16[208,256]{1,0:T(8,128)(2,1)}, s16[208,256]{1,0:T(8,128)(2,1)S(1)}, u32[]{:S(2)}, u32[]{:S(2)}) collective-permute-start(s16[208,256]{1,0:T(8,128)(2,1)} %get-tuple-element.65), channel_id=1, source_target_pairs={{0,4},{4,0},{8,12},{12,8},{1,5},{5,1},{9,13},{13,9},{2,6},{6,2},{1... | collective-permute-start | bytes 319496 | tf_op jit(solution)/shard_map/ppermute | solution.py:138
  28.0 22.6 %collective-permute-start.4 = (s16[208,256]{1,0:T(8,128)(2,1)}, s16[208,256]{1,0:T(8,128)(2,1)S(1)}, u32[]{:S(2)}, u32[]{:S(2)}) collective-permute-start(s16[208,256]{1,0:T(8,128)(2,1)} %get-tuple-element.67), channel_id=1, source_target_pairs={{0,8},{4,12},{8,0},{12,4},{1,9},{5,13},{9,1},{13,5},{2,10},{6,14},... | collective-permute-start | bytes 319496 | tf_op jit(solution)/shard_map/ppermute | solution.py:138
  30.2 20.5 %collective-permute-start.5 = (s16[208,256]{1,0:T(8,128)(2,1)}, s16[208,256]{1,0:T(8,128)(2,1)S(1)}, u32[]{:S(2)}, u32[]{:S(2)}) collective-permute-start(s16[208,256]{1,0:T(8,128)(2,1)} %get-tuple-element.68), channel_id=1, source_target_pairs={{0,12},{4,8},{8,4},{12,0},{1,13},{5,9},{9,5},{13,1},{2,14},{6,10},... | collective-permute-start | bytes 319496 | tf_op jit(solution)/shard_map/ppermute | solution.py:138
  32.1 0.9 %copy-start.4 = (f32[3,104,128]{2,1,0:T(8,128)S(1)}, f32[3,104,128]{2,1,0:T(8,128)}, u32[]{:S(2)}) copy-start(f32[3,104,128]{2,1,0:T(8,128)} %constant.24.clone.lat_ref.rest_1_) | copy-start | bytes 479236
  33.0 0.9 %copy-start.6 = (f32[400,128]{1,0:T(8,128)S(1)}, f32[400,128]{1,0:T(8,128)}, u32[]{:S(2)}) copy-start(f32[400,128]{1,0:T(8,128)} %constant.25.clone.term_ref) | copy-start | bytes 614404
  33.9 0.6 copy-start.9
  39.6 7.4 %copy-start = (f32[13,32,104,128]{3,2,1,0:T(8,128)}, f32[13,32,104,128]{3,2,1,0:T(8,128)S(1)}, u32[]{:S(2)}) copy-start(f32[13,32,104,128]{3,2,1,0:T(8,128)S(1)} %get-tuple-element.63.rest_7_) | copy-start | bytes 66453508
  46.9 2.0 %copy-start.2 = (bf16[4,2,832,208]{3,2,1,0:T(8,128)(2,1)S(1)}, bf16[4,2,832,208]{3,2,1,0:T(8,128)(2,1)}, u32[]{:S(2)}) copy-start(bf16[4,2,832,208]{3,2,1,0:T(8,128)(2,1)} %constant.26.clone.table_ref.rest_0_) | copy-start | bytes 8306692
  48.9 0.9 %copy-start.7 = (s16[208,256]{1,0:T(8,128)(2,1)S(1)}, s16[208,256]{1,0:T(8,128)(2,1)}, u32[]{:S(2)}) copy-start(s16[208,256]{1,0:T(8,128)(2,1)} %get-tuple-element.64.rest_0_) | copy-start | bytes 319492
  50.7 7.3 %copy-start.1 = (f32[13,32,104,128]{3,2,1,0:T(8,128)S(1)}, f32[13,32,104,128]{3,2,1,0:T(8,128)}, u32[]{:S(2)}) copy-start(f32[13,32,104,128]{3,2,1,0:T(8,128)} %copy-done) | copy-start | bytes 66453508
  58.0 2.0 %copy-start.3 = (bf16[4,2,832,208]{3,2,1,0:T(8,128)(2,1)S(1)}, bf16[4,2,832,208]{3,2,1,0:T(8,128)(2,1)}, u32[]{:S(2)}) copy-start(bf16[4,2,832,208]{3,2,1,0:T(8,128)(2,1)} %constant.26.clone.table_ref.rest_0_) | copy-start | bytes 8306692
  60.0 0.9 %copy-start.5 = (f32[3,104,128]{2,1,0:T(8,128)S(1)}, f32[3,104,128]{2,1,0:T(8,128)}, u32[]{:S(2)}) copy-start(f32[3,104,128]{2,1,0:T(8,128)} %constant.24.clone.lat_ref.rest_1_) | copy-start | bytes 479236
  60.9 0.8 %copy-start.8 = (bf16[128,128]{1,0:T(8,128)(2,1)S(1)}, bf16[128,128]{1,0:T(8,128)(2,1)}, u32[]{:S(2)}) copy-start(bf16[128,128]{1,0:T(8,128)(2,1)} %get-tuple-element.66.rest_10_) | copy-start | bytes 98308
  61.6 0.6 copy-start.10

commit v13 on v12

--- a/solution.py
+++ b/solution.py
@@ -20,7 +20,7 @@
 TOP = 32767.0
 WIND_STEP = 1.5 / TOP
 VMEM_BYTES = 60 * 2**20
-LATE_BYTES = 20 * 2**20
+LATE_BYTES = 16 * 2**20
 VMEM_SPEC = pl.BlockSpec(memory_space=pltpu.VMEM)
 SMEM_SPEC = pl.BlockSpec(memory_space=pltpu.SMEM)
 HBM_SPEC = pl.BlockSpec(memory_space=pltpu.HBM)

time: 71.6 us -> 56.5 us (0.79)
  local copies, waits for them, and re-layouts: 25 us -> 10.4 us
    unnamed x30 -> x26, local copies, waits for them, and re-layouts: 25 us -> 10.4 us
  transfers between devices with their start and end apart: 7 -> 7, of which waited for: 1 -> 1; matrix products, arithmetic and copies ran while one was open for 0% -> 0% of each run, Pallas kernels for 13% -> 16%
where the time goes in v13:
time: 56.5 us; the launch traced here: 56.3 us
  Pallas kernels  28.4 us (50%)
  starting transfers between devices  13.8 us (24%)
  local copies, waits for them, and re-layouts  10.4 us (18%)
  waiting for transfers between devices  3.57 us (6%)
    unnamed x26, local copies, waits for them, and re-layouts  10.4 us
    pallas_call x1, Pallas kernels, legendre(): pl.pallas_call(functools.partial(legendre_kernel, early), out_shape=jax.S...  8.69 us
    ppermute x6, starting transfers between devices, exchange(): lax.ppermute(blocks[step], axis, pairs[step])  7.61 us
    all_to_all x1, starting transfers between devices, shards(): lax.all_to_all(edges, ('lat', *axes), split_axis=0, concat_axis=0, tiled=...  6.15 us
    pallas_call x1, Pallas kernels, fourier(): pl.pallas_call(functools.partial(fourier_kernel, ring, lat_count, pieces)...  5.82 us
    pallas_call x1, Pallas kernels, prepare_recurrence(): pl.pallas_call(sweep_kernel, out_shape=[orders, orders, jax.ShapeDtypeStr...  5.04 us
    pallas_call x1, Pallas kernels, advect(): pl.pallas_call(functools.partial(advect_kernel, ring, lat_count), out_sha...  4.93 us
    all_to_all x1, waiting for transfers between devices, shards(): lax.all_to_all(edges, ('lat', *axes), split_axis=0, concat_axis=0, tiled=...  3.55 us
  transfers between devices with their start and end apart: 7, of which 1 were waited for; matrix products, arithmetic and copies ran while one was open for 0% of the time, Pallas kernels for 16%

profile of v13, /device:TPU:0, one launch (start us, length us, event | category | flops | bytes accessed | tf_op | source)
XLA Modules:
  0.0 56.3 jit_solution(6213425330138129722)
XLA Ops:
  0.0 4.9 %shard_map.145 = (s16[208,512]{1,0:T(8,128)(2,1)}, s16[208,512]{1,0:T(8,128)(2,1)}, s16[208,512]{1,0:T(8,128)(2,1)}, s16[208,512]{1,0:T(8,128)(2,1)}, f32[16,1,400]{2,1,0:T(1,128)}) custom-call(bf16[4,200,400]{2,1,0:T(8,128)(2,1)} %tracer_hbm.1, bf16[4,200,400]{2,1,0:T(8,128)(2,1)} %east_hbm.1, bf16[4,200,400]{2,1,0:T(8,128)(2,1)} %north_hbm.1), custom_call_target="tpu_custom_call" | custom-call | flops 6400000 | bytes 2560000 | tf_op jit(solution)/shard_map/pallas_call | solution.py:215
  4.9 0.5 collective-permute-start
  5.5 2.6 %collective-permute-start.1 = (s16[208,512]{1,0:T(8,128)(2,1)}, s16[208,512]{1,0:T(8,128)(2,1)S(1)}, u32[]{:S(2)}, u32[]{:S(2)}) collective-permute-start(s16[208,512]{1,0:T(8,128)(2,1)} %get-tuple-element.43), channel_id=1, source_target_pairs={{0,2},{1,3},{2,0},{3,1},{4,6},{5,7},{6,4},{7,5},{8,10},{9,11},{10,... | collective-permute-start | bytes 638984 | tf_op jit(solution)/shard_map/ppermute | solution.py:138
  8.1 6.2 %all-to-all-start = ((f32[16,1,400]{2,1,0:T(1,128)}), f32[16,1,400]{2,1,0:T(1,128)S(1)}, u32[]{:S(2)}, u32[]{:S(2)}) async-start(f32[16,1,400]{2,1,0:T(1,128)} %get-tuple-element.45), calls=%async_computation | async-start | bytes 65536 | tf_op jit(solution)/shard_map/all_to_all | solution.py:701
  14.3 3.1 %shard_map.146 = (bf16[512,512]{1,0:T(8,128)(2,1)}, f32[1,512]{1,0:T(1,128)}, f32[1,128]{1,0:T(1,128)}, bf16[128,128]{1,0:T(8,128)(2,1)}, f32[200,1]{1,0:T(8,128)}, /*index=5*/f32[200,1]{1,0:T(8,128)}) custom-call(s32[1,400]{1,0:T(1,128)} %bitcast.3, s32[1,200]{1,0:T(1,128)} %bitcast.4, f32[4,1,200]{2,1,0:T(1,128)} %constant.18.clone.sine_ref, ...), custom_call_target="tpu_custom_call" | custom-call | tf_op jit(solution)/shard_map/pallas_call | solution.py:388
  17.3 3.6 %all-to-all-done.rest_4_ = f32[16,1,400]{2,1,0:T(1,128)S(1)} async-done(((f32[16,1,400]{2,1,0:T(1,128)}), f32[16,1,400]{2,1,0:T(1,128)S(1)}, u32[]{:S(2)}, u32[]{:S(2)}) %all-to-all-start) | async-done | bytes 25632 | tf_op jit(solution)/shard_map/all_to_all | solution.py:701
  20.9 0.6 copy-done.12
  21.6 0.1 copy-done.10
  21.8 5.8 %shard_map.147 = (s16[208,256]{1,0:T(8,128)(2,1)}, s16[208,256]{1,0:T(8,128)(2,1)}, s16[208,256]{1,0:T(8,128)(2,1)}, s16[208,256]{1,0:T(8,128)(2,1)}) custom-call(s16[208,512]{1,0:T(8,128)(2,1)} %get-tuple-element.41.rest_0_, s16[208,512]{1,0:T(8,128)(2,1)} %copy-done.9, s16[208,512]{1,0:T(8,128)(2,1)} %copy-done.10, s16[208,512]{1,0:T(8,128)(2,1)} %copy-done.11, ...), custom_call_target="tpu_custom_call" | custom-call | flops 384000000 | bytes 6291456 | tf_op jit(solution)/shard_map/pallas_call | solution.py:322
  27.6 0.4 collective-permute-start.3
  28.0 2.1 %collective-permute-start.4 = (s16[208,256]{1,0:T(8,128)(2,1)}, s16[208,256]{1,0:T(8,128)(2,1)S(1)}, u32[]{:S(2)}, u32[]{:S(2)}) collective-permute-start(s16[208,256]{1,0:T(8,128)(2,1)} %get-tuple-element.67), channel_id=1, source_target_pairs={{0,8},{4,12},{8,0},{12,4},{1,9},{5,13},{9,1},{13,5},{2,10},{6,14},... | collective-permute-start | bytes 319496 | tf_op jit(solution)/shard_map/ppermute | solution.py:138
  30.2 1.9 %collective-permute-start.5 = (s16[208,256]{1,0:T(8,128)(2,1)}, s16[208,256]{1,0:T(8,128)(2,1)S(1)}, u32[]{:S(2)}, u32[]{:S(2)}) collective-permute-start(s16[208,256]{1,0:T(8,128)(2,1)} %get-tuple-element.68), channel_id=1, source_target_pairs={{0,12},{4,8},{8,4},{12,0},{1,13},{5,9},{9,5},{13,1},{2,14},{6,10},... | collective-permute-start | bytes 319496 | tf_op jit(solution)/shard_map/ppermute | solution.py:138
  32.1 0.9 %copy-done.2 = f32[3,104,128]{2,1,0:T(8,128)S(1)} copy-done((f32[3,104,128]{2,1,0:T(8,128)S(1)}, f32[3,104,128]{2,1,0:T(8,128)}, u32[]{:S(2)}) %copy-start.2) | copy-done | bytes 159768
  33.0 0.9 %copy-done.4 = f32[400,128]{1,0:T(8,128)S(1)} copy-done((f32[400,128]{1,0:T(8,128)S(1)}, f32[400,128]{1,0:T(8,128)}, u32[]{:S(2)}) %copy-start.4) | copy-done | bytes 204824
  33.9 0.6 %copy-done.7 = f32[1,128]{1,0:T(1,128)S(1)} copy-done((f32[1,128]{1,0:T(1,128)S(1)}, f32[1,128]{1,0:T(1,128)}, u32[]{:S(2)}) %copy-start.7) | copy-done | bytes 536
  34.5 5.0 %shard_map.148 = (f32[832,128]{1,0:T(8,128)S(1)}, f32[832,128]{1,0:T(8,128)S(1)}, f32[26,128]{1,0:T(8,128)S(1)}, f32[4,104,128]{2,1,0:T(8,128)S(1)}, f32[3,104,1...) custom-call(f32[1,128]{1,0:T(1,128)S(1)} %copy-done.7, f32[3,104,128]{2,1,0:T(8,128)S(1)} %copy-done.2, ...), custom_call_target="tpu_custom_call" | custom-call | tf_op jit(solution)/shard_map/pallas_call | solution.py:506
  39.6 2.0 %copy-done = bf16[4,2,832,208]{3,2,1,0:T(8,128)(2,1)S(1)} copy-done((bf16[4,2,832,208]{3,2,1,0:T(8,128)(2,1)S(1)}, bf16[4,2,832,208]{3,2,1,0:T(8,128)(2,1)}, u32[]{:S(2)}) %copy-start) | copy-done | bytes 2768920
  41.6 0.9 %copy-done.5 = s16[208,256]{1,0:T(8,128)(2,1)S(1)} copy-done((s16[208,256]{1,0:T(8,128)(2,1)S(1)}, s16[208,256]{1,0:T(8,128)(2,1)}, u32[]{:S(2)}) %copy-start.5) | copy-done | bytes 106520
  42.4 0.9 %shard_map.149.rest_8_ = f32[832,256]{1,0:T(8,128)S(1)} custom-call(bf16[4,2,832,208]{3,2,1,0:T(8,128)(2,1)S(1)} %copy-done, s16[208,256]{1,0:T(8,128)(2,1)S(1)} %copy-done.5, s16[208,256]{1,0:T(8,128)(2,1)S(1)} %collective-permute-done.3.rest_1_), custom_call_target="tpu_custom_call" | custom-call | flops 511180800 | bytes 4194304 | tf_op jit(solution)/shard_map/pallas_call | solution.py:547
  43.3 2.0 %copy-done.1 = bf16[4,2,832,208]{3,2,1,0:T(8,128)(2,1)S(1)} copy-done((bf16[4,2,832,208]{3,2,1,0:T(8,128)(2,1)S(1)}, bf16[4,2,832,208]{3,2,1,0:T(8,128)(2,1)}, u32[]{:S(2)}) %copy-start.1) | copy-done | bytes 2768920
  45.3 0.9 %copy-done.3 = f32[3,104,128]{2,1,0:T(8,128)S(1)} copy-done((f32[3,104,128]{2,1,0:T(8,128)S(1)}, f32[3,104,128]{2,1,0:T(8,128)}, u32[]{:S(2)}) %copy-start.3) | copy-done | bytes 159768
  46.2 0.8 %copy-done.6 = bf16[128,128]{1,0:T(8,128)(2,1)S(1)} copy-done((bf16[128,128]{1,0:T(8,128)(2,1)S(1)}, bf16[128,128]{1,0:T(8,128)(2,1)}, u32[]{:S(2)}) %copy-start.6) | copy-done | bytes 32792
  47.0 0.6 %copy-done.8 = f32[1,128]{1,0:T(1,128)S(1)} copy-done((f32[1,128]{1,0:T(1,128)S(1)}, f32[1,128]{1,0:T(1,128)}, u32[]{:S(2)}) %copy-start.8) | copy-done | bytes 536
  47.6 8.7 %shard_map.150 = f32[100,2,400]{2,1,0:T(2,128)} custom-call(bf16[4,2,832,208]{3,2,1,0:T(8,128)(2,1)S(1)} %copy-done.1, f32[3,104,128]{2,1,0:T(8,128)S(1)} %copy-done.3, f32[832,128]{1,0:T(8,128)S(1)} %get-tuple-element.58.rest_2_, f32[832,128]{1,0:T(8,128)S(1)} %get-tuple-element.59.rest_3_, f32[26,128]{1,0:T(8,128)S(1)} %get-tuple-element.60.rest_4_, ...), custom_call_target="tpu_custom_call" | custom-call | flops 37273600 | bytes 6291456 | tf_op jit(solution)/shard_map/pallas_call | solution.py:672
  (22 shorter events, 0.3 us)
Async XLA Ops:
  4.9 16.0 %collective-permute-start = (s16[208,512]{1,0:T(8,128)(2,1)}, s16[208,512]{1,0:T(8,128)(2,1)S(1)}, u32[]{:S(2)}, u32[]{:S(2)}) collective-permute-start(s16[208,512]{1,0:T(8,128)(2,1)} %get-tuple-element.42), channel_id=1, source_target_pairs={{0,1},{1,0},{2,3},{3,2},{4,5},{5,4},{6,7},{7,6},{8,9},{9,8},{10,11... | collective-permute-start | bytes 638984 | tf_op jit(solution)/shard_map/ppermute | solution.py:138
  5.5 15.4 %collective-permute-start.1 = (s16[208,512]{1,0:T(8,128)(2,1)}, s16[208,512]{1,0:T(8,128)(2,1)S(1)}, u32[]{:S(2)}, u32[]{:S(2)}) collective-permute-start(s16[208,512]{1,0:T(8,128)(2,1)} %get-tuple-element.43), channel_id=1, source_target_pairs={{0,2},{1,3},{2,0},{3,1},{4,6},{5,7},{6,4},{7,5},{8,10},{9,11},{10,... | collective-permute-start | bytes 638984 | tf_op jit(solution)/shard_map/ppermute | solution.py:138
  8.0 12.9 %collective-permute-start.2 = (s16[208,512]{1,0:T(8,128)(2,1)}, s16[208,512]{1,0:T(8,128)(2,1)S(1)}, u32[]{:S(2)}, u32[]{:S(2)}) collective-permute-start(s16[208,512]{1,0:T(8,128)(2,1)} %get-tuple-element.44), channel_id=1, source_target_pairs={{0,3},{1,2},{2,1},{3,0},{4,7},{5,6},{6,5},{7,4},{8,11},{9,10},{10,... | collective-permute-start | bytes 638984 | tf_op jit(solution)/shard_map/ppermute | solution.py:138
  8.1 12.8 %all-to-all-start = ((f32[16,1,400]{2,1,0:T(1,128)}), f32[16,1,400]{2,1,0:T(1,128)S(1)}, u32[]{:S(2)}, u32[]{:S(2)}) async-start(f32[16,1,400]{2,1,0:T(1,128)} %get-tuple-element.45), calls=%async_computation | async-start | bytes 65536 | tf_op jit(solution)/shard_map/all_to_all | solution.py:701
  20.9 0.6 %copy-start.12 = (f32[16,1,400]{2,1,0:T(1,128)}, f32[16,1,400]{2,1,0:T(1,128)S(1)}, u32[]{:S(2)}) copy-start(f32[16,1,400]{2,1,0:T(1,128)S(1)} %all-to-all-done.rest_4_) | copy-start | bytes 76804
  20.9 0.7 %copy-start.9 = (s16[208,512]{1,0:T(8,128)(2,1)}, s16[208,512]{1,0:T(8,128)(2,1)S(1)}, u32[]{:S(2)}) copy-start(s16[208,512]{1,0:T(8,128)(2,1)S(1)} %collective-permute-done.rest_1_) | copy-start | bytes 638980
  20.9 0.8 %copy-start.10 = (s16[208,512]{1,0:T(8,128)(2,1)}, s16[208,512]{1,0:T(8,128)(2,1)S(1)}, u32[]{:S(2)}) copy-start(s16[208,512]{1,0:T(8,128)(2,1)S(1)} %collective-permute-done.1.rest_2_) | copy-start | bytes 638980
  20.9 0.8 %copy-start.11 = (s16[208,512]{1,0:T(8,128)(2,1)}, s16[208,512]{1,0:T(8,128)(2,1)S(1)}, u32[]{:S(2)}) copy-start(s16[208,512]{1,0:T(8,128)(2,1)S(1)} %collective-permute-done.2.rest_3_) | copy-start | bytes 638980
  27.6 12.0 %collective-permute-start.3 = (s16[208,256]{1,0:T(8,128)(2,1)}, s16[208,256]{1,0:T(8,128)(2,1)S(1)}, u32[]{:S(2)}, u32[]{:S(2)}) collective-permute-start(s16[208,256]{1,0:T(8,128)(2,1)} %get-tuple-element.65), channel_id=1, source_target_pairs={{0,4},{4,0},{8,12},{12,8},{1,5},{5,1},{9,13},{13,9},{2,6},{6,2},{1... | collective-permute-start | bytes 319496 | tf_op jit(solution)/shard_map/ppermute | solution.py:138
  28.0 15.3 %collective-permute-start.4 = (s16[208,256]{1,0:T(8,128)(2,1)}, s16[208,256]{1,0:T(8,128)(2,1)S(1)}, u32[]{:S(2)}, u32[]{:S(2)}) collective-permute-start(s16[208,256]{1,0:T(8,128)(2,1)} %get-tuple-element.67), channel_id=1, source_target_pairs={{0,8},{4,12},{8,0},{12,4},{1,9},{5,13},{9,1},{13,5},{2,10},{6,14},... | collective-permute-start | bytes 319496 | tf_op jit(solution)/shard_map/ppermute | solution.py:138
  30.2 13.2 %collective-permute-start.5 = (s16[208,256]{1,0:T(8,128)(2,1)}, s16[208,256]{1,0:T(8,128)(2,1)S(1)}, u32[]{:S(2)}, u32[]{:S(2)}) collective-permute-start(s16[208,256]{1,0:T(8,128)(2,1)} %get-tuple-element.68), channel_id=1, source_target_pairs={{0,12},{4,8},{8,4},{12,0},{1,13},{5,9},{9,5},{13,1},{2,14},{6,10},... | collective-permute-start | bytes 319496 | tf_op jit(solution)/shard_map/ppermute | solution.py:138
  32.0 0.9 %copy-start.2 = (f32[3,104,128]{2,1,0:T(8,128)S(1)}, f32[3,104,128]{2,1,0:T(8,128)}, u32[]{:S(2)}) copy-start(f32[3,104,128]{2,1,0:T(8,128)} %constant.24.clone.lat_ref.rest_1_) | copy-start | bytes 479236
  33.0 0.9 %copy-start.4 = (f32[400,128]{1,0:T(8,128)S(1)}, f32[400,128]{1,0:T(8,128)}, u32[]{:S(2)}) copy-start(f32[400,128]{1,0:T(8,128)} %constant.25.clone.term_ref) | copy-start | bytes 614404
  33.9 0.6 %copy-start.7 = (f32[1,128]{1,0:T(1,128)S(1)}, f32[1,128]{1,0:T(1,128)}, u32[]{:S(2)}) copy-start(f32[1,128]{1,0:T(1,128)} %get-tuple-element.57.mine_ref.rest_9_) | copy-start | bytes 1540
  39.6 2.0 %copy-start = (bf16[4,2,832,208]{3,2,1,0:T(8,128)(2,1)S(1)}, bf16[4,2,832,208]{3,2,1,0:T(8,128)(2,1)}, u32[]{:S(2)}) copy-start(bf16[4,2,832,208]{3,2,1,0:T(8,128)(2,1)} %constant.26.clone.table_ref.rest_0_) | copy-start | bytes 8306692
  41.5 0.9 %copy-start.5 = (s16[208,256]{1,0:T(8,128)(2,1)S(1)}, s16[208,256]{1,0:T(8,128)(2,1)}, u32[]{:S(2)}) copy-start(s16[208,256]{1,0:T(8,128)(2,1)} %get-tuple-element.64.rest_0_) | copy-start | bytes 319492
  43.3 2.0 %copy-start.1 = (bf16[4,2,832,208]{3,2,1,0:T(8,128)(2,1)S(1)}, bf16[4,2,832,208]{3,2,1,0:T(8,128)(2,1)}, u32[]{:S(2)}) copy-start(bf16[4,2,832,208]{3,2,1,0:T(8,128)(2,1)} %constant.26.clone.table_ref.rest_0_) | copy-start | bytes 8306692
  45.3 0.9 %copy-start.3 = (f32[3,104,128]{2,1,0:T(8,128)S(1)}, f32[3,104,128]{2,1,0:T(8,128)}, u32[]{:S(2)}) copy-start(f32[3,104,128]{2,1,0:T(8,128)} %constant.24.clone.lat_ref.rest_1_) | copy-start | bytes 479236
  46.2 0.8 %copy-start.6 = (bf16[128,128]{1,0:T(8,128)(2,1)S(1)}, bf16[128,128]{1,0:T(8,128)(2,1)}, u32[]{:S(2)}) copy-start(bf16[128,128]{1,0:T(8,128)(2,1)} %get-tuple-element.66.rest_10_) | copy-start | bytes 98308
  47.0 0.6 %copy-start.8 = (f32[1,128]{1,0:T(1,128)S(1)}, f32[1,128]{1,0:T(1,128)}, u32[]{:S(2)}) copy-start(f32[1,128]{1,0:T(1,128)} %get-tuple-element.57.mine_ref.rest_9_) | copy-start | bytes 1540

commit v14 on v13

--- a/solution.py
+++ b/solution.py
@@ -21,6 +21,7 @@
 WIND_STEP = 1.5 / TOP
 VMEM_BYTES = 60 * 2**20
 LATE_BYTES = 16 * 2**20
+MIDDLE_BYTES = 16 * 2**20
 VMEM_SPEC = pl.BlockSpec(memory_space=pltpu.VMEM)
 SMEM_SPEC = pl.BlockSpec(memory_space=pltpu.SMEM)
 HBM_SPEC = pl.BlockSpec(memory_space=pltpu.HBM)
@@ -228,16 +229,11 @@
 
 
 def fourier_kernel(ring, lat_count, pieces, *rest):
-    grids, (edge_ref, *tables_hbm, wave_ref, keep_ref, sine_ref) = rest[:pieces], rest[pieces : pieces + 9]
-    outs, rest = rest[pieces + 9 :][:lat_count], rest[pieces + 9 + lat_count :]
-    tables, place_ref, (field, sems) = rest[:4], rest[4], rest[5:]
+    grids, (edge_ref, table_ref, place_ref, wave_ref, keep_ref, sine_ref) = rest[:pieces], rest[pieces : pieces + 6]
+    outs, field = rest[pieces + 6 : -1], rest[-1]
     _, rows, width = field.shape
-    lons = tables[0].shape[1]
+    lons = table_ref.shape[1]
     share = pieces // 4
-    copies = []
-    for kind, target in enumerate((*tables, place_ref)):
-        copies.append(pltpu.make_async_copy(tables_hbm[kind], target, sems.at[kind]))
-        copies[-1].start()
 
     end = width - LANES
     spare = lons - end
@@ -273,12 +269,14 @@
         field[spot, :, end:] = tile - jnp.where(lane == spare - 1, loss, 0.0)
         field[spot, :, :LANES] += jnp.where(lane == 0, gain, 0.0)
 
-    def product(value, table, spot):
+    spans = [2 * LANES, 2 * LANES, 4 * LANES, 4 * LANES]
+
+    def product(kind, value, spot):
         high, low = split_bf16(value)
-        width = table.shape[2] // 2
-        both = jnp.dot(high, table[spot], preferred_element_type=jnp.float32)
-        part = jnp.dot(low, table[spot, :, :width], preferred_element_type=jnp.float32)
-        return part + both[:, :width] + both[:, width:]
+        first, span = 2 * sum(spans[:kind]), spans[kind]
+        both = jnp.dot(high, table_ref[spot, :, first : first + 2 * span], preferred_element_type=jnp.float32)
+        part = jnp.dot(low, table_ref[spot, :, first : first + span], preferred_element_type=jnp.float32)
+        return part + both[:, :span] + both[:, span:]
 
     sums = [None, None, None]
     for spot in range(share):
@@ -287,12 +285,9 @@
         sum13, dif13 = quarters[1] + quarters[3], quarters[1] - quarters[3]
         parts = []
         for kind, value in enumerate((sum02 + sum13, sum02 - sum13, dif02, dif13)):
-            if spot == 0:
-                copies[kind].wait()
-            parts.append(product(value, tables[kind], spot))
+            parts.append(product(kind, value, spot))
         parts = [parts[0], parts[1], parts[2] + parts[3]]
         sums = [part if total is None else total + part for total, part in zip(sums, parts)]
-    copies[4].wait()
     placed = []
     for part in range(2):
         columns = []
@@ -322,16 +317,14 @@
     return pl.pallas_call(
         functools.partial(fourier_kernel, ring, lat_count, pieces),
         out_shape=[jax.ShapeDtypeStruct((padded_rows, 2 * LANES), jnp.int16)] * lat_count,
-        in_specs=[VMEM_SPEC] * (pieces + 1) + [HBM_SPEC] * 5 + [VMEM_SPEC] * 3,
+        in_specs=[VMEM_SPEC] * (pieces + 6),
         out_specs=[VMEM_SPEC] * lat_count,
-        scratch_shapes=[pltpu.VMEM(table.shape, jnp.bfloat16) for table in tables]
-        + [pltpu.VMEM(places.shape, jnp.bfloat16)]
-        + [pltpu.VMEM((pieces, rows, width), jnp.float32), pltpu.SemaphoreType.DMA((5,))],
-        compiler_params=pltpu.CompilerParams(vmem_limit_bytes=VMEM_BYTES),
+        scratch_shapes=[pltpu.VMEM((pieces, rows, width), jnp.float32)],
+        compiler_params=pltpu.CompilerParams(vmem_limit_bytes=MIDDLE_BYTES),
         cost_estimate=pl.CostEstimate(
             flops=3 * rows * NLON * M, bytes_accessed=6 * 2**20, transcendentals=0
         ),
-    )(*grids, edges, *tables, places, wave_row, keep_col, sine_col)
+    )(*grids, edges, np.concatenate(tables, axis=-1), places, wave_row, keep_col, sine_col)
 
 
 def places_kernel(
@@ -398,7 +391,7 @@
         in_specs=[VMEM_SPEC] * 4,
         out_specs=[VMEM_SPEC] * 6,
         scratch_shapes=[pltpu.VMEM((groups, 8, LANES), jnp.float32)],
-        compiler_params=pltpu.CompilerParams(vmem_limit_bytes=VMEM_BYTES),
+        compiler_params=pltpu.CompilerParams(vmem_limit_bytes=MIDDLE_BYTES),
     )(
         slot_wave[None], keep_m[None],
         sines.reshape(groups, 1, rows).astype(np.float32), spots,

time: 56.5 us -> 48.1 us (0.85)
  Pallas kernels: 28.4 us -> 24.4 us
  local copies, waits for them, and re-layouts: 10.4 us -> 7.14 us
  waiting for transfers between devices: 3.57 us -> 2.02 us
    unnamed x26 -> x28, local copies, waits for them, and re-layouts: 10.4 us -> 7.14 us
    all_to_all x1, waiting for transfers between devices: 3.55 us -> 1.15 us  [shards(): lax.all_to_all(edges, ('lat', *axes), split_axis=0, concat_axis=0, tiled=...]
    pallas_call x1, Pallas kernels: 5.82 us -> 3.66 us  [fourier(): pl.pallas_call(functools.partial(fourier_kernel, ring, lat_count, pieces)...]
    pallas_call x1, Pallas kernels: 3.08 us -> 1.24 us  [prepare_places(): pl.pallas_call(places_kernel, out_shape=[jax.ShapeDtypeStruct((spots.shap...]
    ppermute x6, waiting for transfers between devices: 0.02 us -> 0.87 us  [exchange(): lax.ppermute(blocks[step], axis, pairs[step])]
  transfers between devices with their start and end apart: 7 -> 7, of which waited for: 1 -> 2; matrix products, arithmetic and copies ran while one was open for 0% -> 0% of each run, Pallas kernels for 16% -> 15%
where the time goes in v14:
time: 48.1 us; the launch traced here: 47.5 us
  Pallas kernels  24.4 us (51%)
  starting transfers between devices  13.8 us (29%)
  local copies, waits for them, and re-layouts  7.14 us (15%)
  waiting for transfers between devices  2.02 us (4%)
    pallas_call x1, Pallas kernels, legendre(): pl.pallas_call(functools.partial(legendre_kernel, early), out_shape=jax.S...  8.55 us
    ppermute x6, starting transfers between devices, exchange(): lax.ppermute(blocks[step], axis, pairs[step])  7.6 us
    unnamed x28, local copies, waits for them, and re-layouts  7.14 us
    all_to_all x1, starting transfers between devices, shards(): lax.all_to_all(edges, ('lat', *axes), split_axis=0, concat_axis=0, tiled=...  6.15 us
    pallas_call x1, Pallas kernels, advect(): pl.pallas_call(functools.partial(advect_kernel, ring, lat_count), out_sha...  5.09 us
    pallas_call x1, Pallas kernels, prepare_recurrence(): pl.pallas_call(sweep_kernel, out_shape=[orders, orders, jax.ShapeDtypeStr...  5.05 us
    pallas_call x1, Pallas kernels, fourier(): pl.pallas_call(functools.partial(fourier_kernel, ring, lat_count, pieces)...  3.66 us
    pallas_call x1, Pallas kernels, prepare_places(): pl.pallas_call(places_kernel, out_shape=[jax.ShapeDtypeStruct((spots.shap...  1.24 us
  transfers between devices with their start and end apart: 7, of which 2 were waited for; matrix products, arithmetic and copies ran while one was open for 0% of the time, Pallas kernels for 15%

profile of v14, /device:TPU:0, one launch (start us, length us, event | category | flops | bytes accessed | tf_op | source)
XLA Modules:
  0.0 47.5 jit_solution(10015862043029716420)
XLA Ops:
  0.0 5.1 %shard_map.118 = (s16[208,512]{1,0:T(8,128)(2,1)}, s16[208,512]{1,0:T(8,128)(2,1)}, s16[208,512]{1,0:T(8,128)(2,1)}, s16[208,512]{1,0:T(8,128)(2,1)}, f32[16,1,400]{2,1,0:T(1,128)}) custom-call(bf16[4,200,400]{2,1,0:T(8,128)(2,1)} %tracer_hbm.1, bf16[4,200,400]{2,1,0:T(8,128)(2,1)} %east_hbm.1, bf16[4,200,400]{2,1,0:T(8,128)(2,1)} %north_hbm.1), custom_call_target="tpu_custom_call" | custom-call | flops 6400000 | bytes 2560000 | tf_op jit(solution)/shard_map/pallas_call | solution.py:216
  5.1 0.5 %collective-permute-start = (s16[208,512]{1,0:T(8,128)(2,1)}, s16[208,512]{1,0:T(8,128)(2,1)S(1)}, u32[]{:S(2)}, u32[]{:S(2)}) collective-permute-start(s16[208,512]{1,0:T(8,128)(2,1)} %get-tuple-element.42), channel_id=1, source_target_pairs={{0,1},{1,0},{2,3},{3,2},{4,5},{5,4},{6,7},{7,6},{8,9},{9,8},{10,11... | collective-permute-start | bytes 638984 | tf_op jit(solution)/shard_map/ppermute | solution.py:139
  5.6 2.6 %collective-permute-start.1 = (s16[208,512]{1,0:T(8,128)(2,1)}, s16[208,512]{1,0:T(8,128)(2,1)S(1)}, u32[]{:S(2)}, u32[]{:S(2)}) collective-permute-start(s16[208,512]{1,0:T(8,128)(2,1)} %get-tuple-element.43), channel_id=1, source_target_pairs={{0,2},{1,3},{2,0},{3,1},{4,6},{5,7},{6,4},{7,5},{8,10},{9,11},{10,... | collective-permute-start | bytes 638984 | tf_op jit(solution)/shard_map/ppermute | solution.py:139
  8.2 0.1 collective-permute-start.2
  8.3 6.2 %all-to-all-start = ((f32[16,1,400]{2,1,0:T(1,128)}), f32[16,1,400]{2,1,0:T(1,128)S(1)}, u32[]{:S(2)}, u32[]{:S(2)}) async-start(f32[16,1,400]{2,1,0:T(1,128)} %get-tuple-element.45), calls=%async_computation | async-start | bytes 65536 | tf_op jit(solution)/shard_map/all_to_all | solution.py:694
  14.4 0.9 %copy-done.4 = f32[512,1]{1,0:T(8,128)S(1)} copy-done((f32[512,1]{1,0:T(8,128)S(1)}, f32[512,1]{1,0:T(8,128)}, u32[]{:S(2)}) %copy-start.4) | copy-done | bytes 2072
  15.4 0.7 %copy-done.11 = f32[4,1,200]{2,1,0:T(1,128)S(1)} copy-done((f32[4,1,200]{2,1,0:T(1,128)S(1)}, f32[4,1,200]{2,1,0:T(1,128)}, u32[]{:S(2)}) %copy-start.11) | copy-done | bytes 3224
  16.1 0.7 %copy-done.12 = s32[400]{0:T(512)S(1)} copy-done((s32[400]{0:T(512)S(1)}, s32[400]{0:T(512)}, u32[]{:S(2)}) %copy-start.12) | copy-done | bytes 1624
  16.7 0.7 %copy-done.13 = s32[200]{0:T(256)S(1)} copy-done((s32[200]{0:T(256)S(1)}, s32[200]{0:T(256)}, u32[]{:S(2)}) %copy-start.13) | copy-done | bytes 824
  17.4 1.2 %shard_map.119 = (bf16[512,512]{1,0:T(8,128)(2,1)S(1)}, f32[1,512]{1,0:T(1,128)S(1)}, f32[1,128]{1,0:T(1,128)S(1)}, bf16[128,128]{1,0:T(8,128)(2,1)S(1)}, f32[200,1]{1,0:T(8,128)S(1)}, /*index=5*/f32[200,1]{1,0:T(8,128)S(1)}) custom-call(s32[1,400]{1,0:T(1,128)S(1)} %bitcast.3, s32[1,200]{1,0:T(1,128)S(1)} %bitcast.4, f32[4,1,200]{2,1,0:T(1,128)S(1)} %copy-done.11, ...), custom_call_target="tpu_custom_call" | custom-call | tf_op jit(solution)/shard_map/pallas_call | solution.py:381
  18.7 0.6 %copy-done.7 = f32[200,1]{1,0:T(8,128)} copy-done((f32[200,1]{1,0:T(8,128)}, f32[200,1]{1,0:T(8,128)S(1)}, u32[]{:S(2)}) %copy-start.7) | copy-done | bytes 824
  19.3 0.6 %copy-done.9 = bf16[128,128]{1,0:T(8,128)(2,1)} copy-done((bf16[128,128]{1,0:T(8,128)(2,1)}, bf16[128,128]{1,0:T(8,128)(2,1)S(1)}, u32[]{:S(2)}) %copy-start.9) | copy-done | bytes 32792
  19.9 1.2 %all-to-all-done.rest_4_ = f32[16,1,400]{2,1,0:T(1,128)S(1)} async-done(((f32[16,1,400]{2,1,0:T(1,128)}), f32[16,1,400]{2,1,0:T(1,128)S(1)}, u32[]{:S(2)}, u32[]{:S(2)}) %all-to-all-start) | async-done | bytes 25632 | tf_op jit(solution)/shard_map/all_to_all | solution.py:694
  21.1 1.1 %copy-done.5 = s16[208,512]{1,0:T(8,128)(2,1)S(1)} copy-done((s16[208,512]{1,0:T(8,128)(2,1)S(1)}, s16[208,512]{1,0:T(8,128)(2,1)}, u32[]{:S(2)}) %copy-start.5) | copy-done | bytes 213016
  22.2 0.9 %copy-done.8 = f32[200,1]{1,0:T(8,128)S(1)} copy-done((f32[200,1]{1,0:T(8,128)S(1)}, f32[200,1]{1,0:T(8,128)}, u32[]{:S(2)}) %copy-start.8) | copy-done | bytes 824
  23.1 3.7 %shard_map.120 = (s16[208,256]{1,0:T(8,128)(2,1)S(1)}, s16[208,256]{1,0:T(8,128)(2,1)S(1)}, s16[208,256]{1,0:T(8,128)(2,1)S(1)}, s16[208,256]{1,0:T(8,128)(2,1)S(1)}) custom-call(s16[208,512]{1,0:T(8,128)(2,1)S(1)} %copy-done.5, s16[208,512]{1,0:T(8,128)(2,1)S(1)} %collective-permute-done.rest_1_, s16[208,512]{1,0:T(8,128)(2,1)S(1)} %collective-permute-done.1.rest_2_, ...), custom_call_target="tpu_custom_call" | custom-call | flops 384000000 | bytes 6291456 | tf_op jit(solution)/shard_map/pallas_call | solution.py:317
  26.7 0.9 %collective-permute-start.3 = (s16[208,256]{1,0:T(8,128)(2,1)S(1)}, s16[208,256]{1,0:T(8,128)(2,1)S(1)}, u32[]{:S(2)}, u32[]{:S(2)}) collective-permute-start(s16[208,256]{1,0:T(8,128)(2,1)S(1)} %get-tuple-element.65), channel_id=1, source_target_pairs={{0,4},{4,0},{8,12},{12,8},{1,5},{5,1},{9,13},{13,9},{2,6},{6,2},{1... | collective-permute-start | bytes 319496 | tf_op jit(solution)/shard_map/ppermute | solution.py:139
  27.6 2.3 %collective-permute-start.4 = (s16[208,256]{1,0:T(8,128)(2,1)S(1)}, s16[208,256]{1,0:T(8,128)(2,1)S(1)}, u32[]{:S(2)}, u32[]{:S(2)}) collective-permute-start(s16[208,256]{1,0:T(8,128)(2,1)S(1)} %get-tuple-element.67), channel_id=1, source_target_pairs={{0,8},{4,12},{8,0},{12,4},{1,9},{5,13},{9,1},{13,5},{2,10},{6,14},... | collective-permute-start | bytes 319496 | tf_op jit(solution)/shard_map/ppermute | solution.py:139
  29.9 1.3 %collective-permute-start.5 = (s16[208,256]{1,0:T(8,128)(2,1)S(1)}, s16[208,256]{1,0:T(8,128)(2,1)S(1)}, u32[]{:S(2)}, u32[]{:S(2)}) collective-permute-start(s16[208,256]{1,0:T(8,128)(2,1)S(1)} %get-tuple-element.68), channel_id=1, source_target_pairs={{0,12},{4,8},{8,4},{12,0},{1,13},{5,9},{9,5},{13,1},{2,14},{6,10},... | collective-permute-start | bytes 319496 | tf_op jit(solution)/shard_map/ppermute | solution.py:139
  31.2 0.9 %copy-done.2 = f32[3,104,128]{2,1,0:T(8,128)S(1)} copy-done((f32[3,104,128]{2,1,0:T(8,128)S(1)}, f32[3,104,128]{2,1,0:T(8,128)}, u32[]{:S(2)}) %copy-start.2) | copy-done | bytes 159768
  32.1 5.0 %shard_map.121 = (f32[832,128]{1,0:T(8,128)S(1)}, f32[832,128]{1,0:T(8,128)S(1)}, f32[26,128]{1,0:T(8,128)S(1)}, f32[4,104,128]{2,1,0:T(8,128)S(1)}, f32[3,104,1...) custom-call(f32[1,128]{1,0:T(1,128)S(1)} %get-tuple-element.57.mine_ref.rest_9_, f32[3,104,128]{2,1,0:T(8,128)S(1)} %copy-done.2, ...), custom_call_target="tpu_custom_call" | custom-call | tf_op jit(solution)/shard_map/pallas_call | solution.py:499
  37.2 0.9 %shard_map.122.rest_8_ = f32[832,256]{1,0:T(8,128)S(1)} custom-call(bf16[4,2,832,208]{3,2,1,0:T(8,128)(2,1)S(1)} %copy-done, s16[208,256]{1,0:T(8,128)(2,1)S(1)} %get-tuple-element.64.rest_0_, s16[208,256]{1,0:T(8,128)(2,1)S(1)} %collective-permute-done.3.rest_1_), custom_call_target="tpu_custom_call" | custom-call | flops 511180800 | bytes 4194304 | tf_op jit(solution)/shard_map/pallas_call | solution.py:540
  38.1 0.9 %collective-permute-done.4.rest_11_ = s16[208,256]{1,0:T(8,128)(2,1)S(1)} collective-permute-done((s16[208,256]{1,0:T(8,128)(2,1)S(1)}, s16[208,256]{1,0:T(8,128)(2,1)S(1)}, u32[]{:S(2)}, u32[]{:S(2)}) %collective-permute-start.4) | collective-permute-done | bytes 106528 | tf_op jit(solution)/shard_map/ppermute | solution.py:139
  38.9 8.5 %shard_map.123 = f32[100,2,400]{2,1,0:T(2,128)} custom-call(bf16[4,2,832,208]{3,2,1,0:T(8,128)(2,1)S(1)} %copy-done, f32[3,104,128]{2,1,0:T(8,128)S(1)} %copy-done.3, f32[832,128]{1,0:T(8,128)S(1)} %get-tuple-element.58.rest_2_, f32[832,128]{1,0:T(8,128)S(1)} %get-tuple-element.59.rest_3_, f32[26,128]{1,0:T(8,128)S(1)} %get-tuple-element.60.rest_4_, ...), custom_call_target="tpu_custom_call" | custom-call | flops 37273600 | bytes 6291456 | tf_op jit(solution)/shard_map/pallas_call | solution.py:665
  (24 shorter events, 0.1 us)
Async XLA Ops:
  0.0 21.1 %copy-start.1 = (bf16[1,400,3072]{2,1,0:T(8,128)(2,1)S(1)}, bf16[1,400,3072]{2,1,0:T(8,128)(2,1)}, u32[]{:S(2)}) copy-start(bf16[1,400,3072]{2,1,0:T(8,128)(2,1)} %constant.14.clone.rest_5_) | copy-start | bytes 7372804
  5.1 16.0 %collective-permute-start = (s16[208,512]{1,0:T(8,128)(2,1)}, s16[208,512]{1,0:T(8,128)(2,1)S(1)}, u32[]{:S(2)}, u32[]{:S(2)}) collective-permute-start(s16[208,512]{1,0:T(8,128)(2,1)} %get-tuple-element.42), channel_id=1, source_target_pairs={{0,1},{1,0},{2,3},{3,2},{4,5},{5,4},{6,7},{7,6},{8,9},{9,8},{10,11... | collective-permute-start | bytes 638984 | tf_op jit(solution)/shard_map/ppermute | solution.py:139
  5.6 15.4 %collective-permute-start.1 = (s16[208,512]{1,0:T(8,128)(2,1)}, s16[208,512]{1,0:T(8,128)(2,1)S(1)}, u32[]{:S(2)}, u32[]{:S(2)}) collective-permute-start(s16[208,512]{1,0:T(8,128)(2,1)} %get-tuple-element.43), channel_id=1, source_target_pairs={{0,2},{1,3},{2,0},{3,1},{4,6},{5,7},{6,4},{7,5},{8,10},{9,11},{10,... | collective-permute-start | bytes 638984 | tf_op jit(solution)/shard_map/ppermute | solution.py:139
  8.2 12.9 %collective-permute-start.2 = (s16[208,512]{1,0:T(8,128)(2,1)}, s16[208,512]{1,0:T(8,128)(2,1)}, u32[]{:S(2)}, u32[]{:S(2)}) collective-permute-start(s16[208,512]{1,0:T(8,128)(2,1)} %get-tuple-element.44), channel_id=1, source_target_pairs={{0,3},{1,2},{2,1},{3,0},{4,7},{5,6},{6,5},{7,4},{8,11},{9,10},{10,... | collective-permute-start | bytes 638984 | tf_op jit(solution)/shard_map/ppermute | solution.py:139
  8.3 12.8 %all-to-all-start = ((f32[16,1,400]{2,1,0:T(1,128)}), f32[16,1,400]{2,1,0:T(1,128)S(1)}, u32[]{:S(2)}, u32[]{:S(2)}) async-start(f32[16,1,400]{2,1,0:T(1,128)} %get-tuple-element.45), calls=%async_computation | async-start | bytes 65536 | tf_op jit(solution)/shard_map/all_to_all | solution.py:694
  14.4 1.0 %copy-start.4 = (f32[512,1]{1,0:T(8,128)S(1)}, f32[512,1]{1,0:T(8,128)}, u32[]{:S(2)}) copy-start(f32[512,1]{1,0:T(8,128)} %constant.13.clone.spot_ref) | copy-start | bytes 6148
  15.4 0.7 %copy-start.11 = (f32[4,1,200]{2,1,0:T(1,128)S(1)}, f32[4,1,200]{2,1,0:T(1,128)}, u32[]{:S(2)}) copy-start(f32[4,1,200]{2,1,0:T(1,128)} %constant.12.clone.sine_ref) | copy-start | bytes 9604
  16.1 0.7 %copy-start.12 = (s32[400]{0:T(512)S(1)}, s32[400]{0:T(512)}, u32[]{:S(2)}) copy-start(s32[400]{0:T(512)} %param.16) | copy-start | bytes 4804
  16.7 0.7 %copy-start.13 = (s32[200]{0:T(256)S(1)}, s32[200]{0:T(256)}, u32[]{:S(2)}) copy-start(s32[200]{0:T(256)} %param.15) | copy-start | bytes 2404
  18.7 0.6 %copy-start.7 = (f32[200,1]{1,0:T(8,128)}, f32[200,1]{1,0:T(8,128)S(1)}, u32[]{:S(2)}) copy-start(f32[200,1]{1,0:T(8,128)S(1)} %get-tuple-element.51.rest_9_) | copy-start | bytes 2404
  19.3 0.6 %copy-start.9 = (bf16[128,128]{1,0:T(8,128)(2,1)}, bf16[128,128]{1,0:T(8,128)(2,1)S(1)}, u32[]{:S(2)}) copy-start(bf16[128,128]{1,0:T(8,128)(2,1)S(1)} %get-tuple-element.66.rest_10_) | copy-start | bytes 98308
  21.0 16.1 %copy-start = (bf16[4,2,832,208]{3,2,1,0:T(8,128)(2,1)S(1)}, bf16[4,2,832,208]{3,2,1,0:T(8,128)(2,1)}, u32[]{:S(2)}) copy-start(bf16[4,2,832,208]{3,2,1,0:T(8,128)(2,1)} %constant.17.clone.table_ref.rest_0_) | copy-start | bytes 8306692
  21.1 1.1 %copy-start.5 = (s16[208,512]{1,0:T(8,128)(2,1)S(1)}, s16[208,512]{1,0:T(8,128)(2,1)}, u32[]{:S(2)}) copy-start(s16[208,512]{1,0:T(8,128)(2,1)} %get-tuple-element.41.rest_0_) | copy-start | bytes 638980
  22.2 0.9 %copy-start.8 = (f32[200,1]{1,0:T(8,128)S(1)}, f32[200,1]{1,0:T(8,128)}, u32[]{:S(2)}) copy-start(f32[200,1]{1,0:T(8,128)} %copy-done.7) | copy-start | bytes 2404
  23.1 8.1 %copy-start.6 = (f32[400,128]{1,0:T(8,128)S(1)}, f32[400,128]{1,0:T(8,128)}, u32[]{:S(2)}) copy-start(f32[400,128]{1,0:T(8,128)} %constant.16.clone.term_ref) | copy-start | bytes 614404
  23.1 15.9 %copy-start.3 = (f32[3,104,128]{2,1,0:T(8,128)S(1)}, f32[3,104,128]{2,1,0:T(8,128)}, u32[]{:S(2)}) copy-start(f32[3,104,128]{2,1,0:T(8,128)} %constant.15.clone.lat_ref.rest_1_) | copy-start | bytes 479236
  23.1 15.9 %copy-start.10 = (bf16[128,128]{1,0:T(8,128)(2,1)S(1)}, bf16[128,128]{1,0:T(8,128)(2,1)}, u32[]{:S(2)}) copy-start(bf16[128,128]{1,0:T(8,128)(2,1)} %copy-done.9) | copy-start | bytes 98308
  26.7 10.4 %collective-permute-start.3 = (s16[208,256]{1,0:T(8,128)(2,1)S(1)}, s16[208,256]{1,0:T(8,128)(2,1)S(1)}, u32[]{:S(2)}, u32[]{:S(2)}) collective-permute-start(s16[208,256]{1,0:T(8,128)(2,1)S(1)} %get-tuple-element.65), channel_id=1, source_target_pairs={{0,4},{4,0},{8,12},{12,8},{1,5},{5,1},{9,13},{13,9},{2,6},{6,2},{1... | collective-permute-start | bytes 319496 | tf_op jit(solution)/shard_map/ppermute | solution.py:139
  27.6 11.3 %collective-permute-start.4 = (s16[208,256]{1,0:T(8,128)(2,1)S(1)}, s16[208,256]{1,0:T(8,128)(2,1)S(1)}, u32[]{:S(2)}, u32[]{:S(2)}) collective-permute-start(s16[208,256]{1,0:T(8,128)(2,1)S(1)} %get-tuple-element.67), channel_id=1, source_target_pairs={{0,8},{4,12},{8,0},{12,4},{1,9},{5,13},{9,1},{13,5},{2,10},{6,14},... | collective-permute-start | bytes 319496 | tf_op jit(solution)/shard_map/ppermute | solution.py:139
  29.9 9.0 %collective-permute-start.5 = (s16[208,256]{1,0:T(8,128)(2,1)S(1)}, s16[208,256]{1,0:T(8,128)(2,1)S(1)}, u32[]{:S(2)}, u32[]{:S(2)}) collective-permute-start(s16[208,256]{1,0:T(8,128)(2,1)S(1)} %get-tuple-element.68), channel_id=1, source_target_pairs={{0,12},{4,8},{8,4},{12,0},{1,13},{5,9},{9,5},{13,1},{2,14},{6,10},... | collective-permute-start | bytes 319496 | tf_op jit(solution)/shard_map/ppermute | solution.py:139
  31.2 0.9 %copy-start.2 = (f32[3,104,128]{2,1,0:T(8,128)S(1)}, f32[3,104,128]{2,1,0:T(8,128)}, u32[]{:S(2)}) copy-start(f32[3,104,128]{2,1,0:T(8,128)} %constant.15.clone.lat_ref.rest_1_) | copy-start | bytes 479236

commit v15 on v14

--- a/solution.py
+++ b/solution.py
@@ -64,11 +64,19 @@
     return [*tables, shaped([cosine, -sine]), shaped([-sign * sine, -sign * cosine])]
 
 
-def column_waves():
-    columns = []
-    for waves in (np.arange(0, M, 4), np.arange(2, M, 4), np.arange(1, M, 2)):
-        columns.append(np.pad(waves, (0, -len(waves) % LANES), constant_values=-1))
-    return np.concatenate(columns).astype(np.float32)[:, None]
+def column_waves(shape):
+    row = lax.broadcasted_iota(jnp.int32, shape, 0)
+    waves, first = jnp.full(shape, -1, jnp.int32), 0
+    for start, step in ((0, 4), (2, 4), (1, 2)):
+        count = len(range(start, M, step))
+        inside = (row >= first) & (row < first + count)
+        waves = jnp.where(inside, start + step * (row - first), waves)
+        first += -(-count // LANES) * LANES
+    return waves.astype(jnp.float32)
+
+
+def column_count():
+    return sum(-(-len(range(start, M, step)) // LANES) * LANES for start, step in ((0, 4), (2, 4), (1, 2)))
 
 
 def resample_table():
@@ -84,7 +92,7 @@
         for sign in (1.0, -1.0):
             folded = (full[:half] + sign * full[::-1][:half]).reshape(2, half // 2, NLAT)
             rows.append(np.pad(folded, ((0, 0), (0, -half // 2 % 8), (0, 0))).reshape(-1, NLAT))
-    return np.concatenate(rows, axis=0)
+    return np.concatenate(rows, axis=0) * (np.sin(fine) * math.sqrt(2.0 / NLAT))
 
 
 def latitude_table():
@@ -139,29 +147,34 @@
     return [blocks[0]] + [lax.ppermute(blocks[step], axis, pairs[step]) for step in range(1, count)]
 
 
-def advect_kernel(ring, lat_count, tracer_hbm, east_hbm, north_hbm, *rest):
+def advect_kernel(ring, lat_count, keep_ref, tracer_hbm, east_hbm, north_hbm, *rest):
     levels, rows, lons = tracer_hbm.shape
-    outs, (edge_ref, tracer, east_wind, north_wind, sems) = rest[:levels], rest[levels:]
+    outs, (edge_ref, tracer, east_wind, north_wind, blocks, sems) = rest[:levels], rest[levels:]
     chosen = [partner(*ring, step) for step in range(levels)]
-    copies = []
-    for step, level in enumerate(chosen):
-        copies.append(
-            [
-                pltpu.make_async_copy(source.at[level], target.at[step], sems.at[step, kind])
-                for kind, (source, target) in enumerate(
-                    ((tracer_hbm, tracer), (east_hbm, east_wind), (north_hbm, north_wind))
-                )
-            ]
-        )
-        for copy in copies[-1]:
+    copies = [None] * levels
+    order = (*range(levels // 2, levels), *range(levels // 2))
+    for step in order:
+        copies[step] = [
+            pltpu.make_async_copy(source.at[chosen[step]], target.at[step], sems.at[kind, step])
+            for kind, (source, target) in enumerate(
+                ((tracer_hbm, tracer), (east_hbm, east_wind), (north_hbm, north_wind))
+            )
+        ]
+        for copy in copies[step]:
             copy.start()
     padded_rows = outs[0].shape[0]
+    same = (rows, rows)
+    same = lax.broadcasted_iota(jnp.int32, same, 0) == lax.broadcasted_iota(jnp.int32, same, 1)
+    keep = jnp.broadcast_to(keep_ref[...].astype(jnp.float32), (rows, rows))
+    keep = jnp.sum(jnp.where(same, keep, 0.0), axis=1, keepdims=True)
     end = (lons - 1) // LANES * LANES
     spare = lons - end
     lane = lax.broadcasted_iota(jnp.int32, (rows, LANES), 1)
     lat_index = lax.axis_index("lat")
     edge_ref[...] = jnp.zeros_like(edge_ref)
-    for step, level in enumerate(chosen):
+    written = []
+    for step in order:
+        level = chosen[step]
         for copy in copies[step]:
             copy.wait()
         field = tracer[step].astype(jnp.float32)
@@ -196,6 +209,7 @@
         winds = jnp.where(lane == spare + 3, eastward[:, :1], eastward[:, lons - 1 :])
         winds = coded(winds, 1.0 / WIND_STEP)
         tile = jnp.where((lane == spare + 3) | (lane == spare + 4), winds, tile)
+        tile = jnp.where(lane == spare + 5, keep, tile)
         wind_rows = jnp.concatenate([northward[:1], northward[rows - 1 :]], axis=0)
         wind_rows = coded(wind_rows, 1.0 / WIND_STEP)
         blank = jnp.zeros((padded_rows - rows - 2, lons), jnp.float32)
@@ -203,11 +217,15 @@
         filler = jnp.zeros((padded_rows - rows, LANES - spare), jnp.float32)
         wind_tile = jnp.concatenate([wind_rows[:, end:], filler], axis=1)
         steps = jnp.concatenate([coded(moved[:, :end], inverse), wind_rows[:, :end]], axis=0)
-        outs[step][:, :end] = as_int16(steps)
-        outs[step][:, end:] = as_int16(jnp.concatenate([tile, wind_tile], axis=0))
-
-
-def advect(tracer, east_wind, north_wind, ring):
+        blocks[step, :, :end] = as_int16(steps)
+        blocks[step, :, end:] = as_int16(jnp.concatenate([tile, wind_tile], axis=0))
+        written.append(pltpu.make_async_copy(blocks.at[step], outs[step], sems.at[3, step]))
+        written[-1].start()
+    for copy in written:
+        copy.wait()
+
+
+def advect(tracer, east_wind, north_wind, keep_m, ring):
     levels, rows, lons = tracer.shape
     lat_count = lax.axis_size("lat")
     width = (lons - 1) // LANES * LANES + LANES
@@ -217,20 +235,21 @@
         functools.partial(advect_kernel, ring, lat_count),
         out_shape=[jax.ShapeDtypeStruct((padded_rows, width), jnp.int16)] * levels
         + [jax.ShapeDtypeStruct((lat_count * levels, 1, lons), jnp.float32)],
-        in_specs=[HBM_SPEC] * 3,
-        out_specs=[VMEM_SPEC] * (levels + 1),
-        scratch_shapes=[held, held, held, pltpu.SemaphoreType.DMA((levels, 3))],
+        in_specs=[VMEM_SPEC] + [HBM_SPEC] * 3,
+        out_specs=[HBM_SPEC] * levels + [VMEM_SPEC],
+        scratch_shapes=[held, held, held]
+        + [pltpu.VMEM((levels, padded_rows, width), jnp.int16), pltpu.SemaphoreType.DMA((4, levels))],
         compiler_params=pltpu.CompilerParams(vmem_limit_bytes=VMEM_BYTES),
         cost_estimate=pl.CostEstimate(
-            flops=20 * levels * rows * lons, bytes_accessed=8 * levels * rows * lons, transcendentals=0
+            flops=5 * 10**9, bytes_accessed=8 * levels * rows * lons, transcendentals=0
         ),
-    )(tracer, east_wind, north_wind)
+    )(keep_m[None], tracer, east_wind, north_wind)
     return list(result[:levels]), result[levels]
 
 
 def fourier_kernel(ring, lat_count, pieces, *rest):
-    grids, (edge_ref, table_ref, place_ref, wave_ref, keep_ref, sine_ref) = rest[:pieces], rest[pieces : pieces + 6]
-    outs, field = rest[pieces + 6 : -1], rest[-1]
+    grids, (edge_ref, table_ref, place_ref, wave_ref) = rest[:pieces], rest[pieces : pieces + 4]
+    outs, field = rest[pieces + 4 : -1], rest[-1]
     _, rows, width = field.shape
     lons = table_ref.shape[1]
     share = pieces // 4
@@ -245,6 +264,7 @@
         values = from_int16(grids[piece][...])
         tile = values[:rows, end:]
         scale = scale_of(tile[:, spare : spare + 1])
+        keep = tile[:, spare + 5 : spare + 6]
         field[spot, :, :end] = values[:rows, :end] * scale
         field[spot, :, end:] = tile * jnp.where(winds, WIND_STEP, scale)
         wind_rows = values[rows : rows + 2, :lons] * WIND_STEP
@@ -297,7 +317,7 @@
         high, low = split_bf16(jnp.concatenate(columns, axis=1))
         value = jnp.dot(high, place_ref[...], preferred_element_type=jnp.float32)
         value += jnp.dot(low, place_ref[...], preferred_element_type=jnp.float32)
-        kept = jnp.where(wave_ref[...] < keep_ref[...], value * sine_ref[...], 0.0)
+        kept = jnp.where(wave_ref[...] < keep, value, 0.0)
         code = scale_code(jnp.max(jnp.abs(kept), axis=0, keepdims=True))
         steps = coded(kept, 1.0 / scale_of(code))
         codes = jnp.broadcast_to(code, (outs[0].shape[0] - rows, code.shape[1]))
@@ -308,30 +328,25 @@
             outs[target][:, part * LANES : (part + 1) * LANES] = placed[part][:, cols]
 
 
-def fourier(grids, edges, ring, places, wave_row, keep_col, sine_col, lat_count):
+def fourier(grids, edges, ring, places, wave_row, rows, lat_count):
     pieces = len(grids)
-    rows = keep_col.shape[0]
     width = grids[0].shape[1]
     padded_rows = -(-(rows + 1) // 16) * 16
     tables = [table_bf16(table) for table in fourier_tables(pieces)]
     return pl.pallas_call(
         functools.partial(fourier_kernel, ring, lat_count, pieces),
         out_shape=[jax.ShapeDtypeStruct((padded_rows, 2 * LANES), jnp.int16)] * lat_count,
-        in_specs=[VMEM_SPEC] * (pieces + 6),
+        in_specs=[VMEM_SPEC] * (pieces + 4),
         out_specs=[VMEM_SPEC] * lat_count,
         scratch_shapes=[pltpu.VMEM((pieces, rows, width), jnp.float32)],
         compiler_params=pltpu.CompilerParams(vmem_limit_bytes=MIDDLE_BYTES),
         cost_estimate=pl.CostEstimate(
-            flops=3 * rows * NLON * M, bytes_accessed=6 * 2**20, transcendentals=0
+            flops=4 * 10**9, bytes_accessed=6 * 2**20, transcendentals=0
         ),
-    )(*grids, edges, np.concatenate(tables, axis=-1), places, wave_row, keep_col, sine_col)
-
-
-def places_kernel(
-    slot_ref, keep_ref, sine_ref, spot_ref,
-    place_ref, wave_ref, mine_ref, back_ref, keep_col, sine_col, sorted_rows,
-):
-    groups, _, rows = sine_ref.shape
+    )(*grids, edges, np.concatenate(tables, axis=-1), places, wave_row)
+
+
+def places_kernel(groups, slot_ref, place_ref, wave_ref, mine_ref, sorted_rows):
     lat_index = lax.axis_index("lat")
     slots = slot_ref.shape[1] // groups
     paired = (slots + 1) // 2
@@ -340,8 +355,9 @@
     across = lax.broadcasted_iota(jnp.int32, shape, 1)
     filler = jnp.full((1, LANES - slots), 2.0 * M, jnp.float32)
     for group in range(groups):
-        row = slot_ref[:, group * slots : (group + 1) * slots].astype(jnp.float32)
-        row = jnp.broadcast_to(jnp.concatenate([row, filler], axis=1), shape)
+        plain = slot_ref[:, group * slots : (group + 1) * slots].astype(jnp.float32)
+        plain = jnp.concatenate([plain, filler], axis=1)
+        row = jnp.broadcast_to(plain, shape)
         column = jnp.sum(jnp.where(down == across, row, 0.0), axis=1, keepdims=True)
         ahead = (row < column) | ((row == column) & (across < down))
         rank = jnp.sum(jnp.where(ahead, 1.0, 0.0), axis=1, keepdims=True)
@@ -355,47 +371,32 @@
 
         @pl.when(group == lat_index)
         def _():
-            mine_ref[...] = values
-            back_ref[...] = hot.astype(jnp.bfloat16)
-
-    spots = jnp.broadcast_to(spot_ref[...], (spot_ref.shape[0], LANES))
+            mine_ref[:1] = values
+            mine_ref[1:] = plain
+
+    spots = column_waves((place_ref.shape[0], LANES))
     for step in range(groups):
         row = sorted_rows[partner(("lat",), (groups,), step), :1]
         cols = slice(step * LANES, (step + 1) * LANES)
         wave_ref[:, cols] = row
         place_ref[:, cols] = jnp.where(spots == row, 1.0, 0.0).astype(jnp.bfloat16)
 
-    shape = (rows, rows)
-    same = lax.broadcasted_iota(jnp.int32, shape, 0) == lax.broadcasted_iota(jnp.int32, shape, 1)
-    kept = jnp.broadcast_to(keep_ref[...].astype(jnp.float32), shape)
-    keep_col[...] = jnp.sum(jnp.where(same, kept, 0.0), axis=1, keepdims=True)
-    sine = jnp.broadcast_to(sine_ref[lat_index], shape)
-    sine_col[...] = jnp.sum(jnp.where(same, sine, 0.0), axis=1, keepdims=True)
-
-
-def prepare_places(slot_wave, keep_m, groups):
-    rows = keep_m.shape[0]
-    sines = np.sin(math.pi / NLAT * (np.arange(NLAT) + 0.5)) * math.sqrt(2.0 / NLAT)
-    spots = column_waves()
+
+def prepare_places(slot_wave, groups):
     width = groups * LANES
     return pl.pallas_call(
-        places_kernel,
+        functools.partial(places_kernel, groups),
         out_shape=[
-            jax.ShapeDtypeStruct((spots.shape[0], width), jnp.bfloat16),
+            jax.ShapeDtypeStruct((column_count(), width), jnp.bfloat16),
             jax.ShapeDtypeStruct((1, width), jnp.float32),
-            jax.ShapeDtypeStruct((1, LANES), jnp.float32),
-            jax.ShapeDtypeStruct((LANES, LANES), jnp.bfloat16),
-            jax.ShapeDtypeStruct((rows, 1), jnp.float32),
-            jax.ShapeDtypeStruct((rows, 1), jnp.float32),
+            jax.ShapeDtypeStruct((2, LANES), jnp.float32),
         ],
-        in_specs=[VMEM_SPEC] * 4,
-        out_specs=[VMEM_SPEC] * 6,
+        in_specs=[VMEM_SPEC],
+        out_specs=[VMEM_SPEC] * 3,
         scratch_shapes=[pltpu.VMEM((groups, 8, LANES), jnp.float32)],
         compiler_params=pltpu.CompilerParams(vmem_limit_bytes=MIDDLE_BYTES),
-    )(
-        slot_wave[None], keep_m[None],
-        sines.reshape(groups, 1, rows).astype(np.float32), spots,
-    )
+        cost_estimate=pl.CostEstimate(flops=2 * 10**9, bytes_accessed=2**20, transcendentals=0),
+    )(slot_wave[None])
 
 
 def lane_pairs(row):
@@ -409,9 +410,16 @@
 
 
 def sweep_kernel(
-    mine_ref, lat_ref, term_ref, beta_ref, scale_ref, growth_ref, start_ref, state_ref, values_ref
+    mine_ref, lat_ref,
+    beta_ref, scale_ref, growth_ref, start_ref, state_ref, values_ref, back_ref,
 ):
-    pair = lane_pairs(jnp.broadcast_to(mine_ref[...], (8, LANES)))
+    shape = (LANES, LANES)
+    same = lax.broadcasted_iota(jnp.int32, shape, 0) == lax.broadcasted_iota(jnp.int32, shape, 1)
+    plain = jnp.broadcast_to(mine_ref[1:], shape)
+    plain = jnp.sum(jnp.where(same, plain, 0.0), axis=1, keepdims=True)
+    hot = (plain == mine_ref[:1]) & (plain < 2.0 * M)
+    back_ref[...] = jnp.where(hot, 1.0, 0.0).astype(jnp.bfloat16)
+    pair = lane_pairs(jnp.broadcast_to(mine_ref[:1], (8, LANES)))
     one, two = pair[0][:1], pair[1][:1]
     blocks = growth_ref.shape[0]
     turn = block_count(one)
@@ -435,10 +443,11 @@
             scale_ref[pl.ds(index, blocks, stride=BLOCK)] = jnp.where(order < limit, scale, 0.0)
     growth_ref[...] = scale
 
+    counter = lax.broadcasted_iota(jnp.int32, (M, LANES), 0).astype(jnp.float32) + 1.0
+    terms = jnp.log(1.0 + 0.5 / counter) * (1.0 / math.log(2.0))
     for kind, wave in enumerate((one, two)):
         wave = jnp.minimum(wave, M - 1.0)
-        counter = lax.broadcasted_iota(jnp.int32, term_ref.shape, 0).astype(jnp.float32)
-        norm = jnp.sum(jnp.where(counter <= wave, term_ref[...], 0.0), axis=0, keepdims=True)
+        norm = jnp.sum(jnp.where(counter <= wave, terms, 0.0), axis=0, keepdims=True)
         coarse = lat_ref[1] * wave
         whole = jnp.floor(coarse)
         start_ref[2 * kind] = jnp.exp2(
@@ -492,9 +501,6 @@
     latitudes = latitude_table()
     points = latitudes.shape[1]
     blocks = 2 * -(-M // BLOCK)
-    counter = np.arange(M)
-    terms = np.log1p(0.5 / np.maximum(counter, 1)) * (counter > 0) / math.log(2.0)
-    terms = np.broadcast_to(terms[:, None], (M, LANES)).astype(np.float32)
     orders = jax.ShapeDtypeStruct((blocks * BLOCK, LANES), jnp.float32)
     return pl.pallas_call(
         sweep_kernel,
@@ -505,11 +511,15 @@
             jax.ShapeDtypeStruct((4, points, LANES), jnp.float32),
             jax.ShapeDtypeStruct((3, points, LANES), jnp.float32),
             jax.ShapeDtypeStruct((HELD, BLOCK, points, LANES), jnp.float32),
+            jax.ShapeDtypeStruct((LANES, LANES), jnp.bfloat16),
         ],
-        in_specs=[VMEM_SPEC] * 3,
-        out_specs=[VMEM_SPEC] * 6,
+        in_specs=[VMEM_SPEC] * 2,
+        out_specs=[VMEM_SPEC] * 7,
         compiler_params=pltpu.CompilerParams(vmem_limit_bytes=late_bytes(pieces)),
-    )(mine, latitudes, terms)
+        cost_estimate=pl.CostEstimate(
+            flops=5 * 10**9, bytes_accessed=25 * 2**20, transcendentals=0
+        ),
+    )(mine, latitudes)
 
 
 def resampled(first, fields, table, total):
@@ -544,18 +554,18 @@
         out_specs=VMEM_SPEC,
         compiler_params=pltpu.CompilerParams(vmem_limit_bytes=late_bytes(count)),
         cost_estimate=pl.CostEstimate(
-            flops=6 * height * span * NLAT // count * len(fields), bytes_accessed=4 * 2**20, transcendentals=0
+            flops=10**9, bytes_accessed=4 * 2**20, transcendentals=0
         ),
     )(table, *fields)
 
 
 def legendre_kernel(early, *rest):
-    table, lat_ref, beta_ref, scale_ref, growth_ref, start_ref, left_ref, values_ref = rest[:8]
-    total_ref, mine_ref, back_ref = rest[8:11]
+    table, lat_ref, beta_ref, scale_ref, growth_ref, start_ref, left_ref, values_ref, back_ref = rest[:9]
+    total_ref, mine_ref = rest[9:11]
     fields, (out_ref, weights, state_ref, sums, result, final) = rest[11:-6], rest[-6:]
     points = lat_ref.shape[1]
     slots = out_ref.shape[0]
-    mine = mine_ref[...]
+    mine = mine_ref[:1]
     odd = mine - 2.0 * jnp.floor(mine * 0.5) > 0.5
     pair = lane_pairs(jnp.broadcast_to(mine, (8, LANES)))
     turn = block_count(pair[0][:1])
@@ -654,7 +664,7 @@
     return table.reshape(pieces, full.shape[0], 2, padded_rows).transpose(0, 2, 1, 3)
 
 
-def legendre(fields, mine, back, prepared, rows, slots):
+def legendre(fields, mine, prepared, rows, slots):
     pieces = len(fields)
     early = pieces // 2
     latitudes = latitude_table()
@@ -676,9 +686,9 @@
         ],
         compiler_params=pltpu.CompilerParams(vmem_limit_bytes=late_bytes(pieces)),
         cost_estimate=pl.CostEstimate(
-            flops=7 * points * LANES * M, bytes_accessed=6 * 2**20, transcendentals=0
+            flops=8 * 10**9, bytes_accessed=6 * 2**20, transcendentals=0
         ),
-    )(table, latitudes, *prepared, total, mine, back, *fields[early:])
+    )(table, latitudes, *prepared, total, mine, *fields[early:])
 
 
 def shards(tracer, wind_east, wind_north, keep_m, slot_wave):
@@ -688,16 +698,16 @@
     axes = ("lev", "fld")
     ring = (axes, tuple(lax.axis_size(axis) for axis in axes))
 
-    blocks, edges = advect(tracer, wind_east, wind_north, ring)
-    blocks, slot_wave, keep_m = lax.optimization_barrier((blocks, slot_wave, keep_m))
+    blocks, edges = advect(tracer, wind_east, wind_north, keep_m, ring)
+    blocks, slot_wave = lax.optimization_barrier((blocks, slot_wave))
     grids = exchange(blocks, axes)
     edges = lax.all_to_all(edges, ("lat", *axes), split_axis=0, concat_axis=0, tiled=True)
-    places, wave_row, mine, back, keep_col, sine_col = prepare_places(slot_wave, keep_m, lat_count)
-    waved = fourier(grids, edges, ring, places, wave_row, keep_col, sine_col, lat_count)
+    places, wave_row, mine = prepare_places(slot_wave, lat_count)
+    waved = fourier(grids, edges, ring, places, wave_row, rows, lat_count)
     waved, mine = lax.optimization_barrier((list(waved), mine))
     fields = exchange(waved, "lat")
     prepared = prepare_recurrence(mine, lat_count)
-    return legendre(fields, mine, back, prepared, rows, slots)[None]
+    return legendre(fields, mine, prepared, rows, slots)[None]
 
 
 def solution(mesh):

time: 48.1 us -> 46.7 us (0.971)
  local copies, waits for them, and re-layouts: 7.14 us -> 1.86 us
  waiting for transfers between devices: 2.02 us -> 5.86 us
    unnamed x28 -> x14, local copies, waits for them, and re-layouts: 7.14 us -> 1.86 us
    all_to_all x1, waiting for transfers between devices: 1.15 us -> 4.68 us  [shards(): lax.all_to_all(edges, ('lat', *axes), split_axis=0, concat_axis=0, tiled=...]
    pallas_call x1, Pallas kernels: 5.09 us -> 6.29 us  [advect(): pl.pallas_call(functools.partial(advect_kernel, ring, lat_count), out_sha...]
    pallas_call x1, Pallas kernels: 3.66 us -> 2.73 us  [fourier(): pl.pallas_call(functools.partial(fourier_kernel, ring, lat_count, pieces)...]
where the time goes in v15:
time: 46.7 us; the launch traced here: 46.1 us
  Pallas kernels  24.5 us (52%)
  starting transfers between devices  13.8 us (30%)
  waiting for transfers between devices  5.86 us (13%)
  local copies, waits for them, and re-layouts  1.86 us (4%)
    pallas_call x1, Pallas kernels, legendre(): pl.pallas_call(functools.partial(legendre_kernel, early), out_shape=jax.S...  8.4 us
    ppermute x6, starting transfers between devices, exchange(): lax.ppermute(blocks[step], axis, pairs[step])  7.6 us
    pallas_call x1, Pallas kernels, advect(): pl.pallas_call(functools.partial(advect_kernel, ring, lat_count), out_sha...  6.29 us
    all_to_all x1, starting transfers between devices, shards(): lax.all_to_all(edges, ('lat', *axes), split_axis=0, concat_axis=0, tiled=...  6.16 us
    pallas_call x1, Pallas kernels, prepare_recurrence(): pl.pallas_call(sweep_kernel, out_shape=[orders, orders, jax.ShapeDtypeStr...  5.13 us
    all_to_all x1, waiting for transfers between devices, shards(): lax.all_to_all(edges, ('lat', *axes), split_axis=0, concat_axis=0, tiled=...  4.68 us
    pallas_call x1, Pallas kernels, fourier(): pl.pallas_call(functools.partial(fourier_kernel, ring, lat_count, pieces)...  2.73 us
    unnamed x14, local copies, waits for them, and re-layouts  1.86 us
  transfers between devices with their start and end apart: 7, of which 2 were waited for; matrix products, arithmetic and copies ran while one was open for 0% of the time, Pallas kernels for 15%

profile of v15, /device:TPU:0, one launch (start us, length us, event | category | flops | bytes accessed | tf_op | source)
XLA Modules:
  0.0 46.1 jit_solution(3529761501082783042)
XLA Ops:
  0.0 6.3 %shard_map.91 = (s16[208,512]{1,0:T(8,128)(2,1)}, s16[208,512]{1,0:T(8,128)(2,1)}, s16[208,512]{1,0:T(8,128)(2,1)}, s16[208,512]{1,0:T(8,128)(2,1)}, f32[16,1,400]{2,1,0:T(1,128)}) custom-call(s32[1,200]{1,0:T(1,128)} %bitcast.4, bf16[4,200,400]{2,1,0:T(8,128)(2,1)} %tracer_hbm.1, bf16[4,200,400]{2,1,0:T(8,128)(2,1)} %east_hbm.1, bf16[4,200,400]{2,1,0:T(8,128)(2,1)} %north_hbm.1), custom_call_target="tpu_custom_call" | custom-call | flops 5000000000 | bytes 2560000 | tf_op jit(solution)/shard_map/pallas_call | solution.py:234
  6.3 0.5 %collective-permute-start = (s16[208,512]{1,0:T(8,128)(2,1)}, s16[208,512]{1,0:T(8,128)(2,1)S(1)}, u32[]{:S(2)}, u32[]{:S(2)}) collective-permute-start(s16[208,512]{1,0:T(8,128)(2,1)} %get-tuple-element.39), channel_id=1, source_target_pairs={{0,1},{1,0},{2,3},{3,2},{4,5},{5,4},{6,7},{7,6},{8,9},{9,8},{10,11... | collective-permute-start | bytes 638984 | tf_op jit(solution)/shard_map/ppermute | solution.py:147
  6.8 2.6 %collective-permute-start.1 = (s16[208,512]{1,0:T(8,128)(2,1)}, s16[208,512]{1,0:T(8,128)(2,1)S(1)}, u32[]{:S(2)}, u32[]{:S(2)}) collective-permute-start(s16[208,512]{1,0:T(8,128)(2,1)} %get-tuple-element.40), channel_id=1, source_target_pairs={{0,2},{1,3},{2,0},{3,1},{4,6},{5,7},{6,4},{7,5},{8,10},{9,11},{10,... | collective-permute-start | bytes 638984 | tf_op jit(solution)/shard_map/ppermute | solution.py:147
  9.4 0.1 collective-permute-start.2
  9.5 6.2 %all-to-all-start = ((f32[16,1,400]{2,1,0:T(1,128)}), f32[16,1,400]{2,1,0:T(1,128)S(1)}, u32[]{:S(2)}, u32[]{:S(2)}) async-start(f32[16,1,400]{2,1,0:T(1,128)} %get-tuple-element.42), calls=%async_computation | async-start | bytes 65536 | tf_op jit(solution)/shard_map/all_to_all | solution.py:704
  15.6 0.0 copy-start.2
  15.6 0.0 copy-start.6
  15.7 1.1 %shard_map.92 = (bf16[512,512]{1,0:T(8,128)(2,1)S(1)}, f32[1,512]{1,0:T(1,128)S(1)}, f32[2,128]{1,0:T(2,128)S(1)}) custom-call(s32[1,400]{1,0:T(1,128)S(1)} %bitcast.3), custom_call_target="tpu_custom_call" | custom-call | flops 2000000000 | bytes 1048576 | tf_op jit(solution)/shard_map/pallas_call | solution.py:387
  16.8 0.8 %copy-done.4 = bf16[512,512]{1,0:T(8,128)(2,1)} copy-done((bf16[512,512]{1,0:T(8,128)(2,1)}, bf16[512,512]{1,0:T(8,128)(2,1)S(1)}, u32[]{:S(2)}) %copy-start.4) | copy-done | bytes 524312
  17.6 4.7 %all-to-all-done.rest_4_ = f32[16,1,400]{2,1,0:T(1,128)S(1)} async-done(((f32[16,1,400]{2,1,0:T(1,128)}), f32[16,1,400]{2,1,0:T(1,128)S(1)}, u32[]{:S(2)}, u32[]{:S(2)}) %all-to-all-start) | async-done | bytes 25632 | tf_op jit(solution)/shard_map/all_to_all | solution.py:704
  22.3 0.0 collective-permute-done.rest_1_
  22.3 0.0 collective-permute-done.1.rest_2_
  22.3 0.0 collective-permute-done.2.rest_3_
  22.3 1.0 %copy-done.5 = bf16[512,512]{1,0:T(8,128)(2,1)S(1)} copy-done((bf16[512,512]{1,0:T(8,128)(2,1)S(1)}, bf16[512,512]{1,0:T(8,128)(2,1)}, u32[]{:S(2)}) %copy-start.5) | copy-done | bytes 524312
  23.3 2.7 %shard_map.93 = (s16[208,256]{1,0:T(8,128)(2,1)S(1)}, s16[208,256]{1,0:T(8,128)(2,1)S(1)}, s16[208,256]{1,0:T(8,128)(2,1)S(1)}, s16[208,256]{1,0:T(8,128)(2,1)S(1)}) custom-call(s16[208,512]{1,0:T(8,128)(2,1)S(1)} %copy-done.6, s16[208,512]{1,0:T(8,128)(2,1)S(1)} %collective-permute-done.rest_1_, s16[208,512]{1,0:T(8,128)(2,1)S(1)} %collective-permute-done.1.rest_2_, ...), custom_call_target="tpu_custom_call" | custom-call | flops 4000000000 | bytes 6291456 | tf_op jit(solution)/shard_map/pallas_call | solution.py:336
  26.1 0.0 copy-start
  26.1 0.4 collective-permute-start.3
  26.5 2.1 %collective-permute-start.4 = (s16[208,256]{1,0:T(8,128)(2,1)S(1)}, s16[208,256]{1,0:T(8,128)(2,1)S(1)}, u32[]{:S(2)}, u32[]{:S(2)}) collective-permute-start(s16[208,256]{1,0:T(8,128)(2,1)S(1)} %get-tuple-element.61), channel_id=1, source_target_pairs={{0,8},{4,12},{8,0},{12,4},{1,9},{5,13},{9,1},{13,5},{2,10},{6,14},... | collective-permute-start | bytes 319496 | tf_op jit(solution)/shard_map/ppermute | solution.py:147
  28.7 1.9 %collective-permute-start.5 = (s16[208,256]{1,0:T(8,128)(2,1)S(1)}, s16[208,256]{1,0:T(8,128)(2,1)S(1)}, u32[]{:S(2)}, u32[]{:S(2)}) collective-permute-start(s16[208,256]{1,0:T(8,128)(2,1)S(1)} %get-tuple-element.62), channel_id=1, source_target_pairs={{0,12},{4,8},{8,4},{12,0},{1,13},{5,9},{9,5},{13,1},{2,14},{6,10},... | collective-permute-start | bytes 319496 | tf_op jit(solution)/shard_map/ppermute | solution.py:147
  30.5 5.1 %shard_map.94 = (f32[832,128]{1,0:T(8,128)S(1)}, f32[832,128]{1,0:T(8,128)S(1)}, f32[26,128]{1,0:T(8,128)S(1)}, f32[4,104,128]{2,1,0:T(8,128)S(1)}, f32[3,104,12...) custom-call(f32[2,128]{1,0:T(2,128)S(1)} %get-tuple-element.51.mine_ref.rest_10_, ...), custom_call_target="tpu_custom_call" | custom-call | flops 5000000000 | bytes 26214400 | tf_op jit(solution)/shard_map/pallas_call | solution.py:505
  35.7 0.8 %shard_map.95.rest_9_ = f32[832,256]{1,0:T(8,128)S(1)} custom-call(bf16[4,2,832,208]{3,2,1,0:T(8,128)(2,1)S(1)} %copy-done, s16[208,256]{1,0:T(8,128)(2,1)S(1)} %get-tuple-element.59.rest_0_, s16[208,256]{1,0:T(8,128)(2,1)S(1)} %collective-permute-done.3.rest_1_), custom_call_target="tpu_custom_call" | custom-call | flops 1000000000 | bytes 4194304 | tf_op jit(solution)/shard_map/pallas_call | solution.py:550
  36.6 1.2 %collective-permute-done.4.rest_11_ = s16[208,256]{1,0:T(8,128)(2,1)S(1)} collective-permute-done((s16[208,256]{1,0:T(8,128)(2,1)S(1)}, s16[208,256]{1,0:T(8,128)(2,1)S(1)}, u32[]{:S(2)}, u32[]{:S(2)}) %collective-permute-start.4) | collective-permute-done | bytes 106528 | tf_op jit(solution)/shard_map/ppermute | solution.py:147
  37.7 0.0 collective-permute-done.5.rest_12_
  37.7 8.4 %shard_map.96 = f32[100,2,400]{2,1,0:T(2,128)} custom-call(bf16[4,2,832,208]{3,2,1,0:T(8,128)(2,1)S(1)} %copy-done, f32[3,104,128]{2,1,0:T(8,128)S(1)} %copy-done.3, f32[832,128]{1,0:T(8,128)S(1)} %get-tuple-element.52.rest_2_, f32[832,128]{1,0:T(8,128)S(1)} %get-tuple-element.53.rest_3_, f32[26,128]{1,0:T(8,128)S(1)} %get-tuple-element.54.rest_4_, ...), custom_call_target="tpu_custom_call" | custom-call | flops 8000000000 | bytes 6291456 | tf_op jit(solution)/shard_map/pallas_call | solution.py:675
  (10 shorter events, 0.0 us)
Async XLA Ops:
  0.0 15.6 %copy-start.1 = (s32[400]{0:T(512)S(1)}, s32[400]{0:T(512)}, u32[]{:S(2)}) copy-start(s32[400]{0:T(512)} %param.13) | copy-start | bytes 4804
  6.3 16.0 %collective-permute-start = (s16[208,512]{1,0:T(8,128)(2,1)}, s16[208,512]{1,0:T(8,128)(2,1)S(1)}, u32[]{:S(2)}, u32[]{:S(2)}) collective-permute-start(s16[208,512]{1,0:T(8,128)(2,1)} %get-tuple-element.39), channel_id=1, source_target_pairs={{0,1},{1,0},{2,3},{3,2},{4,5},{5,4},{6,7},{7,6},{8,9},{9,8},{10,11... | collective-permute-start | bytes 638984 | tf_op jit(solution)/shard_map/ppermute | solution.py:147
  6.8 15.4 %collective-permute-start.1 = (s16[208,512]{1,0:T(8,128)(2,1)}, s16[208,512]{1,0:T(8,128)(2,1)S(1)}, u32[]{:S(2)}, u32[]{:S(2)}) collective-permute-start(s16[208,512]{1,0:T(8,128)(2,1)} %get-tuple-element.40), channel_id=1, source_target_pairs={{0,2},{1,3},{2,0},{3,1},{4,6},{5,7},{6,4},{7,5},{8,10},{9,11},{10,... | collective-permute-start | bytes 638984 | tf_op jit(solution)/shard_map/ppermute | solution.py:147
  9.4 12.9 %collective-permute-start.2 = (s16[208,512]{1,0:T(8,128)(2,1)}, s16[208,512]{1,0:T(8,128)(2,1)S(1)}, u32[]{:S(2)}, u32[]{:S(2)}) collective-permute-start(s16[208,512]{1,0:T(8,128)(2,1)} %get-tuple-element.41), channel_id=1, source_target_pairs={{0,3},{1,2},{2,1},{3,0},{4,7},{5,6},{6,5},{7,4},{8,11},{9,10},{10,... | collective-permute-start | bytes 638984 | tf_op jit(solution)/shard_map/ppermute | solution.py:147
  9.5 12.8 %all-to-all-start = ((f32[16,1,400]{2,1,0:T(1,128)}), f32[16,1,400]{2,1,0:T(1,128)S(1)}, u32[]{:S(2)}, u32[]{:S(2)}) async-start(f32[16,1,400]{2,1,0:T(1,128)} %get-tuple-element.42), calls=%async_computation | async-start | bytes 65536 | tf_op jit(solution)/shard_map/all_to_all | solution.py:704
  15.6 6.6 %copy-start.2 = (bf16[1,400,3072]{2,1,0:T(8,128)(2,1)S(1)}, bf16[1,400,3072]{2,1,0:T(8,128)(2,1)}, u32[]{:S(2)}) copy-start(bf16[1,400,3072]{2,1,0:T(8,128)(2,1)} %constant.6.clone.rest_5_) | copy-start | bytes 7372804
  15.6 6.6 %copy-start.6 = (s16[208,512]{1,0:T(8,128)(2,1)S(1)}, s16[208,512]{1,0:T(8,128)(2,1)}, u32[]{:S(2)}) copy-start(s16[208,512]{1,0:T(8,128)(2,1)} %get-tuple-element.38.rest_0_) | copy-start | bytes 638980
  16.8 0.8 %copy-start.4 = (bf16[512,512]{1,0:T(8,128)(2,1)}, bf16[512,512]{1,0:T(8,128)(2,1)S(1)}, u32[]{:S(2)}) copy-start(bf16[512,512]{1,0:T(8,128)(2,1)S(1)} %get-tuple-element.44.rest_6_) | copy-start | bytes 1572868
  22.3 1.0 %copy-start.5 = (bf16[512,512]{1,0:T(8,128)(2,1)S(1)}, bf16[512,512]{1,0:T(8,128)(2,1)}, u32[]{:S(2)}) copy-start(bf16[512,512]{1,0:T(8,128)(2,1)} %copy-done.4) | copy-start | bytes 1572868
  23.3 7.2 %copy-start.3 = (f32[3,104,128]{2,1,0:T(8,128)S(1)}, f32[3,104,128]{2,1,0:T(8,128)}, u32[]{:S(2)}) copy-start(f32[3,104,128]{2,1,0:T(8,128)} %constant.7.clone.lat_ref.rest_1_) | copy-start | bytes 479236
  26.1 9.6 %copy-start = (bf16[4,2,832,208]{3,2,1,0:T(8,128)(2,1)S(1)}, bf16[4,2,832,208]{3,2,1,0:T(8,128)(2,1)}, u32[]{:S(2)}) copy-start(bf16[4,2,832,208]{3,2,1,0:T(8,128)(2,1)} %constant.8.clone.table_ref.rest_0_) | copy-start | bytes 8306692
  26.1 9.6 %collective-permute-start.3 = (s16[208,256]{1,0:T(8,128)(2,1)S(1)}, s16[208,256]{1,0:T(8,128)(2,1)S(1)}, u32[]{:S(2)}, u32[]{:S(2)}) collective-permute-start(s16[208,256]{1,0:T(8,128)(2,1)S(1)} %get-tuple-element.60), channel_id=1, source_target_pairs={{0,4},{4,0},{8,12},{12,8},{1,5},{5,1},{9,13},{13,9},{2,6},{6,2},{1... | collective-permute-start | bytes 319496 | tf_op jit(solution)/shard_map/ppermute | solution.py:147
  26.5 11.2 %collective-permute-start.4 = (s16[208,256]{1,0:T(8,128)(2,1)S(1)}, s16[208,256]{1,0:T(8,128)(2,1)S(1)}, u32[]{:S(2)}, u32[]{:S(2)}) collective-permute-start(s16[208,256]{1,0:T(8,128)(2,1)S(1)} %get-tuple-element.61), channel_id=1, source_target_pairs={{0,8},{4,12},{8,0},{12,4},{1,9},{5,13},{9,1},{13,5},{2,10},{6,14},... | collective-permute-start | bytes 319496 | tf_op jit(solution)/shard_map/ppermute | solution.py:147
  28.7 9.1 %collective-permute-start.5 = (s16[208,256]{1,0:T(8,128)(2,1)S(1)}, s16[208,256]{1,0:T(8,128)(2,1)S(1)}, u32[]{:S(2)}, u32[]{:S(2)}) collective-permute-start(s16[208,256]{1,0:T(8,128)(2,1)S(1)} %get-tuple-element.62), channel_id=1, source_target_pairs={{0,12},{4,8},{8,4},{12,0},{1,13},{5,9},{9,5},{13,1},{2,14},{6,10},... | collective-permute-start | bytes 319496 | tf_op jit(solution)/shard_map/ppermute | solution.py:147

commit v16 on v15

--- a/solution.py
+++ b/solution.py
@@ -15,10 +15,12 @@
 LANES = 128
 BLOCK = 32
 CHUNKS = (40, 32, 32)
-HELD = -(-M // BLOCK)
+SPAN = -(-M // BLOCK)
+HELD = 13
 SIDE = LANES // 2
 TOP = 32767.0
 WIND_STEP = 1.5 / TOP
+EXTRA = 6
 VMEM_BYTES = 60 * 2**20
 LATE_BYTES = 16 * 2**20
 MIDDLE_BYTES = 16 * 2**20
@@ -149,7 +151,7 @@
 
 def advect_kernel(ring, lat_count, keep_ref, tracer_hbm, east_hbm, north_hbm, *rest):
     levels, rows, lons = tracer_hbm.shape
-    outs, (edge_ref, tracer, east_wind, north_wind, blocks, sems) = rest[:levels], rest[levels:]
+    outs, (edge_ref, tracer, east_wind, north_wind, sems) = rest[:levels], rest[levels:]
     chosen = [partner(*ring, step) for step in range(levels)]
     copies = [None] * levels
     order = (*range(levels // 2, levels), *range(levels // 2))
@@ -162,7 +164,7 @@
         ]
         for copy in copies[step]:
             copy.start()
-    padded_rows = outs[0].shape[0]
+    padded_rows, group_rows, packed_rows = block_shape(rows, lons)
     same = (rows, rows)
     same = lax.broadcasted_iota(jnp.int32, same, 0) == lax.broadcasted_iota(jnp.int32, same, 1)
     keep = jnp.broadcast_to(keep_ref[...].astype(jnp.float32), (rows, rows))
@@ -170,9 +172,9 @@
     end = (lons - 1) // LANES * LANES
     spare = lons - end
     lane = lax.broadcasted_iota(jnp.int32, (rows, LANES), 1)
+    group_lane = lax.broadcasted_iota(jnp.int32, (group_rows, LANES), 1)
     lat_index = lax.axis_index("lat")
     edge_ref[...] = jnp.zeros_like(edge_ref)
-    written = []
     for step in order:
         level = chosen[step]
         for copy in copies[step]:
@@ -217,28 +219,44 @@
         filler = jnp.zeros((padded_rows - rows, LANES - spare), jnp.float32)
         wind_tile = jnp.concatenate([wind_rows[:, end:], filler], axis=1)
         steps = jnp.concatenate([coded(moved[:, :end], inverse), wind_rows[:, :end]], axis=0)
-        blocks[step, :, :end] = as_int16(steps)
-        blocks[step, :, end:] = as_int16(jnp.concatenate([tile, wind_tile], axis=0))
-        written.append(pltpu.make_async_copy(blocks.at[step], outs[step], sems.at[3, step]))
-        written[-1].start()
-    for copy in written:
-        copy.wait()
+        outs[step][:padded_rows] = as_int16(steps)
+        tile = jnp.concatenate([tile, wind_tile], axis=0)
+        wide = spare + EXTRA
+        folded = tile[:group_rows]
+        for group in range(1, -(-padded_rows // group_rows)):
+            part = tile[group * group_rows : (group + 1) * group_rows]
+            if part.shape[0] < group_rows:
+                short = jnp.zeros((group_rows - part.shape[0], LANES), jnp.float32)
+                part = jnp.concatenate([part, short], axis=0)
+            part = pltpu.roll(part, group * wide, 1)
+            folded = jnp.where(group_lane >= group * wide, part, folded)
+        share = packed_rows - padded_rows
+        for place in range(end // LANES):
+            part = folded[place * share : (place + 1) * share]
+            outs[step][padded_rows:, place * LANES : (place + 1) * LANES] = as_int16(part)
+
+
+def block_shape(rows, lons):
+    padded_rows = -(-(rows + 2) // 16) * 16
+    tiles = (lons - 1) // LANES
+    groups = LANES // (lons - tiles * LANES + EXTRA)
+    group_rows = -(-padded_rows // groups // (16 * tiles)) * 16 * tiles
+    return padded_rows, group_rows, padded_rows + group_rows // tiles
 
 
 def advect(tracer, east_wind, north_wind, keep_m, ring):
     levels, rows, lons = tracer.shape
     lat_count = lax.axis_size("lat")
-    width = (lons - 1) // LANES * LANES + LANES
-    padded_rows = -(-(rows + 2) // 16) * 16
+    width = (lons - 1) // LANES * LANES
+    packed_rows = block_shape(rows, lons)[2]
     held = pltpu.VMEM((levels, rows, lons), jnp.bfloat16)
     result = pl.pallas_call(
         functools.partial(advect_kernel, ring, lat_count),
-        out_shape=[jax.ShapeDtypeStruct((padded_rows, width), jnp.int16)] * levels
+        out_shape=[jax.ShapeDtypeStruct((packed_rows, width), jnp.int16)] * levels
         + [jax.ShapeDtypeStruct((lat_count * levels, 1, lons), jnp.float32)],
         in_specs=[VMEM_SPEC] + [HBM_SPEC] * 3,
-        out_specs=[HBM_SPEC] * levels + [VMEM_SPEC],
-        scratch_shapes=[held, held, held]
-        + [pltpu.VMEM((levels, padded_rows, width), jnp.int16), pltpu.SemaphoreType.DMA((4, levels))],
+        out_specs=[VMEM_SPEC] * (levels + 1),
+        scratch_shapes=[held, held, held, pltpu.SemaphoreType.DMA((3, levels))],
         compiler_params=pltpu.CompilerParams(vmem_limit_bytes=VMEM_BYTES),
         cost_estimate=pl.CostEstimate(
             flops=5 * 10**9, bytes_accessed=8 * levels * rows * lons, transcendentals=0
@@ -256,18 +274,28 @@
 
     end = width - LANES
     spare = lons - end
+    padded_rows, group_rows, _ = block_shape(rows, lons)
     lane = lax.broadcasted_iota(jnp.int32, (rows, LANES), 1)
     winds = (lane == spare + 3) | (lane == spare + 4)
     lat_index = lax.axis_index("lat")
     for piece in range(pieces):
         spot = partner(*ring, piece)
         values = from_int16(grids[piece][...])
-        tile = values[:rows, end:]
+        folded = [
+            values[padded_rows:, place * LANES : (place + 1) * LANES] for place in range(end // LANES)
+        ]
+        folded = jnp.concatenate(folded, axis=0)
+        groups = range(-(-padded_rows // group_rows))
+        wide = spare + EXTRA
+        tile = [folded] + [pltpu.roll(folded, LANES - group * wide, 1) for group in groups[1:]]
+        tile = jnp.concatenate(tile, axis=0)
+        wind_tile = tile[rows : rows + 2, :spare]
+        tile = tile[:rows]
         scale = scale_of(tile[:, spare : spare + 1])
         keep = tile[:, spare + 5 : spare + 6]
         field[spot, :, :end] = values[:rows, :end] * scale
         field[spot, :, end:] = tile * jnp.where(winds, WIND_STEP, scale)
-        wind_rows = values[rows : rows + 2, :lons] * WIND_STEP
+        wind_rows = jnp.concatenate([values[rows : rows + 2], wind_tile], axis=1) * WIND_STEP
 
         @pl.when(lat_index > 0)
         def _():
@@ -330,7 +358,7 @@
 
 def fourier(grids, edges, ring, places, wave_row, rows, lat_count):
     pieces = len(grids)
-    width = grids[0].shape[1]
+    width = grids[0].shape[1] + LANES
     padded_rows = -(-(rows + 1) // 16) * 16
     tables = [table_bf16(table) for table in fourier_tables(pieces)]
     return pl.pallas_call(
@@ -500,7 +528,7 @@
 def prepare_recurrence(mine, pieces):
     latitudes = latitude_table()
     points = latitudes.shape[1]
-    blocks = 2 * -(-M // BLOCK)
+    blocks = 2 * SPAN
     orders = jax.ShapeDtypeStruct((blocks * BLOCK, LANES), jnp.float32)
     return pl.pallas_call(
         sweep_kernel,
@@ -635,7 +663,7 @@
     lax.fori_loop(HELD, block_total, step, 0)
 
     left = lax.broadcasted_iota(jnp.int32, (BLOCK, LANES), 1) < SIDE
-    spots = -(-M // BLOCK)
+    spots = SPAN
     chosen = [jnp.broadcast_to(turn, (8, LANES)) == value for value in range(spots + 1)]
     chosen = [jnp.concatenate([mask] * (BLOCK // 8), axis=0) for mask in chosen]
     for place in range(spots):
@@ -671,7 +699,7 @@
     points = latitudes.shape[1]
     table = jnp.asarray(resample_pieces(pieces, rows, fields[0].shape[0]))
     total = resample(fields[:early], table)
-    block_rows = -(-M // BLOCK) * BLOCK
+    block_rows = SPAN * BLOCK
     return pl.pallas_call(
         functools.partial(legendre_kernel, early),
         out_shape=jax.ShapeDtypeStruct((slots, 2, M), jnp.float32),

time: 46.7 us -> 49.6 us (1.062)
  waiting for transfers between devices: 5.86 us -> 10 us
  local copies, waits for them, and re-layouts: 1.86 us -> 0.94 us
    ppermute x6, waiting for transfers between devices: 1.18 us -> 6.6 us  [exchange(): lax.ppermute(blocks[step], axis, pairs[step])]
    all_to_all x1, waiting for transfers between devices: 4.68 us -> 3.43 us  [shards(): lax.all_to_all(edges, ('lat', *axes), split_axis=0, concat_axis=0, tiled=...]
    all_to_all x1, starting transfers between devices: 6.16 us -> 7.38 us  [shards(): lax.all_to_all(edges, ('lat', *axes), split_axis=0, concat_axis=0, tiled=...]
    ppermute x6, starting transfers between devices: 7.6 us -> 6.56 us  [exchange(): lax.ppermute(blocks[step], axis, pairs[step])]
    unnamed x14 -> x10, local copies, waits for them, and re-layouts: 1.86 us -> 0.94 us
  transfers between devices with their start and end apart: 7 -> 7, of which waited for: 2 -> 4; matrix products, arithmetic and copies ran while one was open for 0% -> 0% of each run, Pallas kernels for 15% -> 14%
where the time goes in v16:
time: 49.6 us; the launch traced here: 49.3 us
  Pallas kernels  24.3 us (49%)
  starting transfers between devices  13.9 us (28%)
  waiting for transfers between devices  10 us (20%)
  local copies, waits for them, and re-layouts  0.94 us (2%)
    pallas_call x1, Pallas kernels, legendre(): pl.pallas_call(functools.partial(legendre_kernel, early), out_shape=jax.S...  8.4 us
    all_to_all x1, starting transfers between devices, shards(): lax.all_to_all(edges, ('lat', *axes), split_axis=0, concat_axis=0, tiled=...  7.38 us
    ppermute x6, waiting for transfers between devices, exchange(): lax.ppermute(blocks[step], axis, pairs[step])  6.6 us
    ppermute x6, starting transfers between devices, exchange(): lax.ppermute(blocks[step], axis, pairs[step])  6.56 us
    pallas_call x1, Pallas kernels, advect(): pl.pallas_call(functools.partial(advect_kernel, ring, lat_count), out_sha...  5.94 us
    pallas_call x1, Pallas kernels, prepare_recurrence(): pl.pallas_call(sweep_kernel, out_shape=[orders, orders, jax.ShapeDtypeStr...  5.13 us
    all_to_all x1, waiting for transfers between devices, shards(): lax.all_to_all(edges, ('lat', *axes), split_axis=0, concat_axis=0, tiled=...  3.43 us
    pallas_call x1, Pallas kernels, fourier(): pl.pallas_call(functools.partial(fourier_kernel, ring, lat_count, pieces)...  2.93 us
  transfers between devices with their start and end apart: 7, of which 4 were waited for; matrix products, arithmetic and copies ran while one was open for 0% of the time, Pallas kernels for 14%

profile of v16, /device:TPU:0, one launch (start us, length us, event | category | flops | bytes accessed | tf_op | source)
XLA Modules:
  0.0 49.3 jit_solution(13168939417663645581)
XLA Ops:
  0.0 5.9 %shard_map.91 = (s16[224,384]{1,0:T(8,128)(2,1)}, s16[224,384]{1,0:T(8,128)(2,1)}, s16[224,384]{1,0:T(8,128)(2,1)}, s16[224,384]{1,0:T(8,128)(2,1)}, f32[16,1,400]{2,1,0:T(1,128)}) custom-call(s32[1,200]{1,0:T(1,128)} %bitcast.4, bf16[4,200,400]{2,1,0:T(8,128)(2,1)} %tracer_hbm.1, bf16[4,200,400]{2,1,0:T(8,128)(2,1)} %east_hbm.1, bf16[4,200,400]{2,1,0:T(8,128)(2,1)} %north_hbm.1), custom_call_target="tpu_custom_call" | custom-call | flops 5000000000 | bytes 2560000 | tf_op jit(solution)/shard_map/pallas_call | solution.py:253
  5.9 7.4 %all-to-all-start = ((f32[16,1,400]{2,1,0:T(1,128)}), f32[16,1,400]{2,1,0:T(1,128)S(1)}, u32[]{:S(2)}, u32[]{:S(2)}) async-start(f32[16,1,400]{2,1,0:T(1,128)} %get-tuple-element.42), calls=%async_computation | async-start | bytes 65536 | tf_op jit(solution)/shard_map/all_to_all | solution.py:732
  13.3 0.4 collective-permute-start
  13.7 1.7 %collective-permute-start.1 = (s16[224,384]{1,0:T(8,128)(2,1)}, s16[224,384]{1,0:T(8,128)(2,1)S(1)}, u32[]{:S(2)}, u32[]{:S(2)}) collective-permute-start(s16[224,384]{1,0:T(8,128)(2,1)} %get-tuple-element.40), channel_id=1, source_target_pairs={{0,2},{1,3},{2,0},{3,1},{4,6},{5,7},{6,4},{7,5},{8,10},{9,11},{10,... | collective-permute-start | bytes 516104 | tf_op jit(solution)/shard_map/ppermute | solution.py:149
  15.4 0.0 collective-permute-start.2
  15.4 0.0 copy-done.1
  15.4 1.1 %shard_map.92 = (bf16[512,512]{1,0:T(8,128)(2,1)S(1)}, f32[1,512]{1,0:T(1,128)S(1)}, f32[2,128]{1,0:T(2,128)S(1)}) custom-call(s32[1,400]{1,0:T(1,128)S(1)} %bitcast.3), custom_call_target="tpu_custom_call" | custom-call | flops 2000000000 | bytes 1048576 | tf_op jit(solution)/shard_map/pallas_call | solution.py:415
  16.5 3.4 %all-to-all-done.rest_4_ = f32[16,1,400]{2,1,0:T(1,128)S(1)} async-done(((f32[16,1,400]{2,1,0:T(1,128)}), f32[16,1,400]{2,1,0:T(1,128)S(1)}, u32[]{:S(2)}, u32[]{:S(2)}) %all-to-all-start) | async-done | bytes 25632 | tf_op jit(solution)/shard_map/all_to_all | solution.py:732
  20.0 0.0 collective-permute-done.rest_1_
  20.0 1.4 %collective-permute-done.1.rest_2_ = s16[224,384]{1,0:T(8,128)(2,1)S(1)} collective-permute-done((s16[224,384]{1,0:T(8,128)(2,1)}, s16[224,384]{1,0:T(8,128)(2,1)S(1)}, u32[]{:S(2)}, u32[]{:S(2)}) %collective-permute-start.1) | collective-permute-done | bytes 172064 | tf_op jit(solution)/shard_map/ppermute | solution.py:149
  21.4 2.6 %collective-permute-done.2.rest_3_ = s16[224,384]{1,0:T(8,128)(2,1)S(1)} collective-permute-done((s16[224,384]{1,0:T(8,128)(2,1)}, s16[224,384]{1,0:T(8,128)(2,1)S(1)}, u32[]{:S(2)}, u32[]{:S(2)}) %collective-permute-start.2) | collective-permute-done | bytes 172064 | tf_op jit(solution)/shard_map/ppermute | solution.py:149
  24.0 0.0 copy-done.2
  24.0 0.9 %copy-done.4 = s16[224,384]{1,0:T(8,128)(2,1)S(1)} copy-done((s16[224,384]{1,0:T(8,128)(2,1)S(1)}, s16[224,384]{1,0:T(8,128)(2,1)}, u32[]{:S(2)}) %copy-start.4) | copy-done | bytes 172056
  24.9 2.9 %shard_map.93 = (s16[208,256]{1,0:T(8,128)(2,1)S(1)}, s16[208,256]{1,0:T(8,128)(2,1)S(1)}, s16[208,256]{1,0:T(8,128)(2,1)S(1)}, s16[208,256]{1,0:T(8,128)(2,1)S(1)}) custom-call(s16[224,384]{1,0:T(8,128)(2,1)S(1)} %copy-done.4, s16[224,384]{1,0:T(8,128)(2,1)S(1)} %collective-permute-done.rest_1_, s16[224,384]{1,0:T(8,128)(2,1)S(1)} %collective-permute-done.1.rest_2_, ...), custom_call_target="tpu_custom_call" | custom-call | flops 4000000000 | bytes 6291456 | tf_op jit(solution)/shard_map/pallas_call | solution.py:364
  27.8 0.0 copy-start
  27.8 1.8 %collective-permute-start.3 = (s16[208,256]{1,0:T(8,128)(2,1)S(1)}, s16[208,256]{1,0:T(8,128)(2,1)S(1)}, u32[]{:S(2)}, u32[]{:S(2)}) collective-permute-start(s16[208,256]{1,0:T(8,128)(2,1)S(1)} %get-tuple-element.60), channel_id=1, source_target_pairs={{0,4},{4,0},{8,12},{12,8},{1,5},{5,1},{9,13},{13,9},{2,6},{6,2},{1... | collective-permute-start | bytes 319496 | tf_op jit(solution)/shard_map/ppermute | solution.py:149
  29.6 2.2 %collective-permute-start.4 = (s16[208,256]{1,0:T(8,128)(2,1)S(1)}, s16[208,256]{1,0:T(8,128)(2,1)S(1)}, u32[]{:S(2)}, u32[]{:S(2)}) collective-permute-start(s16[208,256]{1,0:T(8,128)(2,1)S(1)} %get-tuple-element.61), channel_id=1, source_target_pairs={{0,8},{4,12},{8,0},{12,4},{1,9},{5,13},{9,1},{13,5},{2,10},{6,14},... | collective-permute-start | bytes 319496 | tf_op jit(solution)/shard_map/ppermute | solution.py:149
  31.8 0.5 collective-permute-start.5
  32.3 5.1 %shard_map.94 = (f32[832,128]{1,0:T(8,128)S(1)}, f32[832,128]{1,0:T(8,128)S(1)}, f32[26,128]{1,0:T(8,128)S(1)}, f32[4,104,128]{2,1,0:T(8,128)S(1)}, f32[3,104,12...) custom-call(f32[2,128]{1,0:T(2,128)S(1)} %get-tuple-element.51.mine_ref.rest_10_, ...), custom_call_target="tpu_custom_call" | custom-call | flops 5000000000 | bytes 26214400 | tf_op jit(solution)/shard_map/pallas_call | solution.py:533
  37.4 0.0 collective-permute-done.3.rest_1_
  37.5 0.8 %shard_map.95.rest_9_ = f32[832,256]{1,0:T(8,128)S(1)} custom-call(bf16[4,2,832,208]{3,2,1,0:T(8,128)(2,1)S(1)} %copy-done, s16[208,256]{1,0:T(8,128)(2,1)S(1)} %get-tuple-element.59.rest_0_, s16[208,256]{1,0:T(8,128)(2,1)S(1)} %collective-permute-done.3.rest_1_), custom_call_target="tpu_custom_call" | custom-call | flops 1000000000 | bytes 4194304 | tf_op jit(solution)/shard_map/pallas_call | solution.py:578
  38.3 2.6 %collective-permute-done.4.rest_11_ = s16[208,256]{1,0:T(8,128)(2,1)S(1)} collective-permute-done((s16[208,256]{1,0:T(8,128)(2,1)S(1)}, s16[208,256]{1,0:T(8,128)(2,1)S(1)}, u32[]{:S(2)}, u32[]{:S(2)}) %collective-permute-start.4) | collective-permute-done | bytes 106528 | tf_op jit(solution)/shard_map/ppermute | solution.py:149
  40.9 0.0 collective-permute-done.5.rest_12_
  40.9 8.4 %shard_map.96 = f32[100,2,400]{2,1,0:T(2,128)} custom-call(bf16[4,2,832,208]{3,2,1,0:T(8,128)(2,1)S(1)} %copy-done, f32[3,104,128]{2,1,0:T(8,128)S(1)} %copy-done.3, f32[832,128]{1,0:T(8,128)S(1)} %get-tuple-element.52.rest_2_, f32[832,128]{1,0:T(8,128)S(1)} %get-tuple-element.53.rest_3_, f32[26,128]{1,0:T(8,128)S(1)} %get-tuple-element.54.rest_4_, ...), custom_call_target="tpu_custom_call" | custom-call | flops 8000000000 | bytes 6291456 | tf_op jit(solution)/shard_map/pallas_call | solution.py:703
  (6 shorter events, 0.0 us)
Async XLA Ops:
  0.0 15.4 %copy-start.1 = (s32[400]{0:T(512)S(1)}, s32[400]{0:T(512)}, u32[]{:S(2)}) copy-start(s32[400]{0:T(512)} %param.13) | copy-start | bytes 4804
  5.9 14.0 %all-to-all-start = ((f32[16,1,400]{2,1,0:T(1,128)}), f32[16,1,400]{2,1,0:T(1,128)S(1)}, u32[]{:S(2)}, u32[]{:S(2)}) async-start(f32[16,1,400]{2,1,0:T(1,128)} %get-tuple-element.42), calls=%async_computation | async-start | bytes 65536 | tf_op jit(solution)/shard_map/all_to_all | solution.py:732
  13.3 6.6 %collective-permute-start = (s16[224,384]{1,0:T(8,128)(2,1)}, s16[224,384]{1,0:T(8,128)(2,1)S(1)}, u32[]{:S(2)}, u32[]{:S(2)}) collective-permute-start(s16[224,384]{1,0:T(8,128)(2,1)} %get-tuple-element.39), channel_id=1, source_target_pairs={{0,1},{1,0},{2,3},{3,2},{4,5},{5,4},{6,7},{7,6},{8,9},{9,8},{10,11... | collective-permute-start | bytes 516104 | tf_op jit(solution)/shard_map/ppermute | solution.py:149
  13.7 7.6 %collective-permute-start.1 = (s16[224,384]{1,0:T(8,128)(2,1)}, s16[224,384]{1,0:T(8,128)(2,1)S(1)}, u32[]{:S(2)}, u32[]{:S(2)}) collective-permute-start(s16[224,384]{1,0:T(8,128)(2,1)} %get-tuple-element.40), channel_id=1, source_target_pairs={{0,2},{1,3},{2,0},{3,1},{4,6},{5,7},{6,4},{7,5},{8,10},{9,11},{10,... | collective-permute-start | bytes 516104 | tf_op jit(solution)/shard_map/ppermute | solution.py:149
  15.4 8.5 %collective-permute-start.2 = (s16[224,384]{1,0:T(8,128)(2,1)}, s16[224,384]{1,0:T(8,128)(2,1)S(1)}, u32[]{:S(2)}, u32[]{:S(2)}) collective-permute-start(s16[224,384]{1,0:T(8,128)(2,1)} %get-tuple-element.41), channel_id=1, source_target_pairs={{0,3},{1,2},{2,1},{3,0},{4,7},{5,6},{6,5},{7,4},{8,11},{9,10},{10,... | collective-permute-start | bytes 516104 | tf_op jit(solution)/shard_map/ppermute | solution.py:149
  15.4 8.5 %copy-start.2 = (bf16[1,400,3072]{2,1,0:T(8,128)(2,1)S(1)}, bf16[1,400,3072]{2,1,0:T(8,128)(2,1)}, u32[]{:S(2)}) copy-start(bf16[1,400,3072]{2,1,0:T(8,128)(2,1)} %constant.6.clone.rest_5_) | copy-start | bytes 7372804
  24.0 0.9 %copy-start.4 = (s16[224,384]{1,0:T(8,128)(2,1)S(1)}, s16[224,384]{1,0:T(8,128)(2,1)}, u32[]{:S(2)}) copy-start(s16[224,384]{1,0:T(8,128)(2,1)} %get-tuple-element.38.rest_0_) | copy-start | bytes 516100
  24.9 7.4 %copy-start.3 = (f32[3,104,128]{2,1,0:T(8,128)S(1)}, f32[3,104,128]{2,1,0:T(8,128)}, u32[]{:S(2)}) copy-start(f32[3,104,128]{2,1,0:T(8,128)} %constant.7.clone.lat_ref.rest_1_) | copy-start | bytes 479236
  27.8 9.6 %copy-start = (bf16[4,2,832,208]{3,2,1,0:T(8,128)(2,1)S(1)}, bf16[4,2,832,208]{3,2,1,0:T(8,128)(2,1)}, u32[]{:S(2)}) copy-start(bf16[4,2,832,208]{3,2,1,0:T(8,128)(2,1)} %constant.8.clone.table_ref.rest_0_) | copy-start | bytes 8306692
  27.8 9.6 %collective-permute-start.3 = (s16[208,256]{1,0:T(8,128)(2,1)S(1)}, s16[208,256]{1,0:T(8,128)(2,1)S(1)}, u32[]{:S(2)}, u32[]{:S(2)}) collective-permute-start(s16[208,256]{1,0:T(8,128)(2,1)S(1)} %get-tuple-element.60), channel_id=1, source_target_pairs={{0,4},{4,0},{8,12},{12,8},{1,5},{5,1},{9,13},{13,9},{2,6},{6,2},{1... | collective-permute-start | bytes 319496 | tf_op jit(solution)/shard_map/ppermute | solution.py:149
  29.6 11.3 %collective-permute-start.4 = (s16[208,256]{1,0:T(8,128)(2,1)S(1)}, s16[208,256]{1,0:T(8,128)(2,1)S(1)}, u32[]{:S(2)}, u32[]{:S(2)}) collective-permute-start(s16[208,256]{1,0:T(8,128)(2,1)S(1)} %get-tuple-element.61), channel_id=1, source_target_pairs={{0,8},{4,12},{8,0},{12,4},{1,9},{5,13},{9,1},{13,5},{2,10},{6,14},... | collective-permute-start | bytes 319496 | tf_op jit(solution)/shard_map/ppermute | solution.py:149
  31.8 9.1 %collective-permute-start.5 = (s16[208,256]{1,0:T(8,128)(2,1)S(1)}, s16[208,256]{1,0:T(8,128)(2,1)S(1)}, u32[]{:S(2)}, u32[]{:S(2)}) collective-permute-start(s16[208,256]{1,0:T(8,128)(2,1)S(1)} %get-tuple-element.62), channel_id=1, source_target_pairs={{0,12},{4,8},{8,4},{12,0},{1,13},{5,9},{9,5},{13,1},{2,14},{6,10},... | collective-permute-start | bytes 319496 | tf_op jit(solution)/shard_map/ppermute | solution.py:149

commit v17 on v15

--- a/solution.py
+++ b/solution.py
@@ -15,7 +15,8 @@
 LANES = 128
 BLOCK = 32
 CHUNKS = (40, 32, 32)
-HELD = -(-M // BLOCK)
+SPAN = -(-M // BLOCK)
+HELD = 13
 SIDE = LANES // 2
 TOP = 32767.0
 WIND_STEP = 1.5 / TOP
@@ -149,7 +150,7 @@
 
 def advect_kernel(ring, lat_count, keep_ref, tracer_hbm, east_hbm, north_hbm, *rest):
     levels, rows, lons = tracer_hbm.shape
-    outs, (edge_ref, tracer, east_wind, north_wind, blocks, sems) = rest[:levels], rest[levels:]
+    outs, (edge_ref, tracer, east_wind, north_wind, sems) = rest[:levels], rest[levels:]
     chosen = [partner(*ring, step) for step in range(levels)]
     copies = [None] * levels
     order = (*range(levels // 2, levels), *range(levels // 2))
@@ -172,7 +173,6 @@
     lane = lax.broadcasted_iota(jnp.int32, (rows, LANES), 1)
     lat_index = lax.axis_index("lat")
     edge_ref[...] = jnp.zeros_like(edge_ref)
-    written = []
     for step in order:
         level = chosen[step]
         for copy in copies[step]:
@@ -217,12 +217,8 @@
         filler = jnp.zeros((padded_rows - rows, LANES - spare), jnp.float32)
         wind_tile = jnp.concatenate([wind_rows[:, end:], filler], axis=1)
         steps = jnp.concatenate([coded(moved[:, :end], inverse), wind_rows[:, :end]], axis=0)
-        blocks[step, :, :end] = as_int16(steps)
-        blocks[step, :, end:] = as_int16(jnp.concatenate([tile, wind_tile], axis=0))
-        written.append(pltpu.make_async_copy(blocks.at[step], outs[step], sems.at[3, step]))
-        written[-1].start()
-    for copy in written:
-        copy.wait()
+        outs[step][:, :end] = as_int16(steps)
+        outs[step][:, end:] = as_int16(jnp.concatenate([tile, wind_tile], axis=0))
 
 
 def advect(tracer, east_wind, north_wind, keep_m, ring):
@@ -236,9 +232,8 @@
         out_shape=[jax.ShapeDtypeStruct((padded_rows, width), jnp.int16)] * levels
         + [jax.ShapeDtypeStruct((lat_count * levels, 1, lons), jnp.float32)],
         in_specs=[VMEM_SPEC] + [HBM_SPEC] * 3,
-        out_specs=[HBM_SPEC] * levels + [VMEM_SPEC],
-        scratch_shapes=[held, held, held]
-        + [pltpu.VMEM((levels, padded_rows, width), jnp.int16), pltpu.SemaphoreType.DMA((4, levels))],
+        out_specs=[VMEM_SPEC] * (levels + 1),
+        scratch_shapes=[held, held, held, pltpu.SemaphoreType.DMA((3, levels))],
         compiler_params=pltpu.CompilerParams(vmem_limit_bytes=VMEM_BYTES),
         cost_estimate=pl.CostEstimate(
             flops=5 * 10**9, bytes_accessed=8 * levels * rows * lons, transcendentals=0
@@ -248,8 +243,8 @@
 
 
 def fourier_kernel(ring, lat_count, pieces, *rest):
-    grids, (edge_ref, table_ref, place_ref, wave_ref) = rest[:pieces], rest[pieces : pieces + 4]
-    outs, field = rest[pieces + 4 : -1], rest[-1]
+    grids, (edge_ref, table_ref, wave_ref) = rest[:pieces], rest[pieces : pieces + 3]
+    outs, field = rest[pieces + 3 : -1], rest[-1]
     _, rows, width = field.shape
     lons = table_ref.shape[1]
     share = pieces // 4
@@ -308,6 +303,13 @@
             parts.append(product(kind, value, spot))
         parts = [parts[0], parts[1], parts[2] + parts[3]]
         sums = [part if total is None else total + part for total, part in zip(sums, parts)]
+    slot_waves = wave_ref[...]
+    waves = column_waves((column_count(), LANES))
+    places = [
+        jnp.where(waves == slot_waves[:, first : first + LANES], 1.0, 0.0).astype(jnp.bfloat16)
+        for first in range(0, slot_waves.shape[1], LANES)
+    ]
+    places = jnp.concatenate(places, axis=1)
     placed = []
     for part in range(2):
         columns = []
@@ -315,9 +317,9 @@
             half = total.shape[1] // 2
             columns.append(total[:, part * half : (part + 1) * half])
         high, low = split_bf16(jnp.concatenate(columns, axis=1))
-        value = jnp.dot(high, place_ref[...], preferred_element_type=jnp.float32)
-        value += jnp.dot(low, place_ref[...], preferred_element_type=jnp.float32)
-        kept = jnp.where(wave_ref[...] < keep, value, 0.0)
+        value = jnp.dot(high, places, preferred_element_type=jnp.float32)
+        value += jnp.dot(low, places, preferred_element_type=jnp.float32)
+        kept = jnp.where(slot_waves < keep, value, 0.0)
         code = scale_code(jnp.max(jnp.abs(kept), axis=0, keepdims=True))
         steps = coded(kept, 1.0 / scale_of(code))
         codes = jnp.broadcast_to(code, (outs[0].shape[0] - rows, code.shape[1]))
@@ -328,7 +330,7 @@
             outs[target][:, part * LANES : (part + 1) * LANES] = placed[part][:, cols]
 
 
-def fourier(grids, edges, ring, places, wave_row, rows, lat_count):
+def fourier(grids, edges, ring, wave_row, rows, lat_count):
     pieces = len(grids)
     width = grids[0].shape[1]
     padded_rows = -(-(rows + 1) // 16) * 16
@@ -336,17 +338,17 @@
     return pl.pallas_call(
         functools.partial(fourier_kernel, ring, lat_count, pieces),
         out_shape=[jax.ShapeDtypeStruct((padded_rows, 2 * LANES), jnp.int16)] * lat_count,
-        in_specs=[VMEM_SPEC] * (pieces + 4),
+        in_specs=[VMEM_SPEC] * (pieces + 3),
         out_specs=[VMEM_SPEC] * lat_count,
         scratch_shapes=[pltpu.VMEM((pieces, rows, width), jnp.float32)],
         compiler_params=pltpu.CompilerParams(vmem_limit_bytes=MIDDLE_BYTES),
         cost_estimate=pl.CostEstimate(
             flops=4 * 10**9, bytes_accessed=6 * 2**20, transcendentals=0
         ),
-    )(*grids, edges, np.concatenate(tables, axis=-1), places, wave_row)
-
-
-def places_kernel(groups, slot_ref, place_ref, wave_ref, mine_ref, sorted_rows):
+    )(*grids, edges, np.concatenate(tables, axis=-1), wave_row)
+
+
+def places_kernel(groups, slot_ref, wave_ref, mine_ref, sorted_rows):
     lat_index = lax.axis_index("lat")
     slots = slot_ref.shape[1] // groups
     paired = (slots + 1) // 2
@@ -374,12 +376,9 @@
             mine_ref[:1] = values
             mine_ref[1:] = plain
 
-    spots = column_waves((place_ref.shape[0], LANES))
     for step in range(groups):
         row = sorted_rows[partner(("lat",), (groups,), step), :1]
-        cols = slice(step * LANES, (step + 1) * LANES)
-        wave_ref[:, cols] = row
-        place_ref[:, cols] = jnp.where(spots == row, 1.0, 0.0).astype(jnp.bfloat16)
+        wave_ref[:, step * LANES : (step + 1) * LANES] = row
 
 
 def prepare_places(slot_wave, groups):
@@ -387,12 +386,11 @@
     return pl.pallas_call(
         functools.partial(places_kernel, groups),
         out_shape=[
-            jax.ShapeDtypeStruct((column_count(), width), jnp.bfloat16),
             jax.ShapeDtypeStruct((1, width), jnp.float32),
             jax.ShapeDtypeStruct((2, LANES), jnp.float32),
         ],
         in_specs=[VMEM_SPEC],
-        out_specs=[VMEM_SPEC] * 3,
+        out_specs=[VMEM_SPEC] * 2,
         scratch_shapes=[pltpu.VMEM((groups, 8, LANES), jnp.float32)],
         compiler_params=pltpu.CompilerParams(vmem_limit_bytes=MIDDLE_BYTES),
         cost_estimate=pl.CostEstimate(flops=2 * 10**9, bytes_accessed=2**20, transcendentals=0),
@@ -500,7 +498,7 @@
 def prepare_recurrence(mine, pieces):
     latitudes = latitude_table()
     points = latitudes.shape[1]
-    blocks = 2 * -(-M // BLOCK)
+    blocks = 2 * SPAN
     orders = jax.ShapeDtypeStruct((blocks * BLOCK, LANES), jnp.float32)
     return pl.pallas_call(
         sweep_kernel,
@@ -635,7 +633,7 @@
     lax.fori_loop(HELD, block_total, step, 0)
 
     left = lax.broadcasted_iota(jnp.int32, (BLOCK, LANES), 1) < SIDE
-    spots = -(-M // BLOCK)
+    spots = SPAN
     chosen = [jnp.broadcast_to(turn, (8, LANES)) == value for value in range(spots + 1)]
     chosen = [jnp.concatenate([mask] * (BLOCK // 8), axis=0) for mask in chosen]
     for place in range(spots):
@@ -671,7 +669,7 @@
     points = latitudes.shape[1]
     table = jnp.asarray(resample_pieces(pieces, rows, fields[0].shape[0]))
     total = resample(fields[:early], table)
-    block_rows = -(-M // BLOCK) * BLOCK
+    block_rows = SPAN * BLOCK
     return pl.pallas_call(
         functools.partial(legendre_kernel, early),
         out_shape=jax.ShapeDtypeStruct((slots, 2, M), jnp.float32),
@@ -702,8 +700,8 @@
     blocks, slot_wave = lax.optimization_barrier((blocks, slot_wave))
     grids = exchange(blocks, axes)
     edges = lax.all_to_all(edges, ("lat", *axes), split_axis=0, concat_axis=0, tiled=True)
-    places, wave_row, mine = prepare_places(slot_wave, lat_count)
-    waved = fourier(grids, edges, ring, places, wave_row, rows, lat_count)
+    wave_row, mine = prepare_places(slot_wave, lat_count)
+    waved = fourier(grids, edges, ring, wave_row, rows, lat_count)
     waved, mine = lax.optimization_barrier((list(waved), mine))
     fields = exchange(waved, "lat")
     prepared = prepare_recurrence(mine, lat_count)

time: 46.7 us -> 45.4 us (0.972); the launches traced: 46.1 us -> 45.8 us
  local copies, waits for them, and re-layouts: 1.86 us -> 0.03 us
  waiting for transfers between devices: 5.86 us -> 6.78 us
  Pallas kernels: 24.5 us -> 25.1 us
    unnamed x14 -> x10, local copies, waits for them, and re-layouts: 1.86 us -> 0.03 us
    pallas_call x1, Pallas kernels: 8.4 us -> 9.69 us  [legendre(): pl.pallas_call(functools.partial(legendre_kernel, early), out_shape=jax.S...]
    all_to_all x1, waiting for transfers between devices: 4.68 us -> 5.61 us  [shards(): lax.all_to_all(edges, ('lat', *axes), split_axis=0, concat_axis=0, tiled=...]
    pallas_call x1, Pallas kernels: 6.29 us -> 5.71 us  [advect(): pl.pallas_call(functools.partial(advect_kernel, ring, lat_count), out_sha...]
where the time goes in v17:
time: 45.4 us; the launch traced here: 45.8 us
  Pallas kernels  25.1 us (55%)
  starting transfers between devices  13.8 us (30%)
  waiting for transfers between devices  6.78 us (15%)
    pallas_call x1, Pallas kernels, legendre(): pl.pallas_call(functools.partial(legendre_kernel, early), out_shape=jax.S...  9.69 us
    ppermute x6, starting transfers between devices, exchange(): lax.ppermute(blocks[step], axis, pairs[step])  7.6 us
    all_to_all x1, starting transfers between devices, shards(): lax.all_to_all(edges, ('lat', *axes), split_axis=0, concat_axis=0, tiled=...  6.16 us
    pallas_call x1, Pallas kernels, advect(): pl.pallas_call(functools.partial(advect_kernel, ring, lat_count), out_sha...  5.71 us
    all_to_all x1, waiting for transfers between devices, shards(): lax.all_to_all(edges, ('lat', *axes), split_axis=0, concat_axis=0, tiled=...  5.61 us
    pallas_call x1, Pallas kernels, prepare_recurrence(): pl.pallas_call(sweep_kernel, out_shape=[orders, orders, jax.ShapeDtypeStr...  5.13 us
    pallas_call x1, Pallas kernels, fourier(): pl.pallas_call(functools.partial(fourier_kernel, ring, lat_count, pieces)...  2.73 us
    ppermute x6, waiting for transfers between devices, exchange(): lax.ppermute(blocks[step], axis, pairs[step])  1.17 us
  transfers between devices with their start and end apart: 7, of which 2 were waited for; matrix products, arithmetic and copies ran while one was open for 0% of the time, Pallas kernels for 15%

profile of v17, /device:TPU:0, one launch (start us, length us, event | category | flops | bytes accessed | tf_op | source)
XLA Modules:
  0.0 45.8 jit_solution(17554399742257359327)
XLA Ops:
  0.0 5.7 %shard_map.91 = (s16[208,512]{1,0:T(8,128)(2,1)}, s16[208,512]{1,0:T(8,128)(2,1)}, s16[208,512]{1,0:T(8,128)(2,1)}, s16[208,512]{1,0:T(8,128)(2,1)}, f32[16,1,400]{2,1,0:T(1,128)}) custom-call(s32[1,200]{1,0:T(1,128)} %bitcast.4, bf16[4,200,400]{2,1,0:T(8,128)(2,1)} %tracer_hbm.1, bf16[4,200,400]{2,1,0:T(8,128)(2,1)} %east_hbm.1, bf16[4,200,400]{2,1,0:T(8,128)(2,1)} %north_hbm.1), custom_call_target="tpu_custom_call" | custom-call | flops 5000000000 | bytes 2560000 | tf_op jit(solution)/shard_map/pallas_call | solution.py:230
  5.7 0.5 %collective-permute-start = (s16[208,512]{1,0:T(8,128)(2,1)}, s16[208,512]{1,0:T(8,128)(2,1)S(1)}, u32[]{:S(2)}, u32[]{:S(2)}) collective-permute-start(s16[208,512]{1,0:T(8,128)(2,1)} %get-tuple-element.38), channel_id=1, source_target_pairs={{0,1},{1,0},{2,3},{3,2},{4,5},{5,4},{6,7},{7,6},{8,9},{9,8},{10,11... | collective-permute-start | bytes 638984 | tf_op jit(solution)/shard_map/ppermute | solution.py:148
  6.2 2.6 %collective-permute-start.1 = (s16[208,512]{1,0:T(8,128)(2,1)}, s16[208,512]{1,0:T(8,128)(2,1)S(1)}, u32[]{:S(2)}, u32[]{:S(2)}) collective-permute-start(s16[208,512]{1,0:T(8,128)(2,1)} %get-tuple-element.39), channel_id=1, source_target_pairs={{0,2},{1,3},{2,0},{3,1},{4,6},{5,7},{6,4},{7,5},{8,10},{9,11},{10,... | collective-permute-start | bytes 638984 | tf_op jit(solution)/shard_map/ppermute | solution.py:148
  8.8 0.1 collective-permute-start.2
  8.9 6.2 %all-to-all-start = ((f32[16,1,400]{2,1,0:T(1,128)}), f32[16,1,400]{2,1,0:T(1,128)S(1)}, u32[]{:S(2)}, u32[]{:S(2)}) async-start(f32[16,1,400]{2,1,0:T(1,128)} %get-tuple-element.41), calls=%async_computation | async-start | bytes 65536 | tf_op jit(solution)/shard_map/all_to_all | solution.py:702
  15.0 0.0 copy-start.2
  15.1 0.0 copy-start.4
  15.1 1.0 %shard_map.92 = (f32[1,512]{1,0:T(1,128)S(1)}, f32[2,128]{1,0:T(2,128)S(1)}) custom-call(s32[1,400]{1,0:T(1,128)S(1)} %bitcast.3), custom_call_target="tpu_custom_call" | custom-call | flops 2000000000 | bytes 1048576 | tf_op jit(solution)/shard_map/pallas_call | solution.py:386
  16.1 5.6 %all-to-all-done.rest_4_ = f32[16,1,400]{2,1,0:T(1,128)S(1)} async-done(((f32[16,1,400]{2,1,0:T(1,128)}), f32[16,1,400]{2,1,0:T(1,128)S(1)}, u32[]{:S(2)}, u32[]{:S(2)}) %all-to-all-start) | async-done | bytes 25632 | tf_op jit(solution)/shard_map/all_to_all | solution.py:702
  21.7 0.0 collective-permute-done.rest_1_
  21.7 0.0 collective-permute-done.1.rest_2_
  21.7 0.0 collective-permute-done.2.rest_3_
  21.7 0.0 copy-start.3
  21.7 2.7 %shard_map.93 = (s16[208,256]{1,0:T(8,128)(2,1)S(1)}, s16[208,256]{1,0:T(8,128)(2,1)S(1)}, s16[208,256]{1,0:T(8,128)(2,1)S(1)}, s16[208,256]{1,0:T(8,128)(2,1)S(1)}) custom-call(s16[208,512]{1,0:T(8,128)(2,1)S(1)} %copy-done.4, s16[208,512]{1,0:T(8,128)(2,1)S(1)} %collective-permute-done.rest_1_, s16[208,512]{1,0:T(8,128)(2,1)S(1)} %collective-permute-done.1.rest_2_, ...), custom_call_target="tpu_custom_call" | custom-call | flops 4000000000 | bytes 6291456 | tf_op jit(solution)/shard_map/pallas_call | solution.py:338
  24.5 0.0 copy-start
  24.5 0.4 collective-permute-start.3
  24.9 2.1 %collective-permute-start.4 = (s16[208,256]{1,0:T(8,128)(2,1)S(1)}, s16[208,256]{1,0:T(8,128)(2,1)S(1)}, u32[]{:S(2)}, u32[]{:S(2)}) collective-permute-start(s16[208,256]{1,0:T(8,128)(2,1)S(1)} %get-tuple-element.59), channel_id=1, source_target_pairs={{0,8},{4,12},{8,0},{12,4},{1,9},{5,13},{9,1},{13,5},{2,10},{6,14},... | collective-permute-start | bytes 319496 | tf_op jit(solution)/shard_map/ppermute | solution.py:148
  27.0 1.9 %collective-permute-start.5 = (s16[208,256]{1,0:T(8,128)(2,1)S(1)}, s16[208,256]{1,0:T(8,128)(2,1)S(1)}, u32[]{:S(2)}, u32[]{:S(2)}) collective-permute-start(s16[208,256]{1,0:T(8,128)(2,1)S(1)} %get-tuple-element.60), channel_id=1, source_target_pairs={{0,12},{4,8},{8,4},{12,0},{1,13},{5,9},{9,5},{13,1},{2,14},{6,10},... | collective-permute-start | bytes 319496 | tf_op jit(solution)/shard_map/ppermute | solution.py:148
  28.9 5.1 %shard_map.94 = (f32[832,128]{1,0:T(8,128)S(1)}, f32[832,128]{1,0:T(8,128)S(1)}, f32[26,128]{1,0:T(8,128)S(1)}, f32[4,104,128]{2,1,0:T(8,128)S(1)}, f32[3,104,12...) custom-call(f32[2,128]{1,0:T(2,128)S(1)} %get-tuple-element.49.mine_ref.rest_10_, ...), custom_call_target="tpu_custom_call" | custom-call | flops 5000000000 | bytes 26214400 | tf_op jit(solution)/shard_map/pallas_call | solution.py:503
  34.1 0.0 collective-permute-done.3.rest_1_
  34.1 0.8 %shard_map.95.rest_9_ = f32[832,256]{1,0:T(8,128)S(1)} custom-call(bf16[4,2,832,208]{3,2,1,0:T(8,128)(2,1)S(1)} %copy-done, s16[208,256]{1,0:T(8,128)(2,1)S(1)} %get-tuple-element.57.rest_0_, s16[208,256]{1,0:T(8,128)(2,1)S(1)} %collective-permute-done.3.rest_1_), custom_call_target="tpu_custom_call" | custom-call | flops 1000000000 | bytes 4194304 | tf_op jit(solution)/shard_map/pallas_call | solution.py:548
  34.9 1.2 %collective-permute-done.4.rest_11_ = s16[208,256]{1,0:T(8,128)(2,1)S(1)} collective-permute-done((s16[208,256]{1,0:T(8,128)(2,1)S(1)}, s16[208,256]{1,0:T(8,128)(2,1)S(1)}, u32[]{:S(2)}, u32[]{:S(2)}) %collective-permute-start.4) | collective-permute-done | bytes 106528 | tf_op jit(solution)/shard_map/ppermute | solution.py:148
  36.1 0.0 collective-permute-done.5.rest_12_
  36.1 9.7 %shard_map.96 = f32[100,2,400]{2,1,0:T(2,128)} custom-call(bf16[4,2,832,208]{3,2,1,0:T(8,128)(2,1)S(1)} %copy-done, f32[3,104,128]{2,1,0:T(8,128)S(1)} %copy-done.3, f32[832,128]{1,0:T(8,128)S(1)} %get-tuple-element.50.rest_2_, f32[832,128]{1,0:T(8,128)S(1)} %get-tuple-element.51.rest_3_, f32[26,128]{1,0:T(8,128)S(1)} %get-tuple-element.52.rest_4_, ...), custom_call_target="tpu_custom_call" | custom-call | flops 8000000000 | bytes 6291456 | tf_op jit(solution)/shard_map/pallas_call | solution.py:673
  (6 shorter events, 0.0 us)
Async XLA Ops:
  0.0 15.0 %copy-start.1 = (s32[400]{0:T(512)S(1)}, s32[400]{0:T(512)}, u32[]{:S(2)}) copy-start(s32[400]{0:T(512)} %param.13) | copy-start | bytes 4804
  5.7 16.0 %collective-permute-start = (s16[208,512]{1,0:T(8,128)(2,1)}, s16[208,512]{1,0:T(8,128)(2,1)S(1)}, u32[]{:S(2)}, u32[]{:S(2)}) collective-permute-start(s16[208,512]{1,0:T(8,128)(2,1)} %get-tuple-element.38), channel_id=1, source_target_pairs={{0,1},{1,0},{2,3},{3,2},{4,5},{5,4},{6,7},{7,6},{8,9},{9,8},{10,11... | collective-permute-start | bytes 638984 | tf_op jit(solution)/shard_map/ppermute | solution.py:148
  6.2 15.4 %collective-permute-start.1 = (s16[208,512]{1,0:T(8,128)(2,1)}, s16[208,512]{1,0:T(8,128)(2,1)S(1)}, u32[]{:S(2)}, u32[]{:S(2)}) collective-permute-start(s16[208,512]{1,0:T(8,128)(2,1)} %get-tuple-element.39), channel_id=1, source_target_pairs={{0,2},{1,3},{2,0},{3,1},{4,6},{5,7},{6,4},{7,5},{8,10},{9,11},{10,... | collective-permute-start | bytes 638984 | tf_op jit(solution)/shard_map/ppermute | solution.py:148
  8.8 12.9 %collective-permute-start.2 = (s16[208,512]{1,0:T(8,128)(2,1)}, s16[208,512]{1,0:T(8,128)(2,1)S(1)}, u32[]{:S(2)}, u32[]{:S(2)}) collective-permute-start(s16[208,512]{1,0:T(8,128)(2,1)} %get-tuple-element.40), channel_id=1, source_target_pairs={{0,3},{1,2},{2,1},{3,0},{4,7},{5,6},{6,5},{7,4},{8,11},{9,10},{10,... | collective-permute-start | bytes 638984 | tf_op jit(solution)/shard_map/ppermute | solution.py:148
  8.9 12.8 %all-to-all-start = ((f32[16,1,400]{2,1,0:T(1,128)}), f32[16,1,400]{2,1,0:T(1,128)S(1)}, u32[]{:S(2)}, u32[]{:S(2)}) async-start(f32[16,1,400]{2,1,0:T(1,128)} %get-tuple-element.41), calls=%async_computation | async-start | bytes 65536 | tf_op jit(solution)/shard_map/all_to_all | solution.py:702
  15.0 6.6 %copy-start.2 = (bf16[1,400,3072]{2,1,0:T(8,128)(2,1)S(1)}, bf16[1,400,3072]{2,1,0:T(8,128)(2,1)}, u32[]{:S(2)}) copy-start(bf16[1,400,3072]{2,1,0:T(8,128)(2,1)} %constant.6.clone.rest_5_) | copy-start | bytes 7372804
  15.1 6.6 %copy-start.4 = (s16[208,512]{1,0:T(8,128)(2,1)S(1)}, s16[208,512]{1,0:T(8,128)(2,1)}, u32[]{:S(2)}) copy-start(s16[208,512]{1,0:T(8,128)(2,1)} %get-tuple-element.37.rest_0_) | copy-start | bytes 638980
  21.7 7.2 %copy-start.3 = (f32[3,104,128]{2,1,0:T(8,128)S(1)}, f32[3,104,128]{2,1,0:T(8,128)}, u32[]{:S(2)}) copy-start(f32[3,104,128]{2,1,0:T(8,128)} %constant.7.clone.lat_ref.rest_1_) | copy-start | bytes 479236
  24.5 9.6 %copy-start = (bf16[4,2,832,208]{3,2,1,0:T(8,128)(2,1)S(1)}, bf16[4,2,832,208]{3,2,1,0:T(8,128)(2,1)}, u32[]{:S(2)}) copy-start(bf16[4,2,832,208]{3,2,1,0:T(8,128)(2,1)} %constant.8.clone.table_ref.rest_0_) | copy-start | bytes 8306692
  24.5 9.6 %collective-permute-start.3 = (s16[208,256]{1,0:T(8,128)(2,1)S(1)}, s16[208,256]{1,0:T(8,128)(2,1)S(1)}, u32[]{:S(2)}, u32[]{:S(2)}) collective-permute-start(s16[208,256]{1,0:T(8,128)(2,1)S(1)} %get-tuple-element.58), channel_id=1, source_target_pairs={{0,4},{4,0},{8,12},{12,8},{1,5},{5,1},{9,13},{13,9},{2,6},{6,2},{1... | collective-permute-start | bytes 319496 | tf_op jit(solution)/shard_map/ppermute | solution.py:148
  24.9 11.2 %collective-permute-start.4 = (s16[208,256]{1,0:T(8,128)(2,1)S(1)}, s16[208,256]{1,0:T(8,128)(2,1)S(1)}, u32[]{:S(2)}, u32[]{:S(2)}) collective-permute-start(s16[208,256]{1,0:T(8,128)(2,1)S(1)} %get-tuple-element.59), channel_id=1, source_target_pairs={{0,8},{4,12},{8,0},{12,4},{1,9},{5,13},{9,1},{13,5},{2,10},{6,14},... | collective-permute-start | bytes 319496 | tf_op jit(solution)/shard_map/ppermute | solution.py:148
  27.0 9.1 %collective-permute-start.5 = (s16[208,256]{1,0:T(8,128)(2,1)S(1)}, s16[208,256]{1,0:T(8,128)(2,1)S(1)}, u32[]{:S(2)}, u32[]{:S(2)}) collective-permute-start(s16[208,256]{1,0:T(8,128)(2,1)S(1)} %get-tuple-element.60), channel_id=1, source_target_pairs={{0,12},{4,8},{8,4},{12,0},{1,13},{5,9},{9,5},{13,1},{2,14},{6,10},... | collective-permute-start | bytes 319496 | tf_op jit(solution)/shard_map/ppermute | solution.py:148

commit v18 on v17

--- a/solution.py
+++ b/solution.py
@@ -17,11 +17,12 @@
 CHUNKS = (40, 32, 32)
 SPAN = -(-M // BLOCK)
 HELD = 13
+MORE = 3
 SIDE = LANES // 2
 TOP = 32767.0
 WIND_STEP = 1.5 / TOP
 VMEM_BYTES = 60 * 2**20
-LATE_BYTES = 16 * 2**20
+LATE_BYTES = 10 * 2**20
 MIDDLE_BYTES = 16 * 2**20
 VMEM_SPEC = pl.BlockSpec(memory_space=pltpu.VMEM)
 SMEM_SPEC = pl.BlockSpec(memory_space=pltpu.SMEM)
@@ -148,9 +149,9 @@
     return [blocks[0]] + [lax.ppermute(blocks[step], axis, pairs[step]) for step in range(1, count)]
 
 
-def advect_kernel(ring, lat_count, keep_ref, tracer_hbm, east_hbm, north_hbm, *rest):
+def advect_kernel(ring, lat_count, keep_hbm, tracer_hbm, east_hbm, north_hbm, *rest):
     levels, rows, lons = tracer_hbm.shape
-    outs, (edge_ref, tracer, east_wind, north_wind, sems) = rest[:levels], rest[levels:]
+    outs, (edge_ref, tracer, east_wind, north_wind, keep_ref, sems, keep_sem) = rest[:levels], rest[levels:]
     chosen = [partner(*ring, step) for step in range(levels)]
     copies = [None] * levels
     order = (*range(levels // 2, levels), *range(levels // 2))
@@ -163,7 +164,10 @@
         ]
         for copy in copies[step]:
             copy.start()
+    keep_copy = pltpu.make_async_copy(keep_hbm, keep_ref, keep_sem)
+    keep_copy.start()
     padded_rows = outs[0].shape[0]
+    keep_copy.wait()
     same = (rows, rows)
     same = lax.broadcasted_iota(jnp.int32, same, 0) == lax.broadcasted_iota(jnp.int32, same, 1)
     keep = jnp.broadcast_to(keep_ref[...].astype(jnp.float32), (rows, rows))
@@ -231,9 +235,16 @@
         functools.partial(advect_kernel, ring, lat_count),
         out_shape=[jax.ShapeDtypeStruct((padded_rows, width), jnp.int16)] * levels
         + [jax.ShapeDtypeStruct((lat_count * levels, 1, lons), jnp.float32)],
-        in_specs=[VMEM_SPEC] + [HBM_SPEC] * 3,
+        in_specs=[HBM_SPEC] * 4,
         out_specs=[VMEM_SPEC] * (levels + 1),
-        scratch_shapes=[held, held, held, pltpu.SemaphoreType.DMA((3, levels))],
+        scratch_shapes=[
+            held,
+            held,
+            held,
+            pltpu.VMEM((1, rows), jnp.int32),
+            pltpu.SemaphoreType.DMA((3, levels)),
+            pltpu.SemaphoreType.DMA,
+        ],
         compiler_params=pltpu.CompilerParams(vmem_limit_bytes=VMEM_BYTES),
         cost_estimate=pl.CostEstimate(
             flops=5 * 10**9, bytes_accessed=8 * levels * rows * lons, transcendentals=0
@@ -409,7 +420,7 @@
 
 def sweep_kernel(
     mine_ref, lat_ref,
-    beta_ref, scale_ref, growth_ref, start_ref, state_ref, values_ref, back_ref,
+    beta_ref, scale_ref, growth_ref, start_ref, state_ref, values_ref, more_ref, back_ref,
 ):
     shape = (LANES, LANES)
     same = lax.broadcasted_iota(jnp.int32, shape, 0) == lax.broadcasted_iota(jnp.int32, shape, 1)
@@ -458,20 +469,22 @@
     state_ref[2] = start_ref[1]
     points = lat_ref.shape[1]
 
-    def step(block, carry):
+    def step(target_ref, start, block, carry):
         first = 0
         for chunk in (points // 16 * 8, points - points // 16 * 8):
             rows = slice(first, first + chunk)
 
             def keep(order, value):
-                values_ref[block, order, rows] = value
+                target_ref[block - start, order, rows] = value
 
             sweep_block(block, turn, rows, lat_ref, beta_ref, growth_ref, start_ref, state_ref, keep)
             first += chunk
         return carry
 
     total = jnp.max(turn + block_count(two)).astype(jnp.int32)
-    lax.fori_loop(0, jnp.minimum(total, HELD), step, 0)
+    lax.fori_loop(0, jnp.minimum(total, HELD), functools.partial(step, values_ref, 0), 0)
+    more = functools.partial(step, more_ref, HELD)
+    lax.fori_loop(HELD, jnp.minimum(total, HELD + MORE), more, 0)
 
 
 def sweep_block(block, turn, rows, lat_ref, beta_ref, growth_ref, start_ref, state_ref, use):
@@ -509,10 +522,11 @@
             jax.ShapeDtypeStruct((4, points, LANES), jnp.float32),
             jax.ShapeDtypeStruct((3, points, LANES), jnp.float32),
             jax.ShapeDtypeStruct((HELD, BLOCK, points, LANES), jnp.float32),
+            jax.ShapeDtypeStruct((MORE, BLOCK, points, LANES), jnp.float32),
             jax.ShapeDtypeStruct((LANES, LANES), jnp.bfloat16),
         ],
         in_specs=[VMEM_SPEC] * 2,
-        out_specs=[VMEM_SPEC] * 7,
+        out_specs=[VMEM_SPEC] * 8,
         compiler_params=pltpu.CompilerParams(vmem_limit_bytes=late_bytes(pieces)),
         cost_estimate=pl.CostEstimate(
             flops=5 * 10**9, bytes_accessed=25 * 2**20, transcendentals=0
@@ -558,9 +572,9 @@
 
 
 def legendre_kernel(early, *rest):
-    table, lat_ref, beta_ref, scale_ref, growth_ref, start_ref, left_ref, values_ref, back_ref = rest[:9]
-    total_ref, mine_ref = rest[9:11]
-    fields, (out_ref, weights, state_ref, sums, result, final) = rest[11:-6], rest[-6:]
+    table, lat_ref, beta_ref, scale_ref, growth_ref, start_ref, left_ref, values_ref = rest[:8]
+    more_ref, back_ref, total_ref, mine_ref = rest[8:12]
+    fields, (out_ref, weights, state_ref, sums, result, final) = rest[12:-6], rest[-6:]
     points = lat_ref.shape[1]
     slots = out_ref.shape[0]
     mine = mine_ref[:1]
@@ -592,7 +606,7 @@
             total = total * scale_ref[pl.ds(base, BLOCK)]
             result[comp, pl.ds(base, BLOCK)] = total + pltpu.roll(total, SIDE, 1)
 
-    def held_step(block, carry):
+    def held_step(source_ref, start, block, carry):
         second = block.astype(jnp.float32) >= turn
         for parity in range(2):
             scaled = [
@@ -600,7 +614,7 @@
                 for comp in range(2)
             ]
             for order in range(parity, BLOCK, 2):
-                value = values_ref[block, order]
+                value = source_ref[block - start, order]
                 for comp in range(2):
                     product = (value * scaled[comp]).reshape(points // 8, 8, LANES)
                     sums[pl.ds((order * 2 + comp) * 8, 8)] = product.sum(axis=0)
@@ -629,8 +643,11 @@
         reduced(block)
         return carry
 
-    lax.fori_loop(0, jnp.minimum(block_total, HELD), held_step, 0)
-    lax.fori_loop(HELD, block_total, step, 0)
+    held = functools.partial(held_step, values_ref, 0)
+    lax.fori_loop(0, jnp.minimum(block_total, HELD), held, 0)
+    held = functools.partial(held_step, more_ref, HELD)
+    lax.fori_loop(HELD, jnp.minimum(block_total, HELD + MORE), held, 0)
+    lax.fori_loop(HELD + MORE, block_total, step, 0)
 
     left = lax.broadcasted_iota(jnp.int32, (BLOCK, LANES), 1) < SIDE
     spots = SPAN
@@ -673,7 +690,7 @@
     return pl.pallas_call(
         functools.partial(legendre_kernel, early),
         out_shape=jax.ShapeDtypeStruct((slots, 2, M), jnp.float32),
-        in_specs=[VMEM_SPEC] * (11 + pieces - early),
+        in_specs=[VMEM_SPEC] * (12 + pieces - early),
         out_specs=VMEM_SPEC,
         scratch_shapes=[
             pltpu.VMEM((2, 4, points, LANES), jnp.float32),

time: 45.4 us -> 46.1 us (1.015)
  local copies, waits for them, and re-layouts: 0.03 us -> 1.71 us
  waiting for transfers between devices: 6.78 us -> 5.99 us
  Pallas kernels: 25.1 us -> 24.5 us
    unnamed x10, local copies, waits for them, and re-layouts: 0.03 us -> 1.71 us
    pallas_call x1, Pallas kernels: 9.69 us -> 8.54 us  [legendre(): pl.pallas_call(functools.partial(legendre_kernel, early), out_shape=jax.S...]
    ppermute x6, waiting for transfers between devices: 1.17 us -> 0.36 us  [exchange(): lax.ppermute(blocks[step], axis, pairs[step])]
    pallas_call x1, Pallas kernels: 5.13 us -> 5.93 us  [prepare_recurrence(): pl.pallas_call(sweep_kernel, out_shape=[orders, orders, jax.ShapeDtypeStr...]
  transfers between devices with their start and end apart: 7 -> 7, of which waited for: 2 -> 2; matrix products, arithmetic and copies ran while one was open for 0% -> 0% of each run, Pallas kernels for 15% -> 17%
where the time goes in v18:
time: 46.1 us
  Pallas kernels  24.5 us (53%)
  starting transfers between devices  13.8 us (30%)
  waiting for transfers between devices  5.99 us (13%)
  local copies, waits for them, and re-layouts  1.71 us (4%)
    pallas_call x1, Pallas kernels, legendre(): pl.pallas_call(functools.partial(legendre_kernel, early), out_shape=jax.S...  8.54 us
    ppermute x6, starting transfers between devices, exchange(): lax.ppermute(blocks[step], axis, pairs[step])  7.6 us
    all_to_all x1, starting transfers between devices, shards(): lax.all_to_all(edges, ('lat', *axes), split_axis=0, concat_axis=0, tiled=...  6.16 us
    pallas_call x1, Pallas kernels, prepare_recurrence(): pl.pallas_call(sweep_kernel, out_shape=[orders, orders, jax.ShapeDtypeStr...  5.93 us
    all_to_all x1, waiting for transfers between devices, shards(): lax.all_to_all(edges, ('lat', *axes), split_axis=0, concat_axis=0, tiled=...  5.63 us
    pallas_call x1, Pallas kernels, advect(): pl.pallas_call(functools.partial(advect_kernel, ring, lat_count), out_sha...  5.53 us
    pallas_call x1, Pallas kernels, fourier(): pl.pallas_call(functools.partial(fourier_kernel, ring, lat_count, pieces)...  2.69 us
    unnamed x10, local copies, waits for them, and re-layouts  1.71 us
  transfers between devices with their start and end apart: 7, of which 2 were waited for; matrix products, arithmetic and copies ran while one was open for 0% of the time, Pallas kernels for 17%

profile of v18, /device:TPU:0, one launch (start us, length us, event | category | flops | bytes accessed | tf_op | source)
XLA Modules:
  0.0 46.1 jit_solution(12687616900320227466)
XLA Ops:
  0.0 5.5 %shard_map.91 = (s16[208,512]{1,0:T(8,128)(2,1)}, s16[208,512]{1,0:T(8,128)(2,1)}, s16[208,512]{1,0:T(8,128)(2,1)}, s16[208,512]{1,0:T(8,128)(2,1)}, f32[16,1,400]{2,1,0:T(1,128)}) custom-call(s32[1,200]{1,0:T(1,128)} %bitcast.4, bf16[4,200,400]{2,1,0:T(8,128)(2,1)} %tracer_hbm.1, bf16[4,200,400]{2,1,0:T(8,128)(2,1)} %east_hbm.1, bf16[4,200,400]{2,1,0:T(8,128)(2,1)} %north_hbm.1), custom_call_target="tpu_custom_call" | custom-call | flops 5000000000 | bytes 2560000 | tf_op jit(solution)/shard_map/pallas_call | solution.py:234
  5.5 0.0 copy-start.4
  5.6 0.5 %collective-permute-start = (s16[208,512]{1,0:T(8,128)(2,1)}, s16[208,512]{1,0:T(8,128)(2,1)S(1)}, u32[]{:S(2)}, u32[]{:S(2)}) collective-permute-start(s16[208,512]{1,0:T(8,128)(2,1)} %get-tuple-element.39), channel_id=1, source_target_pairs={{0,1},{1,0},{2,3},{3,2},{4,5},{5,4},{6,7},{7,6},{8,9},{9,8},{10,11... | collective-permute-start | bytes 638984 | tf_op jit(solution)/shard_map/ppermute | solution.py:149
  6.1 2.6 %collective-permute-start.1 = (s16[208,512]{1,0:T(8,128)(2,1)}, s16[208,512]{1,0:T(8,128)(2,1)S(1)}, u32[]{:S(2)}, u32[]{:S(2)}) collective-permute-start(s16[208,512]{1,0:T(8,128)(2,1)} %get-tuple-element.40), channel_id=1, source_target_pairs={{0,2},{1,3},{2,0},{3,1},{4,6},{5,7},{6,4},{7,5},{8,10},{9,11},{10,... | collective-permute-start | bytes 638984 | tf_op jit(solution)/shard_map/ppermute | solution.py:149
  8.6 0.1 collective-permute-start.2
  8.7 6.2 %all-to-all-start = ((f32[16,1,400]{2,1,0:T(1,128)}), f32[16,1,400]{2,1,0:T(1,128)S(1)}, u32[]{:S(2)}, u32[]{:S(2)}) async-start(f32[16,1,400]{2,1,0:T(1,128)} %get-tuple-element.42), calls=%async_computation | async-start | bytes 65536 | tf_op jit(solution)/shard_map/all_to_all | solution.py:719
  14.9 1.0 %shard_map.92 = (f32[1,512]{1,0:T(1,128)S(1)}, f32[2,128]{1,0:T(2,128)S(1)}) custom-call(s32[1,400]{1,0:T(1,128)S(1)} %bitcast.3), custom_call_target="tpu_custom_call" | custom-call | flops 2000000000 | bytes 1048576 | tf_op jit(solution)/shard_map/pallas_call | solution.py:397
  15.9 5.6 %all-to-all-done.rest_4_ = f32[16,1,400]{2,1,0:T(1,128)S(1)} async-done(((f32[16,1,400]{2,1,0:T(1,128)}), f32[16,1,400]{2,1,0:T(1,128)S(1)}, u32[]{:S(2)}, u32[]{:S(2)}) %all-to-all-start) | async-done | bytes 25632 | tf_op jit(solution)/shard_map/all_to_all | solution.py:719
  21.5 0.0 collective-permute-done.rest_1_
  21.5 0.0 collective-permute-done.1.rest_2_
  21.5 0.0 collective-permute-done.2.rest_3_
  21.5 0.0 copy-start.3
  21.5 1.7 %copy-done.3 = bf16[1,400,3072]{2,1,0:T(8,128)(2,1)S(1)} copy-done((bf16[1,400,3072]{2,1,0:T(8,128)(2,1)S(1)}, bf16[1,400,3072]{2,1,0:T(8,128)(2,1)}, u32[]{:S(2)}) %copy-start.3) | copy-done | bytes 2457624
  23.2 2.7 %shard_map.93 = (s16[208,256]{1,0:T(8,128)(2,1)S(1)}, s16[208,256]{1,0:T(8,128)(2,1)S(1)}, s16[208,256]{1,0:T(8,128)(2,1)S(1)}, s16[208,256]{1,0:T(8,128)(2,1)S(1)}) custom-call(s16[208,512]{1,0:T(8,128)(2,1)S(1)} %copy-done.4, s16[208,512]{1,0:T(8,128)(2,1)S(1)} %collective-permute-done.rest_1_, s16[208,512]{1,0:T(8,128)(2,1)S(1)} %collective-permute-done.1.rest_2_, ...), custom_call_target="tpu_custom_call" | custom-call | flops 4000000000 | bytes 6291456 | tf_op jit(solution)/shard_map/pallas_call | solution.py:349
  25.9 0.0 copy-start
  25.9 0.4 collective-permute-start.3
  26.4 2.1 %collective-permute-start.4 = (s16[208,256]{1,0:T(8,128)(2,1)S(1)}, s16[208,256]{1,0:T(8,128)(2,1)S(1)}, u32[]{:S(2)}, u32[]{:S(2)}) collective-permute-start(s16[208,256]{1,0:T(8,128)(2,1)S(1)} %get-tuple-element.61), channel_id=1, source_target_pairs={{0,8},{4,12},{8,0},{12,4},{1,9},{5,13},{9,1},{13,5},{2,10},{6,14},... | collective-permute-start | bytes 319496 | tf_op jit(solution)/shard_map/ppermute | solution.py:149
  28.5 1.9 %collective-permute-start.5 = (s16[208,256]{1,0:T(8,128)(2,1)S(1)}, s16[208,256]{1,0:T(8,128)(2,1)S(1)}, u32[]{:S(2)}, u32[]{:S(2)}) collective-permute-start(s16[208,256]{1,0:T(8,128)(2,1)S(1)} %get-tuple-element.62), channel_id=1, source_target_pairs={{0,12},{4,8},{8,4},{12,0},{1,13},{5,9},{9,5},{13,1},{2,14},{6,10},... | collective-permute-start | bytes 319496 | tf_op jit(solution)/shard_map/ppermute | solution.py:149
  30.4 5.9 %shard_map.94 = (f32[832,128]{1,0:T(8,128)S(1)}, f32[832,128]{1,0:T(8,128)S(1)}, f32[26,128]{1,0:T(8,128)S(1)}, f32[4,104,128]{2,1,0:T(8,128)S(1)}, f32[3,104,12...) custom-call(f32[2,128]{1,0:T(2,128)S(1)} %get-tuple-element.50.mine_, ...), custom_call_target="tpu_custom_call" | custom-call | flops 5000000000 | bytes 26214400 | tf_op jit(solution)/shard_map/pallas_call | solution.py:516
  36.3 0.0 collective-permute-done.3.rest_1_
  36.4 0.9 %shard_map.95.rest_10_ = f32[832,256]{1,0:T(8,128)S(1)} custom-call(bf16[4,2,832,208]{3,2,1,0:T(8,128)(2,1)S(1)} %copy-done, s16[208,256]{1,0:T(8,128)(2,1)S(1)} %get-tuple-element.59.rest_0_, s16[208,256]{1,0:T(8,128)(2,1)S(1)} %collective-permute-done.3.rest_1_), custom_call_target="tpu_custom_call" | custom-call | flops 1000000000 | bytes 4194304 | tf_op jit(solution)/shard_map/pallas_call | solution.py:562
  37.2 0.3 collective-permute-done.4.rest_12_
  37.6 0.0 collective-permute-done.5.rest_13_
  37.6 8.5 %shard_map.96 = f32[100,2,400]{2,1,0:T(2,128)} custom-call(bf16[4,2,832,208]{3,2,1,0:T(8,128)(2,1)S(1)} %copy-done, f32[3,104,128]{2,1,0:T(8,128)S(1)} %copy-done.1, f32[832,128]{1,0:T(8,128)S(1)} %get-tuple-element.51.rest_2_, f32[832,128]{1,0:T(8,128)S(1)} %get-tuple-element.52.rest_3_, f32[26,128]{1,0:T(8,128)S(1)} %get-tuple-element.53.rest_4_, ...), custom_call_target="tpu_custom_call" | custom-call | flops 8000000000 | bytes 6291456 | tf_op jit(solution)/shard_map/pallas_call | solution.py:690
  (6 shorter events, 0.0 us)
Async XLA Ops:
  0.0 14.9 %copy-start.2 = (s32[400]{0:T(512)S(1)}, s32[400]{0:T(512)}, u32[]{:S(2)}) copy-start(s32[400]{0:T(512)} %param.13) | copy-start | bytes 4804
  5.5 16.0 %copy-start.4 = (s16[208,512]{1,0:T(8,128)(2,1)S(1)}, s16[208,512]{1,0:T(8,128)(2,1)}, u32[]{:S(2)}) copy-start(s16[208,512]{1,0:T(8,128)(2,1)} %get-tuple-element.38.rest_0_) | copy-start | bytes 638980
  5.6 16.0 %collective-permute-start = (s16[208,512]{1,0:T(8,128)(2,1)}, s16[208,512]{1,0:T(8,128)(2,1)S(1)}, u32[]{:S(2)}, u32[]{:S(2)}) collective-permute-start(s16[208,512]{1,0:T(8,128)(2,1)} %get-tuple-element.39), channel_id=1, source_target_pairs={{0,1},{1,0},{2,3},{3,2},{4,5},{5,4},{6,7},{7,6},{8,9},{9,8},{10,11... | collective-permute-start | bytes 638984 | tf_op jit(solution)/shard_map/ppermute | solution.py:149
  6.1 15.4 %collective-permute-start.1 = (s16[208,512]{1,0:T(8,128)(2,1)}, s16[208,512]{1,0:T(8,128)(2,1)S(1)}, u32[]{:S(2)}, u32[]{:S(2)}) collective-permute-start(s16[208,512]{1,0:T(8,128)(2,1)} %get-tuple-element.40), channel_id=1, source_target_pairs={{0,2},{1,3},{2,0},{3,1},{4,6},{5,7},{6,4},{7,5},{8,10},{9,11},{10,... | collective-permute-start | bytes 638984 | tf_op jit(solution)/shard_map/ppermute | solution.py:149
  8.6 12.9 %collective-permute-start.2 = (s16[208,512]{1,0:T(8,128)(2,1)}, s16[208,512]{1,0:T(8,128)(2,1)S(1)}, u32[]{:S(2)}, u32[]{:S(2)}) collective-permute-start(s16[208,512]{1,0:T(8,128)(2,1)} %get-tuple-element.41), channel_id=1, source_target_pairs={{0,3},{1,2},{2,1},{3,0},{4,7},{5,6},{6,5},{7,4},{8,11},{9,10},{10,... | collective-permute-start | bytes 638984 | tf_op jit(solution)/shard_map/ppermute | solution.py:149
  8.7 12.8 %all-to-all-start = ((f32[16,1,400]{2,1,0:T(1,128)}), f32[16,1,400]{2,1,0:T(1,128)S(1)}, u32[]{:S(2)}, u32[]{:S(2)}) async-start(f32[16,1,400]{2,1,0:T(1,128)} %get-tuple-element.42), calls=%async_computation | async-start | bytes 65536 | tf_op jit(solution)/shard_map/all_to_all | solution.py:719
  21.5 1.7 %copy-start.3 = (bf16[1,400,3072]{2,1,0:T(8,128)(2,1)S(1)}, bf16[1,400,3072]{2,1,0:T(8,128)(2,1)}, u32[]{:S(2)}) copy-start(bf16[1,400,3072]{2,1,0:T(8,128)(2,1)} %constant.6.clone.rest_5_) | copy-start | bytes 7372804
  23.2 7.2 %copy-start.1 = (f32[3,104,128]{2,1,0:T(8,128)S(1)}, f32[3,104,128]{2,1,0:T(8,128)}, u32[]{:S(2)}) copy-start(f32[3,104,128]{2,1,0:T(8,128)} %constant.7.clone.lat_ref.rest_1_) | copy-start | bytes 479236
  25.9 10.4 %copy-start = (bf16[4,2,832,208]{3,2,1,0:T(8,128)(2,1)S(1)}, bf16[4,2,832,208]{3,2,1,0:T(8,128)(2,1)}, u32[]{:S(2)}) copy-start(bf16[4,2,832,208]{3,2,1,0:T(8,128)(2,1)} %constant.8.clone.table_ref.rest_0_) | copy-start | bytes 8306692
  25.9 10.4 %collective-permute-start.3 = (s16[208,256]{1,0:T(8,128)(2,1)S(1)}, s16[208,256]{1,0:T(8,128)(2,1)S(1)}, u32[]{:S(2)}, u32[]{:S(2)}) collective-permute-start(s16[208,256]{1,0:T(8,128)(2,1)S(1)} %get-tuple-element.60), channel_id=1, source_target_pairs={{0,4},{4,0},{8,12},{12,8},{1,5},{5,1},{9,13},{13,9},{2,6},{6,2},{1... | collective-permute-start | bytes 319496 | tf_op jit(solution)/shard_map/ppermute | solution.py:149
  26.4 11.2 %collective-permute-start.4 = (s16[208,256]{1,0:T(8,128)(2,1)S(1)}, s16[208,256]{1,0:T(8,128)(2,1)S(1)}, u32[]{:S(2)}, u32[]{:S(2)}) collective-permute-start(s16[208,256]{1,0:T(8,128)(2,1)S(1)} %get-tuple-element.61), channel_id=1, source_target_pairs={{0,8},{4,12},{8,0},{12,4},{1,9},{5,13},{9,1},{13,5},{2,10},{6,14},... | collective-permute-start | bytes 319496 | tf_op jit(solution)/shard_map/ppermute | solution.py:149
  28.5 9.1 %collective-permute-start.5 = (s16[208,256]{1,0:T(8,128)(2,1)S(1)}, s16[208,256]{1,0:T(8,128)(2,1)S(1)}, u32[]{:S(2)}, u32[]{:S(2)}) collective-permute-start(s16[208,256]{1,0:T(8,128)(2,1)S(1)} %get-tuple-element.62), channel_id=1, source_target_pairs={{0,12},{4,8},{8,4},{12,0},{1,13},{5,9},{9,5},{13,1},{2,14},{6,10},... | collective-permute-start | bytes 319496 | tf_op jit(solution)/shard_map/ppermute | solution.py:149

commit v19 on v18

--- a/solution.py
+++ b/solution.py
@@ -254,10 +254,10 @@
 
 
 def fourier_kernel(ring, lat_count, pieces, *rest):
-    grids, (edge_ref, table_ref, wave_ref) = rest[:pieces], rest[pieces : pieces + 3]
-    outs, field = rest[pieces + 3 : -1], rest[-1]
+    grids, (edge_ref, *tables, wave_ref) = rest[:pieces], rest[pieces : pieces + 6]
+    outs, field = rest[pieces + 6 : -1], rest[-1]
     _, rows, width = field.shape
-    lons = table_ref.shape[1]
+    lons = tables[0].shape[1]
     share = pieces // 4
 
     end = width - LANES
@@ -295,13 +295,12 @@
         field[spot, :, end:] = tile - jnp.where(lane == spare - 1, loss, 0.0)
         field[spot, :, :LANES] += jnp.where(lane == 0, gain, 0.0)
 
-    spans = [2 * LANES, 2 * LANES, 4 * LANES, 4 * LANES]
-
     def product(kind, value, spot):
         high, low = split_bf16(value)
-        first, span = 2 * sum(spans[:kind]), spans[kind]
-        both = jnp.dot(high, table_ref[spot, :, first : first + 2 * span], preferred_element_type=jnp.float32)
-        part = jnp.dot(low, table_ref[spot, :, first : first + span], preferred_element_type=jnp.float32)
+        table = tables[kind]
+        span = table.shape[2] // 2
+        both = jnp.dot(high, table[spot], preferred_element_type=jnp.float32)
+        part = jnp.dot(low, table[spot, :, :span], preferred_element_type=jnp.float32)
         return part + both[:, :span] + both[:, span:]
 
     sums = [None, None, None]
@@ -349,14 +348,14 @@
     return pl.pallas_call(
         functools.partial(fourier_kernel, ring, lat_count, pieces),
         out_shape=[jax.ShapeDtypeStruct((padded_rows, 2 * LANES), jnp.int16)] * lat_count,
-        in_specs=[VMEM_SPEC] * (pieces + 3),
+        in_specs=[VMEM_SPEC] * (pieces + 6),
         out_specs=[VMEM_SPEC] * lat_count,
         scratch_shapes=[pltpu.VMEM((pieces, rows, width), jnp.float32)],
         compiler_params=pltpu.CompilerParams(vmem_limit_bytes=MIDDLE_BYTES),
         cost_estimate=pl.CostEstimate(
             flops=4 * 10**9, bytes_accessed=6 * 2**20, transcendentals=0
         ),
-    )(*grids, edges, np.concatenate(tables, axis=-1), wave_row)
+    )(*grids, edges, *tables, wave_row)
 
 
 def places_kernel(groups, slot_ref, wave_ref, mine_ref, sorted_rows):
@@ -679,12 +678,11 @@
     return table.reshape(pieces, full.shape[0], 2, padded_rows).transpose(0, 2, 1, 3)
 
 
-def legendre(fields, mine, prepared, rows, slots):
+def legendre(fields, mine, prepared, table, slots):
     pieces = len(fields)
     early = pieces // 2
     latitudes = latitude_table()
     points = latitudes.shape[1]
-    table = jnp.asarray(resample_pieces(pieces, rows, fields[0].shape[0]))
     total = resample(fields[:early], table)
     block_rows = SPAN * BLOCK
     return pl.pallas_call(
@@ -719,10 +717,11 @@
     edges = lax.all_to_all(edges, ("lat", *axes), split_axis=0, concat_axis=0, tiled=True)
     wave_row, mine = prepare_places(slot_wave, lat_count)
     waved = fourier(grids, edges, ring, wave_row, rows, lat_count)
-    waved, mine = lax.optimization_barrier((list(waved), mine))
+    table = jnp.asarray(resample_pieces(lat_count, rows, waved[0].shape[0]))
+    waved, mine, table = lax.optimization_barrier((list(waved), mine, table))
     fields = exchange(waved, "lat")
     prepared = prepare_recurrence(mine, lat_count)
-    return legendre(fields, mine, prepared, rows, slots)[None]
+    return legendre(fields, mine, prepared, table, slots)[None]
 
 
 def solution(mesh):

time: 46.1 us -> 44.3 us (0.961); the launches traced: 46.1 us -> 43.8 us
  local copies, waits for them, and re-layouts: 1.71 us -> 0.05 us
  Pallas kernels: 24.5 us -> 23.2 us
  waiting for transfers between devices: 5.99 us -> 6.57 us
    unnamed x10 -> x16, local copies, waits for them, and re-layouts: 1.71 us -> 0.05 us
    pallas_call x1, Pallas kernels: 8.54 us -> 7.79 us  [legendre(): pl.pallas_call(functools.partial(legendre_kernel, early), out_shape=jax.S...]
    ppermute x6, waiting for transfers between devices: 0.36 us -> 0.94 us  [exchange(): lax.ppermute(blocks[step], axis, pairs[step])]
    pallas_call x1, Pallas kernels: 5.93 us -> 5.35 us  [prepare_recurrence(): pl.pallas_call(sweep_kernel, out_shape=[orders, orders, jax.ShapeDtypeStr...]
  transfers between devices with their start and end apart: 7 -> 7, of which waited for: 2 -> 2; matrix products, arithmetic and copies ran while one was open for 0% -> 0% of each run, Pallas kernels for 17% -> 16%
where the time goes in v19:
time: 44.3 us; the launch traced here: 43.8 us
  Pallas kernels  23.2 us (52%)
  starting transfers between devices  13.8 us (31%)
  waiting for transfers between devices  6.57 us (15%)
    pallas_call x1, Pallas kernels, legendre(): pl.pallas_call(functools.partial(legendre_kernel, early), out_shape=jax.S...  7.79 us
    ppermute x6, starting transfers between devices, exchange(): lax.ppermute(blocks[step], axis, pairs[step])  7.6 us
    all_to_all x1, starting transfers between devices, shards(): lax.all_to_all(edges, ('lat', *axes), split_axis=0, concat_axis=0, tiled=...  6.16 us
    all_to_all x1, waiting for transfers between devices, shards(): lax.all_to_all(edges, ('lat', *axes), split_axis=0, concat_axis=0, tiled=...  5.63 us
    pallas_call x1, Pallas kernels, advect(): pl.pallas_call(functools.partial(advect_kernel, ring, lat_count), out_sha...  5.52 us
    pallas_call x1, Pallas kernels, prepare_recurrence(): pl.pallas_call(sweep_kernel, out_shape=[orders, orders, jax.ShapeDtypeStr...  5.35 us
    pallas_call x1, Pallas kernels, fourier(): pl.pallas_call(functools.partial(fourier_kernel, ring, lat_count, pieces)...  2.69 us
    pallas_call x1, Pallas kernels, prepare_places(): pl.pallas_call(functools.partial(places_kernel, groups), out_shape=[jax.S...  0.99 us
  transfers between devices with their start and end apart: 7, of which 2 were waited for; matrix products, arithmetic and copies ran while one was open for 0% of the time, Pallas kernels for 16%

profile of v19, /device:TPU:0, one launch (start us, length us, event | category | flops | bytes accessed | tf_op | source)
XLA Modules:
  0.0 43.8 jit_solution(6048335745632210929)
XLA Ops:
  0.0 5.5 %shard_map.118 = (s16[208,512]{1,0:T(8,128)(2,1)}, s16[208,512]{1,0:T(8,128)(2,1)}, s16[208,512]{1,0:T(8,128)(2,1)}, s16[208,512]{1,0:T(8,128)(2,1)}, f32[16,1,400]{2,1,0:T(1,128)}) custom-call(s32[1,200]{1,0:T(1,128)} %bitcast.4, bf16[4,200,400]{2,1,0:T(8,128)(2,1)} %tracer_hbm.1, bf16[4,200,400]{2,1,0:T(8,128)(2,1)} %east_hbm.1, bf16[4,200,400]{2,1,0:T(8,128)(2,1)} %north_hbm.1), custom_call_target="tpu_custom_call" | custom-call | flops 5000000000 | bytes 2560000 | tf_op jit(solution)/shard_map/pallas_call | solution.py:234
  5.5 0.0 copy-start.3
  5.5 0.0 copy-start.4
  5.6 0.0 copy-start.5
  5.6 0.0 copy-start.6
  5.6 0.0 copy-start.7
  5.6 0.5 %collective-permute-start = (s16[208,512]{1,0:T(8,128)(2,1)}, s16[208,512]{1,0:T(8,128)(2,1)S(1)}, u32[]{:S(2)}, u32[]{:S(2)}) collective-permute-start(s16[208,512]{1,0:T(8,128)(2,1)} %get-tuple-element.40), channel_id=1, source_target_pairs={{0,1},{1,0},{2,3},{3,2},{4,5},{5,4},{6,7},{7,6},{8,9},{9,8},{10,11... | collective-permute-start | bytes 638984 | tf_op jit(solution)/shard_map/ppermute | solution.py:149
  6.1 2.6 %collective-permute-start.1 = (s16[208,512]{1,0:T(8,128)(2,1)}, s16[208,512]{1,0:T(8,128)(2,1)S(1)}, u32[]{:S(2)}, u32[]{:S(2)}) collective-permute-start(s16[208,512]{1,0:T(8,128)(2,1)} %get-tuple-element.41), channel_id=1, source_target_pairs={{0,2},{1,3},{2,0},{3,1},{4,6},{5,7},{6,4},{7,5},{8,10},{9,11},{10,... | collective-permute-start | bytes 638984 | tf_op jit(solution)/shard_map/ppermute | solution.py:149
  8.7 0.1 collective-permute-start.2
  8.7 6.2 %all-to-all-start = ((f32[16,1,400]{2,1,0:T(1,128)}), f32[16,1,400]{2,1,0:T(1,128)S(1)}, u32[]{:S(2)}, u32[]{:S(2)}) async-start(f32[16,1,400]{2,1,0:T(1,128)} %get-tuple-element.43), calls=%async_computation | async-start | bytes 65536 | tf_op jit(solution)/shard_map/all_to_all | solution.py:717
  14.9 1.0 %shard_map.119 = (f32[1,512]{1,0:T(1,128)S(1)}, f32[2,128]{1,0:T(2,128)S(1)}) custom-call(s32[1,400]{1,0:T(1,128)S(1)} %bitcast.3), custom_call_target="tpu_custom_call" | custom-call | flops 2000000000 | bytes 1048576 | tf_op jit(solution)/shard_map/pallas_call | solution.py:396
  15.9 5.6 %all-to-all-done.rest_4_ = f32[16,1,400]{2,1,0:T(1,128)S(1)} async-done(((f32[16,1,400]{2,1,0:T(1,128)}), f32[16,1,400]{2,1,0:T(1,128)S(1)}, u32[]{:S(2)}, u32[]{:S(2)}) %all-to-all-start) | async-done | bytes 25632 | tf_op jit(solution)/shard_map/all_to_all | solution.py:717
  21.5 0.0 collective-permute-done.rest_1_
  21.6 0.0 copy-start.1
  21.6 2.7 %shard_map.120 = (s16[208,256]{1,0:T(8,128)(2,1)S(1)}, s16[208,256]{1,0:T(8,128)(2,1)S(1)}, s16[208,256]{1,0:T(8,128)(2,1)S(1)}, s16[208,256]{1,0:T(8,128)(2,1)S(1)}) custom-call(s16[208,512]{1,0:T(8,128)(2,1)S(1)} %copy-done.7, s16[208,512]{1,0:T(8,128)(2,1)S(1)} %collective-permute-done.rest_1_, s16[208,512]{1,0:T(8,128)(2,1)S(1)} %collective-permute-done.1.rest_2_, ...), custom_call_target="tpu_custom_call" | custom-call | flops 4000000000 | bytes 6291456 | tf_op jit(solution)/shard_map/pallas_call | solution.py:348
  24.3 0.0 copy-start
  24.3 0.4 collective-permute-start.3
  24.8 2.1 %collective-permute-start.4 = (s16[208,256]{1,0:T(8,128)(2,1)S(1)}, s16[208,256]{1,0:T(8,128)(2,1)S(1)}, u32[]{:S(2)}, u32[]{:S(2)}) collective-permute-start(s16[208,256]{1,0:T(8,128)(2,1)S(1)} %get-tuple-element.63), channel_id=1, source_target_pairs={{0,8},{4,12},{8,0},{12,4},{1,9},{5,13},{9,1},{13,5},{2,10},{6,14},... | collective-permute-start | bytes 319496 | tf_op jit(solution)/shard_map/ppermute | solution.py:149
  26.9 1.9 %collective-permute-start.5 = (s16[208,256]{1,0:T(8,128)(2,1)S(1)}, s16[208,256]{1,0:T(8,128)(2,1)S(1)}, u32[]{:S(2)}, u32[]{:S(2)}) collective-permute-start(s16[208,256]{1,0:T(8,128)(2,1)S(1)} %get-tuple-element.64), channel_id=1, source_target_pairs={{0,12},{4,8},{8,4},{12,0},{1,13},{5,9},{9,5},{13,1},{2,14},{6,10},... | collective-permute-start | bytes 319496 | tf_op jit(solution)/shard_map/ppermute | solution.py:149
  28.8 5.4 %shard_map.121 = (f32[832,128]{1,0:T(8,128)S(1)}, f32[832,128]{1,0:T(8,128)S(1)}, f32[26,128]{1,0:T(8,128)S(1)}, f32[4,104,128]{2,1,0:T(8,128)S(1)}, f32[3,104,1...) custom-call(f32[2,128]{1,0:T(2,128)S(1)} %get-tuple-element.52.mine_, ...), custom_call_target="tpu_custom_call" | custom-call | flops 5000000000 | bytes 26214400 | tf_op jit(solution)/shard_map/pallas_call | solution.py:515
  34.2 0.9 %shard_map.122.rest_10_ = f32[832,256]{1,0:T(8,128)S(1)} custom-call(bf16[4,2,832,208]{3,2,1,0:T(8,128)(2,1)S(1)} %copy-done, s16[208,256]{1,0:T(8,128)(2,1)S(1)} %get-tuple-element.61.rest_0_, s16[208,256]{1,0:T(8,128)(2,1)S(1)} %collective-permute-done.3.rest_1_), custom_call_target="tpu_custom_call" | custom-call | flops 1000000000 | bytes 4194304 | tf_op jit(solution)/shard_map/pallas_call | solution.py:561
  35.0 0.9 %collective-permute-done.4.rest_12_ = s16[208,256]{1,0:T(8,128)(2,1)S(1)} collective-permute-done((s16[208,256]{1,0:T(8,128)(2,1)S(1)}, s16[208,256]{1,0:T(8,128)(2,1)S(1)}, u32[]{:S(2)}, u32[]{:S(2)}) %collective-permute-start.4) | collective-permute-done | bytes 106528 | tf_op jit(solution)/shard_map/ppermute | solution.py:149
  36.0 0.0 collective-permute-done.5.rest_13_
  36.0 7.8 %shard_map.123 = f32[100,2,400]{2,1,0:T(2,128)} custom-call(bf16[4,2,832,208]{3,2,1,0:T(8,128)(2,1)S(1)} %copy-done, f32[3,104,128]{2,1,0:T(8,128)S(1)} %copy-done.1, f32[832,128]{1,0:T(8,128)S(1)} %get-tuple-element.53.rest_2_, f32[832,128]{1,0:T(8,128)S(1)} %get-tuple-element.54.rest_3_, f32[26,128]{1,0:T(8,128)S(1)} %get-tuple-element.55.rest_4_, ...), custom_call_target="tpu_custom_call" | custom-call | flops 8000000000 | bytes 6291456 | tf_op jit(solution)/shard_map/pallas_call | solution.py:688
  (12 shorter events, 0.0 us)
Async XLA Ops:
  0.0 14.9 %copy-start.2 = (s32[400]{0:T(512)S(1)}, s32[400]{0:T(512)}, u32[]{:S(2)}) copy-start(s32[400]{0:T(512)} %param.16) | copy-start | bytes 4804
  5.5 16.0 %copy-start.3 = (bf16[1,400,1024]{2,1,0:T(8,128)(2,1)S(1)}, bf16[1,400,1024]{2,1,0:T(8,128)(2,1)}, u32[]{:S(2)}) copy-start(bf16[1,400,1024]{2,1,0:T(8,128)(2,1)} %constant.15.clone.rest_8_) | copy-start | bytes 2457604
  5.5 16.0 %copy-start.4 = (bf16[1,400,1024]{2,1,0:T(8,128)(2,1)S(1)}, bf16[1,400,1024]{2,1,0:T(8,128)(2,1)}, u32[]{:S(2)}) copy-start(bf16[1,400,1024]{2,1,0:T(8,128)(2,1)} %constant.14.clone.rest_7_) | copy-start | bytes 2457604
  5.6 16.0 %copy-start.5 = (bf16[1,400,512]{2,1,0:T(8,128)(2,1)S(1)}, bf16[1,400,512]{2,1,0:T(8,128)(2,1)}, u32[]{:S(2)}) copy-start(bf16[1,400,512]{2,1,0:T(8,128)(2,1)} %constant.13.clone.rest_6_) | copy-start | bytes 1228804
  5.6 16.0 %copy-start.6 = (bf16[1,400,512]{2,1,0:T(8,128)(2,1)S(1)}, bf16[1,400,512]{2,1,0:T(8,128)(2,1)}, u32[]{:S(2)}) copy-start(bf16[1,400,512]{2,1,0:T(8,128)(2,1)} %constant.12.clone.rest_5_) | copy-start | bytes 1228804
  5.6 16.0 %copy-start.7 = (s16[208,512]{1,0:T(8,128)(2,1)S(1)}, s16[208,512]{1,0:T(8,128)(2,1)}, u32[]{:S(2)}) copy-start(s16[208,512]{1,0:T(8,128)(2,1)} %get-tuple-element.39.rest_0_) | copy-start | bytes 638980
  5.6 16.0 %collective-permute-start = (s16[208,512]{1,0:T(8,128)(2,1)}, s16[208,512]{1,0:T(8,128)(2,1)S(1)}, u32[]{:S(2)}, u32[]{:S(2)}) collective-permute-start(s16[208,512]{1,0:T(8,128)(2,1)} %get-tuple-element.40), channel_id=1, source_target_pairs={{0,1},{1,0},{2,3},{3,2},{4,5},{5,4},{6,7},{7,6},{8,9},{9,8},{10,11... | collective-permute-start | bytes 638984 | tf_op jit(solution)/shard_map/ppermute | solution.py:149
  6.1 15.4 %collective-permute-start.1 = (s16[208,512]{1,0:T(8,128)(2,1)}, s16[208,512]{1,0:T(8,128)(2,1)S(1)}, u32[]{:S(2)}, u32[]{:S(2)}) collective-permute-start(s16[208,512]{1,0:T(8,128)(2,1)} %get-tuple-element.41), channel_id=1, source_target_pairs={{0,2},{1,3},{2,0},{3,1},{4,6},{5,7},{6,4},{7,5},{8,10},{9,11},{10,... | collective-permute-start | bytes 638984 | tf_op jit(solution)/shard_map/ppermute | solution.py:149
  8.7 12.9 %collective-permute-start.2 = (s16[208,512]{1,0:T(8,128)(2,1)}, s16[208,512]{1,0:T(8,128)(2,1)S(1)}, u32[]{:S(2)}, u32[]{:S(2)}) collective-permute-start(s16[208,512]{1,0:T(8,128)(2,1)} %get-tuple-element.42), channel_id=1, source_target_pairs={{0,3},{1,2},{2,1},{3,0},{4,7},{5,6},{6,5},{7,4},{8,11},{9,10},{10,... | collective-permute-start | bytes 638984 | tf_op jit(solution)/shard_map/ppermute | solution.py:149
  8.7 12.8 %all-to-all-start = ((f32[16,1,400]{2,1,0:T(1,128)}), f32[16,1,400]{2,1,0:T(1,128)S(1)}, u32[]{:S(2)}, u32[]{:S(2)}) async-start(f32[16,1,400]{2,1,0:T(1,128)} %get-tuple-element.43), calls=%async_computation | async-start | bytes 65536 | tf_op jit(solution)/shard_map/all_to_all | solution.py:717
  21.6 7.2 %copy-start.1 = (f32[3,104,128]{2,1,0:T(8,128)S(1)}, f32[3,104,128]{2,1,0:T(8,128)}, u32[]{:S(2)}) copy-start(f32[3,104,128]{2,1,0:T(8,128)} %constant.17.clone.lat_ref.rest_1_) | copy-start | bytes 479236
  24.3 9.8 %copy-start = (bf16[4,2,832,208]{3,2,1,0:T(8,128)(2,1)S(1)}, bf16[4,2,832,208]{3,2,1,0:T(8,128)(2,1)}, u32[]{:S(2)}) copy-start(bf16[4,2,832,208]{3,2,1,0:T(8,128)(2,1)} %constant.16.clone.table_ref.rest_0_) | copy-start | bytes 8306692
  24.3 9.8 %collective-permute-start.3 = (s16[208,256]{1,0:T(8,128)(2,1)S(1)}, s16[208,256]{1,0:T(8,128)(2,1)S(1)}, u32[]{:S(2)}, u32[]{:S(2)}) collective-permute-start(s16[208,256]{1,0:T(8,128)(2,1)S(1)} %get-tuple-element.62), channel_id=1, source_target_pairs={{0,4},{4,0},{8,12},{12,8},{1,5},{5,1},{9,13},{13,9},{2,6},{6,2},{1... | collective-permute-start | bytes 319496 | tf_op jit(solution)/shard_map/ppermute | solution.py:149
  24.8 11.2 %collective-permute-start.4 = (s16[208,256]{1,0:T(8,128)(2,1)S(1)}, s16[208,256]{1,0:T(8,128)(2,1)S(1)}, u32[]{:S(2)}, u32[]{:S(2)}) collective-permute-start(s16[208,256]{1,0:T(8,128)(2,1)S(1)} %get-tuple-element.63), channel_id=1, source_target_pairs={{0,8},{4,12},{8,0},{12,4},{1,9},{5,13},{9,1},{13,5},{2,10},{6,14},... | collective-permute-start | bytes 319496 | tf_op jit(solution)/shard_map/ppermute | solution.py:149
  26.9 9.1 %collective-permute-start.5 = (s16[208,256]{1,0:T(8,128)(2,1)S(1)}, s16[208,256]{1,0:T(8,128)(2,1)S(1)}, u32[]{:S(2)}, u32[]{:S(2)}) collective-permute-start(s16[208,256]{1,0:T(8,128)(2,1)S(1)} %get-tuple-element.64), channel_id=1, source_target_pairs={{0,12},{4,8},{8,4},{12,0},{1,13},{5,9},{9,5},{13,1},{2,14},{6,10},... | collective-permute-start | bytes 319496 | tf_op jit(solution)/shard_map/ppermute | solution.py:149

commit v20 on v19

--- a/solution.py
+++ b/solution.py
@@ -253,7 +253,57 @@
     return list(result[:levels]), result[levels]
 
 
-def fourier_kernel(ring, lat_count, pieces, *rest):
+def exchanged_rows(rows):
+    return -(-(rows + 1) // 16) * 16
+
+
+def folded_rows(rows, slots):
+    if 2 * slots <= LANES:
+        return rows
+    fits = 2 * slots <= LANES + SIDE + 8 and rows % 16 == 0 and rows <= 16 * 16
+    return -(-(rows + rows // 2 + 16) // 16) * 16 if fits else 0
+
+
+def fold(one, two, slots):
+    rows = one.shape[0]
+    total = folded_rows(rows, slots)
+    if not total:
+        return jnp.concatenate([one, two], axis=1)
+    lane = lax.broadcasted_iota(jnp.int32, one.shape, 1)
+    turned = pltpu.roll(two, slots, 1)
+    whole = jnp.where(lane < slots, one, turned)
+    if total == rows:
+        return whole
+    half = rows // 2
+    halves = jnp.where(lane[:half] < SIDE, turned[:half], pltpu.roll(turned[half:], SIDE, 1))
+    last = jnp.zeros((16, LANES), jnp.float32)
+    for group in range(rows // 16):
+        part = pltpu.roll(turned[16 * group : 16 * group + 16], (8 * group - SIDE) % LANES, 1)
+        last = jnp.where(lane[:16] // 8 == group, part, last)
+    filler = jnp.zeros((total - rows - half - 16, LANES), jnp.float32)
+    return jnp.concatenate([whole, halves, last, filler], axis=0)
+
+
+def unfold(block, rows, slots):
+    total = folded_rows(rows, slots)
+    if not total:
+        return block[:, :LANES], block[:, LANES:]
+    whole = block[:rows]
+    lane = lax.broadcasted_iota(jnp.int32, whole.shape, 1)
+    two = pltpu.roll(whole, (LANES - slots) % LANES, 1)
+    if total != rows:
+        half = rows // 2
+        halves = block[rows : rows + half]
+        last = block[rows + half : rows + half + 16]
+        last = [pltpu.roll(last, (SIDE - 8 * group) % LANES, 1) for group in range(rows // 16)]
+        halves = jnp.concatenate([halves, pltpu.roll(halves, SIDE, 1)], axis=0)
+        rest = jnp.where(lane < SIDE, halves, jnp.concatenate(last, axis=0))
+        two = jnp.where(lane < LANES - slots, two, pltpu.roll(rest, LANES - slots, 1))
+    inside = lane < slots
+    return jnp.where(inside, whole, 0.0), jnp.where(inside, two, 0.0)
+
+
+def fourier_kernel(ring, lat_count, pieces, slots, *rest):
     grids, (edge_ref, *tables, wave_ref) = rest[:pieces], rest[pieces : pieces + 6]
     outs, field = rest[pieces + 6 : -1], rest[-1]
     _, rows, width = field.shape
@@ -332,22 +382,23 @@
         kept = jnp.where(slot_waves < keep, value, 0.0)
         code = scale_code(jnp.max(jnp.abs(kept), axis=0, keepdims=True))
         steps = coded(kept, 1.0 / scale_of(code))
-        codes = jnp.broadcast_to(code, (outs[0].shape[0] - rows, code.shape[1]))
-        placed.append(as_int16(jnp.concatenate([steps, codes], axis=0)))
+        codes = jnp.broadcast_to(code, (exchanged_rows(rows) - rows, code.shape[1]))
+        placed.append(jnp.concatenate([steps, codes], axis=0))
     for target in range(lat_count):
-        for part in range(2):
-            cols = slice(target * LANES, (target + 1) * LANES)
-            outs[target][:, part * LANES : (part + 1) * LANES] = placed[part][:, cols]
-
-
-def fourier(grids, edges, ring, wave_row, rows, lat_count):
+        cols = slice(target * LANES, (target + 1) * LANES)
+        outs[target][...] = as_int16(fold(placed[0][:, cols], placed[1][:, cols], slots))
+
+
+def fourier(grids, edges, ring, wave_row, rows, slots, lat_count):
     pieces = len(grids)
     width = grids[0].shape[1]
-    padded_rows = -(-(rows + 1) // 16) * 16
+    full = exchanged_rows(rows)
+    folded = folded_rows(full, slots)
+    shape = (folded, LANES) if folded else (full, 2 * LANES)
     tables = [table_bf16(table) for table in fourier_tables(pieces)]
     return pl.pallas_call(
-        functools.partial(fourier_kernel, ring, lat_count, pieces),
-        out_shape=[jax.ShapeDtypeStruct((padded_rows, 2 * LANES), jnp.int16)] * lat_count,
+        functools.partial(fourier_kernel, ring, lat_count, pieces, slots),
+        out_shape=[jax.ShapeDtypeStruct(shape, jnp.int16)] * lat_count,
         in_specs=[VMEM_SPEC] * (pieces + 6),
         out_specs=[VMEM_SPEC] * lat_count,
         scratch_shapes=[pltpu.VMEM((pieces, rows, width), jnp.float32)],
@@ -373,17 +424,19 @@
         column = jnp.sum(jnp.where(down == across, row, 0.0), axis=1, keepdims=True)
         ahead = (row < column) | ((row == column) & (across < down))
         rank = jnp.sum(jnp.where(ahead, 1.0, 0.0), axis=1, keepdims=True)
-        place = jnp.where(rank < paired, rank, SIDE + slots - 1.0 - rank)
-        place = jnp.where(rank < slots, place, -1.0)
-        hot = jnp.where(place == across.astype(jnp.float32), 1.0, 0.0)
-        filled = jnp.sum(hot, axis=0, keepdims=True)
-        values = jnp.sum(hot * column, axis=0, keepdims=True)
-        values = jnp.where(filled > 0.5, values, 2.0 * M)
-        sorted_rows[group] = jnp.broadcast_to(values, sorted_rows.shape[1:])
+        def ordered(side):
+            place = jnp.where(rank < paired, rank, side + slots - 1.0 - rank)
+            place = jnp.where(rank < slots, place, -1.0)
+            hot = jnp.where(place == across.astype(jnp.float32), 1.0, 0.0)
+            filled = jnp.sum(hot, axis=0, keepdims=True)
+            values = jnp.sum(hot * column, axis=0, keepdims=True)
+            return jnp.where(filled > 0.5, values, 2.0 * M)
+
+        sorted_rows[group] = jnp.broadcast_to(ordered(paired), sorted_rows.shape[1:])
 
         @pl.when(group == lat_index)
         def _():
-            mine_ref[:1] = values
+            mine_ref[:1] = ordered(SIDE)
             mine_ref[1:] = plain
 
     for step in range(groups):
@@ -533,10 +586,16 @@
     )(mine, latitudes)
 
 
-def resampled(first, fields, table, total):
+def resampled(first, fields, table, slots, total):
     for piece, field in enumerate(fields):
-        values = from_int16(field[...])
-        values = values * scale_of(values[field.shape[0] - 1 :])
+        rows = table.shape[3]
+        parts = []
+        for part in unfold(from_int16(field[...]), rows, slots):
+            part = part * scale_of(part[rows - 1 :])
+            lane = lax.broadcasted_iota(jnp.int32, part.shape, 1)
+            shift = SIDE - (slots + 1) // 2
+            parts.append(jnp.where(lane < SIDE, part, pltpu.roll(part, shift, 1)))
+        values = jnp.concatenate(parts, axis=1)
         high, low = split_bf16(values)
         spot = partner(("lat",), table.shape[:1], first + piece)
         both = jnp.concatenate([high, low], axis=1)
@@ -547,19 +606,19 @@
     return total
 
 
-def resample_kernel(table_ref, *rest):
-    rest[-1][...] = resampled(0, rest[:-1], table_ref, None)
+def resample_kernel(slots, table_ref, *rest):
+    rest[-1][...] = resampled(0, rest[:-1], table_ref, slots, None)
 
 
 def late_bytes(pieces):
     return LATE_BYTES if pieces <= 4 else VMEM_BYTES
 
 
-def resample(fields, table):
+def resample(fields, table, slots):
     count, _, height, _ = table.shape
-    span = fields[0].shape[1]
+    span = 2 * LANES
     return pl.pallas_call(
-        resample_kernel,
+        functools.partial(resample_kernel, slots),
         out_shape=jax.ShapeDtypeStruct((height, span), jnp.float32),
         in_specs=[VMEM_SPEC] * (1 + len(fields)),
         out_specs=VMEM_SPEC,
@@ -582,7 +641,7 @@
     turn = block_count(pair[0][:1])
     block_total = jnp.max(turn + block_count(pair[1][:1])).astype(jnp.int32)
 
-    total = resampled(early, fields, table, total_ref[...])
+    total = resampled(early, fields, table, slots, total_ref[...])
     totals = [total[2 * points * kind : 2 * points * (kind + 1)] for kind in range(4)]
     left = lax.broadcasted_iota(jnp.int32, (points, LANES), 1) < SIDE
     for parity in range(2):
@@ -683,7 +742,7 @@
     early = pieces // 2
     latitudes = latitude_table()
     points = latitudes.shape[1]
-    total = resample(fields[:early], table)
+    total = resample(fields[:early], table, slots)
     block_rows = SPAN * BLOCK
     return pl.pallas_call(
         functools.partial(legendre_kernel, early),
@@ -716,8 +775,8 @@
     grids = exchange(blocks, axes)
     edges = lax.all_to_all(edges, ("lat", *axes), split_axis=0, concat_axis=0, tiled=True)
     wave_row, mine = prepare_places(slot_wave, lat_count)
-    waved = fourier(grids, edges, ring, wave_row, rows, lat_count)
-    table = jnp.asarray(resample_pieces(lat_count, rows, waved[0].shape[0]))
+    waved = fourier(grids, edges, ring, wave_row, rows, slots, lat_count)
+    table = jnp.asarray(resample_pieces(lat_count, rows, exchanged_rows(rows)))
     waved, mine, table = lax.optimization_barrier((list(waved), mine, table))
     fields = exchange(waved, "lat")
     prepared = prepare_recurrence(mine, lat_count)

time: 44.3 us -> 44.6 us (level); the launches traced: 43.8 us -> 45.1 us
  Pallas kernels: 23.2 us -> 25.5 us
  waiting for transfers between devices: 6.57 us -> 5.61 us
    pallas_call x1, Pallas kernels: 7.79 us -> 8.84 us  [legendre(): pl.pallas_call(functools.partial(legendre_kernel, early), out_shape=jax.S...]
    ppermute x6, waiting for transfers between devices: 0.94 us -> 0.02 us  [exchange(): lax.ppermute(blocks[step], axis, pairs[step])]
    pallas_call x1, Pallas kernels: 5.35 us -> 5.98 us  [prepare_recurrence(): pl.pallas_call(sweep_kernel, out_shape=[orders, orders, jax.ShapeDtypeStr...]
    pallas_call x2, Pallas kernels: 3.55 us -> 4.09 us  [the longest x1 2.92 us: fourier(): pl.pallas_call(functools.partial(fourier_kernel, ring, lat_count, pieces,...]
  transfers between devices with their start and end apart: 7 -> 7, of which waited for: 2 -> 1; matrix products, arithmetic and copies ran while one was open for 0% -> 0% of each run, Pallas kernels for 16% -> 18%
where the time goes in v20:
time: 44.6 us; the launch traced here: 45.1 us
  Pallas kernels  25.5 us (57%)
  starting transfers between devices  13.8 us (31%)
  waiting for transfers between devices  5.61 us (13%)
    pallas_call x1, Pallas kernels, legendre(): pl.pallas_call(functools.partial(legendre_kernel, early), out_shape=jax.S...  8.84 us
    ppermute x6, starting transfers between devices, exchange(): lax.ppermute(blocks[step], axis, pairs[step])  7.6 us
    all_to_all x1, starting transfers between devices, shards(): lax.all_to_all(edges, ('lat', *axes), split_axis=0, concat_axis=0, tiled=...  6.16 us
    pallas_call x1, Pallas kernels, prepare_recurrence(): pl.pallas_call(sweep_kernel, out_shape=[orders, orders, jax.ShapeDtypeStr...  5.98 us
    all_to_all x1, waiting for transfers between devices, shards(): lax.all_to_all(edges, ('lat', *axes), split_axis=0, concat_axis=0, tiled=...  5.6 us
    pallas_call x1, Pallas kernels, advect(): pl.pallas_call(functools.partial(advect_kernel, ring, lat_count), out_sha...  5.52 us
    pallas_call x1, Pallas kernels, fourier(): pl.pallas_call(functools.partial(fourier_kernel, ring, lat_count, pieces,...  2.92 us
    pallas_call x1, Pallas kernels, resample(): pl.pallas_call(functools.partial(resample_kernel, slots), out_shape=jax.S...  1.17 us
  transfers between devices with their start and end apart: 7, of which 1 were waited for; matrix products, arithmetic and copies ran while one was open for 0% of the time, Pallas kernels for 18%

profile of v20, /device:TPU:0, one launch (start us, length us, event | category | flops | bytes accessed | tf_op | source)
XLA Modules:
  0.0 45.1 jit_solution(7026243253750121253)
XLA Ops:
  0.0 5.5 %shard_map.118 = (s16[208,512]{1,0:T(8,128)(2,1)}, s16[208,512]{1,0:T(8,128)(2,1)}, s16[208,512]{1,0:T(8,128)(2,1)}, s16[208,512]{1,0:T(8,128)(2,1)}, f32[16,1,400]{2,1,0:T(1,128)}) custom-call(s32[1,200]{1,0:T(1,128)} %bitcast.4, bf16[4,200,400]{2,1,0:T(8,128)(2,1)} %tracer_hbm.1, bf16[4,200,400]{2,1,0:T(8,128)(2,1)} %east_hbm.1, bf16[4,200,400]{2,1,0:T(8,128)(2,1)} %north_hbm.1), custom_call_target="tpu_custom_call" | custom-call | flops 5000000000 | bytes 2560000 | tf_op jit(solution)/shard_map/pallas_call | solution.py:234
  5.5 0.0 copy-start.3
  5.5 0.0 copy-start.4
  5.6 0.0 copy-start.5
  5.6 0.0 copy-start.6
  5.6 0.0 copy-start.7
  5.6 0.5 %collective-permute-start = (s16[208,512]{1,0:T(8,128)(2,1)}, s16[208,512]{1,0:T(8,128)(2,1)S(1)}, u32[]{:S(2)}, u32[]{:S(2)}) collective-permute-start(s16[208,512]{1,0:T(8,128)(2,1)} %get-tuple-element.40), channel_id=1, source_target_pairs={{0,1},{1,0},{2,3},{3,2},{4,5},{5,4},{6,7},{7,6},{8,9},{9,8},{10,11... | collective-permute-start | bytes 638984 | tf_op jit(solution)/shard_map/ppermute | solution.py:149
  6.1 2.6 %collective-permute-start.1 = (s16[208,512]{1,0:T(8,128)(2,1)}, s16[208,512]{1,0:T(8,128)(2,1)S(1)}, u32[]{:S(2)}, u32[]{:S(2)}) collective-permute-start(s16[208,512]{1,0:T(8,128)(2,1)} %get-tuple-element.41), channel_id=1, source_target_pairs={{0,2},{1,3},{2,0},{3,1},{4,6},{5,7},{6,4},{7,5},{8,10},{9,11},{10,... | collective-permute-start | bytes 638984 | tf_op jit(solution)/shard_map/ppermute | solution.py:149
  8.7 0.1 collective-permute-start.2
  8.7 6.2 %all-to-all-start = ((f32[16,1,400]{2,1,0:T(1,128)}), f32[16,1,400]{2,1,0:T(1,128)S(1)}, u32[]{:S(2)}, u32[]{:S(2)}) async-start(f32[16,1,400]{2,1,0:T(1,128)} %get-tuple-element.43), calls=%async_computation | async-start | bytes 65536 | tf_op jit(solution)/shard_map/all_to_all | solution.py:776
  14.9 1.0 %shard_map.119 = (f32[1,512]{1,0:T(1,128)S(1)}, f32[2,128]{1,0:T(2,128)S(1)}) custom-call(s32[1,400]{1,0:T(1,128)S(1)} %bitcast.3), custom_call_target="tpu_custom_call" | custom-call | flops 2000000000 | bytes 1048576 | tf_op jit(solution)/shard_map/pallas_call | solution.py:449
  15.9 5.6 %all-to-all-done.rest_4_ = f32[16,1,400]{2,1,0:T(1,128)S(1)} async-done(((f32[16,1,400]{2,1,0:T(1,128)}), f32[16,1,400]{2,1,0:T(1,128)S(1)}, u32[]{:S(2)}, u32[]{:S(2)}) %all-to-all-start) | async-done | bytes 25632 | tf_op jit(solution)/shard_map/all_to_all | solution.py:776
  21.5 0.0 collective-permute-done.rest_1_
  21.6 0.0 collective-permute-done.2.rest_3_
  21.6 0.0 copy-start.1
  21.6 2.9 %shard_map.120 = (s16[336,128]{1,0:T(8,128)(2,1)S(1)}, s16[336,128]{1,0:T(8,128)(2,1)S(1)}, s16[336,128]{1,0:T(8,128)(2,1)S(1)}, s16[336,128]{1,0:T(8,128)(2,1)S(1)}) custom-call(s16[208,512]{1,0:T(8,128)(2,1)S(1)} %copy-done.7, s16[208,512]{1,0:T(8,128)(2,1)S(1)} %collective-permute-done.rest_1_, s16[208,512]{1,0:T(8,128)(2,1)S(1)} %collective-permute-done.1.rest_2_, ...), custom_call_target="tpu_custom_call" | custom-call | flops 4000000000 | bytes 6291456 | tf_op jit(solution)/shard_map/pallas_call | solution.py:399
  24.6 0.0 copy-start
  24.6 0.4 collective-permute-start.3
  25.0 2.1 %collective-permute-start.4 = (s16[336,128]{1,0:T(8,128)(2,1)S(1)}, s16[336,128]{1,0:T(8,128)(2,1)S(1)}, u32[]{:S(2)}, u32[]{:S(2)}) collective-permute-start(s16[336,128]{1,0:T(8,128)(2,1)S(1)} %get-tuple-element.63), channel_id=1, source_target_pairs={{0,8},{4,12},{8,0},{12,4},{1,9},{5,13},{9,1},{13,5},{2,10},{6,14},... | collective-permute-start | bytes 258056 | tf_op jit(solution)/shard_map/ppermute | solution.py:149
  27.1 1.9 %collective-permute-start.5 = (s16[336,128]{1,0:T(8,128)(2,1)S(1)}, s16[336,128]{1,0:T(8,128)(2,1)S(1)}, u32[]{:S(2)}, u32[]{:S(2)}) collective-permute-start(s16[336,128]{1,0:T(8,128)(2,1)S(1)} %get-tuple-element.64), channel_id=1, source_target_pairs={{0,12},{4,8},{8,4},{12,0},{1,13},{5,9},{9,5},{13,1},{2,14},{6,10},... | collective-permute-start | bytes 258056 | tf_op jit(solution)/shard_map/ppermute | solution.py:149
  29.0 6.0 %shard_map.121 = (f32[832,128]{1,0:T(8,128)S(1)}, f32[832,128]{1,0:T(8,128)S(1)}, f32[26,128]{1,0:T(8,128)S(1)}, f32[4,104,128]{2,1,0:T(8,128)S(1)}, f32[3,104,1...) custom-call(f32[2,128]{1,0:T(2,128)S(1)} %get-tuple-element.52.mine_, ...), custom_call_target="tpu_custom_call" | custom-call | flops 5000000000 | bytes 26214400 | tf_op jit(solution)/shard_map/pallas_call | solution.py:568
  35.0 1.2 %shard_map.122.rest_10_ = f32[832,256]{1,0:T(8,128)S(1)} custom-call(bf16[4,2,832,208]{3,2,1,0:T(8,128)(2,1)S(1)} %copy-done, s16[336,128]{1,0:T(8,128)(2,1)S(1)} %get-tuple-element.61.rest_0_, s16[336,128]{1,0:T(8,128)(2,1)S(1)} %collective-permute-done.3.rest_1_), custom_call_target="tpu_custom_call" | custom-call | flops 1000000000 | bytes 4194304 | tf_op jit(solution)/shard_map/pallas_call | solution.py:620
  36.2 0.0 collective-permute-done.5.rest_13_
  36.2 8.8 %shard_map.123 = f32[100,2,400]{2,1,0:T(2,128)} custom-call(bf16[4,2,832,208]{3,2,1,0:T(8,128)(2,1)S(1)} %copy-done, f32[3,104,128]{2,1,0:T(8,128)S(1)} %copy-done.1, f32[832,128]{1,0:T(8,128)S(1)} %get-tuple-element.53.rest_2_, f32[832,128]{1,0:T(8,128)S(1)} %get-tuple-element.54.rest_3_, f32[26,128]{1,0:T(8,128)S(1)} %get-tuple-element.55.rest_4_, ...), custom_call_target="tpu_custom_call" | custom-call | flops 8000000000 | bytes 6291456 | tf_op jit(solution)/shard_map/pallas_call | solution.py:747
  (12 shorter events, 0.0 us)
Async XLA Ops:
  0.0 14.9 %copy-start.2 = (s32[400]{0:T(512)S(1)}, s32[400]{0:T(512)}, u32[]{:S(2)}) copy-start(s32[400]{0:T(512)} %param.16) | copy-start | bytes 4804
  5.5 16.0 %copy-start.3 = (bf16[1,400,1024]{2,1,0:T(8,128)(2,1)S(1)}, bf16[1,400,1024]{2,1,0:T(8,128)(2,1)}, u32[]{:S(2)}) copy-start(bf16[1,400,1024]{2,1,0:T(8,128)(2,1)} %constant.15.clone.rest_8_) | copy-start | bytes 2457604
  5.5 16.0 %copy-start.4 = (bf16[1,400,1024]{2,1,0:T(8,128)(2,1)S(1)}, bf16[1,400,1024]{2,1,0:T(8,128)(2,1)}, u32[]{:S(2)}) copy-start(bf16[1,400,1024]{2,1,0:T(8,128)(2,1)} %constant.14.clone.rest_7_) | copy-start | bytes 2457604
  5.6 16.0 %copy-start.5 = (bf16[1,400,512]{2,1,0:T(8,128)(2,1)S(1)}, bf16[1,400,512]{2,1,0:T(8,128)(2,1)}, u32[]{:S(2)}) copy-start(bf16[1,400,512]{2,1,0:T(8,128)(2,1)} %constant.13.clone.rest_6_) | copy-start | bytes 1228804
  5.6 16.0 %copy-start.6 = (bf16[1,400,512]{2,1,0:T(8,128)(2,1)S(1)}, bf16[1,400,512]{2,1,0:T(8,128)(2,1)}, u32[]{:S(2)}) copy-start(bf16[1,400,512]{2,1,0:T(8,128)(2,1)} %constant.12.clone.rest_5_) | copy-start | bytes 1228804
  5.6 16.0 %copy-start.7 = (s16[208,512]{1,0:T(8,128)(2,1)S(1)}, s16[208,512]{1,0:T(8,128)(2,1)}, u32[]{:S(2)}) copy-start(s16[208,512]{1,0:T(8,128)(2,1)} %get-tuple-element.39.rest_0_) | copy-start | bytes 638980
  5.6 16.0 %collective-permute-start = (s16[208,512]{1,0:T(8,128)(2,1)}, s16[208,512]{1,0:T(8,128)(2,1)S(1)}, u32[]{:S(2)}, u32[]{:S(2)}) collective-permute-start(s16[208,512]{1,0:T(8,128)(2,1)} %get-tuple-element.40), channel_id=1, source_target_pairs={{0,1},{1,0},{2,3},{3,2},{4,5},{5,4},{6,7},{7,6},{8,9},{9,8},{10,11... | collective-permute-start | bytes 638984 | tf_op jit(solution)/shard_map/ppermute | solution.py:149
  6.1 15.4 %collective-permute-start.1 = (s16[208,512]{1,0:T(8,128)(2,1)}, s16[208,512]{1,0:T(8,128)(2,1)S(1)}, u32[]{:S(2)}, u32[]{:S(2)}) collective-permute-start(s16[208,512]{1,0:T(8,128)(2,1)} %get-tuple-element.41), channel_id=1, source_target_pairs={{0,2},{1,3},{2,0},{3,1},{4,6},{5,7},{6,4},{7,5},{8,10},{9,11},{10,... | collective-permute-start | bytes 638984 | tf_op jit(solution)/shard_map/ppermute | solution.py:149
  8.7 12.9 %collective-permute-start.2 = (s16[208,512]{1,0:T(8,128)(2,1)}, s16[208,512]{1,0:T(8,128)(2,1)S(1)}, u32[]{:S(2)}, u32[]{:S(2)}) collective-permute-start(s16[208,512]{1,0:T(8,128)(2,1)} %get-tuple-element.42), channel_id=1, source_target_pairs={{0,3},{1,2},{2,1},{3,0},{4,7},{5,6},{6,5},{7,4},{8,11},{9,10},{10,... | collective-permute-start | bytes 638984 | tf_op jit(solution)/shard_map/ppermute | solution.py:149
  8.7 12.8 %all-to-all-start = ((f32[16,1,400]{2,1,0:T(1,128)}), f32[16,1,400]{2,1,0:T(1,128)S(1)}, u32[]{:S(2)}, u32[]{:S(2)}) async-start(f32[16,1,400]{2,1,0:T(1,128)} %get-tuple-element.43), calls=%async_computation | async-start | bytes 65536 | tf_op jit(solution)/shard_map/all_to_all | solution.py:776
  21.6 7.4 %copy-start.1 = (f32[3,104,128]{2,1,0:T(8,128)S(1)}, f32[3,104,128]{2,1,0:T(8,128)}, u32[]{:S(2)}) copy-start(f32[3,104,128]{2,1,0:T(8,128)} %constant.17.clone.lat_ref.rest_1_) | copy-start | bytes 479236
  24.6 10.5 %copy-start = (bf16[4,2,832,208]{3,2,1,0:T(8,128)(2,1)S(1)}, bf16[4,2,832,208]{3,2,1,0:T(8,128)(2,1)}, u32[]{:S(2)}) copy-start(bf16[4,2,832,208]{3,2,1,0:T(8,128)(2,1)} %constant.16.clone.table_ref.rest_0_) | copy-start | bytes 8306692
  24.6 10.4 %collective-permute-start.3 = (s16[336,128]{1,0:T(8,128)(2,1)S(1)}, s16[336,128]{1,0:T(8,128)(2,1)S(1)}, u32[]{:S(2)}, u32[]{:S(2)}) collective-permute-start(s16[336,128]{1,0:T(8,128)(2,1)S(1)} %get-tuple-element.62), channel_id=1, source_target_pairs={{0,4},{4,0},{8,12},{12,8},{1,5},{5,1},{9,13},{13,9},{2,6},{6,2},{1... | collective-permute-start | bytes 258056 | tf_op jit(solution)/shard_map/ppermute | solution.py:149
  25.0 11.2 %collective-permute-start.4 = (s16[336,128]{1,0:T(8,128)(2,1)S(1)}, s16[336,128]{1,0:T(8,128)(2,1)S(1)}, u32[]{:S(2)}, u32[]{:S(2)}) collective-permute-start(s16[336,128]{1,0:T(8,128)(2,1)S(1)} %get-tuple-element.63), channel_id=1, source_target_pairs={{0,8},{4,12},{8,0},{12,4},{1,9},{5,13},{9,1},{13,5},{2,10},{6,14},... | collective-permute-start | bytes 258056 | tf_op jit(solution)/shard_map/ppermute | solution.py:149
  27.1 9.1 %collective-permute-start.5 = (s16[336,128]{1,0:T(8,128)(2,1)S(1)}, s16[336,128]{1,0:T(8,128)(2,1)S(1)}, u32[]{:S(2)}, u32[]{:S(2)}) collective-permute-start(s16[336,128]{1,0:T(8,128)(2,1)S(1)} %get-tuple-element.64), channel_id=1, source_target_pairs={{0,12},{4,8},{8,4},{12,0},{1,13},{5,9},{9,5},{13,1},{2,14},{6,10},... | collective-permute-start | bytes 258056 | tf_op jit(solution)/shard_map/ppermute | solution.py:149

commit v21 on v20

--- a/solution.py
+++ b/solution.py
@@ -60,10 +60,8 @@
     for first in (0, 2):
         cosine, sine = parts(np.arange(first, M, 4))
         tables.append(shaped([cosine, -sine]))
-    waves = np.arange(1, M, 2)
-    sign = np.where(waves % 4 == 1, 1.0, -1.0)[None, :]
-    cosine, sine = parts(waves)
-    return [*tables, shaped([cosine, -sine]), shaped([-sign * sine, -sign * cosine])]
+    cosine, sine = parts(np.arange(1, M, 2))
+    return [*tables, shaped([cosine, -sine])]
 
 
 def column_waves(shape):
@@ -304,8 +302,8 @@
 
 
 def fourier_kernel(ring, lat_count, pieces, slots, *rest):
-    grids, (edge_ref, *tables, wave_ref) = rest[:pieces], rest[pieces : pieces + 6]
-    outs, field = rest[pieces + 6 : -1], rest[-1]
+    grids, (edge_ref, *tables, wave_ref) = rest[:pieces], rest[pieces : pieces + 5]
+    outs, field = rest[pieces + 5 : -1], rest[-1]
     _, rows, width = field.shape
     lons = tables[0].shape[1]
     share = pieces // 4
@@ -358,10 +356,13 @@
         quarters = [field[quarter * share + spot, :, :lons] for quarter in range(4)]
         sum02, dif02 = quarters[0] + quarters[2], quarters[0] - quarters[2]
         sum13, dif13 = quarters[1] + quarters[3], quarters[1] - quarters[3]
-        parts = []
-        for kind, value in enumerate((sum02 + sum13, sum02 - sum13, dif02, dif13)):
-            parts.append(product(kind, value, spot))
-        parts = [parts[0], parts[1], parts[2] + parts[3]]
+        odd, turned = product(2, dif02, spot), product(2, dif13, spot)
+        half = odd.shape[1] // 2
+        cosine, sine = turned[:, :half], turned[:, half:]
+        even = lax.broadcasted_iota(jnp.int32, cosine.shape, 1) % 2 == 0
+        turned = [jnp.where(even, sine, -sine), jnp.where(even, -cosine, cosine)]
+        odd = odd + jnp.concatenate(turned, axis=1)
+        parts = [product(0, sum02 + sum13, spot), product(1, sum02 - sum13, spot), odd]
         sums = [part if total is None else total + part for total, part in zip(sums, parts)]
     slot_waves = wave_ref[...]
     waves = column_waves((column_count(), LANES))
@@ -399,7 +400,7 @@
     return pl.pallas_call(
         functools.partial(fourier_kernel, ring, lat_count, pieces, slots),
         out_shape=[jax.ShapeDtypeStruct(shape, jnp.int16)] * lat_count,
-        in_specs=[VMEM_SPEC] * (pieces + 6),
+        in_specs=[VMEM_SPEC] * (pieces + 5),
         out_specs=[VMEM_SPEC] * lat_count,
         scratch_shapes=[pltpu.VMEM((pieces, rows, width), jnp.float32)],
         compiler_params=pltpu.CompilerParams(vmem_limit_bytes=MIDDLE_BYTES),
@@ -409,7 +410,9 @@
     )(*grids, edges, *tables, wave_row)
 
 
-def places_kernel(groups, slot_ref, wave_ref, mine_ref, sorted_rows):
+def places_kernel(
+    groups, slot_ref, lat_ref, wave_ref, mine_ref, beta_ref, start_ref, back_ref, sorted_rows
+):
     lat_index = lax.axis_index("lat")
     slots = slot_ref.shape[1] // groups
     paired = (slots + 1) // 2
@@ -442,22 +445,28 @@
     for step in range(groups):
         row = sorted_rows[partner(("lat",), (groups,), step), :1]
         wave_ref[:, step * LANES : (step + 1) * LANES] = row
-
-
-def prepare_places(slot_wave, groups):
+    recurrence_tables(mine_ref, lat_ref, beta_ref, start_ref, back_ref)
+
+
+def prepare_places(slot_wave, groups, latitudes):
     width = groups * LANES
+    blocks = 2 * SPAN
+    orders = jax.ShapeDtypeStruct((blocks * BLOCK, LANES), jnp.float32)
     return pl.pallas_call(
         functools.partial(places_kernel, groups),
         out_shape=[
             jax.ShapeDtypeStruct((1, width), jnp.float32),
             jax.ShapeDtypeStruct((2, LANES), jnp.float32),
+            orders,
+            jax.ShapeDtypeStruct((4, latitudes.shape[1], LANES), jnp.float32),
+            jax.ShapeDtypeStruct((LANES, LANES), jnp.bfloat16),
         ],
-        in_specs=[VMEM_SPEC],
-        out_specs=[VMEM_SPEC] * 2,
+        in_specs=[VMEM_SPEC] * 2,
+        out_specs=[VMEM_SPEC] * 5,
         scratch_shapes=[pltpu.VMEM((groups, 8, LANES), jnp.float32)],
         compiler_params=pltpu.CompilerParams(vmem_limit_bytes=MIDDLE_BYTES),
         cost_estimate=pl.CostEstimate(flops=2 * 10**9, bytes_accessed=2**20, transcendentals=0),
-    )(slot_wave[None])
+    )(slot_wave[None], latitudes)
 
 
 def lane_pairs(row):
@@ -470,10 +479,14 @@
     return jnp.floor((jnp.maximum(M - wave, 0.0) + (BLOCK - 1)) * (1.0 / BLOCK))
 
 
-def sweep_kernel(
-    mine_ref, lat_ref,
-    beta_ref, scale_ref, growth_ref, start_ref, state_ref, values_ref, more_ref, back_ref,
-):
+def lane_orders(one, two, blocks):
+    turn = block_count(one)
+    block = lax.broadcasted_iota(jnp.int32, (blocks, LANES), 0).astype(jnp.float32)
+    second = block >= turn
+    return jnp.where(second, two, one), (block - jnp.where(second, turn, 0.0)) * BLOCK
+
+
+def recurrence_tables(mine_ref, lat_ref, beta_ref, start_ref, back_ref):
     shape = (LANES, LANES)
     same = lax.broadcasted_iota(jnp.int32, shape, 0) == lax.broadcasted_iota(jnp.int32, shape, 1)
     plain = jnp.broadcast_to(mine_ref[1:], shape)
@@ -482,27 +495,15 @@
     back_ref[...] = jnp.where(hot, 1.0, 0.0).astype(jnp.bfloat16)
     pair = lane_pairs(jnp.broadcast_to(mine_ref[:1], (8, LANES)))
     one, two = pair[0][:1], pair[1][:1]
-    blocks = growth_ref.shape[0]
-    turn = block_count(one)
-    block = lax.broadcasted_iota(jnp.int32, (blocks, LANES), 0).astype(jnp.float32)
-    second = block >= turn
-    wave = jnp.where(second, two, one)
-    limit = M - wave
+    blocks = beta_ref.shape[0] // BLOCK
+    wave, first = lane_orders(one, two, blocks)
     wave = jnp.minimum(wave, M - 1.0)
-    first = (block - jnp.where(second, turn, 0.0)) * BLOCK
-
-    scale = jnp.ones((blocks, LANES), jnp.float32)
-    for index in range(BLOCK + 1):
+    for index in range(BLOCK):
         order = first + index
         degree = wave + order
         square = 4.0 * degree * degree - 1.0
         spread = 4.0 * order * (degree + wave)
-        if index > 0:
-            scale = scale * jnp.sqrt(square / spread)
-        if index < BLOCK:
-            beta_ref[pl.ds(index, blocks, stride=BLOCK)] = spread / jnp.maximum(square, 1.0)
-            scale_ref[pl.ds(index, blocks, stride=BLOCK)] = jnp.where(order < limit, scale, 0.0)
-    growth_ref[...] = scale
+        beta_ref[pl.ds(index, blocks, stride=BLOCK)] = spread / jnp.maximum(square, 1.0)
 
     counter = lax.broadcasted_iota(jnp.int32, (M, LANES), 0).astype(jnp.float32) + 1.0
     terms = jnp.log(1.0 + 0.5 / counter) * (1.0 / math.log(2.0))
@@ -515,6 +516,29 @@
             (coarse - whole) + lat_ref[2] * wave + 0.5 * (norm - 1.0)
         )
         start_ref[2 * kind + 1] = whole
+
+
+def sweep_kernel(
+    mine_ref, lat_ref, beta_ref, start_ref,
+    scale_ref, growth_ref, state_ref, values_ref, more_ref,
+):
+    pair = lane_pairs(jnp.broadcast_to(mine_ref[:1], (8, LANES)))
+    one, two = pair[0][:1], pair[1][:1]
+    turn = block_count(one)
+
+    blocks = growth_ref.shape[0]
+    wave, first_order = lane_orders(one, two, blocks)
+    limit = M - wave
+    scale = jnp.ones((blocks, LANES), jnp.float32)
+    for index in range(BLOCK):
+        if index > 0:
+            beta = beta_ref[pl.ds(index, blocks, stride=BLOCK)]
+            scale = scale * lax.rsqrt(jnp.maximum(beta, 1e-6))
+        inside = first_order + index < limit
+        scale_ref[pl.ds(index, blocks, stride=BLOCK)] = jnp.where(inside, scale, 0.0)
+    beta = beta_ref[pl.ds(BLOCK, blocks - 1, stride=BLOCK)]
+    beta = jnp.concatenate([beta, jnp.ones((1, LANES), jnp.float32)], axis=0)
+    growth_ref[...] = scale * lax.rsqrt(jnp.maximum(beta, 1e-6))
 
     state_ref[0] = jnp.zeros_like(state_ref[0])
     state_ref[1] = start_ref[0]
@@ -560,30 +584,25 @@
     state_ref[2, rows] = height + shift
 
 
-def prepare_recurrence(mine, pieces):
-    latitudes = latitude_table()
+def sweep(mine, latitudes, beta, start, pieces):
     points = latitudes.shape[1]
-    blocks = 2 * SPAN
-    orders = jax.ShapeDtypeStruct((blocks * BLOCK, LANES), jnp.float32)
+    blocks = beta.shape[0] // BLOCK
     return pl.pallas_call(
         sweep_kernel,
         out_shape=[
-            orders,
-            orders,
+            jax.ShapeDtypeStruct(beta.shape, jnp.float32),
             jax.ShapeDtypeStruct((blocks, LANES), jnp.float32),
-            jax.ShapeDtypeStruct((4, points, LANES), jnp.float32),
             jax.ShapeDtypeStruct((3, points, LANES), jnp.float32),
             jax.ShapeDtypeStruct((HELD, BLOCK, points, LANES), jnp.float32),
             jax.ShapeDtypeStruct((MORE, BLOCK, points, LANES), jnp.float32),
-            jax.ShapeDtypeStruct((LANES, LANES), jnp.bfloat16),
         ],
-        in_specs=[VMEM_SPEC] * 2,
-        out_specs=[VMEM_SPEC] * 8,
+        in_specs=[VMEM_SPEC] * 4,
+        out_specs=[VMEM_SPEC] * 5,
         compiler_params=pltpu.CompilerParams(vmem_limit_bytes=late_bytes(pieces)),
         cost_estimate=pl.CostEstimate(
             flops=5 * 10**9, bytes_accessed=25 * 2**20, transcendentals=0
         ),
-    )(mine, latitudes)
+    )(mine, latitudes, beta, start)
 
 
 def resampled(first, fields, table, slots, total):
@@ -737,10 +756,9 @@
     return table.reshape(pieces, full.shape[0], 2, padded_rows).transpose(0, 2, 1, 3)
 
 
-def legendre(fields, mine, prepared, table, slots):
+def legendre(fields, mine, latitudes, prepared, table, slots):
     pieces = len(fields)
     early = pieces // 2
-    latitudes = latitude_table()
     points = latitudes.shape[1]
     total = resample(fields[:early], table, slots)
     block_rows = SPAN * BLOCK
@@ -774,13 +792,15 @@
     blocks, slot_wave = lax.optimization_barrier((blocks, slot_wave))
     grids = exchange(blocks, axes)
     edges = lax.all_to_all(edges, ("lat", *axes), split_axis=0, concat_axis=0, tiled=True)
-    wave_row, mine = prepare_places(slot_wave, lat_count)
+    latitudes = jnp.asarray(latitude_table())
+    wave_row, mine, beta, start, back = prepare_places(slot_wave, lat_count, latitudes)
     waved = fourier(grids, edges, ring, wave_row, rows, slots, lat_count)
     table = jnp.asarray(resample_pieces(lat_count, rows, exchanged_rows(rows)))
     waved, mine, table = lax.optimization_barrier((list(waved), mine, table))
     fields = exchange(waved, "lat")
-    prepared = prepare_recurrence(mine, lat_count)
-    return legendre(fields, mine, prepared, table, slots)[None]
+    scale, growth, state, values, more = sweep(mine, latitudes, beta, start, lat_count)
+    prepared = (beta, scale, growth, start, state, values, more, back)
+    return legendre(fields, mine, latitudes, prepared, table, slots)[None]
 
 
 def solution(mesh):

time: 44.6 us -> 43.9 us (0.984)
  waiting for transfers between devices: 5.61 us -> 4.84 us
    all_to_all x1, waiting for transfers between devices: 5.6 us -> 4.83 us  [shards(): lax.all_to_all(edges, ('lat', *axes), split_axis=0, concat_axis=0, tiled=...]
    pallas_call x1, Pallas kernels: 1.02 us -> 1.78 us  [prepare_places(): pl.pallas_call(functools.partial(places_kernel, groups), out_shape=[jax.S...]
    pallas_call x1, Pallas kernels: 5.98 us -> 5.34 us  [sweep(): pl.pallas_call(sweep_kernel, out_shape=[jax.ShapeDtypeStruct(beta.shape,...]
  transfers between devices with their start and end apart: 7 -> 7, of which waited for: 1 -> 1; matrix products, arithmetic and copies ran while one was open for 0% -> 0% of each run, Pallas kernels for 18% -> 19%
where the time goes in v21:
time: 43.9 us; the launch traced here: 44.4 us
  Pallas kernels  25.6 us (58%)
  starting transfers between devices  13.8 us (31%)
  waiting for transfers between devices  4.84 us (11%)
    pallas_call x1, Pallas kernels, legendre(): pl.pallas_call(functools.partial(legendre_kernel, early), out_shape=jax.S...  8.86 us
    ppermute x6, starting transfers between devices, exchange(): lax.ppermute(blocks[step], axis, pairs[step])  7.61 us
    all_to_all x1, starting transfers between devices, shards(): lax.all_to_all(edges, ('lat', *axes), split_axis=0, concat_axis=0, tiled=...  6.16 us
    pallas_call x1, Pallas kernels, advect(): pl.pallas_call(functools.partial(advect_kernel, ring, lat_count), out_sha...  5.56 us
    pallas_call x1, Pallas kernels, sweep(): pl.pallas_call(sweep_kernel, out_shape=[jax.ShapeDtypeStruct(beta.shape,...  5.34 us
    all_to_all x1, waiting for transfers between devices, shards(): lax.all_to_all(edges, ('lat', *axes), split_axis=0, concat_axis=0, tiled=...  4.83 us
    pallas_call x1, Pallas kernels, fourier(): pl.pallas_call(functools.partial(fourier_kernel, ring, lat_count, pieces,...  2.88 us
    pallas_call x1, Pallas kernels, prepare_places(): pl.pallas_call(functools.partial(places_kernel, groups), out_shape=[jax.S...  1.78 us
  transfers between devices with their start and end apart: 7, of which 1 were waited for; matrix products, arithmetic and copies ran while one was open for 0% of the time, Pallas kernels for 19%

profile of v21, /device:TPU:0, one launch (start us, length us, event | category | flops | bytes accessed | tf_op | source)
XLA Modules:
  0.0 44.4 jit_solution(14705847055800370286)
XLA Ops:
  0.0 5.6 %shard_map.100 = (s16[208,512]{1,0:T(8,128)(2,1)}, s16[208,512]{1,0:T(8,128)(2,1)}, s16[208,512]{1,0:T(8,128)(2,1)}, s16[208,512]{1,0:T(8,128)(2,1)}, f32[16,1,400]{2,1,0:T(1,128)}) custom-call(s32[1,200]{1,0:T(1,128)} %bitcast.4, bf16[4,200,400]{2,1,0:T(8,128)(2,1)} %tracer_hbm.1, bf16[4,200,400]{2,1,0:T(8,128)(2,1)} %east_hbm.1, bf16[4,200,400]{2,1,0:T(8,128)(2,1)} %north_hbm.1), custom_call_target="tpu_custom_call" | custom-call | flops 5000000000 | bytes 2560000 | tf_op jit(solution)/shard_map/pallas_call | solution.py:232
  5.6 0.0 copy-start.3
  5.6 0.0 copy-start.4
  5.6 0.0 copy-start.5
  5.6 0.0 copy-start.6
  5.6 0.5 %collective-permute-start = (s16[208,512]{1,0:T(8,128)(2,1)}, s16[208,512]{1,0:T(8,128)(2,1)S(1)}, u32[]{:S(2)}, u32[]{:S(2)}) collective-permute-start(s16[208,512]{1,0:T(8,128)(2,1)} %get-tuple-element.40), channel_id=1, source_target_pairs={{0,1},{1,0},{2,3},{3,2},{4,5},{5,4},{6,7},{7,6},{8,9},{9,8},{10,11... | collective-permute-start | bytes 638984 | tf_op jit(solution)/shard_map/ppermute | solution.py:147
  6.1 2.6 %collective-permute-start.1 = (s16[208,512]{1,0:T(8,128)(2,1)}, s16[208,512]{1,0:T(8,128)(2,1)S(1)}, u32[]{:S(2)}, u32[]{:S(2)}) collective-permute-start(s16[208,512]{1,0:T(8,128)(2,1)} %get-tuple-element.41), channel_id=1, source_target_pairs={{0,2},{1,3},{2,0},{3,1},{4,6},{5,7},{6,4},{7,5},{8,10},{9,11},{10,... | collective-permute-start | bytes 638984 | tf_op jit(solution)/shard_map/ppermute | solution.py:147
  8.7 0.1 collective-permute-start.2
  8.8 6.2 %all-to-all-start = ((f32[16,1,400]{2,1,0:T(1,128)}), f32[16,1,400]{2,1,0:T(1,128)S(1)}, u32[]{:S(2)}, u32[]{:S(2)}) async-start(f32[16,1,400]{2,1,0:T(1,128)} %get-tuple-element.43), calls=%async_computation | async-start | bytes 65536 | tf_op jit(solution)/shard_map/all_to_all | solution.py:794
  15.0 1.8 %shard_map.101 = (f32[1,512]{1,0:T(1,128)S(1)}, f32[2,128]{1,0:T(2,128)S(1)}, f32[832,128]{1,0:T(8,128)S(1)}, f32[4,104,128]{2,1,0:T(8,128)S(1)}, bf16[128,128]{1,0:T(8,128)(2,1)S(1)}) custom-call(s32[1,400]{1,0:T(1,128)S(1)} %bitcast.3, f32[3,104,128]{2,1,0:T(8,128)S(1)} %copy-done.1), custom_call_target="tpu_custom_call" | custom-call | flops 2000000000 | bytes 1048576 | tf_op jit(solution)/shard_map/pallas_call | solution.py:455
  16.8 4.8 %all-to-all-done.rest_4_ = f32[16,1,400]{2,1,0:T(1,128)S(1)} async-done(((f32[16,1,400]{2,1,0:T(1,128)}), f32[16,1,400]{2,1,0:T(1,128)S(1)}, u32[]{:S(2)}, u32[]{:S(2)}) %all-to-all-start) | async-done | bytes 25632 | tf_op jit(solution)/shard_map/all_to_all | solution.py:794
  21.6 0.0 collective-permute-done.rest_1_
  21.6 0.0 collective-permute-done.1.rest_2_
  21.6 0.0 collective-permute-done.2.rest_3_
  21.6 2.9 %shard_map.102 = (s16[336,128]{1,0:T(8,128)(2,1)S(1)}, s16[336,128]{1,0:T(8,128)(2,1)S(1)}, s16[336,128]{1,0:T(8,128)(2,1)S(1)}, s16[336,128]{1,0:T(8,128)(2,1)S(1)}) custom-call(s16[208,512]{1,0:T(8,128)(2,1)S(1)} %copy-done.6, s16[208,512]{1,0:T(8,128)(2,1)S(1)} %collective-permute-done.rest_1_, s16[208,512]{1,0:T(8,128)(2,1)S(1)} %collective-permute-done.1.rest_2_, ...), custom_call_target="tpu_custom_call" | custom-call | flops 4000000000 | bytes 6291456 | tf_op jit(solution)/shard_map/pallas_call | solution.py:400
  24.5 0.4 collective-permute-start.3
  24.9 2.1 %collective-permute-start.4 = (s16[336,128]{1,0:T(8,128)(2,1)S(1)}, s16[336,128]{1,0:T(8,128)(2,1)S(1)}, u32[]{:S(2)}, u32[]{:S(2)}) collective-permute-start(s16[336,128]{1,0:T(8,128)(2,1)S(1)} %get-tuple-element.63), channel_id=1, source_target_pairs={{0,8},{4,12},{8,0},{12,4},{1,9},{5,13},{9,1},{13,5},{2,10},{6,14},... | collective-permute-start | bytes 258056 | tf_op jit(solution)/shard_map/ppermute | solution.py:147
  27.1 1.9 %collective-permute-start.5 = (s16[336,128]{1,0:T(8,128)(2,1)S(1)}, s16[336,128]{1,0:T(8,128)(2,1)S(1)}, u32[]{:S(2)}, u32[]{:S(2)}) collective-permute-start(s16[336,128]{1,0:T(8,128)(2,1)S(1)} %get-tuple-element.64), channel_id=1, source_target_pairs={{0,12},{4,8},{8,4},{12,0},{1,13},{5,9},{9,5},{13,1},{2,14},{6,10},... | collective-permute-start | bytes 258056 | tf_op jit(solution)/shard_map/ppermute | solution.py:147
  29.0 5.3 %shard_map.103 = (f32[832,128]{1,0:T(8,128)S(1)}, f32[26,128]{1,0:T(8,128)S(1)}, f32[3,104,128]{2,1,0:T(8,128)S(1)}, f32[13,32,104,128]{3,2,1,0:T(8,128)S(1)}, f32[3,32,104,128]{3,2,1,0:T(8,128)S(1)}) custom-call(f32[2,128]{1,0:T(2,128)S(1)} %get-tuple-element.53.mine_ref.rest_11_, f32[3,104,128]{2,1,0:T(8,128)S(1)} %copy-done.1, ...), custom_call_target="tpu_custom_call" | custom-call | flops 5000000000 | bytes 26214400 | tf_op jit(solution)/shard_map/pallas_call | solution.py:590
  34.3 0.0 collective-permute-done.3.rest_1_
  34.3 1.2 %shard_map.104.rest_10_ = f32[832,256]{1,0:T(8,128)S(1)} custom-call(bf16[4,2,832,208]{3,2,1,0:T(8,128)(2,1)S(1)} %copy-done, s16[336,128]{1,0:T(8,128)(2,1)S(1)} %get-tuple-element.61.rest_0_, s16[336,128]{1,0:T(8,128)(2,1)S(1)} %collective-permute-done.3.rest_1_), custom_call_target="tpu_custom_call" | custom-call | flops 1000000000 | bytes 4194304 | tf_op jit(solution)/shard_map/pallas_call | solution.py:639
  35.5 0.0 collective-permute-done.4.rest_12_
  35.5 0.0 collective-permute-done.5.rest_13_
  35.5 8.9 %shard_map.105 = f32[100,2,400]{2,1,0:T(2,128)} custom-call(bf16[4,2,832,208]{3,2,1,0:T(8,128)(2,1)S(1)} %copy-done, f32[3,104,128]{2,1,0:T(8,128)S(1)} %copy-done.1, f32[832,128]{1,0:T(8,128)S(1)} %get-tuple-element.52.beta_ref.rest_2_, f32[832,128]{1,0:T(8,128)S(1)} %get-tuple-element.55.rest_3_, f32[26,128]{1,0:T(8,128)S(1)} %get-tuple-element.56.rest_4_, ...), custom_call_target="tpu_custom_call" | custom-call | flops 8000000000 | bytes 6291456 | tf_op jit(solution)/shard_map/pallas_call | solution.py:765
  (10 shorter events, 0.0 us)
Async XLA Ops:
  0.0 14.9 %copy-start.1 = (f32[3,104,128]{2,1,0:T(8,128)S(1)}, f32[3,104,128]{2,1,0:T(8,128)}, u32[]{:S(2)}) copy-start(f32[3,104,128]{2,1,0:T(8,128)} %constant.10.clone.lat_ref.rest_1_) | copy-start | bytes 479236
  0.0 15.0 %copy-start.2 = (s32[400]{0:T(512)S(1)}, s32[400]{0:T(512)}, u32[]{:S(2)}) copy-start(s32[400]{0:T(512)} %param.14) | copy-start | bytes 4804
  5.6 16.0 %copy-start.3 = (bf16[1,400,1024]{2,1,0:T(8,128)(2,1)S(1)}, bf16[1,400,1024]{2,1,0:T(8,128)(2,1)}, u32[]{:S(2)}) copy-start(bf16[1,400,1024]{2,1,0:T(8,128)(2,1)} %constant.13.clone.rest_7_) | copy-start | bytes 2457604
  5.6 16.0 %copy-start.4 = (bf16[1,400,512]{2,1,0:T(8,128)(2,1)S(1)}, bf16[1,400,512]{2,1,0:T(8,128)(2,1)}, u32[]{:S(2)}) copy-start(bf16[1,400,512]{2,1,0:T(8,128)(2,1)} %constant.12.clone.rest_6_) | copy-start | bytes 1228804
  5.6 16.0 %copy-start.5 = (bf16[1,400,512]{2,1,0:T(8,128)(2,1)S(1)}, bf16[1,400,512]{2,1,0:T(8,128)(2,1)}, u32[]{:S(2)}) copy-start(bf16[1,400,512]{2,1,0:T(8,128)(2,1)} %constant.11.clone.rest_5_) | copy-start | bytes 1228804
  5.6 16.0 %copy-start.6 = (s16[208,512]{1,0:T(8,128)(2,1)S(1)}, s16[208,512]{1,0:T(8,128)(2,1)}, u32[]{:S(2)}) copy-start(s16[208,512]{1,0:T(8,128)(2,1)} %get-tuple-element.39.rest_0_) | copy-start | bytes 638980
  5.6 16.0 %collective-permute-start = (s16[208,512]{1,0:T(8,128)(2,1)}, s16[208,512]{1,0:T(8,128)(2,1)S(1)}, u32[]{:S(2)}, u32[]{:S(2)}) collective-permute-start(s16[208,512]{1,0:T(8,128)(2,1)} %get-tuple-element.40), channel_id=1, source_target_pairs={{0,1},{1,0},{2,3},{3,2},{4,5},{5,4},{6,7},{7,6},{8,9},{9,8},{10,11... | collective-permute-start | bytes 638984 | tf_op jit(solution)/shard_map/ppermute | solution.py:147
  6.1 15.4 %collective-permute-start.1 = (s16[208,512]{1,0:T(8,128)(2,1)}, s16[208,512]{1,0:T(8,128)(2,1)S(1)}, u32[]{:S(2)}, u32[]{:S(2)}) collective-permute-start(s16[208,512]{1,0:T(8,128)(2,1)} %get-tuple-element.41), channel_id=1, source_target_pairs={{0,2},{1,3},{2,0},{3,1},{4,6},{5,7},{6,4},{7,5},{8,10},{9,11},{10,... | collective-permute-start | bytes 638984 | tf_op jit(solution)/shard_map/ppermute | solution.py:147
  8.7 12.9 %collective-permute-start.2 = (s16[208,512]{1,0:T(8,128)(2,1)}, s16[208,512]{1,0:T(8,128)(2,1)S(1)}, u32[]{:S(2)}, u32[]{:S(2)}) collective-permute-start(s16[208,512]{1,0:T(8,128)(2,1)} %get-tuple-element.42), channel_id=1, source_target_pairs={{0,3},{1,2},{2,1},{3,0},{4,7},{5,6},{6,5},{7,4},{8,11},{9,10},{10,... | collective-permute-start | bytes 638984 | tf_op jit(solution)/shard_map/ppermute | solution.py:147
  8.8 12.8 %all-to-all-start = ((f32[16,1,400]{2,1,0:T(1,128)}), f32[16,1,400]{2,1,0:T(1,128)S(1)}, u32[]{:S(2)}, u32[]{:S(2)}) async-start(f32[16,1,400]{2,1,0:T(1,128)} %get-tuple-element.43), calls=%async_computation | async-start | bytes 65536 | tf_op jit(solution)/shard_map/all_to_all | solution.py:794
  24.5 9.8 %collective-permute-start.3 = (s16[336,128]{1,0:T(8,128)(2,1)S(1)}, s16[336,128]{1,0:T(8,128)(2,1)S(1)}, u32[]{:S(2)}, u32[]{:S(2)}) collective-permute-start(s16[336,128]{1,0:T(8,128)(2,1)S(1)} %get-tuple-element.62), channel_id=1, source_target_pairs={{0,4},{4,0},{8,12},{12,8},{1,5},{5,1},{9,13},{13,9},{2,6},{6,2},{1... | collective-permute-start | bytes 258056 | tf_op jit(solution)/shard_map/ppermute | solution.py:147
  24.9 10.6 %collective-permute-start.4 = (s16[336,128]{1,0:T(8,128)(2,1)S(1)}, s16[336,128]{1,0:T(8,128)(2,1)S(1)}, u32[]{:S(2)}, u32[]{:S(2)}) collective-permute-start(s16[336,128]{1,0:T(8,128)(2,1)S(1)} %get-tuple-element.63), channel_id=1, source_target_pairs={{0,8},{4,12},{8,0},{12,4},{1,9},{5,13},{9,1},{13,5},{2,10},{6,14},... | collective-permute-start | bytes 258056 | tf_op jit(solution)/shard_map/ppermute | solution.py:147
  27.1 8.4 %collective-permute-start.5 = (s16[336,128]{1,0:T(8,128)(2,1)S(1)}, s16[336,128]{1,0:T(8,128)(2,1)S(1)}, u32[]{:S(2)}, u32[]{:S(2)}) collective-permute-start(s16[336,128]{1,0:T(8,128)(2,1)S(1)} %get-tuple-element.64), channel_id=1, source_target_pairs={{0,12},{4,8},{8,4},{12,0},{1,13},{5,9},{9,5},{13,1},{2,14},{6,10},... | collective-permute-start | bytes 258056 | tf_op jit(solution)/shard_map/ppermute | solution.py:147
  29.0 5.4 %copy-start = (bf16[4,2,832,208]{3,2,1,0:T(8,128)(2,1)S(1)}, bf16[4,2,832,208]{3,2,1,0:T(8,128)(2,1)}, u32[]{:S(2)}) copy-start(bf16[4,2,832,208]{3,2,1,0:T(8,128)(2,1)} %constant.14.clone.table_ref.rest_0_) | copy-start | bytes 8306692

commit v22 on v21

--- a/solution.py
+++ b/solution.py
@@ -129,21 +129,26 @@
     return codes.astype(jnp.int32).astype(jnp.float32)
 
 
-def partner(axes, sizes, step):
-    count = math.prod(sizes)
-    if count != 4:
-        return step
+def group_index(axes, sizes):
     index = lax.axis_index(axes[0])
     for axis, size in zip(axes[1:], sizes[1:]):
         index = index * size + lax.axis_index(axis)
-    return index ^ step
+    return index
+
+
+def mask(step):
+    return -step % 4
+
+
+def partner(axes, sizes, step):
+    return group_index(axes, sizes) ^ mask(step) if math.prod(sizes) == 4 else step
 
 
 def exchange(blocks, axis):
     count = len(blocks)
     if count != 4:
         return list(lax.all_to_all(jnp.stack(blocks), axis, split_axis=0, concat_axis=0, tiled=True))
-    pairs = [[(i, i ^ step) for i in range(count)] for step in range(count)]
+    pairs = [[(i, i ^ mask(step)) for i in range(count)] for step in range(count)]
     return [blocks[0]] + [lax.ppermute(blocks[step], axis, pairs[step]) for step in range(1, count)]
 
 

time: 43.9 us -> 43.2 us (0.984); the launches traced: 44.4 us -> 43 us
  Pallas kernels: 25.6 us -> 24.2 us
    pallas_call x1, Pallas kernels: 8.86 us -> 8.09 us  [legendre(): pl.pallas_call(functools.partial(legendre_kernel, early), out_shape=jax.S...]
    pallas_call x1, Pallas kernels: 5.34 us -> 4.75 us  [sweep(): pl.pallas_call(sweep_kernel, out_shape=[jax.ShapeDtypeStruct(beta.shape,...]
  transfers between devices with their start and end apart: 7 -> 7, of which waited for: 1 -> 1; matrix products, arithmetic and copies ran while one was open for 0% -> 0% of each run, Pallas kernels for 19% -> 18%
where the time goes in v22:
time: 43.2 us; the launch traced here: 43 us
  Pallas kernels  24.2 us (56%)
  starting transfers between devices  13.8 us (32%)
  waiting for transfers between devices  4.84 us (11%)
    pallas_call x1, Pallas kernels, legendre(): pl.pallas_call(functools.partial(legendre_kernel, early), out_shape=jax.S...  8.09 us
    ppermute x6, starting transfers between devices, exchange(): lax.ppermute(blocks[step], axis, pairs[step])  7.58 us
    all_to_all x1, starting transfers between devices, shards(): lax.all_to_all(edges, ('lat', *axes), split_axis=0, concat_axis=0, tiled=...  6.17 us
    pallas_call x1, Pallas kernels, advect(): pl.pallas_call(functools.partial(advect_kernel, ring, lat_count), out_sha...  5.56 us
    all_to_all x1, waiting for transfers between devices, shards(): lax.all_to_all(edges, ('lat', *axes), split_axis=0, concat_axis=0, tiled=...  4.83 us
    pallas_call x1, Pallas kernels, sweep(): pl.pallas_call(sweep_kernel, out_shape=[jax.ShapeDtypeStruct(beta.shape,...  4.75 us
    pallas_call x1, Pallas kernels, fourier(): pl.pallas_call(functools.partial(fourier_kernel, ring, lat_count, pieces,...  2.88 us
    pallas_call x1, Pallas kernels, prepare_places(): pl.pallas_call(functools.partial(places_kernel, groups), out_shape=[jax.S...  1.78 us
  transfers between devices with their start and end apart: 7, of which 1 were waited for; matrix products, arithmetic and copies ran while one was open for 0% of the time, Pallas kernels for 18%

profile of v22, /device:TPU:0, one launch (start us, length us, event | category | flops | bytes accessed | tf_op | source)
XLA Modules:
  0.0 43.0 jit_solution(10268222503545452940)
XLA Ops:
  0.0 5.6 %shard_map.100 = (s16[208,512]{1,0:T(8,128)(2,1)}, s16[208,512]{1,0:T(8,128)(2,1)}, s16[208,512]{1,0:T(8,128)(2,1)}, s16[208,512]{1,0:T(8,128)(2,1)}, f32[16,1,400]{2,1,0:T(1,128)}) custom-call(s32[1,200]{1,0:T(1,128)} %bitcast.4, bf16[4,200,400]{2,1,0:T(8,128)(2,1)} %tracer_hbm.1, bf16[4,200,400]{2,1,0:T(8,128)(2,1)} %east_hbm.1, bf16[4,200,400]{2,1,0:T(8,128)(2,1)} %north_hbm.1), custom_call_target="tpu_custom_call" | custom-call | flops 5000000000 | bytes 2560000 | tf_op jit(solution)/shard_map/pallas_call | solution.py:237
  5.6 0.0 copy-start.3
  5.6 0.0 copy-start.4
  5.6 0.0 copy-start.5
  5.6 0.0 copy-start.6
  5.6 2.5 %collective-permute-start = (s16[208,512]{1,0:T(8,128)(2,1)}, s16[208,512]{1,0:T(8,128)(2,1)S(1)}, u32[]{:S(2)}, u32[]{:S(2)}) collective-permute-start(s16[208,512]{1,0:T(8,128)(2,1)} %get-tuple-element.40), channel_id=1, source_target_pairs={{0,3},{1,2},{2,1},{3,0},{4,7},{5,6},{6,5},{7,4},{8,11},{9,10},{10,... | collective-permute-start | bytes 638984 | tf_op jit(solution)/shard_map/ppermute | solution.py:152
  8.1 0.6 %collective-permute-start.1 = (s16[208,512]{1,0:T(8,128)(2,1)}, s16[208,512]{1,0:T(8,128)(2,1)S(1)}, u32[]{:S(2)}, u32[]{:S(2)}) collective-permute-start(s16[208,512]{1,0:T(8,128)(2,1)} %get-tuple-element.41), channel_id=1, source_target_pairs={{0,2},{1,3},{2,0},{3,1},{4,6},{5,7},{6,4},{7,5},{8,10},{9,11},{10,... | collective-permute-start | bytes 638984 | tf_op jit(solution)/shard_map/ppermute | solution.py:152
  8.7 0.0 collective-permute-start.2
  8.8 6.2 %all-to-all-start = ((f32[16,1,400]{2,1,0:T(1,128)}), f32[16,1,400]{2,1,0:T(1,128)S(1)}, u32[]{:S(2)}, u32[]{:S(2)}) async-start(f32[16,1,400]{2,1,0:T(1,128)} %get-tuple-element.43), calls=%async_computation | async-start | bytes 65536 | tf_op jit(solution)/shard_map/all_to_all | solution.py:799
  15.0 1.8 %shard_map.101 = (f32[1,512]{1,0:T(1,128)S(1)}, f32[2,128]{1,0:T(2,128)S(1)}, f32[832,128]{1,0:T(8,128)S(1)}, f32[4,104,128]{2,1,0:T(8,128)S(1)}, bf16[128,128]{1,0:T(8,128)(2,1)S(1)}) custom-call(s32[1,400]{1,0:T(1,128)S(1)} %bitcast.3, f32[3,104,128]{2,1,0:T(8,128)S(1)} %copy-done.1), custom_call_target="tpu_custom_call" | custom-call | flops 2000000000 | bytes 1048576 | tf_op jit(solution)/shard_map/pallas_call | solution.py:460
  16.7 4.8 %all-to-all-done.rest_4_ = f32[16,1,400]{2,1,0:T(1,128)S(1)} async-done(((f32[16,1,400]{2,1,0:T(1,128)}), f32[16,1,400]{2,1,0:T(1,128)S(1)}, u32[]{:S(2)}, u32[]{:S(2)}) %all-to-all-start) | async-done | bytes 25632 | tf_op jit(solution)/shard_map/all_to_all | solution.py:799
  21.6 0.0 collective-permute-done.rest_1_
  21.6 0.0 collective-permute-done.1.rest_2_
  21.6 0.0 collective-permute-done.2.rest_3_
  21.6 2.9 %shard_map.102 = (s16[336,128]{1,0:T(8,128)(2,1)S(1)}, s16[336,128]{1,0:T(8,128)(2,1)S(1)}, s16[336,128]{1,0:T(8,128)(2,1)S(1)}, s16[336,128]{1,0:T(8,128)(2,1)S(1)}) custom-call(s16[208,512]{1,0:T(8,128)(2,1)S(1)} %copy-done.6, s16[208,512]{1,0:T(8,128)(2,1)S(1)} %collective-permute-done.rest_1_, s16[208,512]{1,0:T(8,128)(2,1)S(1)} %collective-permute-done.1.rest_2_, ...), custom_call_target="tpu_custom_call" | custom-call | flops 4000000000 | bytes 6291456 | tf_op jit(solution)/shard_map/pallas_call | solution.py:405
  24.5 1.9 %collective-permute-start.3 = (s16[336,128]{1,0:T(8,128)(2,1)S(1)}, s16[336,128]{1,0:T(8,128)(2,1)S(1)}, u32[]{:S(2)}, u32[]{:S(2)}) collective-permute-start(s16[336,128]{1,0:T(8,128)(2,1)S(1)} %get-tuple-element.62), channel_id=1, source_target_pairs={{0,12},{4,8},{8,4},{12,0},{1,13},{5,9},{9,5},{13,1},{2,14},{6,10},... | collective-permute-start | bytes 258056 | tf_op jit(solution)/shard_map/ppermute | solution.py:152
  26.4 0.0 collective-permute-start.4
  26.4 2.6 %collective-permute-start.5 = (s16[336,128]{1,0:T(8,128)(2,1)S(1)}, s16[336,128]{1,0:T(8,128)(2,1)S(1)}, u32[]{:S(2)}, u32[]{:S(2)}) collective-permute-start(s16[336,128]{1,0:T(8,128)(2,1)S(1)} %get-tuple-element.64), channel_id=1, source_target_pairs={{0,4},{4,0},{8,12},{12,8},{1,5},{5,1},{9,13},{13,9},{2,6},{6,2},{1... | collective-permute-start | bytes 258056 | tf_op jit(solution)/shard_map/ppermute | solution.py:152
  29.0 4.7 %shard_map.103 = (f32[832,128]{1,0:T(8,128)S(1)}, f32[26,128]{1,0:T(8,128)S(1)}, f32[3,104,128]{2,1,0:T(8,128)S(1)}, f32[13,32,104,128]{3,2,1,0:T(8,128)S(1)}, f32[3,32,104,128]{3,2,1,0:T(8,128)S(1)}) custom-call(f32[2,128]{1,0:T(2,128)S(1)} %get-tuple-element.53.mine_ref.rest_11_, f32[3,104,128]{2,1,0:T(8,128)S(1)} %copy-done.1, ...), custom_call_target="tpu_custom_call" | custom-call | flops 5000000000 | bytes 26214400 | tf_op jit(solution)/shard_map/pallas_call | solution.py:595
  33.7 0.0 collective-permute-done.3.rest_1_
  33.7 1.2 %shard_map.104.rest_10_ = f32[832,256]{1,0:T(8,128)S(1)} custom-call(bf16[4,2,832,208]{3,2,1,0:T(8,128)(2,1)S(1)} %copy-done, s16[336,128]{1,0:T(8,128)(2,1)S(1)} %get-tuple-element.61.rest_0_, s16[336,128]{1,0:T(8,128)(2,1)S(1)} %collective-permute-done.3.rest_1_), custom_call_target="tpu_custom_call" | custom-call | flops 1000000000 | bytes 4194304 | tf_op jit(solution)/shard_map/pallas_call | solution.py:644
  34.9 0.0 collective-permute-done.4.rest_12_
  34.9 0.0 collective-permute-done.5.rest_13_
  34.9 8.1 %shard_map.105 = f32[100,2,400]{2,1,0:T(2,128)} custom-call(bf16[4,2,832,208]{3,2,1,0:T(8,128)(2,1)S(1)} %copy-done, f32[3,104,128]{2,1,0:T(8,128)S(1)} %copy-done.1, f32[832,128]{1,0:T(8,128)S(1)} %get-tuple-element.52.beta_ref.rest_2_, f32[832,128]{1,0:T(8,128)S(1)} %get-tuple-element.55.rest_3_, f32[26,128]{1,0:T(8,128)S(1)} %get-tuple-element.56.rest_4_, ...), custom_call_target="tpu_custom_call" | custom-call | flops 8000000000 | bytes 6291456 | tf_op jit(solution)/shard_map/pallas_call | solution.py:770
  (10 shorter events, 0.0 us)
Async XLA Ops:
  0.0 14.9 %copy-start.1 = (f32[3,104,128]{2,1,0:T(8,128)S(1)}, f32[3,104,128]{2,1,0:T(8,128)}, u32[]{:S(2)}) copy-start(f32[3,104,128]{2,1,0:T(8,128)} %constant.10.clone.lat_ref.rest_1_) | copy-start | bytes 479236
  0.0 14.9 %copy-start.2 = (s32[400]{0:T(512)S(1)}, s32[400]{0:T(512)}, u32[]{:S(2)}) copy-start(s32[400]{0:T(512)} %param.14) | copy-start | bytes 4804
  5.6 16.0 %copy-start.3 = (bf16[1,400,1024]{2,1,0:T(8,128)(2,1)S(1)}, bf16[1,400,1024]{2,1,0:T(8,128)(2,1)}, u32[]{:S(2)}) copy-start(bf16[1,400,1024]{2,1,0:T(8,128)(2,1)} %constant.13.clone.rest_7_) | copy-start | bytes 2457604
  5.6 16.0 %copy-start.4 = (bf16[1,400,512]{2,1,0:T(8,128)(2,1)S(1)}, bf16[1,400,512]{2,1,0:T(8,128)(2,1)}, u32[]{:S(2)}) copy-start(bf16[1,400,512]{2,1,0:T(8,128)(2,1)} %constant.12.clone.rest_6_) | copy-start | bytes 1228804
  5.6 16.0 %copy-start.5 = (bf16[1,400,512]{2,1,0:T(8,128)(2,1)S(1)}, bf16[1,400,512]{2,1,0:T(8,128)(2,1)}, u32[]{:S(2)}) copy-start(bf16[1,400,512]{2,1,0:T(8,128)(2,1)} %constant.11.clone.rest_5_) | copy-start | bytes 1228804
  5.6 16.0 %copy-start.6 = (s16[208,512]{1,0:T(8,128)(2,1)S(1)}, s16[208,512]{1,0:T(8,128)(2,1)}, u32[]{:S(2)}) copy-start(s16[208,512]{1,0:T(8,128)(2,1)} %get-tuple-element.39.rest_0_) | copy-start | bytes 638980
  5.6 15.9 %collective-permute-start = (s16[208,512]{1,0:T(8,128)(2,1)}, s16[208,512]{1,0:T(8,128)(2,1)S(1)}, u32[]{:S(2)}, u32[]{:S(2)}) collective-permute-start(s16[208,512]{1,0:T(8,128)(2,1)} %get-tuple-element.40), channel_id=1, source_target_pairs={{0,3},{1,2},{2,1},{3,0},{4,7},{5,6},{6,5},{7,4},{8,11},{9,10},{10,... | collective-permute-start | bytes 638984 | tf_op jit(solution)/shard_map/ppermute | solution.py:152
  8.1 13.5 %collective-permute-start.1 = (s16[208,512]{1,0:T(8,128)(2,1)}, s16[208,512]{1,0:T(8,128)(2,1)S(1)}, u32[]{:S(2)}, u32[]{:S(2)}) collective-permute-start(s16[208,512]{1,0:T(8,128)(2,1)} %get-tuple-element.41), channel_id=1, source_target_pairs={{0,2},{1,3},{2,0},{3,1},{4,6},{5,7},{6,4},{7,5},{8,10},{9,11},{10,... | collective-permute-start | bytes 638984 | tf_op jit(solution)/shard_map/ppermute | solution.py:152
  8.7 12.9 %collective-permute-start.2 = (s16[208,512]{1,0:T(8,128)(2,1)}, s16[208,512]{1,0:T(8,128)(2,1)S(1)}, u32[]{:S(2)}, u32[]{:S(2)}) collective-permute-start(s16[208,512]{1,0:T(8,128)(2,1)} %get-tuple-element.42), channel_id=1, source_target_pairs={{0,1},{1,0},{2,3},{3,2},{4,5},{5,4},{6,7},{7,6},{8,9},{9,8},{10,11... | collective-permute-start | bytes 638984 | tf_op jit(solution)/shard_map/ppermute | solution.py:152
  8.8 12.8 %all-to-all-start = ((f32[16,1,400]{2,1,0:T(1,128)}), f32[16,1,400]{2,1,0:T(1,128)S(1)}, u32[]{:S(2)}, u32[]{:S(2)}) async-start(f32[16,1,400]{2,1,0:T(1,128)} %get-tuple-element.43), calls=%async_computation | async-start | bytes 65536 | tf_op jit(solution)/shard_map/all_to_all | solution.py:799
  24.5 9.2 %collective-permute-start.3 = (s16[336,128]{1,0:T(8,128)(2,1)S(1)}, s16[336,128]{1,0:T(8,128)(2,1)S(1)}, u32[]{:S(2)}, u32[]{:S(2)}) collective-permute-start(s16[336,128]{1,0:T(8,128)(2,1)S(1)} %get-tuple-element.62), channel_id=1, source_target_pairs={{0,12},{4,8},{8,4},{12,0},{1,13},{5,9},{9,5},{13,1},{2,14},{6,10},... | collective-permute-start | bytes 258056 | tf_op jit(solution)/shard_map/ppermute | solution.py:152
  26.4 8.5 %collective-permute-start.4 = (s16[336,128]{1,0:T(8,128)(2,1)S(1)}, s16[336,128]{1,0:T(8,128)(2,1)S(1)}, u32[]{:S(2)}, u32[]{:S(2)}) collective-permute-start(s16[336,128]{1,0:T(8,128)(2,1)S(1)} %get-tuple-element.63), channel_id=1, source_target_pairs={{0,8},{4,12},{8,0},{12,4},{1,9},{5,13},{9,1},{13,5},{2,10},{6,14},... | collective-permute-start | bytes 258056 | tf_op jit(solution)/shard_map/ppermute | solution.py:152
  26.4 8.5 %collective-permute-start.5 = (s16[336,128]{1,0:T(8,128)(2,1)S(1)}, s16[336,128]{1,0:T(8,128)(2,1)S(1)}, u32[]{:S(2)}, u32[]{:S(2)}) collective-permute-start(s16[336,128]{1,0:T(8,128)(2,1)S(1)} %get-tuple-element.64), channel_id=1, source_target_pairs={{0,4},{4,0},{8,12},{12,8},{1,5},{5,1},{9,13},{13,9},{2,6},{6,2},{1... | collective-permute-start | bytes 258056 | tf_op jit(solution)/shard_map/ppermute | solution.py:152
  29.0 4.8 %copy-start = (bf16[4,2,832,208]{3,2,1,0:T(8,128)(2,1)S(1)}, bf16[4,2,832,208]{3,2,1,0:T(8,128)(2,1)}, u32[]{:S(2)}) copy-start(bf16[4,2,832,208]{3,2,1,0:T(8,128)(2,1)} %constant.14.clone.table_ref.rest_0_) | copy-start | bytes 8306692

commit v23 on v22

--- a/solution.py
+++ b/solution.py
@@ -260,53 +260,7 @@
     return -(-(rows + 1) // 16) * 16
 
 
-def folded_rows(rows, slots):
-    if 2 * slots <= LANES:
-        return rows
-    fits = 2 * slots <= LANES + SIDE + 8 and rows % 16 == 0 and rows <= 16 * 16
-    return -(-(rows + rows // 2 + 16) // 16) * 16 if fits else 0
-
-
-def fold(one, two, slots):
-    rows = one.shape[0]
-    total = folded_rows(rows, slots)
-    if not total:
-        return jnp.concatenate([one, two], axis=1)
-    lane = lax.broadcasted_iota(jnp.int32, one.shape, 1)
-    turned = pltpu.roll(two, slots, 1)
-    whole = jnp.where(lane < slots, one, turned)
-    if total == rows:
-        return whole
-    half = rows // 2
-    halves = jnp.where(lane[:half] < SIDE, turned[:half], pltpu.roll(turned[half:], SIDE, 1))
-    last = jnp.zeros((16, LANES), jnp.float32)
-    for group in range(rows // 16):
-        part = pltpu.roll(turned[16 * group : 16 * group + 16], (8 * group - SIDE) % LANES, 1)
-        last = jnp.where(lane[:16] // 8 == group, part, last)
-    filler = jnp.zeros((total - rows - half - 16, LANES), jnp.float32)
-    return jnp.concatenate([whole, halves, last, filler], axis=0)
-
-
-def unfold(block, rows, slots):
-    total = folded_rows(rows, slots)
-    if not total:
-        return block[:, :LANES], block[:, LANES:]
-    whole = block[:rows]
-    lane = lax.broadcasted_iota(jnp.int32, whole.shape, 1)
-    two = pltpu.roll(whole, (LANES - slots) % LANES, 1)
-    if total != rows:
-        half = rows // 2
-        halves = block[rows : rows + half]
-        last = block[rows + half : rows + half + 16]
-        last = [pltpu.roll(last, (SIDE - 8 * group) % LANES, 1) for group in range(rows // 16)]
-        halves = jnp.concatenate([halves, pltpu.roll(halves, SIDE, 1)], axis=0)
-        rest = jnp.where(lane < SIDE, halves, jnp.concatenate(last, axis=0))
-        two = jnp.where(lane < LANES - slots, two, pltpu.roll(rest, LANES - slots, 1))
-    inside = lane < slots
-    return jnp.where(inside, whole, 0.0), jnp.where(inside, two, 0.0)
-
-
-def fourier_kernel(ring, lat_count, pieces, slots, *rest):
+def fourier_kernel(ring, lat_count, pieces, *rest):
     grids, (edge_ref, *tables, wave_ref) = rest[:pieces], rest[pieces : pieces + 5]
     outs, field = rest[pieces + 5 : -1], rest[-1]
     _, rows, width = field.shape
@@ -392,18 +346,17 @@
         placed.append(jnp.concatenate([steps, codes], axis=0))
     for target in range(lat_count):
         cols = slice(target * LANES, (target + 1) * LANES)
-        outs[target][...] = as_int16(fold(placed[0][:, cols], placed[1][:, cols], slots))
-
-
-def fourier(grids, edges, ring, wave_row, rows, slots, lat_count):
+        for part in range(2):
+            outs[target][:, part * LANES : (part + 1) * LANES] = as_int16(placed[part][:, cols])
+
+
+def fourier(grids, edges, ring, wave_row, rows, lat_count):
     pieces = len(grids)
     width = grids[0].shape[1]
-    full = exchanged_rows(rows)
-    folded = folded_rows(full, slots)
-    shape = (folded, LANES) if folded else (full, 2 * LANES)
+    shape = (exchanged_rows(rows), 2 * LANES)
     tables = [table_bf16(table) for table in fourier_tables(pieces)]
     return pl.pallas_call(
-        functools.partial(fourier_kernel, ring, lat_count, pieces, slots),
+        functools.partial(fourier_kernel, ring, lat_count, pieces),
         out_shape=[jax.ShapeDtypeStruct(shape, jnp.int16)] * lat_count,
         in_specs=[VMEM_SPEC] * (pieces + 5),
         out_specs=[VMEM_SPEC] * lat_count,
@@ -432,19 +385,17 @@
         column = jnp.sum(jnp.where(down == across, row, 0.0), axis=1, keepdims=True)
         ahead = (row < column) | ((row == column) & (across < down))
         rank = jnp.sum(jnp.where(ahead, 1.0, 0.0), axis=1, keepdims=True)
-        def ordered(side):
-            place = jnp.where(rank < paired, rank, side + slots - 1.0 - rank)
-            place = jnp.where(rank < slots, place, -1.0)
-            hot = jnp.where(place == across.astype(jnp.float32), 1.0, 0.0)
-            filled = jnp.sum(hot, axis=0, keepdims=True)
-            values = jnp.sum(hot * column, axis=0, keepdims=True)
-            return jnp.where(filled > 0.5, values, 2.0 * M)
-
-        sorted_rows[group] = jnp.broadcast_to(ordered(paired), sorted_rows.shape[1:])
+        place = jnp.where(rank < paired, rank, SIDE + slots - 1.0 - rank)
+        place = jnp.where(rank < slots, place, -1.0)
+        hot = jnp.where(place == across.astype(jnp.float32), 1.0, 0.0)
+        filled = jnp.sum(hot, axis=0, keepdims=True)
+        values = jnp.sum(hot * column, axis=0, keepdims=True)
+        values = jnp.where(filled > 0.5, values, 2.0 * M)
+        sorted_rows[group] = jnp.broadcast_to(values, sorted_rows.shape[1:])
 
         @pl.when(group == lat_index)
         def _():
-            mine_ref[:1] = ordered(SIDE)
+            mine_ref[:1] = values
             mine_ref[1:] = plain
 
     for step in range(groups):
@@ -610,16 +561,10 @@
     )(mine, latitudes, beta, start)
 
 
-def resampled(first, fields, table, slots, total):
+def resampled(first, fields, table, total):
     for piece, field in enumerate(fields):
-        rows = table.shape[3]
-        parts = []
-        for part in unfold(from_int16(field[...]), rows, slots):
-            part = part * scale_of(part[rows - 1 :])
-            lane = lax.broadcasted_iota(jnp.int32, part.shape, 1)
-            shift = SIDE - (slots + 1) // 2
-            parts.append(jnp.where(lane < SIDE, part, pltpu.roll(part, shift, 1)))
-        values = jnp.concatenate(parts, axis=1)
+        values = from_int16(field[...])
+        values = values * scale_of(values[field.shape[0] - 1 :])
         high, low = split_bf16(values)
         spot = partner(("lat",), table.shape[:1], first + piece)
         both = jnp.concatenate([high, low], axis=1)
@@ -630,19 +575,19 @@
     return total
 
 
-def resample_kernel(slots, table_ref, *rest):
-    rest[-1][...] = resampled(0, rest[:-1], table_ref, slots, None)
+def resample_kernel(table_ref, *rest):
+    rest[-1][...] = resampled(0, rest[:-1], table_ref, None)
 
 
 def late_bytes(pieces):
     return LATE_BYTES if pieces <= 4 else VMEM_BYTES
 
 
-def resample(fields, table, slots):
+def resample(fields, table):
     count, _, height, _ = table.shape
     span = 2 * LANES
     return pl.pallas_call(
-        functools.partial(resample_kernel, slots),
+        resample_kernel,
         out_shape=jax.ShapeDtypeStruct((height, span), jnp.float32),
         in_specs=[VMEM_SPEC] * (1 + len(fields)),
         out_specs=VMEM_SPEC,
@@ -665,7 +610,7 @@
     turn = block_count(pair[0][:1])
     block_total = jnp.max(turn + block_count(pair[1][:1])).astype(jnp.int32)
 
-    total = resampled(early, fields, table, slots, total_ref[...])
+    total = resampled(early, fields, table, total_ref[...])
     totals = [total[2 * points * kind : 2 * points * (kind + 1)] for kind in range(4)]
     left = lax.broadcasted_iota(jnp.int32, (points, LANES), 1) < SIDE
     for parity in range(2):
@@ -765,7 +710,7 @@
     pieces = len(fields)
     early = pieces // 2
     points = latitudes.shape[1]
-    total = resample(fields[:early], table, slots)
+    total = resample(fields[:early], table)
     block_rows = SPAN * BLOCK
     return pl.pallas_call(
         functools.partial(legendre_kernel, early),
@@ -799,7 +744,7 @@
     edges = lax.all_to_all(edges, ("lat", *axes), split_axis=0, concat_axis=0, tiled=True)
     latitudes = jnp.asarray(latitude_table())
     wave_row, mine, beta, start, back = prepare_places(slot_wave, lat_count, latitudes)
-    waved = fourier(grids, edges, ring, wave_row, rows, slots, lat_count)
+    waved = fourier(grids, edges, ring, wave_row, rows, lat_count)
     table = jnp.asarray(resample_pieces(lat_count, rows, exchanged_rows(rows)))
     waved, mine, table = lax.optimization_barrier((list(waved), mine, table))
     fields = exchange(waved, "lat")

time: 43.2 us -> 44.2 us (1.023)
  waiting for transfers between devices: 4.84 us -> 6.51 us
  Pallas kernels: 24.2 us -> 23.3 us
    ppermute x6, waiting for transfers between devices: 0.02 us -> 1.66 us  [exchange(): lax.ppermute(blocks[step], axis, pairs[step])]
    pallas_call x2, Pallas kernels: 4.03 us -> 3.48 us  [the longest x1 2.62 us: fourier(): pl.pallas_call(functools.partial(fourier_kernel, ring, lat_count, pieces)...]
  transfers between devices with their start and end apart: 7 -> 7, of which waited for: 1 -> 2; matrix products, arithmetic and copies ran while one was open for 0% -> 0% of each run, Pallas kernels for 18% -> 17%
where the time goes in v23:
time: 44.2 us; the launch traced here: 43.7 us
  Pallas kernels  23.3 us (53%)
  starting transfers between devices  13.8 us (31%)
  waiting for transfers between devices  6.51 us (15%)
    pallas_call x1, Pallas kernels, legendre(): pl.pallas_call(functools.partial(legendre_kernel, early), out_shape=jax.S...  7.79 us
    ppermute x6, starting transfers between devices, exchange(): lax.ppermute(blocks[step], axis, pairs[step])  7.58 us
    all_to_all x1, starting transfers between devices, shards(): lax.all_to_all(edges, ('lat', *axes), split_axis=0, concat_axis=0, tiled=...  6.17 us
    pallas_call x1, Pallas kernels, advect(): pl.pallas_call(functools.partial(advect_kernel, ring, lat_count), out_sha...  5.56 us
    all_to_all x1, waiting for transfers between devices, shards(): lax.all_to_all(edges, ('lat', *axes), split_axis=0, concat_axis=0, tiled=...  4.86 us
    pallas_call x1, Pallas kernels, sweep(): pl.pallas_call(sweep_kernel, out_shape=[jax.ShapeDtypeStruct(beta.shape,...  4.71 us
    pallas_call x1, Pallas kernels, fourier(): pl.pallas_call(functools.partial(fourier_kernel, ring, lat_count, pieces)...  2.62 us
    pallas_call x1, Pallas kernels, prepare_places(): pl.pallas_call(functools.partial(places_kernel, groups), out_shape=[jax.S...  1.75 us
  transfers between devices with their start and end apart: 7, of which 2 were waited for; matrix products, arithmetic and copies ran while one was open for 0% of the time, Pallas kernels for 17%

profile of v23, /device:TPU:0, one launch (start us, length us, event | category | flops | bytes accessed | tf_op | source)
XLA Modules:
  0.0 43.7 jit_solution(17925036181958683551)
XLA Ops:
  0.0 5.6 %shard_map.100 = (s16[208,512]{1,0:T(8,128)(2,1)}, s16[208,512]{1,0:T(8,128)(2,1)}, s16[208,512]{1,0:T(8,128)(2,1)}, s16[208,512]{1,0:T(8,128)(2,1)}, f32[16,1,400]{2,1,0:T(1,128)}) custom-call(s32[1,200]{1,0:T(1,128)} %bitcast.4, bf16[4,200,400]{2,1,0:T(8,128)(2,1)} %tracer_hbm.1, bf16[4,200,400]{2,1,0:T(8,128)(2,1)} %east_hbm.1, bf16[4,200,400]{2,1,0:T(8,128)(2,1)} %north_hbm.1), custom_call_target="tpu_custom_call" | custom-call | flops 5000000000 | bytes 2560000 | tf_op jit(solution)/shard_map/pallas_call | solution.py:237
  5.6 0.0 copy-start.3
  5.6 0.0 copy-start.4
  5.6 0.0 copy-start.5
  5.6 0.0 copy-start.6
  5.6 2.5 %collective-permute-start = (s16[208,512]{1,0:T(8,128)(2,1)}, s16[208,512]{1,0:T(8,128)(2,1)S(1)}, u32[]{:S(2)}, u32[]{:S(2)}) collective-permute-start(s16[208,512]{1,0:T(8,128)(2,1)} %get-tuple-element.40), channel_id=1, source_target_pairs={{0,3},{1,2},{2,1},{3,0},{4,7},{5,6},{6,5},{7,4},{8,11},{9,10},{10,... | collective-permute-start | bytes 638984 | tf_op jit(solution)/shard_map/ppermute | solution.py:152
  8.1 0.6 %collective-permute-start.1 = (s16[208,512]{1,0:T(8,128)(2,1)}, s16[208,512]{1,0:T(8,128)(2,1)S(1)}, u32[]{:S(2)}, u32[]{:S(2)}) collective-permute-start(s16[208,512]{1,0:T(8,128)(2,1)} %get-tuple-element.41), channel_id=1, source_target_pairs={{0,2},{1,3},{2,0},{3,1},{4,6},{5,7},{6,4},{7,5},{8,10},{9,11},{10,... | collective-permute-start | bytes 638984 | tf_op jit(solution)/shard_map/ppermute | solution.py:152
  8.7 0.0 collective-permute-start.2
  8.8 6.2 %all-to-all-start = ((f32[16,1,400]{2,1,0:T(1,128)}), f32[16,1,400]{2,1,0:T(1,128)S(1)}, u32[]{:S(2)}, u32[]{:S(2)}) async-start(f32[16,1,400]{2,1,0:T(1,128)} %get-tuple-element.43), calls=%async_computation | async-start | bytes 65536 | tf_op jit(solution)/shard_map/all_to_all | solution.py:744
  15.0 1.8 %shard_map.101 = (f32[1,512]{1,0:T(1,128)S(1)}, f32[2,128]{1,0:T(2,128)S(1)}, f32[832,128]{1,0:T(8,128)S(1)}, f32[4,104,128]{2,1,0:T(8,128)S(1)}, bf16[128,128]{1,0:T(8,128)(2,1)S(1)}) custom-call(s32[1,400]{1,0:T(1,128)S(1)} %bitcast.3, f32[3,104,128]{2,1,0:T(8,128)S(1)} %copy-done.1), custom_call_target="tpu_custom_call" | custom-call | flops 2000000000 | bytes 1048576 | tf_op jit(solution)/shard_map/pallas_call | solution.py:411
  16.7 4.9 %all-to-all-done.rest_4_ = f32[16,1,400]{2,1,0:T(1,128)S(1)} async-done(((f32[16,1,400]{2,1,0:T(1,128)}), f32[16,1,400]{2,1,0:T(1,128)S(1)}, u32[]{:S(2)}, u32[]{:S(2)}) %all-to-all-start) | async-done | bytes 25632 | tf_op jit(solution)/shard_map/all_to_all | solution.py:744
  21.6 0.0 collective-permute-done.rest_1_
  21.6 0.0 collective-permute-done.1.rest_2_
  21.6 0.0 collective-permute-done.2.rest_3_
  21.6 2.6 %shard_map.102 = (s16[208,256]{1,0:T(8,128)(2,1)S(1)}, s16[208,256]{1,0:T(8,128)(2,1)S(1)}, s16[208,256]{1,0:T(8,128)(2,1)S(1)}, s16[208,256]{1,0:T(8,128)(2,1)S(1)}) custom-call(s16[208,512]{1,0:T(8,128)(2,1)S(1)} %copy-done.6, s16[208,512]{1,0:T(8,128)(2,1)S(1)} %collective-permute-done.rest_1_, s16[208,512]{1,0:T(8,128)(2,1)S(1)} %collective-permute-done.1.rest_2_, ...), custom_call_target="tpu_custom_call" | custom-call | flops 4000000000 | bytes 6291456 | tf_op jit(solution)/shard_map/pallas_call | solution.py:358
  24.3 1.9 %collective-permute-start.3 = (s16[208,256]{1,0:T(8,128)(2,1)S(1)}, s16[208,256]{1,0:T(8,128)(2,1)S(1)}, u32[]{:S(2)}, u32[]{:S(2)}) collective-permute-start(s16[208,256]{1,0:T(8,128)(2,1)S(1)} %get-tuple-element.62), channel_id=1, source_target_pairs={{0,12},{4,8},{8,4},{12,0},{1,13},{5,9},{9,5},{13,1},{2,14},{6,10},... | collective-permute-start | bytes 319496 | tf_op jit(solution)/shard_map/ppermute | solution.py:152
  26.1 0.0 collective-permute-start.4
  26.1 2.6 %collective-permute-start.5 = (s16[208,256]{1,0:T(8,128)(2,1)S(1)}, s16[208,256]{1,0:T(8,128)(2,1)S(1)}, u32[]{:S(2)}, u32[]{:S(2)}) collective-permute-start(s16[208,256]{1,0:T(8,128)(2,1)S(1)} %get-tuple-element.64), channel_id=1, source_target_pairs={{0,4},{4,0},{8,12},{12,8},{1,5},{5,1},{9,13},{13,9},{2,6},{6,2},{1... | collective-permute-start | bytes 319496 | tf_op jit(solution)/shard_map/ppermute | solution.py:152
  28.7 4.7 %shard_map.103 = (f32[832,128]{1,0:T(8,128)S(1)}, f32[26,128]{1,0:T(8,128)S(1)}, f32[3,104,128]{2,1,0:T(8,128)S(1)}, f32[13,32,104,128]{3,2,1,0:T(8,128)S(1)}, f32[3,32,104,128]{3,2,1,0:T(8,128)S(1)}) custom-call(f32[2,128]{1,0:T(2,128)S(1)} %get-tuple-element.53.mine_ref.rest_11_, f32[3,104,128]{2,1,0:T(8,128)S(1)} %copy-done.1, ...), custom_call_target="tpu_custom_call" | custom-call | flops 5000000000 | bytes 26214400 | tf_op jit(solution)/shard_map/pallas_call | solution.py:546
  33.4 0.0 collective-permute-done.3.rest_1_
  33.4 0.9 %shard_map.104.rest_10_ = f32[832,256]{1,0:T(8,128)S(1)} custom-call(bf16[4,2,832,208]{3,2,1,0:T(8,128)(2,1)S(1)} %copy-done, s16[208,256]{1,0:T(8,128)(2,1)S(1)} %get-tuple-element.61.rest_0_, s16[208,256]{1,0:T(8,128)(2,1)S(1)} %collective-permute-done.3.rest_1_), custom_call_target="tpu_custom_call" | custom-call | flops 1000000000 | bytes 4194304 | tf_op jit(solution)/shard_map/pallas_call | solution.py:589
  34.3 1.6 %collective-permute-done.4.rest_12_ = s16[208,256]{1,0:T(8,128)(2,1)S(1)} collective-permute-done((s16[208,256]{1,0:T(8,128)(2,1)S(1)}, s16[208,256]{1,0:T(8,128)(2,1)S(1)}, u32[]{:S(2)}, u32[]{:S(2)}) %collective-permute-start.4) | collective-permute-done | bytes 106528 | tf_op jit(solution)/shard_map/ppermute | solution.py:152
  36.0 0.0 collective-permute-done.5.rest_13_
  36.0 7.8 %shard_map.105 = f32[100,2,400]{2,1,0:T(2,128)} custom-call(bf16[4,2,832,208]{3,2,1,0:T(8,128)(2,1)S(1)} %copy-done, f32[3,104,128]{2,1,0:T(8,128)S(1)} %copy-done.1, f32[832,128]{1,0:T(8,128)S(1)} %get-tuple-element.52.beta_ref.rest_2_, f32[832,128]{1,0:T(8,128)S(1)} %get-tuple-element.55.rest_3_, f32[26,128]{1,0:T(8,128)S(1)} %get-tuple-element.56.rest_4_, ...), custom_call_target="tpu_custom_call" | custom-call | flops 8000000000 | bytes 6291456 | tf_op jit(solution)/shard_map/pallas_call | solution.py:715
  (10 shorter events, 0.0 us)
Async XLA Ops:
  0.0 14.9 %copy-start.1 = (f32[3,104,128]{2,1,0:T(8,128)S(1)}, f32[3,104,128]{2,1,0:T(8,128)}, u32[]{:S(2)}) copy-start(f32[3,104,128]{2,1,0:T(8,128)} %constant.10.clone.lat_ref.rest_1_) | copy-start | bytes 479236
  0.0 14.9 %copy-start.2 = (s32[400]{0:T(512)S(1)}, s32[400]{0:T(512)}, u32[]{:S(2)}) copy-start(s32[400]{0:T(512)} %param.14) | copy-start | bytes 4804
  5.6 16.0 %copy-start.3 = (bf16[1,400,1024]{2,1,0:T(8,128)(2,1)S(1)}, bf16[1,400,1024]{2,1,0:T(8,128)(2,1)}, u32[]{:S(2)}) copy-start(bf16[1,400,1024]{2,1,0:T(8,128)(2,1)} %constant.13.clone.rest_7_) | copy-start | bytes 2457604
  5.6 16.0 %copy-start.4 = (bf16[1,400,512]{2,1,0:T(8,128)(2,1)S(1)}, bf16[1,400,512]{2,1,0:T(8,128)(2,1)}, u32[]{:S(2)}) copy-start(bf16[1,400,512]{2,1,0:T(8,128)(2,1)} %constant.12.clone.rest_6_) | copy-start | bytes 1228804
  5.6 16.0 %copy-start.5 = (bf16[1,400,512]{2,1,0:T(8,128)(2,1)S(1)}, bf16[1,400,512]{2,1,0:T(8,128)(2,1)}, u32[]{:S(2)}) copy-start(bf16[1,400,512]{2,1,0:T(8,128)(2,1)} %constant.11.clone.rest_5_) | copy-start | bytes 1228804
  5.6 16.0 %copy-start.6 = (s16[208,512]{1,0:T(8,128)(2,1)S(1)}, s16[208,512]{1,0:T(8,128)(2,1)}, u32[]{:S(2)}) copy-start(s16[208,512]{1,0:T(8,128)(2,1)} %get-tuple-element.39.rest_0_) | copy-start | bytes 638980
  5.6 15.9 %collective-permute-start = (s16[208,512]{1,0:T(8,128)(2,1)}, s16[208,512]{1,0:T(8,128)(2,1)S(1)}, u32[]{:S(2)}, u32[]{:S(2)}) collective-permute-start(s16[208,512]{1,0:T(8,128)(2,1)} %get-tuple-element.40), channel_id=1, source_target_pairs={{0,3},{1,2},{2,1},{3,0},{4,7},{5,6},{6,5},{7,4},{8,11},{9,10},{10,... | collective-permute-start | bytes 638984 | tf_op jit(solution)/shard_map/ppermute | solution.py:152
  8.1 13.5 %collective-permute-start.1 = (s16[208,512]{1,0:T(8,128)(2,1)}, s16[208,512]{1,0:T(8,128)(2,1)S(1)}, u32[]{:S(2)}, u32[]{:S(2)}) collective-permute-start(s16[208,512]{1,0:T(8,128)(2,1)} %get-tuple-element.41), channel_id=1, source_target_pairs={{0,2},{1,3},{2,0},{3,1},{4,6},{5,7},{6,4},{7,5},{8,10},{9,11},{10,... | collective-permute-start | bytes 638984 | tf_op jit(solution)/shard_map/ppermute | solution.py:152
  8.7 12.9 %collective-permute-start.2 = (s16[208,512]{1,0:T(8,128)(2,1)}, s16[208,512]{1,0:T(8,128)(2,1)S(1)}, u32[]{:S(2)}, u32[]{:S(2)}) collective-permute-start(s16[208,512]{1,0:T(8,128)(2,1)} %get-tuple-element.42), channel_id=1, source_target_pairs={{0,1},{1,0},{2,3},{3,2},{4,5},{5,4},{6,7},{7,6},{8,9},{9,8},{10,11... | collective-permute-start | bytes 638984 | tf_op jit(solution)/shard_map/ppermute | solution.py:152
  8.8 12.8 %all-to-all-start = ((f32[16,1,400]{2,1,0:T(1,128)}), f32[16,1,400]{2,1,0:T(1,128)S(1)}, u32[]{:S(2)}, u32[]{:S(2)}) async-start(f32[16,1,400]{2,1,0:T(1,128)} %get-tuple-element.43), calls=%async_computation | async-start | bytes 65536 | tf_op jit(solution)/shard_map/all_to_all | solution.py:744
  24.3 9.2 %collective-permute-start.3 = (s16[208,256]{1,0:T(8,128)(2,1)S(1)}, s16[208,256]{1,0:T(8,128)(2,1)S(1)}, u32[]{:S(2)}, u32[]{:S(2)}) collective-permute-start(s16[208,256]{1,0:T(8,128)(2,1)S(1)} %get-tuple-element.62), channel_id=1, source_target_pairs={{0,12},{4,8},{8,4},{12,0},{1,13},{5,9},{9,5},{13,1},{2,14},{6,10},... | collective-permute-start | bytes 319496 | tf_op jit(solution)/shard_map/ppermute | solution.py:152
  26.1 9.8 %collective-permute-start.4 = (s16[208,256]{1,0:T(8,128)(2,1)S(1)}, s16[208,256]{1,0:T(8,128)(2,1)S(1)}, u32[]{:S(2)}, u32[]{:S(2)}) collective-permute-start(s16[208,256]{1,0:T(8,128)(2,1)S(1)} %get-tuple-element.63), channel_id=1, source_target_pairs={{0,8},{4,12},{8,0},{12,4},{1,9},{5,13},{9,1},{13,5},{2,10},{6,14},... | collective-permute-start | bytes 319496 | tf_op jit(solution)/shard_map/ppermute | solution.py:152
  26.1 9.8 %collective-permute-start.5 = (s16[208,256]{1,0:T(8,128)(2,1)S(1)}, s16[208,256]{1,0:T(8,128)(2,1)S(1)}, u32[]{:S(2)}, u32[]{:S(2)}) collective-permute-start(s16[208,256]{1,0:T(8,128)(2,1)S(1)} %get-tuple-element.64), channel_id=1, source_target_pairs={{0,4},{4,0},{8,12},{12,8},{1,5},{5,1},{9,13},{13,9},{2,6},{6,2},{1... | collective-permute-start | bytes 319496 | tf_op jit(solution)/shard_map/ppermute | solution.py:152
  28.7 4.7 %copy-start = (bf16[4,2,832,208]{3,2,1,0:T(8,128)(2,1)S(1)}, bf16[4,2,832,208]{3,2,1,0:T(8,128)(2,1)}, u32[]{:S(2)}) copy-start(bf16[4,2,832,208]{3,2,1,0:T(8,128)(2,1)} %constant.14.clone.table_ref.rest_0_) | copy-start | bytes 8306692

commit v24 on v21

--- a/solution.py
+++ b/solution.py
@@ -694,7 +694,9 @@
                 value = source_ref[block - start, order]
                 for comp in range(2):
                     product = (value * scaled[comp]).reshape(points // 8, 8, LANES)
-                    sums[pl.ds((order * 2 + comp) * 8, 8)] = product.sum(axis=0)
+                    middle = (points // 8 + 1) // 2
+                    total = product[:middle].sum(axis=0) + product[middle:].sum(axis=0)
+                    sums[pl.ds((order * 2 + comp) * 8, 8)] = total
         reduced(block)
         return carry
 

time: 43.9 us -> 43.6 us (level)
  Pallas kernels: 25.6 us -> 24.9 us
  transfers between devices with their start and end apart: 7 -> 7, of which waited for: 1 -> 1; matrix products, arithmetic and copies ran while one was open for 0% -> 0% of each run, Pallas kernels for 19% -> 18%
where the time goes in v24:
time: 43.6 us; the launch traced here: 43.7 us
  Pallas kernels  24.9 us (57%)
  starting transfers between devices  13.8 us (32%)
  waiting for transfers between devices  4.84 us (11%)
    pallas_call x1, Pallas kernels, legendre(): pl.pallas_call(functools.partial(legendre_kernel, early), out_shape=jax.S...  8.47 us
    ppermute x6, starting transfers between devices, exchange(): lax.ppermute(blocks[step], axis, pairs[step])  7.61 us
    all_to_all x1, starting transfers between devices, shards(): lax.all_to_all(edges, ('lat', *axes), split_axis=0, concat_axis=0, tiled=...  6.16 us
    pallas_call x1, Pallas kernels, advect(): pl.pallas_call(functools.partial(advect_kernel, ring, lat_count), out_sha...  5.56 us
    pallas_call x1, Pallas kernels, sweep(): pl.pallas_call(sweep_kernel, out_shape=[jax.ShapeDtypeStruct(beta.shape,...  5.05 us
    all_to_all x1, waiting for transfers between devices, shards(): lax.all_to_all(edges, ('lat', *axes), split_axis=0, concat_axis=0, tiled=...  4.83 us
    pallas_call x1, Pallas kernels, fourier(): pl.pallas_call(functools.partial(fourier_kernel, ring, lat_count, pieces,...  2.88 us
    pallas_call x1, Pallas kernels, prepare_places(): pl.pallas_call(functools.partial(places_kernel, groups), out_shape=[jax.S...  1.78 us
  transfers between devices with their start and end apart: 7, of which 1 were waited for; matrix products, arithmetic and copies ran while one was open for 0% of the time, Pallas kernels for 18%

profile of v24, /device:TPU:0, one launch (start us, length us, event | category | flops | bytes accessed | tf_op | source)
XLA Modules:
  0.0 43.7 jit_solution(8523868793358881055)
XLA Ops:
  0.0 5.6 %shard_map.100 = (s16[208,512]{1,0:T(8,128)(2,1)}, s16[208,512]{1,0:T(8,128)(2,1)}, s16[208,512]{1,0:T(8,128)(2,1)}, s16[208,512]{1,0:T(8,128)(2,1)}, f32[16,1,400]{2,1,0:T(1,128)}) custom-call(s32[1,200]{1,0:T(1,128)} %bitcast.4, bf16[4,200,400]{2,1,0:T(8,128)(2,1)} %tracer_hbm.1, bf16[4,200,400]{2,1,0:T(8,128)(2,1)} %east_hbm.1, bf16[4,200,400]{2,1,0:T(8,128)(2,1)} %north_hbm.1), custom_call_target="tpu_custom_call" | custom-call | flops 5000000000 | bytes 2560000 | tf_op jit(solution)/shard_map/pallas_call | solution.py:232
  5.6 0.0 copy-start.3
  5.6 0.0 copy-start.4
  5.6 0.0 copy-start.5
  5.6 0.0 copy-start.6
  5.6 0.5 %collective-permute-start = (s16[208,512]{1,0:T(8,128)(2,1)}, s16[208,512]{1,0:T(8,128)(2,1)S(1)}, u32[]{:S(2)}, u32[]{:S(2)}) collective-permute-start(s16[208,512]{1,0:T(8,128)(2,1)} %get-tuple-element.40), channel_id=1, source_target_pairs={{0,1},{1,0},{2,3},{3,2},{4,5},{5,4},{6,7},{7,6},{8,9},{9,8},{10,11... | collective-permute-start | bytes 638984 | tf_op jit(solution)/shard_map/ppermute | solution.py:147
  6.1 2.6 %collective-permute-start.1 = (s16[208,512]{1,0:T(8,128)(2,1)}, s16[208,512]{1,0:T(8,128)(2,1)S(1)}, u32[]{:S(2)}, u32[]{:S(2)}) collective-permute-start(s16[208,512]{1,0:T(8,128)(2,1)} %get-tuple-element.41), channel_id=1, source_target_pairs={{0,2},{1,3},{2,0},{3,1},{4,6},{5,7},{6,4},{7,5},{8,10},{9,11},{10,... | collective-permute-start | bytes 638984 | tf_op jit(solution)/shard_map/ppermute | solution.py:147
  8.7 0.1 collective-permute-start.2
  8.8 6.2 %all-to-all-start = ((f32[16,1,400]{2,1,0:T(1,128)}), f32[16,1,400]{2,1,0:T(1,128)S(1)}, u32[]{:S(2)}, u32[]{:S(2)}) async-start(f32[16,1,400]{2,1,0:T(1,128)} %get-tuple-element.43), calls=%async_computation | async-start | bytes 65536 | tf_op jit(solution)/shard_map/all_to_all | solution.py:796
  15.0 1.8 %shard_map.101 = (f32[1,512]{1,0:T(1,128)S(1)}, f32[2,128]{1,0:T(2,128)S(1)}, f32[832,128]{1,0:T(8,128)S(1)}, f32[4,104,128]{2,1,0:T(8,128)S(1)}, bf16[128,128]{1,0:T(8,128)(2,1)S(1)}) custom-call(s32[1,400]{1,0:T(1,128)S(1)} %bitcast.3, f32[3,104,128]{2,1,0:T(8,128)S(1)} %copy-done.1), custom_call_target="tpu_custom_call" | custom-call | flops 2000000000 | bytes 1048576 | tf_op jit(solution)/shard_map/pallas_call | solution.py:455
  16.8 4.8 %all-to-all-done.rest_4_ = f32[16,1,400]{2,1,0:T(1,128)S(1)} async-done(((f32[16,1,400]{2,1,0:T(1,128)}), f32[16,1,400]{2,1,0:T(1,128)S(1)}, u32[]{:S(2)}, u32[]{:S(2)}) %all-to-all-start) | async-done | bytes 25632 | tf_op jit(solution)/shard_map/all_to_all | solution.py:796
  21.6 0.0 collective-permute-done.rest_1_
  21.6 0.0 collective-permute-done.1.rest_2_
  21.6 0.0 collective-permute-done.2.rest_3_
  21.6 2.9 %shard_map.102 = (s16[336,128]{1,0:T(8,128)(2,1)S(1)}, s16[336,128]{1,0:T(8,128)(2,1)S(1)}, s16[336,128]{1,0:T(8,128)(2,1)S(1)}, s16[336,128]{1,0:T(8,128)(2,1)S(1)}) custom-call(s16[208,512]{1,0:T(8,128)(2,1)S(1)} %copy-done.6, s16[208,512]{1,0:T(8,128)(2,1)S(1)} %collective-permute-done.rest_1_, s16[208,512]{1,0:T(8,128)(2,1)S(1)} %collective-permute-done.1.rest_2_, ...), custom_call_target="tpu_custom_call" | custom-call | flops 4000000000 | bytes 6291456 | tf_op jit(solution)/shard_map/pallas_call | solution.py:400
  24.5 0.4 collective-permute-start.3
  24.9 2.1 %collective-permute-start.4 = (s16[336,128]{1,0:T(8,128)(2,1)S(1)}, s16[336,128]{1,0:T(8,128)(2,1)S(1)}, u32[]{:S(2)}, u32[]{:S(2)}) collective-permute-start(s16[336,128]{1,0:T(8,128)(2,1)S(1)} %get-tuple-element.63), channel_id=1, source_target_pairs={{0,8},{4,12},{8,0},{12,4},{1,9},{5,13},{9,1},{13,5},{2,10},{6,14},... | collective-permute-start | bytes 258056 | tf_op jit(solution)/shard_map/ppermute | solution.py:147
  27.1 1.9 %collective-permute-start.5 = (s16[336,128]{1,0:T(8,128)(2,1)S(1)}, s16[336,128]{1,0:T(8,128)(2,1)S(1)}, u32[]{:S(2)}, u32[]{:S(2)}) collective-permute-start(s16[336,128]{1,0:T(8,128)(2,1)S(1)} %get-tuple-element.64), channel_id=1, source_target_pairs={{0,12},{4,8},{8,4},{12,0},{1,13},{5,9},{9,5},{13,1},{2,14},{6,10},... | collective-permute-start | bytes 258056 | tf_op jit(solution)/shard_map/ppermute | solution.py:147
  29.0 5.0 %shard_map.103 = (f32[832,128]{1,0:T(8,128)S(1)}, f32[26,128]{1,0:T(8,128)S(1)}, f32[3,104,128]{2,1,0:T(8,128)S(1)}, f32[13,32,104,128]{3,2,1,0:T(8,128)S(1)}, f32[3,32,104,128]{3,2,1,0:T(8,128)S(1)}) custom-call(f32[2,128]{1,0:T(2,128)S(1)} %get-tuple-element.53.mine_ref.rest_11_, f32[3,104,128]{2,1,0:T(8,128)S(1)} %copy-done.1, ...), custom_call_target="tpu_custom_call" | custom-call | flops 5000000000 | bytes 26214400 | tf_op jit(solution)/shard_map/pallas_call | solution.py:590
  34.0 0.0 collective-permute-done.3.rest_1_
  34.0 1.2 %shard_map.104.rest_10_ = f32[832,256]{1,0:T(8,128)S(1)} custom-call(bf16[4,2,832,208]{3,2,1,0:T(8,128)(2,1)S(1)} %copy-done, s16[336,128]{1,0:T(8,128)(2,1)S(1)} %get-tuple-element.61.rest_0_, s16[336,128]{1,0:T(8,128)(2,1)S(1)} %collective-permute-done.3.rest_1_), custom_call_target="tpu_custom_call" | custom-call | flops 1000000000 | bytes 4194304 | tf_op jit(solution)/shard_map/pallas_call | solution.py:639
  35.2 0.0 collective-permute-done.4.rest_12_
  35.2 0.0 collective-permute-done.5.rest_13_
  35.2 8.5 %shard_map.105 = f32[100,2,400]{2,1,0:T(2,128)} custom-call(bf16[4,2,832,208]{3,2,1,0:T(8,128)(2,1)S(1)} %copy-done, f32[3,104,128]{2,1,0:T(8,128)S(1)} %copy-done.1, f32[832,128]{1,0:T(8,128)S(1)} %get-tuple-element.52.beta_ref.rest_2_, f32[832,128]{1,0:T(8,128)S(1)} %get-tuple-element.55.rest_3_, f32[26,128]{1,0:T(8,128)S(1)} %get-tuple-element.56.rest_4_, ...), custom_call_target="tpu_custom_call" | custom-call | flops 8000000000 | bytes 6291456 | tf_op jit(solution)/shard_map/pallas_call | solution.py:767
  (10 shorter events, 0.0 us)
Async XLA Ops:
  0.0 14.9 %copy-start.1 = (f32[3,104,128]{2,1,0:T(8,128)S(1)}, f32[3,104,128]{2,1,0:T(8,128)}, u32[]{:S(2)}) copy-start(f32[3,104,128]{2,1,0:T(8,128)} %constant.10.clone.lat_ref.rest_1_) | copy-start | bytes 479236
  0.0 15.0 %copy-start.2 = (s32[400]{0:T(512)S(1)}, s32[400]{0:T(512)}, u32[]{:S(2)}) copy-start(s32[400]{0:T(512)} %param.14) | copy-start | bytes 4804
  5.6 16.0 %copy-start.3 = (bf16[1,400,1024]{2,1,0:T(8,128)(2,1)S(1)}, bf16[1,400,1024]{2,1,0:T(8,128)(2,1)}, u32[]{:S(2)}) copy-start(bf16[1,400,1024]{2,1,0:T(8,128)(2,1)} %constant.13.clone.rest_7_) | copy-start | bytes 2457604
  5.6 16.0 %copy-start.4 = (bf16[1,400,512]{2,1,0:T(8,128)(2,1)S(1)}, bf16[1,400,512]{2,1,0:T(8,128)(2,1)}, u32[]{:S(2)}) copy-start(bf16[1,400,512]{2,1,0:T(8,128)(2,1)} %constant.12.clone.rest_6_) | copy-start | bytes 1228804
  5.6 16.0 %copy-start.5 = (bf16[1,400,512]{2,1,0:T(8,128)(2,1)S(1)}, bf16[1,400,512]{2,1,0:T(8,128)(2,1)}, u32[]{:S(2)}) copy-start(bf16[1,400,512]{2,1,0:T(8,128)(2,1)} %constant.11.clone.rest_5_) | copy-start | bytes 1228804
  5.6 16.0 %copy-start.6 = (s16[208,512]{1,0:T(8,128)(2,1)S(1)}, s16[208,512]{1,0:T(8,128)(2,1)}, u32[]{:S(2)}) copy-start(s16[208,512]{1,0:T(8,128)(2,1)} %get-tuple-element.39.rest_0_) | copy-start | bytes 638980
  5.6 16.0 %collective-permute-start = (s16[208,512]{1,0:T(8,128)(2,1)}, s16[208,512]{1,0:T(8,128)(2,1)S(1)}, u32[]{:S(2)}, u32[]{:S(2)}) collective-permute-start(s16[208,512]{1,0:T(8,128)(2,1)} %get-tuple-element.40), channel_id=1, source_target_pairs={{0,1},{1,0},{2,3},{3,2},{4,5},{5,4},{6,7},{7,6},{8,9},{9,8},{10,11... | collective-permute-start | bytes 638984 | tf_op jit(solution)/shard_map/ppermute | solution.py:147
  6.1 15.4 %collective-permute-start.1 = (s16[208,512]{1,0:T(8,128)(2,1)}, s16[208,512]{1,0:T(8,128)(2,1)S(1)}, u32[]{:S(2)}, u32[]{:S(2)}) collective-permute-start(s16[208,512]{1,0:T(8,128)(2,1)} %get-tuple-element.41), channel_id=1, source_target_pairs={{0,2},{1,3},{2,0},{3,1},{4,6},{5,7},{6,4},{7,5},{8,10},{9,11},{10,... | collective-permute-start | bytes 638984 | tf_op jit(solution)/shard_map/ppermute | solution.py:147
  8.7 12.9 %collective-permute-start.2 = (s16[208,512]{1,0:T(8,128)(2,1)}, s16[208,512]{1,0:T(8,128)(2,1)S(1)}, u32[]{:S(2)}, u32[]{:S(2)}) collective-permute-start(s16[208,512]{1,0:T(8,128)(2,1)} %get-tuple-element.42), channel_id=1, source_target_pairs={{0,3},{1,2},{2,1},{3,0},{4,7},{5,6},{6,5},{7,4},{8,11},{9,10},{10,... | collective-permute-start | bytes 638984 | tf_op jit(solution)/shard_map/ppermute | solution.py:147
  8.8 12.8 %all-to-all-start = ((f32[16,1,400]{2,1,0:T(1,128)}), f32[16,1,400]{2,1,0:T(1,128)S(1)}, u32[]{:S(2)}, u32[]{:S(2)}) async-start(f32[16,1,400]{2,1,0:T(1,128)} %get-tuple-element.43), calls=%async_computation | async-start | bytes 65536 | tf_op jit(solution)/shard_map/all_to_all | solution.py:796
  24.5 9.5 %collective-permute-start.3 = (s16[336,128]{1,0:T(8,128)(2,1)S(1)}, s16[336,128]{1,0:T(8,128)(2,1)S(1)}, u32[]{:S(2)}, u32[]{:S(2)}) collective-permute-start(s16[336,128]{1,0:T(8,128)(2,1)S(1)} %get-tuple-element.62), channel_id=1, source_target_pairs={{0,4},{4,0},{8,12},{12,8},{1,5},{5,1},{9,13},{13,9},{2,6},{6,2},{1... | collective-permute-start | bytes 258056 | tf_op jit(solution)/shard_map/ppermute | solution.py:147
  24.9 10.3 %collective-permute-start.4 = (s16[336,128]{1,0:T(8,128)(2,1)S(1)}, s16[336,128]{1,0:T(8,128)(2,1)S(1)}, u32[]{:S(2)}, u32[]{:S(2)}) collective-permute-start(s16[336,128]{1,0:T(8,128)(2,1)S(1)} %get-tuple-element.63), channel_id=1, source_target_pairs={{0,8},{4,12},{8,0},{12,4},{1,9},{5,13},{9,1},{13,5},{2,10},{6,14},... | collective-permute-start | bytes 258056 | tf_op jit(solution)/shard_map/ppermute | solution.py:147
  27.1 8.1 %collective-permute-start.5 = (s16[336,128]{1,0:T(8,128)(2,1)S(1)}, s16[336,128]{1,0:T(8,128)(2,1)S(1)}, u32[]{:S(2)}, u32[]{:S(2)}) collective-permute-start(s16[336,128]{1,0:T(8,128)(2,1)S(1)} %get-tuple-element.64), channel_id=1, source_target_pairs={{0,12},{4,8},{8,4},{12,0},{1,13},{5,9},{9,5},{13,1},{2,14},{6,10},... | collective-permute-start | bytes 258056 | tf_op jit(solution)/shard_map/ppermute | solution.py:147
  29.0 5.1 %copy-start = (bf16[4,2,832,208]{3,2,1,0:T(8,128)(2,1)S(1)}, bf16[4,2,832,208]{3,2,1,0:T(8,128)(2,1)}, u32[]{:S(2)}) copy-start(bf16[4,2,832,208]{3,2,1,0:T(8,128)(2,1)} %constant.14.clone.table_ref.rest_0_) | copy-start | bytes 8306692
